TPU v7x, 32 devices: a whole 2x2x4 slice. The times are simulated.
32 devices in a mesh: ctx: 8 (over z, x), tp: 4 (over y, core).
Axes of the slice: x: 2, y: 2, z: 4, core: 2. Of those that a mesh axis runs over, the one named last changes fastest.
Arguments:
- trace_q: bfloat16 [1024, 5120], P(('ctx', 'tp')), may hold values from -120 to 120
- trace_key_value: bfloat16 [1024, 2048], P(('ctx', 'tp')), may hold values from -6 to 6
- suffix_q: bfloat16 [8, 128, 5120], P('ctx', 'tp'), may hold values from -120 to 120
- suffix_key_value: bfloat16 [8, 128, 2048], P('ctx', 'tp'), may hold values from -6 to 6
- prefix_len: int32 [8], P('ctx'), may hold values from 256 to 1024, as said below
- del_start: int32 [8], P('ctx'), may hold values from 0 to 1023, as said below
- del_end: int32 [8], P('ctx'), may hold values from 1 to 1024, as said below
Outputs:
- trace_out: bfloat16 [1024, 5120], P(('ctx', 'tp'))
- suffix_out: bfloat16 [8, 128, 5120], P('ctx', 'tp')
Inputs may be any that keep to these rules, and one draw needn't show every extreme that they name: `prefix_len`: one variant keeps the whole trace as prefix and deletes only its last position. del_start < prefix_len of the same variant. del_start < del_end <= prefix_len of the same variant, and del_end - del_start <= 128.
All inputs are finite; a program needn't handle non-finite values.
Results may differ from a plain program's by a relative error of at most 0.0075.
Values may be sent and summed in bfloat16 or wider, within the bound.
No kernel may reach another device: no remote copies, remote signals or barrier semaphores. Data moves between devices by JAX's collectives and lax.ppermute only.
A program may use at most 192 MiB of HBM per device.

v0:
```python
import functools

import jax
import jax.numpy as jnp
from jax import lax
from jax.experimental import pallas as pl
from jax.experimental.pallas import tpu as pltpu
from jax.sharding import PartitionSpec as P

QUERY_HEADS = 40
KEY_VALUE_HEADS = 8
HEAD_SIZE = 128
GROUP = QUERY_HEADS // KEY_VALUE_HEADS
PAIR = 2 * HEAD_SIZE
LOG2E = 1.4426950408889634
SCALE = HEAD_SIZE ** (-0.5) * LOG2E
MASKED = -1e30
CHUNK_ROWS = 1024


def dot_t(a, b):
    return lax.dot_general(a, b, (((1,), (1,)), ((), ())), preferred_element_type=jnp.float32)


def dot(a, b):
    return lax.dot_general(a, b, (((1,), (0,)), ((), ())), preferred_element_type=jnp.float32)


def attend_kernel(piece_rows, first_call, last_call, *refs):
    refs = list(refs)
    starts, place, span = refs[:3]
    tq, sq = refs[3:5]
    del refs[:5]
    own_pieces = []
    if first_call:
        own_pieces, refs = refs[:4], refs[4:]
    pieces, refs = refs[: len(piece_rows)], refs[len(piece_rows):]
    if not first_call:
        m_in, l_in, acc_in = refs[:3]
        del refs[:3]
    if last_call:
        t_out, s_out = refs[:2]
        del refs[:2]
    else:
        m_out, l_out, acc_out = refs[:3]
        del refs[:3]
    kv, sems = refs

    rows = tq.shape[0]
    total = sum(piece_rows)
    copies, at = [], 0
    for index, (piece, size) in enumerate(zip(pieces, piece_rows)):
        copies.append(pltpu.make_async_copy(piece, kv.at[pl.ds(at, size)], sems.at[index]))
        at += size
    for index, piece in enumerate(own_pieces):
        copies.append(
            pltpu.make_async_copy(piece, kv.at[pl.ds(at, rows)], sems.at[len(piece_rows) + index])
        )
        at += rows
    for copy in copies:
        copy.start()

    first_position = place[0]
    suffix_row = place[1]
    prefix, del_start, del_end = span[0], span[1], span[2]
    lanes = 128
    lane = lax.broadcasted_iota(jnp.int32, (rows, lanes), 1)
    row = lax.broadcasted_iota(jnp.int32, (rows, lanes), 0)
    q_trace_aug = jnp.where(lane == row, 1.0, 0.0).astype(jnp.bfloat16)
    q_suffix_aug = jnp.where((lane == rows) | (lane == rows + 1 + row), 1.0, 0.0).astype(jnp.bfloat16)
    q_aug = jnp.concatenate([q_trace_aug] * GROUP + [q_suffix_aug] * GROUP, axis=0)
    k_aug = []
    for index, size in enumerate(piece_rows):
        lane_k = lax.broadcasted_iota(jnp.int32, (size, lanes), 1)
        position = starts[index] + lax.broadcasted_iota(jnp.int32, (size, lanes), 0)
        hidden_trace = (lane_k < rows) & (position > first_position + lane_k)
        hidden_suffix = (lane_k == rows) & (
            (position >= prefix) | ((position >= del_start) & (position < del_end))
        )
        k_aug.append(jnp.where(hidden_trace | hidden_suffix, MASKED, 0.0).astype(jnp.bfloat16))
    k_aug = jnp.concatenate(k_aug, axis=0)
    if first_call:
        own_aug = []
        for index in range(len(own_pieces)):
            position = place[2 + index] + row
            hidden = (lane > rows) & (position > suffix_row + (lane - rows - 1))
            own_aug.append(jnp.where(hidden, MASKED, 0.0).astype(jnp.bfloat16))
        own_aug = jnp.concatenate(own_aug, axis=0)
        own_total = rows * len(own_pieces)
        own_ones = jnp.ones((own_total, HEAD_SIZE), jnp.bfloat16)
    ones = jnp.ones((total, HEAD_SIZE), jnp.bfloat16)
    for copy in copies:
        copy.wait()

    half = GROUP * rows
    for g in range(KEY_VALUE_HEADS):
        def heads(ref):
            return [ref[:, (g * GROUP + j) * HEAD_SIZE:(g * GROUP + j + 1) * HEAD_SIZE] for j in range(GROUP)]

        query = jnp.concatenate(heads(tq) + heads(sq), axis=0)
        query = jnp.concatenate([query, q_aug], axis=1)
        key = kv[0:total, g * PAIR:g * PAIR + HEAD_SIZE]
        value = kv[0:total, g * PAIR + HEAD_SIZE:(g + 1) * PAIR]
        scores = dot_t(query, jnp.concatenate([key, k_aug], axis=1))
        top = jnp.max(scores, axis=1, keepdims=True)
        if first_call:
            own_key = kv[total:total + own_total, g * PAIR:g * PAIR + HEAD_SIZE]
            own_value = kv[total:total + own_total, g * PAIR + HEAD_SIZE:(g + 1) * PAIR]
            own_scores = dot_t(query[half:], jnp.concatenate([own_key, own_aug], axis=1))
            own_top = jnp.maximum(top[half:], jnp.max(own_scores, axis=1, keepdims=True))
            top = jnp.concatenate([top[:half], own_top], axis=0)
        else:
            old = m_in[g * 2 * half:(g + 1) * 2 * half, :]
            top = jnp.maximum(old, top)
        weights = jnp.exp2((scores - top[:, 0:1]) * SCALE).astype(jnp.bfloat16)
        both = dot(weights, jnp.concatenate([value, ones], axis=1))
        summed, denominator = both[:, :HEAD_SIZE], both[:, HEAD_SIZE:]
        if first_call:
            own_weights = jnp.exp2((own_scores - top[half:]) * SCALE).astype(jnp.bfloat16)
            own_both = dot(own_weights, jnp.concatenate([own_value, own_ones], axis=1))
            summed = jnp.concatenate([summed[:half], summed[half:] + own_both[:, :HEAD_SIZE]], axis=0)
            denominator = jnp.concatenate(
                [denominator[:half], denominator[half:] + own_both[:, HEAD_SIZE:]], axis=0
            )
        else:
            here = slice(g * 2 * half, (g + 1) * 2 * half)
            rescale = jnp.exp2((old - top) * SCALE)
            summed = summed + acc_in[here, :] * rescale
            denominator = denominator + l_in[here, :] * rescale
        if last_call:
            result = (summed / denominator).astype(jnp.bfloat16)
            for j in range(GROUP):
                columns = slice((g * GROUP + j) * HEAD_SIZE, (g * GROUP + j + 1) * HEAD_SIZE)
                t_out[:, columns] = result[j * rows:(j + 1) * rows]
                s_out[:, columns] = result[half + j * rows:half + (j + 1) * rows]
        else:
            here = slice(g * 2 * half, (g + 1) * 2 * half)
            m_out[here, :] = jnp.broadcast_to(top, (2 * half, HEAD_SIZE))
            l_out[here, :] = denominator
            acc_out[here, :] = summed


def attend(starts, place, span, tq, sq, own_pieces, pieces, carry, last_call):
    first_call = carry is None
    piece_rows = tuple(p.shape[0] for p in pieces)
    rows = tq.shape[0]
    own_count = 4 if first_call else 0
    smem = pl.BlockSpec(memory_space=pltpu.SMEM)
    vmem = pl.BlockSpec(memory_space=pltpu.VMEM)
    hbm = pl.BlockSpec(memory_space=pl.ANY)
    operands = [starts, place, span, tq, sq]
    in_specs = [smem, smem, smem, vmem, vmem]
    if first_call:
        operands += list(own_pieces)
        in_specs += [hbm] * own_count
    operands += list(pieces)
    in_specs += [hbm] * len(pieces)
    if not first_call:
        operands += list(carry)
        in_specs += [vmem] * 3
    if last_call:
        out_shape = [jax.ShapeDtypeStruct(tq.shape, jnp.bfloat16)] * 2
    else:
        state = jax.ShapeDtypeStruct((2 * QUERY_HEADS * rows, HEAD_SIZE), jnp.float32)
        out_shape = [state] * 3
    all_rows = sum(piece_rows) + own_count * rows
    flops = 2 * 2 * QUERY_HEADS * rows * all_rows * PAIR * 2
    return pl.pallas_call(
        functools.partial(attend_kernel, piece_rows, first_call, last_call),
        out_shape=out_shape,
        in_specs=in_specs,
        out_specs=[vmem] * len(out_shape),
        scratch_shapes=[
            pltpu.VMEM((all_rows, tq.shape[1] // GROUP * 2), jnp.bfloat16),
            pltpu.SemaphoreType.DMA((len(pieces) + own_count,)),
        ],
        compiler_params=pltpu.CompilerParams(vmem_limit_bytes=48 * 1024 * 1024),
        cost_estimate=pl.CostEstimate(
            flops=flops, bytes_accessed=all_rows * 4096, transcendentals=2 * QUERY_HEADS * rows * all_rows
        ),
    )(*operands)


def swap(array, axis, bit, size):
    return lax.ppermute(array, axis, [(i, i ^ bit) for i in range(size)])


def local(ctx_size, tp_size, trace_q, trace_key_value, suffix_q, suffix_key_value, prefix_len, del_start, del_end):
    rows = trace_q.shape[0]
    ctx = lax.axis_index("ctx").astype(jnp.int32)
    tp = lax.axis_index("tp").astype(jnp.int32)
    span = jnp.concatenate([prefix_len, del_start, del_end])
    sq = suffix_q[0]
    suffix_own = suffix_key_value[0]

    core = lambda a: swap(a, "tp", 1, tp_size)
    across_y = lambda a: swap(a, "tp", 2, tp_size)
    across_x = lambda a: swap(a, "ctx", 1, ctx_size)

    suffix_y = across_y(suffix_own)
    suffix_pieces = [suffix_own, suffix_y, core(suffix_own), core(suffix_y)]
    suffix_tp = [tp, tp ^ 2, tp ^ 1, tp ^ 3]
    place = jnp.stack([(ctx * tp_size + tp) * rows, tp * rows] + [t * rows for t in suffix_tp])

    if ctx_size == 8:
        planes = ctx_size // 2
        pieces, starts = [], []

        def add(piece, piece_ctx, piece_tp):
            pieces.append(piece)
            starts.append((piece_ctx * tp_size + piece_tp) * rows)
            pieces.append(core(piece))
            starts.append((piece_ctx * tp_size + (piece_tp ^ 1)) * rows)

        for shift in (0, 1, 3, 2):
            if shift == 0:
                mine = trace_key_value
            else:
                mine = lax.ppermute(
                    trace_key_value, "ctx", [(i, (i + 2 * shift) % ctx_size) for i in range(ctx_size)]
                )
            source = (ctx - 2 * shift) % ctx_size
            from_x = across_x(mine)
            from_y = across_y(mine)
            diagonal = across_x(from_y) if shift in (0, 1) else across_y(from_x)
            add(mine, source, tp)
            add(from_x, source ^ 1, tp)
            add(from_y, source, tp ^ 2)
            add(diagonal, source ^ 1, tp ^ 2)
        groups = [(pieces, jnp.stack(starts))]
    else:
        gathered = lax.all_gather(trace_key_value, ("ctx", "tp"), axis=0, tiled=True)
        groups = [
            ([gathered[at:at + CHUNK_ROWS]], jnp.full((1,), at, jnp.int32))
            for at in range(0, gathered.shape[0], CHUNK_ROWS)
        ]

    carry = None
    for index, (group, group_starts) in enumerate(groups):
        carry = attend(
            group_starts, place, span, trace_q, sq, suffix_pieces, group, carry, index == len(groups) - 1
        )
    trace_out, suffix_out = carry
    return trace_out, suffix_out[None]


def solution(mesh):
    return jax.shard_map(
        functools.partial(local, mesh.shape["ctx"], mesh.shape["tp"]),
        mesh=mesh,
        in_specs=(
            P(("ctx", "tp"), None),
            P(("ctx", "tp"), None),
            P("ctx", "tp", None),
            P("ctx", "tp", None),
            P("ctx"),
            P("ctx"),
            P("ctx"),
        ),
        out_specs=(P(("ctx", "tp"), None), P("ctx", "tp", None)),
        check_vma=False,
    )
```

profile of v0, /device:TPU:1, one launch (start us, length us, event | category | flops | bytes accessed | tf_op | source)
XLA Modules:
  0.0 63.5 jit_solution(10800650060797570886)
XLA Ops:
  0.8 2.7 %collective-permute-start = (bf16[32,2048]{1,0:T(8,128)(2,1)}, bf16[32,2048]{1,0:T(8,128)(2,1)S(1)}, u32[]{:S(2)}, u32[]{:S(2)}) collective-permute-start(bf16[32,2048]{1,0:T(8,128)(2,1)} %bitcast.42), channel_id=1, source_target_pairs={{0,2},{1,3},{2,0},{3,1},{4,6},{5,7},{6,4},{7,5},{8,10},{9,11},{10,... | collective-permute-start | bytes 393224 | tf_op jit(solution)/shard_map/ppermute | solution.py:185
  3.5 3.3 %collective-permute-start.18 = (bf16[32,2048]{1,0:T(8,128)(2,1)}, bf16[32,2048]{1,0:T(8,128)(2,1)S(1)}, u32[]{:S(2)}, u32[]{:S(2)}) collective-permute-start(bf16[32,2048]{1,0:T(8,128)(2,1)} %refs_9_.1), channel_id=1, source_target_pairs={{0,24},{4,28},{8,0},{12,4},{16,8},{20,12},{24,16},{28,20},{1,25},{... | collective-permute-start | bytes 393224 | tf_op jit(solution)/shard_map/ppermute | solution.py:219
  7.0 1.2 %collective-permute-start.4 = (bf16[32,2048]{1,0:T(8,128)(2,1)}, bf16[32,2048]{1,0:T(8,128)(2,1)S(1)}, u32[]{:S(2)}, u32[]{:S(2)}) collective-permute-start(bf16[32,2048]{1,0:T(8,128)(2,1)} %refs_9_.1), channel_id=1, source_target_pairs={{0,4},{4,0},{8,12},{12,8},{16,20},{20,16},{24,28},{28,24},{1,5},{5... | collective-permute-start | bytes 393224 | tf_op jit(solution)/shard_map/ppermute | solution.py:185
  8.2 1.2 %collective-permute-start.3 = (bf16[32,2048]{1,0:T(8,128)(2,1)}, bf16[32,2048]{1,0:T(8,128)(2,1)S(1)}, u32[]{:S(2)}, u32[]{:S(2)}) collective-permute-start(bf16[32,2048]{1,0:T(8,128)(2,1)} %refs_9_.1), channel_id=1, source_target_pairs={{0,1},{1,0},{2,3},{3,2},{4,5},{5,4},{6,7},{7,6},{8,9},{9,8},{10,11... | collective-permute-start | bytes 393224 | tf_op jit(solution)/shard_map/ppermute | solution.py:185
  9.7 1.0 %collective-permute-start.26 = (bf16[32,2048]{1,0:T(8,128)(2,1)}, bf16[32,2048]{1,0:T(8,128)(2,1)S(1)}, u32[]{:S(2)}, u32[]{:S(2)}) collective-permute-start(bf16[32,2048]{1,0:T(8,128)(2,1)} %refs_9_.1), channel_id=1, source_target_pairs={{0,16},{4,20},{8,24},{12,28},{16,0},{20,4},{24,8},{28,12},{1,17},{... | collective-permute-start | bytes 393224 | tf_op jit(solution)/shard_map/ppermute | solution.py:219
  10.7 2.5 %collective-permute-done.10.refs_17_ = bf16[32,2048]{1,0:T(8,128)(2,1)S(1)} collective-permute-done((bf16[32,2048]{1,0:T(8,128)(2,1)}, bf16[32,2048]{1,0:T(8,128)(2,1)S(1)}, u32[]{:S(2)}, u32[]{:S(2)}) %collective-permute-start.10) | collective-permute-done | bytes 131104 | tf_op jit(solution)/shard_map/ppermute | solution.py:219
  13.2 1.6 %collective-permute-start.2 = (bf16[32,2048]{1,0:T(8,128)(2,1)S(1)}, bf16[32,2048]{1,0:T(8,128)(2,1)S(1)}, u32[]{:S(2)}, u32[]{:S(2)}) collective-permute-start(bf16[32,2048]{1,0:T(8,128)(2,1)S(1)} %collective-permute-done.refs_6_), channel_id=1, source_target_pairs={{0,1},{1,0},{2,3},{3,2},{4,5},{5,4},{6,7},{7,6},{8,9},{9,8},{10,11... | collective-permute-start | bytes 393224 | tf_op jit(solution)/shard_map/ppermute | solution.py:185
  14.9 1.3 %collective-permute-start.20 = (bf16[32,2048]{1,0:T(8,128)(2,1)S(1)}, bf16[32,2048]{1,0:T(8,128)(2,1)S(1)}, u32[]{:S(2)}, u32[]{:S(2)}) collective-permute-start(bf16[32,2048]{1,0:T(8,128)(2,1)S(1)} %collective-permute-done.18.refs_25_), channel_id=1, source_target_pairs={{0,4},{4,0},{8,12},{12,8},{16,20},{20,16},{24,28},{28,24},{1,5},{5... | collective-permute-start | bytes 393224 | tf_op jit(solution)/shard_map/ppermute | solution.py:185
  16.8 2.2 %collective-permute-done.26.refs_33_ = bf16[32,2048]{1,0:T(8,128)(2,1)S(1)} collective-permute-done((bf16[32,2048]{1,0:T(8,128)(2,1)}, bf16[32,2048]{1,0:T(8,128)(2,1)S(1)}, u32[]{:S(2)}, u32[]{:S(2)}) %collective-permute-start.26) | collective-permute-done | bytes 131104 | tf_op jit(solution)/shard_map/ppermute | solution.py:219
  19.0 1.4 %collective-permute-start.12 = (bf16[32,2048]{1,0:T(8,128)(2,1)S(1)}, bf16[32,2048]{1,0:T(8,128)(2,1)S(1)}, u32[]{:S(2)}, u32[]{:S(2)}) collective-permute-start(bf16[32,2048]{1,0:T(8,128)(2,1)S(1)} %collective-permute-done.10.refs_17_), channel_id=1, source_target_pairs={{0,4},{4,0},{8,12},{12,8},{16,20},{20,16},{24,28},{28,24},{1,5},{5... | collective-permute-start | bytes 393224 | tf_op jit(solution)/shard_map/ppermute | solution.py:185
  20.5 1.8 %collective-permute-start.11 = (bf16[32,2048]{1,0:T(8,128)(2,1)S(1)}, bf16[32,2048]{1,0:T(8,128)(2,1)S(1)}, u32[]{:S(2)}, u32[]{:S(2)}) collective-permute-start(bf16[32,2048]{1,0:T(8,128)(2,1)S(1)} %collective-permute-done.10.refs_17_), channel_id=1, source_target_pairs={{0,1},{1,0},{2,3},{3,2},{4,5},{5,4},{6,7},{7,6},{8,9},{9,8},{10,11... | collective-permute-start | bytes 393224 | tf_op jit(solution)/shard_map/ppermute | solution.py:185
  22.9 2.3 %collective-permute-start.5 = (bf16[32,2048]{1,0:T(8,128)(2,1)S(1)}, bf16[32,2048]{1,0:T(8,128)(2,1)S(1)}, u32[]{:S(2)}, u32[]{:S(2)}) collective-permute-start(bf16[32,2048]{1,0:T(8,128)(2,1)S(1)} %collective-permute-done.4.refs_11_), channel_id=1, source_target_pairs={{0,1},{1,0},{2,3},{3,2},{4,5},{5,4},{6,7},{7,6},{8,9},{9,8},{10,11... | collective-permute-start | bytes 393224 | tf_op jit(solution)/shard_map/ppermute | solution.py:185
  25.5 1.2 %collective-permute-start.28 = (bf16[32,2048]{1,0:T(8,128)(2,1)S(1)}, bf16[32,2048]{1,0:T(8,128)(2,1)S(1)}, u32[]{:S(2)}, u32[]{:S(2)}) collective-permute-start(bf16[32,2048]{1,0:T(8,128)(2,1)S(1)} %collective-permute-done.26.refs_33_), channel_id=1, source_target_pairs={{0,4},{4,0},{8,12},{12,8},{16,20},{20,16},{24,28},{28,24},{1,5},{5... | collective-permute-start | bytes 393224 | tf_op jit(solution)/shard_map/ppermute | solution.py:185
  26.7 1.1 %collective-permute-done.8.refs_15_ = bf16[32,2048]{1,0:T(8,128)(2,1)S(1)} collective-permute-done((bf16[32,2048]{1,0:T(8,128)(2,1)S(1)}, bf16[32,2048]{1,0:T(8,128)(2,1)S(1)}, u32[]{:S(2)}, u32[]{:S(2)}) %collective-permute-start.8) | collective-permute-done | bytes 131104 | tf_op jit(solution)/shard_map/ppermute | solution.py:185
  27.9 2.3 %collective-permute-start.27 = (bf16[32,2048]{1,0:T(8,128)(2,1)S(1)}, bf16[32,2048]{1,0:T(8,128)(2,1)S(1)}, u32[]{:S(2)}, u32[]{:S(2)}) collective-permute-start(bf16[32,2048]{1,0:T(8,128)(2,1)S(1)} %collective-permute-done.26.refs_33_), channel_id=1, source_target_pairs={{0,1},{1,0},{2,3},{3,2},{4,5},{5,4},{6,7},{7,6},{8,9},{9,8},{10,11... | collective-permute-start | bytes 393224 | tf_op jit(solution)/shard_map/ppermute | solution.py:185
  31.2 2.2 %collective-permute-start.16 = (bf16[32,2048]{1,0:T(8,128)(2,1)S(1)}, bf16[32,2048]{1,0:T(8,128)(2,1)}, u32[]{:S(2)}, u32[]{:S(2)}) collective-permute-start(bf16[32,2048]{1,0:T(8,128)(2,1)S(1)} %collective-permute-done.14.refs_21_), channel_id=1, source_target_pairs={{0,4},{4,0},{8,12},{12,8},{16,20},{20,16},{24,28},{28,24},{1,5},{5... | collective-permute-start | bytes 393224 | tf_op jit(solution)/shard_map/ppermute | solution.py:185
  33.5 1.7 %collective-permute-start.15 = (bf16[32,2048]{1,0:T(8,128)(2,1)S(1)}, bf16[32,2048]{1,0:T(8,128)(2,1)S(1)}, u32[]{:S(2)}, u32[]{:S(2)}) collective-permute-start(bf16[32,2048]{1,0:T(8,128)(2,1)S(1)} %collective-permute-done.14.refs_21_), channel_id=1, source_target_pairs={{0,1},{1,0},{2,3},{3,2},{4,5},{5,4},{6,7},{7,6},{8,9},{9,8},{10,11... | collective-permute-start | bytes 393224 | tf_op jit(solution)/shard_map/ppermute | solution.py:185
  35.2 0.9 %collective-permute-start.9 = (bf16[32,2048]{1,0:T(8,128)(2,1)S(1)}, bf16[32,2048]{1,0:T(8,128)(2,1)S(1)}, u32[]{:S(2)}, u32[]{:S(2)}) collective-permute-start(bf16[32,2048]{1,0:T(8,128)(2,1)S(1)} %collective-permute-done.8.refs_15_), channel_id=1, source_target_pairs={{0,1},{1,0},{2,3},{3,2},{4,5},{5,4},{6,7},{7,6},{8,9},{9,8},{10,11... | collective-permute-start | bytes 393224 | tf_op jit(solution)/shard_map/ppermute | solution.py:185
  36.4 1.8 %collective-permute-start.29 = (bf16[32,2048]{1,0:T(8,128)(2,1)S(1)}, bf16[32,2048]{1,0:T(8,128)(2,1)}, u32[]{:S(2)}, u32[]{:S(2)}) collective-permute-start(bf16[32,2048]{1,0:T(8,128)(2,1)S(1)} %collective-permute-done.28.refs_35_), channel_id=1, source_target_pairs={{0,1},{1,0},{2,3},{3,2},{4,5},{5,4},{6,7},{7,6},{8,9},{9,8},{10,11... | collective-permute-start | bytes 393224 | tf_op jit(solution)/shard_map/ppermute | solution.py:185
  44.4 1.0 %copy-done.1 = bf16[1,32,5120]{2,1,0:T(8,128)(2,1)S(1)} copy-done((bf16[1,32,5120]{2,1,0:T(8,128)(2,1)S(1)}, bf16[1,32,5120]{2,1,0:T(8,128)(2,1)}, u32[]{:S(2)}) %copy-start.1) | copy-done | bytes 327704
  45.4 0.9 %copy-done.2 = bf16[1,32,2048]{2,1,0:T(8,128)(2,1)S(1)} copy-done((bf16[1,32,2048]{2,1,0:T(8,128)(2,1)S(1)}, bf16[1,32,2048]{2,1,0:T(8,128)(2,1)}, u32[]{:S(2)}) %copy-start.2) | copy-done | bytes 131096
  47.2 0.9 %copy-done.5 = bf16[32,2048]{1,0:T(8,128)(2,1)S(1)} copy-done((bf16[32,2048]{1,0:T(8,128)(2,1)S(1)}, bf16[32,2048]{1,0:T(8,128)(2,1)}, u32[]{:S(2)}) %copy-start.5) | copy-done | bytes 131096
  48.1 0.9 %copy-done.7 = bf16[32,2048]{1,0:T(8,128)(2,1)S(1)} copy-done((bf16[32,2048]{1,0:T(8,128)(2,1)S(1)}, bf16[32,2048]{1,0:T(8,128)(2,1)}, u32[]{:S(2)}) %copy-start.7) | copy-done | bytes 131096
  49.9 13.6 %shard_map.86 = (bf16[32,5120]{1,0:T(8,128)(2,1)}, bf16[32,5120]{1,0:T(8,128)(2,1)}) custom-call(s32[32]{0:T(128)S(1)} %stack.150.refs_0_, s32[6]{0:T(128)S(1)} %stack.156.refs_1_, s32[3]{0:T(128)S(1)} %pad_add_fusion.refs_2_, bf16[32,5120]{1,0:T(8,128)(2,1)S(1)} %copy-done, bf16[32,5120]{1,0:T(8,128)(2,1)S(1)} %bitcast.40, bf16[32,2048]{1,0:T(8,128)(2,1)S(1)} %bitcast.43, ...), custom_call_target="tpu_custom_call" | custom-call | flops 3019898880 | bytes 4718592 | tf_op jit(solution)/shard_map/pallas_call | solution.py:168
  (68 shorter events, 9.7 us)
Async XLA Ops:
  0.6 6.4 %collective-permute-start.1 = (bf16[32,2048]{1,0:T(8,128)(2,1)}, bf16[32,2048]{1,0:T(8,128)(2,1)S(1)}, u32[]{:S(2)}, u32[]{:S(2)}) collective-permute-start(bf16[32,2048]{1,0:T(8,128)(2,1)} %bitcast.41), channel_id=1, source_target_pairs={{0,1},{1,0},{2,3},{3,2},{4,5},{5,4},{6,7},{7,6},{8,9},{9,8},{10,11... | collective-permute-start | bytes 393224 | tf_op jit(solution)/shard_map/ppermute | solution.py:185
  0.8 7.5 %collective-permute-start = (bf16[32,2048]{1,0:T(8,128)(2,1)}, bf16[32,2048]{1,0:T(8,128)(2,1)S(1)}, u32[]{:S(2)}, u32[]{:S(2)}) collective-permute-start(bf16[32,2048]{1,0:T(8,128)(2,1)} %bitcast.42), channel_id=1, source_target_pairs={{0,2},{1,3},{2,0},{3,1},{4,6},{5,7},{6,4},{7,5},{8,10},{9,11},{10,... | collective-permute-start | bytes 393224 | tf_op jit(solution)/shard_map/ppermute | solution.py:185
  3.5 6.2 %collective-permute-start.18 = (bf16[32,2048]{1,0:T(8,128)(2,1)}, bf16[32,2048]{1,0:T(8,128)(2,1)S(1)}, u32[]{:S(2)}, u32[]{:S(2)}) collective-permute-start(bf16[32,2048]{1,0:T(8,128)(2,1)} %refs_9_.1), channel_id=1, source_target_pairs={{0,24},{4,28},{8,0},{12,4},{16,8},{20,12},{24,16},{28,20},{1,25},{... | collective-permute-start | bytes 393224 | tf_op jit(solution)/shard_map/ppermute | solution.py:219
  6.8 6.4 %collective-permute-start.10 = (bf16[32,2048]{1,0:T(8,128)(2,1)}, bf16[32,2048]{1,0:T(8,128)(2,1)S(1)}, u32[]{:S(2)}, u32[]{:S(2)}) collective-permute-start(bf16[32,2048]{1,0:T(8,128)(2,1)} %refs_9_.1), channel_id=1, source_target_pairs={{0,8},{4,12},{8,16},{12,20},{16,24},{20,28},{24,0},{28,4},{1,9},{5... | collective-permute-start | bytes 393224 | tf_op jit(solution)/shard_map/ppermute | solution.py:219
  6.8 8.0 %collective-permute-start.6 = (bf16[32,2048]{1,0:T(8,128)(2,1)}, bf16[32,2048]{1,0:T(8,128)(2,1)S(1)}, u32[]{:S(2)}, u32[]{:S(2)}) collective-permute-start(bf16[32,2048]{1,0:T(8,128)(2,1)} %refs_9_.1), channel_id=1, source_target_pairs={{0,2},{1,3},{2,0},{3,1},{4,6},{5,7},{6,4},{7,5},{8,10},{9,11},{10,... | collective-permute-start | bytes 393224 | tf_op jit(solution)/shard_map/ppermute | solution.py:185
  7.0 7.9 %collective-permute-start.4 = (bf16[32,2048]{1,0:T(8,128)(2,1)}, bf16[32,2048]{1,0:T(8,128)(2,1)S(1)}, u32[]{:S(2)}, u32[]{:S(2)}) collective-permute-start(bf16[32,2048]{1,0:T(8,128)(2,1)} %refs_9_.1), channel_id=1, source_target_pairs={{0,4},{4,0},{8,12},{12,8},{16,20},{20,16},{24,28},{28,24},{1,5},{5... | collective-permute-start | bytes 393224 | tf_op jit(solution)/shard_map/ppermute | solution.py:185
  8.2 8.0 %collective-permute-start.3 = (bf16[32,2048]{1,0:T(8,128)(2,1)}, bf16[32,2048]{1,0:T(8,128)(2,1)S(1)}, u32[]{:S(2)}, u32[]{:S(2)}) collective-permute-start(bf16[32,2048]{1,0:T(8,128)(2,1)} %refs_9_.1), channel_id=1, source_target_pairs={{0,1},{1,0},{2,3},{3,2},{4,5},{5,4},{6,7},{7,6},{8,9},{9,8},{10,11... | collective-permute-start | bytes 393224 | tf_op jit(solution)/shard_map/ppermute | solution.py:185
  9.7 9.4 %collective-permute-start.26 = (bf16[32,2048]{1,0:T(8,128)(2,1)}, bf16[32,2048]{1,0:T(8,128)(2,1)S(1)}, u32[]{:S(2)}, u32[]{:S(2)}) collective-permute-start(bf16[32,2048]{1,0:T(8,128)(2,1)} %refs_9_.1), channel_id=1, source_target_pairs={{0,16},{4,20},{8,24},{12,28},{16,0},{20,4},{24,8},{28,12},{1,17},{... | collective-permute-start | bytes 393224 | tf_op jit(solution)/shard_map/ppermute | solution.py:219
  13.2 5.8 %collective-permute-start.2 = (bf16[32,2048]{1,0:T(8,128)(2,1)S(1)}, bf16[32,2048]{1,0:T(8,128)(2,1)S(1)}, u32[]{:S(2)}, u32[]{:S(2)}) collective-permute-start(bf16[32,2048]{1,0:T(8,128)(2,1)S(1)} %collective-permute-done.refs_6_), channel_id=1, source_target_pairs={{0,1},{1,0},{2,3},{3,2},{4,5},{5,4},{6,7},{7,6},{8,9},{9,8},{10,11... | collective-permute-start | bytes 393224 | tf_op jit(solution)/shard_map/ppermute | solution.py:185
  14.8 5.7 %collective-permute-start.22 = (bf16[32,2048]{1,0:T(8,128)(2,1)S(1)}, bf16[32,2048]{1,0:T(8,128)(2,1)S(1)}, u32[]{:S(2)}, u32[]{:S(2)}) collective-permute-start(bf16[32,2048]{1,0:T(8,128)(2,1)S(1)} %collective-permute-done.18.refs_25_), channel_id=1, source_target_pairs={{0,2},{1,3},{2,0},{3,1},{4,6},{5,7},{6,4},{7,5},{8,10},{9,11},{10,... | collective-permute-start | bytes 393224 | tf_op jit(solution)/shard_map/ppermute | solution.py:185
  14.9 7.4 %collective-permute-start.20 = (bf16[32,2048]{1,0:T(8,128)(2,1)S(1)}, bf16[32,2048]{1,0:T(8,128)(2,1)S(1)}, u32[]{:S(2)}, u32[]{:S(2)}) collective-permute-start(bf16[32,2048]{1,0:T(8,128)(2,1)S(1)} %collective-permute-done.18.refs_25_), channel_id=1, source_target_pairs={{0,4},{4,0},{8,12},{12,8},{16,20},{20,16},{24,28},{28,24},{1,5},{5... | collective-permute-start | bytes 393224 | tf_op jit(solution)/shard_map/ppermute | solution.py:185
  16.2 6.4 %collective-permute-start.19 = (bf16[32,2048]{1,0:T(8,128)(2,1)S(1)}, bf16[32,2048]{1,0:T(8,128)(2,1)S(1)}, u32[]{:S(2)}, u32[]{:S(2)}) collective-permute-start(bf16[32,2048]{1,0:T(8,128)(2,1)S(1)} %collective-permute-done.18.refs_25_), channel_id=1, source_target_pairs={{0,1},{1,0},{2,3},{3,2},{4,5},{5,4},{6,7},{7,6},{8,9},{9,8},{10,11... | collective-permute-start | bytes 393224 | tf_op jit(solution)/shard_map/ppermute | solution.py:185
  19.0 6.2 %collective-permute-start.12 = (bf16[32,2048]{1,0:T(8,128)(2,1)S(1)}, bf16[32,2048]{1,0:T(8,128)(2,1)S(1)}, u32[]{:S(2)}, u32[]{:S(2)}) collective-permute-start(bf16[32,2048]{1,0:T(8,128)(2,1)S(1)} %collective-permute-done.10.refs_17_), channel_id=1, source_target_pairs={{0,4},{4,0},{8,12},{12,8},{16,20},{20,16},{24,28},{28,24},{1,5},{5... | collective-permute-start | bytes 393224 | tf_op jit(solution)/shard_map/ppermute | solution.py:185
  22.3 5.5 %collective-permute-start.8 = (bf16[32,2048]{1,0:T(8,128)(2,1)S(1)}, bf16[32,2048]{1,0:T(8,128)(2,1)S(1)}, u32[]{:S(2)}, u32[]{:S(2)}) collective-permute-start(bf16[32,2048]{1,0:T(8,128)(2,1)S(1)} %collective-permute-done.6.refs_13_), channel_id=1, source_target_pairs={{0,4},{4,0},{8,12},{12,8},{16,20},{20,16},{24,28},{28,24},{1,5},{5... | collective-permute-start | bytes 393224 | tf_op jit(solution)/shard_map/ppermute | solution.py:185
  22.6 7.5 %collective-permute-start.7 = (bf16[32,2048]{1,0:T(8,128)(2,1)S(1)}, bf16[32,2048]{1,0:T(8,128)(2,1)S(1)}, u32[]{:S(2)}, u32[]{:S(2)}) collective-permute-start(bf16[32,2048]{1,0:T(8,128)(2,1)S(1)} %collective-permute-done.6.refs_13_), channel_id=1, source_target_pairs={{0,1},{1,0},{2,3},{3,2},{4,5},{5,4},{6,7},{7,6},{8,9},{9,8},{10,11... | collective-permute-start | bytes 393224 | tf_op jit(solution)/shard_map/ppermute | solution.py:185
  22.9 7.3 %collective-permute-start.5 = (bf16[32,2048]{1,0:T(8,128)(2,1)S(1)}, bf16[32,2048]{1,0:T(8,128)(2,1)S(1)}, u32[]{:S(2)}, u32[]{:S(2)}) collective-permute-start(bf16[32,2048]{1,0:T(8,128)(2,1)S(1)} %collective-permute-done.4.refs_11_), channel_id=1, source_target_pairs={{0,1},{1,0},{2,3},{3,2},{4,5},{5,4},{6,7},{7,6},{8,9},{9,8},{10,11... | collective-permute-start | bytes 393224 | tf_op jit(solution)/shard_map/ppermute | solution.py:185
  25.3 5.2 %collective-permute-start.30 = (bf16[32,2048]{1,0:T(8,128)(2,1)S(1)}, bf16[32,2048]{1,0:T(8,128)(2,1)S(1)}, u32[]{:S(2)}, u32[]{:S(2)}) collective-permute-start(bf16[32,2048]{1,0:T(8,128)(2,1)S(1)} %collective-permute-done.26.refs_33_), channel_id=1, source_target_pairs={{0,2},{1,3},{2,0},{3,1},{4,6},{5,7},{6,4},{7,5},{8,10},{9,11},{10,... | collective-permute-start | bytes 393224 | tf_op jit(solution)/shard_map/ppermute | solution.py:185
  25.5 5.7 %collective-permute-start.28 = (bf16[32,2048]{1,0:T(8,128)(2,1)S(1)}, bf16[32,2048]{1,0:T(8,128)(2,1)S(1)}, u32[]{:S(2)}, u32[]{:S(2)}) collective-permute-start(bf16[32,2048]{1,0:T(8,128)(2,1)S(1)} %collective-permute-done.26.refs_33_), channel_id=1, source_target_pairs={{0,4},{4,0},{8,12},{12,8},{16,20},{20,16},{24,28},{28,24},{1,5},{5... | collective-permute-start | bytes 393224 | tf_op jit(solution)/shard_map/ppermute | solution.py:185
  27.9 5.6 %collective-permute-start.27 = (bf16[32,2048]{1,0:T(8,128)(2,1)S(1)}, bf16[32,2048]{1,0:T(8,128)(2,1)S(1)}, u32[]{:S(2)}, u32[]{:S(2)}) collective-permute-start(bf16[32,2048]{1,0:T(8,128)(2,1)S(1)} %collective-permute-done.26.refs_33_), channel_id=1, source_target_pairs={{0,1},{1,0},{2,3},{3,2},{4,5},{5,4},{6,7},{7,6},{8,9},{9,8},{10,11... | collective-permute-start | bytes 393224 | tf_op jit(solution)/shard_map/ppermute | solution.py:185
  30.4 5.7 %collective-permute-start.21 = (bf16[32,2048]{1,0:T(8,128)(2,1)S(1)}, bf16[32,2048]{1,0:T(8,128)(2,1)S(1)}, u32[]{:S(2)}, u32[]{:S(2)}) collective-permute-start(bf16[32,2048]{1,0:T(8,128)(2,1)S(1)} %collective-permute-done.20.refs_27_), channel_id=1, source_target_pairs={{0,1},{1,0},{2,3},{3,2},{4,5},{5,4},{6,7},{7,6},{8,9},{9,8},{10,11... | collective-permute-start | bytes 393224 | tf_op jit(solution)/shard_map/ppermute | solution.py:185
  31.2 5.2 %collective-permute-start.16 = (bf16[32,2048]{1,0:T(8,128)(2,1)S(1)}, bf16[32,2048]{1,0:T(8,128)(2,1)}, u32[]{:S(2)}, u32[]{:S(2)}) collective-permute-start(bf16[32,2048]{1,0:T(8,128)(2,1)S(1)} %collective-permute-done.14.refs_21_), channel_id=1, source_target_pairs={{0,4},{4,0},{8,12},{12,8},{16,20},{20,16},{24,28},{28,24},{1,5},{5... | collective-permute-start | bytes 393224 | tf_op jit(solution)/shard_map/ppermute | solution.py:185
  36.1 5.2 %collective-permute-start.32 = (bf16[32,2048]{1,0:T(8,128)(2,1)S(1)}, bf16[32,2048]{1,0:T(8,128)(2,1)}, u32[]{:S(2)}, u32[]{:S(2)}) collective-permute-start(bf16[32,2048]{1,0:T(8,128)(2,1)S(1)} %collective-permute-done.28.refs_35_), channel_id=1, source_target_pairs={{0,2},{1,3},{2,0},{3,1},{4,6},{5,7},{6,4},{7,5},{8,10},{9,11},{10,... | collective-permute-start | bytes 393224 | tf_op jit(solution)/shard_map/ppermute | solution.py:185
  36.4 8.0 %collective-permute-start.29 = (bf16[32,2048]{1,0:T(8,128)(2,1)S(1)}, bf16[32,2048]{1,0:T(8,128)(2,1)}, u32[]{:S(2)}, u32[]{:S(2)}) collective-permute-start(bf16[32,2048]{1,0:T(8,128)(2,1)S(1)} %collective-permute-done.28.refs_35_), channel_id=1, source_target_pairs={{0,1},{1,0},{2,3},{3,2},{4,5},{5,4},{6,7},{7,6},{8,9},{9,8},{10,11... | collective-permute-start | bytes 393224 | tf_op jit(solution)/shard_map/ppermute | solution.py:185
  38.8 5.6 %collective-permute-start.31 = (bf16[32,2048]{1,0:T(8,128)(2,1)S(1)}, bf16[32,2048]{1,0:T(8,128)(2,1)}, u32[]{:S(2)}, u32[]{:S(2)}) collective-permute-start(bf16[32,2048]{1,0:T(8,128)(2,1)S(1)} %collective-permute-done.30.refs_37_), channel_id=1, source_target_pairs={{0,1},{1,0},{2,3},{3,2},{4,5},{5,4},{6,7},{7,6},{8,9},{9,8},{10,11... | collective-permute-start | bytes 393224 | tf_op jit(solution)/shard_map/ppermute | solution.py:185
  (20 other events, 95.1 us)
where the time goes:
time: 63.8 us; the launch traced here: 63.5 us
  starting transfers between devices  32.6 us (51%)
  Pallas kernels  13.6 us (21%)
  local copies, waits for them, and re-layouts  7.65 us (12%)
  waiting for transfers between devices  6.91 us (11%)
  between operations  2.67 us (4%)
    ppermute x31, starting transfers between devices, swap(): return lax.ppermute(array, axis, [(i, i ^ bit) for i in range(size)])  28.3 us
    pallas_call x1, Pallas kernels, attend(): pl.pallas_call(functools.partial(attend_kernel, piece_rows, first_call, l...  13.6 us
    unnamed x20, local copies, waits for them, and re-layouts  7.45 us
    ppermute x3, waiting for transfers between devices, local(): lax.ppermute(trace_key_value, 'ctx', [(i, (i + 2 * shift) % ctx_size) for...  4.99 us
    ppermute x3, starting transfers between devices, local(): lax.ppermute(trace_key_value, 'ctx', [(i, (i + 2 * shift) % ctx_size) for...  4.36 us
    ppermute x31, waiting for transfers between devices, swap(): return lax.ppermute(array, axis, [(i, i ^ bit) for i in range(size)])  1.91 us
  transfers between devices with their start and end apart: 34, of which 5 were waited for; matrix products, arithmetic and copies ran while one was open for 0% of the time, Pallas kernels for 0%

commit v1 on v0

v1 whole, which is shorter than its diff:
```python
import functools

import jax
import jax.numpy as jnp
from jax import lax
from jax.experimental import pallas as pl
from jax.experimental.pallas import tpu as pltpu
from jax.sharding import PartitionSpec as P

QUERY_HEADS = 40
KEY_VALUE_HEADS = 8
HEAD_SIZE = 128
GROUP = QUERY_HEADS // KEY_VALUE_HEADS
PAIR = 2 * HEAD_SIZE
LOG2E = 1.4426950408889634
SCALE = HEAD_SIZE ** (-0.5) * LOG2E
MASKED = -1e30
CHUNK_ROWS = 1024
OWN_ORDER = (0, 2, 1, 3)


def dot_t(a, b):
    return lax.dot_general(a, b, (((1,), (1,)), ((), ())), preferred_element_type=jnp.float32)


def dot(a, b):
    return lax.dot_general(a, b, (((1,), (0,)), ((), ())), preferred_element_type=jnp.float32)


def attend_kernel(slots, own_order, own_count, tp_size, first_call, last_call, *refs):
    refs = list(refs)
    prefix_ref, del_start_ref, del_end_ref, tq, sq = refs[:5]
    del refs[:5]
    own_pieces, refs = refs[:own_count], refs[own_count:]
    piece_count = len(refs) - 2 - (2 if not first_call else 0) - 2
    pieces, refs = refs[:piece_count], refs[piece_count:]
    if not first_call:
        stats_in, sum_in = refs[:2]
        del refs[:2]
    out_a, out_b, kv, sems = refs

    rows = tq.shape[0]
    copies, at = [], 0
    for index, piece in enumerate(list(pieces) + list(own_pieces)):
        size = piece.shape[0]
        copies.append(pltpu.make_async_copy(piece, kv.at[pl.ds(at, size)], sems.at[index]))
        at += size
    for copy in copies:
        copy.start()

    ctx = lax.axis_index("ctx").astype(jnp.int32)
    tp = lax.axis_index("tp").astype(jnp.int32)
    first_position = (ctx * tp_size + tp) * rows
    prefix, del_start, del_end = prefix_ref[0], del_start_ref[0], del_end_ref[0]
    lanes = 128
    lane = lax.broadcasted_iota(jnp.int32, (rows, lanes), 1)
    row = lax.broadcasted_iota(jnp.int32, (rows, lanes), 0)
    q_trace_aug = jnp.where(lane == row, 1.0, 0.0).astype(jnp.bfloat16)
    q_suffix_aug = jnp.where((lane == rows) | (lane == rows + 1 + row), 1.0, 0.0).astype(jnp.bfloat16)
    q_aug = jnp.concatenate([q_trace_aug] * GROUP + [q_suffix_aug] * GROUP, axis=0)
    k_aug = []
    for slot in slots:
        position = slot(ctx, tp) * rows + row
        hidden_trace = (lane < rows) & (position > first_position + lane)
        hidden_suffix = (lane == rows) & (
            (position >= prefix) | ((position >= del_start) & (position < del_end))
        )
        k_aug.append(jnp.where(hidden_trace | hidden_suffix, MASKED, 0.0).astype(jnp.bfloat16))
    k_aug = jnp.concatenate(k_aug, axis=0)
    total = rows * len(slots)
    if first_call:
        own_aug = []
        for flip in own_order:
            position = (tp ^ flip) * rows + row
            hidden = (lane > rows) & (position > tp * rows + (lane - rows - 1))
            own_aug.append(jnp.where(hidden, MASKED, 0.0).astype(jnp.bfloat16))
        own_aug = jnp.concatenate(own_aug, axis=0)
        own_total = rows * len(own_order)
        own_ones = jnp.ones((own_total, HEAD_SIZE), jnp.bfloat16)
    ones = jnp.ones((total, HEAD_SIZE), jnp.bfloat16)
    for copy in copies:
        copy.wait()

    half = GROUP * rows
    lane_out = lax.broadcasted_iota(jnp.int32, (2 * half, HEAD_SIZE), 1)
    for g in range(KEY_VALUE_HEADS):
        def heads(ref):
            return [ref[:, (g * GROUP + j) * HEAD_SIZE:(g * GROUP + j + 1) * HEAD_SIZE] for j in range(GROUP)]

        here = slice(g * 2 * half, (g + 1) * 2 * half)
        query = jnp.concatenate(heads(tq) + heads(sq), axis=0)
        query = jnp.concatenate([query, q_aug], axis=1)
        key = kv[0:total, g * PAIR:g * PAIR + HEAD_SIZE]
        value = kv[0:total, g * PAIR + HEAD_SIZE:(g + 1) * PAIR]
        scores = dot_t(query, jnp.concatenate([key, k_aug], axis=1))
        top = jnp.max(scores, axis=1, keepdims=True)
        if first_call:
            own_key = kv[total:total + own_total, g * PAIR:g * PAIR + HEAD_SIZE]
            own_value = kv[total:total + own_total, g * PAIR + HEAD_SIZE:(g + 1) * PAIR]
            own_scores = dot_t(query[half:], jnp.concatenate([own_key, own_aug], axis=1))
            own_top = jnp.maximum(top[half:], jnp.max(own_scores, axis=1, keepdims=True))
            top = jnp.concatenate([top[:half], own_top], axis=0)
        else:
            old_top = stats_in[here, 0:1]
            top = jnp.maximum(old_top, top)
        weights = jnp.exp2((scores - top) * SCALE).astype(jnp.bfloat16)
        both = dot(weights, jnp.concatenate([value, ones], axis=1))
        summed, denominator = both[:, :HEAD_SIZE], both[:, HEAD_SIZE:]
        if first_call:
            own_weights = jnp.exp2((own_scores - top[half:]) * SCALE).astype(jnp.bfloat16)
            own_both = dot(own_weights, jnp.concatenate([own_value, own_ones], axis=1))
            summed = jnp.concatenate([summed[:half], summed[half:] + own_both[:, :HEAD_SIZE]], axis=0)
            denominator = jnp.concatenate(
                [denominator[:half], denominator[half:] + own_both[:, HEAD_SIZE:]], axis=0
            )
        else:
            rescale = jnp.exp2((old_top - top) * SCALE)
            summed = summed + sum_in[here, :] * rescale
            denominator = denominator + stats_in[here, 1:2] * rescale
        if last_call:
            result = (summed / denominator).astype(jnp.bfloat16)
            for j in range(GROUP):
                columns = slice((g * GROUP + j) * HEAD_SIZE, (g * GROUP + j + 1) * HEAD_SIZE)
                out_a[:, columns] = result[j * rows:(j + 1) * rows]
                out_b[:, columns] = result[half + j * rows:half + (j + 1) * rows]
        else:
            out_a[here, :] = jnp.where(lane_out == 0, top, denominator)
            out_b[here, :] = summed


def attend(spans, tq, sq, own_pieces, pieces, slots, tp_size, carry, last_call):
    first_call = carry is None
    rows = tq.shape[0]
    own_pieces = list(own_pieces) if first_call else []
    smem = pl.BlockSpec(memory_space=pltpu.SMEM)
    vmem = pl.BlockSpec(memory_space=pltpu.VMEM)
    hbm = pl.BlockSpec(memory_space=pl.ANY)
    operands = [*spans, tq, sq, *own_pieces, *pieces]
    in_specs = [smem] * 3 + [vmem] * 2 + [hbm] * (len(own_pieces) + len(pieces))
    if not first_call:
        operands += list(carry)
        in_specs += [vmem] * 2
    if last_call:
        out_shape = [jax.ShapeDtypeStruct(tq.shape, jnp.bfloat16)] * 2
    else:
        out_shape = [jax.ShapeDtypeStruct((2 * QUERY_HEADS * rows, HEAD_SIZE), jnp.float32)] * 2
    all_rows = sum(p.shape[0] for p in pieces) + sum(p.shape[0] for p in own_pieces)
    flops = 2 * 2 * QUERY_HEADS * rows * all_rows * PAIR * 2
    return pl.pallas_call(
        functools.partial(
            attend_kernel, slots, OWN_ORDER, len(own_pieces), tp_size, first_call, last_call
        ),
        out_shape=out_shape,
        in_specs=in_specs,
        out_specs=[vmem] * len(out_shape),
        scratch_shapes=[
            pltpu.VMEM((all_rows, tq.shape[1] // GROUP * 2), jnp.bfloat16),
            pltpu.SemaphoreType.DMA((len(pieces) + len(own_pieces),)),
        ],
        compiler_params=pltpu.CompilerParams(vmem_limit_bytes=32 * 1024 * 1024),
        cost_estimate=pl.CostEstimate(
            flops=flops, bytes_accessed=all_rows * 4096, transcendentals=2 * QUERY_HEADS * rows * all_rows
        ),
    )(*operands)


def swap(array, axis, bit, size):
    return lax.ppermute(array, axis, [(i, i ^ bit) for i in range(size)])


def after(array, *others):
    return lax.optimization_barrier((array, *others))[0]


def local(ctx_size, tp_size, trace_q, trace_key_value, suffix_q, suffix_key_value, prefix_len, del_start, del_end):
    rows = trace_q.shape[0]
    spans = (prefix_len, del_start, del_end)
    sq = suffix_q[0]
    suffix_own = suffix_key_value[0]

    core = lambda a: swap(a, "tp", 1, tp_size)
    across_y = lambda a: swap(a, "tp", 2, tp_size)
    across_x = lambda a: swap(a, "ctx", 1, ctx_size)
    along_z = lambda a, shift: lax.ppermute(
        a, "ctx", [(i, (i + 2 * shift) % ctx_size) for i in range(ctx_size)]
    )

    def slot(shift, x, y, c=0):
        return lambda ctx, tp: (((ctx + ctx_size - 2 * shift) % ctx_size) ^ x) * tp_size + (tp ^ (2 * y + c))

    def absorb(pieces, slots, state, last_call):
        return attend(spans, trace_q, sq, suffix_pieces, pieces, slots, tp_size, state, last_call)

    def with_core(names):
        return [slot(*n) for n in names] + [slot(*n, 1) for n in names]

    if ctx_size == 8 and tp_size == 4:
        own = trace_key_value
        up, down = along_z(own, 1), along_z(own, 3)
        own_x, own_y = across_x(own), across_y(own)
        own_d = across_x(own_y)
        suffix_near = jnp.concatenate([suffix_own, across_y(suffix_own)], axis=0)
        suffix_pieces = [suffix_near, core(suffix_near)]
        plane = jnp.concatenate([own, own_x, own_y, own_d], axis=0)
        first = ([plane, core(plane)], with_core([(0, 0, 0), (0, 1, 0), (0, 0, 1), (0, 1, 1)]))

        far = along_z(after(own, up, down), 2)
        near = jnp.concatenate([up, down], axis=0)
        near_x, near_y = across_x(near), across_y(near)
        state = absorb(*first, None, False)
        near_x, near_y, state = lax.optimization_barrier((near_x, near_y, state))
        up_d, down_d = across_x(near_y[:rows]), across_y(near_x[rows:])
        far_x, far_y = across_x(far), across_y(far)
        planes = jnp.concatenate([near, near_x, near_y, up_d, down_d], axis=0)
        second = (
            [planes, core(planes)],
            with_core([(1, 0, 0), (3, 0, 0), (1, 1, 0), (3, 1, 0), (1, 0, 1), (3, 0, 1), (1, 1, 1), (3, 1, 1)]),
        )
        far_d = across_y(far_x)
        sides = jnp.concatenate([far, far_x, far_y], axis=0)
        sides_core = core(sides)
        state = absorb(*second, state, False)
        far_d, sides_core, state = lax.optimization_barrier((far_d, sides_core, state))
        third = (
            [sides, sides_core, far_d, core(far_d)],
            with_core([(2, 0, 0), (2, 1, 0), (2, 0, 1)]) + with_core([(2, 1, 1)]),
        )
        trace_out, suffix_out = absorb(*third, state, True)
    else:
        gathered = lax.all_gather(trace_key_value, ("ctx", "tp"), axis=0, tiled=True)
        own_parts = lax.all_gather(suffix_own, "tp", axis=0, tiled=False)
        tp = lax.axis_index("tp")
        suffix_pieces = [own_parts[tp ^ flip] for flip in OWN_ORDER]
        groups = [
            (
                [gathered[at:at + CHUNK_ROWS]],
                [lambda ctx, tp, number=number: number for number in range(at // rows, (at + CHUNK_ROWS) // rows)],
            )
            for at in range(0, gathered.shape[0], CHUNK_ROWS)
        ]

        state = None
        for index, (pieces, slots) in enumerate(groups):
            state = absorb(pieces, slots, state, index == len(groups) - 1)
        trace_out, suffix_out = state
    return trace_out, suffix_out[None]


def solution(mesh):
    return jax.shard_map(
        functools.partial(local, mesh.shape["ctx"], mesh.shape["tp"]),
        mesh=mesh,
        in_specs=(
            P(("ctx", "tp"), None),
            P(("ctx", "tp"), None),
            P("ctx", "tp", None),
            P("ctx", "tp", None),
            P("ctx"),
            P("ctx"),
            P("ctx"),
        ),
        out_specs=(P(("ctx", "tp"), None), P("ctx", "tp", None)),
        check_vma=False,
    )
```

time: 63.8 us -> 57.6 us (0.903)
  starting transfers between devices: 32.6 us -> 18.1 us
  waiting for transfers between devices: 6.91 us -> 19.4 us
  local copies, waits for them, and re-layouts: 7.65 us -> 1.1 us
  Pallas kernels: 13.6 us -> 14.9 us
  other arithmetic: 0.08 us -> 0.92 us
    ppermute x31 -> x16, waiting for transfers between devices: 1.91 us -> 19.4 us  [swap(): return lax.ppermute(array, axis, [(i, i ^ bit) for i in range(size)])]
    ppermute x31 -> x16, starting transfers between devices: 28.3 us -> 14 us  [swap(): return lax.ppermute(array, axis, [(i, i ^ bit) for i in range(size)])]
    unnamed x20 -> x15, local copies, waits for them, and re-layouts: 7.45 us -> 1.03 us
    ppermute x3, waiting for transfers between devices: 4.99 us -> 0.01 us  [local(): lax.ppermute(a, 'ctx', [(i, (i + 2 * shift) % ctx_size) for i in range(ct...]
    pallas_call x1 -> x3, Pallas kernels: 13.6 us -> 14.9 us  [attend(): pl.pallas_call(functools.partial(attend_kernel, slots, OWN_ORDER, len(own...]
    concatenate x1, other arithmetic: 0.08 us -> 0.92 us  [local(): suffix_near = jnp.concatenate([suffix_own, across_y(suffix_own)], axis=0)]
  transfers between devices with their start and end apart: 34 -> 19, of which waited for: 5 -> 8; matrix products, arithmetic and copies ran while one was open for 0% -> 4% of each run, Pallas kernels for 0% -> 14%
where the time goes in v1:
time: 57.6 us; the launch traced here: 57.1 us
  waiting for transfers between devices  19.4 us (34%)
  starting transfers between devices  18.1 us (31%)
  Pallas kernels  14.9 us (26%)
  between operations  2.75 us (5%)
  local copies, waits for them, and re-layouts  1.1 us (2%)
  other arithmetic  0.92 us (2%)
    ppermute x16, waiting for transfers between devices, swap(): return lax.ppermute(array, axis, [(i, i ^ bit) for i in range(size)])  19.4 us
    pallas_call x3, Pallas kernels, attend(): pl.pallas_call(functools.partial(attend_kernel, slots, OWN_ORDER, len(own...  14.9 us
    ppermute x16, starting transfers between devices, swap(): return lax.ppermute(array, axis, [(i, i ^ bit) for i in range(size)])  14 us
    ppermute x3, starting transfers between devices, local(): lax.ppermute(a, 'ctx', [(i, (i + 2 * shift) % ctx_size) for i in range(ct...  4.09 us
  transfers between devices with their start and end apart: 19, of which 8 were waited for; matrix products, arithmetic and copies ran while one was open for 4% of the time, Pallas kernels for 14%

profile of v1, /device:TPU:1, one launch (start us, length us, event | category | flops | bytes accessed | tf_op | source)
XLA Modules:
  0.0 57.1 jit_solution(7778106766860886357)
XLA Ops:
  0.7 2.1 %collective-permute-start.12 = (bf16[32,2048]{1,0:T(8,128)(2,1)}, bf16[32,2048]{1,0:T(8,128)(2,1)S(1)}, u32[]{:S(2)}, u32[]{:S(2)}) collective-permute-start(bf16[32,2048]{1,0:T(8,128)(2,1)} %param.8), channel_id=1, source_target_pairs={{0,2},{1,3},{2,0},{3,1},{4,6},{5,7},{6,4},{7,5},{8,10},{9,11},{10,... | collective-permute-start | bytes 393224 | tf_op jit(solution)/shard_map/ppermute | solution.py:168
  2.8 1.2 %collective-permute-start.11 = (bf16[32,2048]{1,0:T(8,128)(2,1)}, bf16[32,2048]{1,0:T(8,128)(2,1)S(1)}, u32[]{:S(2)}, u32[]{:S(2)}) collective-permute-start(bf16[32,2048]{1,0:T(8,128)(2,1)} %param.8), channel_id=1, source_target_pairs={{0,4},{4,0},{8,12},{12,8},{16,20},{20,16},{24,28},{28,24},{1,5},{5... | collective-permute-start | bytes 393224 | tf_op jit(solution)/shard_map/ppermute | solution.py:168
  4.0 1.3 %collective-permute-start = (bf16[32,2048]{1,0:T(8,128)(2,1)}, bf16[32,2048]{1,0:T(8,128)(2,1)S(1)}, u32[]{:S(2)}, u32[]{:S(2)}) collective-permute-start(bf16[32,2048]{1,0:T(8,128)(2,1)} %param.8), channel_id=1, source_target_pairs={{0,8},{4,12},{8,16},{12,20},{16,24},{20,28},{24,0},{28,4},{1,9},{5... | collective-permute-start | bytes 393224 | tf_op jit(solution)/shard_map/ppermute | solution.py:184
  5.3 2.0 %collective-permute-start.1 = (bf16[32,2048]{1,0:T(8,128)(2,1)}, bf16[32,2048]{1,0:T(8,128)(2,1)S(1)}, u32[]{:S(2)}, u32[]{:S(2)}) collective-permute-start(bf16[32,2048]{1,0:T(8,128)(2,1)} %param.8), channel_id=1, source_target_pairs={{0,24},{4,28},{8,0},{12,4},{16,8},{20,12},{24,16},{28,20},{1,25},{... | collective-permute-start | bytes 393224 | tf_op jit(solution)/shard_map/ppermute | solution.py:184
  7.6 0.9 %constant_dynamic-update-slice_fusion.8 = bf16[128,2048]{1,0:T(8,128)(2,1)S(1)} fusion(bf16[32,2048]{1,0:T(8,128)(2,1)} %param.8), kind=kLoop, calls=%fused_computation.9 | loop fusion | bytes 262144
  8.5 3.2 %collective-permute-done.9 = bf16[32,2048]{1,0:T(8,128)(2,1)S(1)} collective-permute-done((bf16[32,2048]{1,0:T(8,128)(2,1)}, bf16[32,2048]{1,0:T(8,128)(2,1)S(1)}, u32[]{:S(2)}, u32[]{:S(2)}) %collective-permute-start.9) | collective-permute-done | bytes 131104 | tf_op jit(solution)/shard_map/ppermute | solution.py:168
  11.7 0.9 %pad_maximum_fusion.refs_5_ = bf16[64,2048]{1,0:T(8,128)(2,1)S(1)} fusion(bf16[32,2048]{1,0:T(8,128)(2,1)S(1)} %collective-permute-done.9, bf16[32,2048]{1,0:T(8,128)(2,1)} %bitcast.7), kind=kLoop, calls=%fused_computation | loop fusion | flops 524288 | bytes 524288 | tf_op jit(solution)/shard_map/concatenate | solution.py:202
  12.6 2.7 %collective-permute-start.10 = (bf16[64,2048]{1,0:T(8,128)(2,1)S(1)}, bf16[64,2048]{1,0:T(8,128)(2,1)S(1)}, u32[]{:S(2)}, u32[]{:S(2)}) collective-permute-start(bf16[64,2048]{1,0:T(8,128)(2,1)S(1)} %pad_maximum_fusion.refs_5_), channel_id=1, source_target_pairs={{0,1},{1,0},{2,3},{3,2},{4,5},{5,4},{6,7},{7,6},{8,9},{9,8},{10,11... | collective-permute-start | bytes 786440 | tf_op jit(solution)/shard_map/ppermute | solution.py:168
  15.5 4.8 %collective-permute-done.13 = bf16[32,2048]{1,0:T(8,128)(2,1)S(1)} collective-permute-done((bf16[32,2048]{1,0:T(8,128)(2,1)S(1)}, bf16[32,2048]{1,0:T(8,128)(2,1)S(1)}, u32[]{:S(2)}, u32[]{:S(2)}) %collective-permute-start.13) | collective-permute-done | bytes 131104 | tf_op jit(solution)/shard_map/ppermute | solution.py:168
  20.3 0.9 %collective-permute-start.14 = (bf16[128,2048]{1,0:T(8,128)(2,1)S(1)}, bf16[128,2048]{1,0:T(8,128)(2,1)S(1)}, u32[]{:S(2)}, u32[]{:S(2)}) collective-permute-start(bf16[128,2048]{1,0:T(8,128)(2,1)S(1)} %constant_dynamic-update-slice_fusion.5.refs_7_), channel_id=1, source_target_pairs={{0,1},{1,0},{2,3},{3,2},{4,5},{5,4},{6,7},{7,6},{8,9},{9,8},{10,11... | collective-permute-start | bytes 1572872 | tf_op jit(solution)/shard_map/ppermute | solution.py:168
  23.6 0.8 %collective-permute-start.2 = (bf16[32,2048]{1,0:T(8,128)(2,1)S(1)}, bf16[32,2048]{1,0:T(8,128)(2,1)S(1)}, u32[]{:S(2)}, u32[]{:S(2)}) collective-permute-start(bf16[32,2048]{1,0:T(8,128)(2,1)S(1)} %copy-done.2), channel_id=1, source_target_pairs={{0,16},{4,20},{8,24},{12,28},{16,0},{20,4},{24,8},{28,12},{1,17},{... | collective-permute-start | bytes 393224 | tf_op jit(solution)/shard_map/ppermute | solution.py:184
  24.4 3.8 %shard_map.86 = (f32[2560,128]{1,0:T(8,128)S(1)}, f32[2560,128]{1,0:T(8,128)S(1)}) custom-call(s32[1]{0:T(128)S(6)} %copy.20.refs_0_, s32[1]{0:T(128)S(6)} %copy.21.refs_1_, s32[1]{0:T(128)S(6)} %copy.22.refs_2_, bf16[32,5120]{1,0:T(8,128)(2,1)S(1)} %copy-done, bf16[32,5120]{1,0:T(8,128)(2,1)S(1)} %bitcast.3, bf16[64,2048]{1,0:T(8,128)(2,1)S(1)} %pad_maximum_fusion.refs_5_, ...), custom_call_target="tpu_custom_call" | custom-call | flops 1006632960 | bytes 1572864 | tf_op jit(solution)/shard_map/pallas_call | solution.py:149
  28.2 1.1 %collective-permute-done.7 = bf16[64,2048]{1,0:T(8,128)(2,1)S(1)} collective-permute-done((bf16[64,2048]{1,0:T(8,128)(2,1)S(1)}, bf16[64,2048]{1,0:T(8,128)(2,1)S(1)}, u32[]{:S(2)}, u32[]{:S(2)}) %collective-permute-start.7) | collective-permute-done | bytes 262176 | tf_op jit(solution)/shard_map/ppermute | solution.py:168
  29.4 1.2 %collective-permute-start.15 = (bf16[32,2048]{1,0:T(8,128)(2,1)S(1)}, bf16[32,2048]{1,0:T(8,128)(2,1)S(1)}, u32[]{:S(2)}, u32[]{:S(2)}) collective-permute-start(bf16[32,2048]{1,0:T(8,128)(2,1)S(1)} %slice.6), channel_id=1, source_target_pairs={{0,4},{4,0},{8,12},{12,8},{16,20},{20,16},{24,28},{28,24},{1,5},{5... | collective-permute-start | bytes 393224 | tf_op jit(solution)/shard_map/ppermute | solution.py:168
  30.8 2.4 %collective-permute-done.15 = bf16[32,2048]{1,0:T(8,128)(2,1)S(1)} collective-permute-done((bf16[32,2048]{1,0:T(8,128)(2,1)S(1)}, bf16[32,2048]{1,0:T(8,128)(2,1)S(1)}, u32[]{:S(2)}, u32[]{:S(2)}) %collective-permute-start.15) | collective-permute-done | bytes 131104 | tf_op jit(solution)/shard_map/ppermute | solution.py:168
  33.2 1.4 %collective-permute-done.16 = bf16[32,2048]{1,0:T(8,128)(2,1)S(1)} collective-permute-done((bf16[32,2048]{1,0:T(8,128)(2,1)S(1)}, bf16[32,2048]{1,0:T(8,128)(2,1)S(1)}, u32[]{:S(2)}, u32[]{:S(2)}) %collective-permute-start.16) | collective-permute-done | bytes 131104 | tf_op jit(solution)/shard_map/ppermute | solution.py:168
  34.7 2.3 %collective-permute-start.17 = (bf16[256,2048]{1,0:T(8,128)(2,1)S(1)}, bf16[256,2048]{1,0:T(8,128)(2,1)S(1)}, u32[]{:S(2)}, u32[]{:S(2)}) collective-permute-start(bf16[256,2048]{1,0:T(8,128)(2,1)S(1)} %constant_dynamic-update-slice_fusion.9.refs_5_), channel_id=1, source_target_pairs={{0,1},{1,0},{2,3},{3,2},{4,5},{5,4},{6,7},{7,6},{8,9},{9,8},{10,11... | collective-permute-start | bytes 3145736 | tf_op jit(solution)/shard_map/ppermute | solution.py:168
  37.4 4.7 %collective-permute-done.3 = bf16[32,2048]{1,0:T(8,128)(2,1)S(1)} collective-permute-done((bf16[32,2048]{1,0:T(8,128)(2,1)S(1)}, bf16[32,2048]{1,0:T(8,128)(2,1)S(1)}, u32[]{:S(2)}, u32[]{:S(2)}) %collective-permute-start.3) | collective-permute-done | bytes 131104 | tf_op jit(solution)/shard_map/ppermute | solution.py:168
  42.1 1.2 %collective-permute-start.6 = (bf16[96,2048]{1,0:T(8,128)(2,1)S(1)}, bf16[96,2048]{1,0:T(8,128)(2,1)S(1)}, u32[]{:S(2)}, u32[]{:S(2)}) collective-permute-start(bf16[96,2048]{1,0:T(8,128)(2,1)S(1)} %constant_dynamic-update-slice_fusion.refs_5_), channel_id=1, source_target_pairs={{0,1},{1,0},{2,3},{3,2},{4,5},{5,4},{6,7},{7,6},{8,9},{9,8},{10,11... | collective-permute-start | bytes 1179656 | tf_op jit(solution)/shard_map/ppermute | solution.py:168
  43.3 4.2 %shard_map.87 = (f32[2560,128]{1,0:T(8,128)S(1)}, f32[2560,128]{1,0:T(8,128)S(1)}) custom-call(s32[1]{0:T(128)S(6)} %copy.20.refs_0_, s32[1]{0:T(128)S(6)} %copy.21.refs_1_, s32[1]{0:T(128)S(6)} %copy.22.refs_2_, bf16[32,5120]{1,0:T(8,128)(2,1)S(1)} %copy-done, bf16[32,5120]{1,0:T(8,128)(2,1)S(1)} %bitcast.4, ...), custom_call_target="tpu_custom_call" | custom-call | flops 1342177280 | bytes 2097152 | tf_op jit(solution)/shard_map/pallas_call | solution.py:149
  47.5 0.8 %collective-permute-done.5.refs_7_ = bf16[32,2048]{1,0:T(8,128)(2,1)S(1)} collective-permute-done((bf16[32,2048]{1,0:T(8,128)(2,1)S(1)}, bf16[32,2048]{1,0:T(8,128)(2,1)S(1)}, u32[]{:S(2)}, u32[]{:S(2)}) %collective-permute-start.5) | collective-permute-done | bytes 131104 | tf_op jit(solution)/shard_map/ppermute | solution.py:168
  48.4 0.9 %collective-permute-start.18 = (bf16[32,2048]{1,0:T(8,128)(2,1)S(1)}, bf16[32,2048]{1,0:T(8,128)(2,1)S(1)}, u32[]{:S(2)}, u32[]{:S(2)}) collective-permute-start(bf16[32,2048]{1,0:T(8,128)(2,1)S(1)} %collective-permute-done.5.refs_7_), channel_id=1, source_target_pairs={{0,1},{1,0},{2,3},{3,2},{4,5},{5,4},{6,7},{7,6},{8,9},{9,8},{10,11... | collective-permute-start | bytes 393224 | tf_op jit(solution)/shard_map/ppermute | solution.py:168
  49.2 1.0 %collective-permute-done.18.refs_8_ = bf16[32,2048]{1,0:T(8,128)(2,1)S(1)} collective-permute-done((bf16[32,2048]{1,0:T(8,128)(2,1)S(1)}, bf16[32,2048]{1,0:T(8,128)(2,1)S(1)}, u32[]{:S(2)}, u32[]{:S(2)}) %collective-permute-start.18) | collective-permute-done | bytes 131104 | tf_op jit(solution)/shard_map/ppermute | solution.py:168
  50.2 6.9 %shard_map.88 = (bf16[32,5120]{1,0:T(8,128)(2,1)}, bf16[32,5120]{1,0:T(8,128)(2,1)}) custom-call(s32[1]{0:T(128)S(6)} %copy.20.refs_0_, s32[1]{0:T(128)S(6)} %copy.21.refs_1_, s32[1]{0:T(128)S(6)} %copy.22.refs_2_, bf16[32,5120]{1,0:T(8,128)(2,1)S(1)} %copy-done, bf16[32,5120]{1,0:T(8,128)(2,1)S(1)} %bitcast.5, ...), custom_call_target="tpu_custom_call" | custom-call | flops 671088640 | bytes 1048576 | tf_op jit(solution)/shard_map/pallas_call | solution.py:149
  (39 shorter events, 1.7 us)
Async XLA Ops:
  0.6 23.0 %copy-start.2 = (bf16[32,2048]{1,0:T(8,128)(2,1)S(1)}, bf16[32,2048]{1,0:T(8,128)(2,1)}, u32[]{:S(2)}) copy-start(bf16[32,2048]{1,0:T(8,128)(2,1)} %param.8) | copy-start | bytes 393220
  0.6 23.8 %copy-start.1 = (bf16[1,32,5120]{2,1,0:T(8,128)(2,1)S(1)}, bf16[1,32,5120]{2,1,0:T(8,128)(2,1)}, u32[]{:S(2)}) copy-start(bf16[1,32,5120]{2,1,0:T(8,128)(2,1)} %param.9) | copy-start | bytes 983044
  0.6 23.8 %copy-start = (bf16[32,5120]{1,0:T(8,128)(2,1)S(1)}, bf16[32,5120]{1,0:T(8,128)(2,1)}, u32[]{:S(2)}) copy-start(bf16[32,5120]{1,0:T(8,128)(2,1)} %refs_3_.5) | copy-start | bytes 983044
  0.7 14.6 %collective-permute-start.12 = (bf16[32,2048]{1,0:T(8,128)(2,1)}, bf16[32,2048]{1,0:T(8,128)(2,1)S(1)}, u32[]{:S(2)}, u32[]{:S(2)}) collective-permute-start(bf16[32,2048]{1,0:T(8,128)(2,1)} %param.8), channel_id=1, source_target_pairs={{0,2},{1,3},{2,0},{3,1},{4,6},{5,7},{6,4},{7,5},{8,10},{9,11},{10,... | collective-permute-start | bytes 393224 | tf_op jit(solution)/shard_map/ppermute | solution.py:168
  2.8 12.7 %collective-permute-start.11 = (bf16[32,2048]{1,0:T(8,128)(2,1)}, bf16[32,2048]{1,0:T(8,128)(2,1)S(1)}, u32[]{:S(2)}, u32[]{:S(2)}) collective-permute-start(bf16[32,2048]{1,0:T(8,128)(2,1)} %param.8), channel_id=1, source_target_pairs={{0,4},{4,0},{8,12},{12,8},{16,20},{20,16},{24,28},{28,24},{1,5},{5... | collective-permute-start | bytes 393224 | tf_op jit(solution)/shard_map/ppermute | solution.py:168
  4.0 17.2 %collective-permute-start = (bf16[32,2048]{1,0:T(8,128)(2,1)}, bf16[32,2048]{1,0:T(8,128)(2,1)S(1)}, u32[]{:S(2)}, u32[]{:S(2)}) collective-permute-start(bf16[32,2048]{1,0:T(8,128)(2,1)} %param.8), channel_id=1, source_target_pairs={{0,8},{4,12},{8,16},{12,20},{16,24},{20,28},{24,0},{28,4},{1,9},{5... | collective-permute-start | bytes 393224 | tf_op jit(solution)/shard_map/ppermute | solution.py:184
  5.3 16.0 %collective-permute-start.1 = (bf16[32,2048]{1,0:T(8,128)(2,1)}, bf16[32,2048]{1,0:T(8,128)(2,1)S(1)}, u32[]{:S(2)}, u32[]{:S(2)}) collective-permute-start(bf16[32,2048]{1,0:T(8,128)(2,1)} %param.8), channel_id=1, source_target_pairs={{0,24},{4,28},{8,0},{12,4},{16,8},{20,12},{24,16},{28,20},{1,25},{... | collective-permute-start | bytes 393224 | tf_op jit(solution)/shard_map/ppermute | solution.py:184
  7.3 4.3 %collective-permute-start.9 = (bf16[32,2048]{1,0:T(8,128)(2,1)}, bf16[32,2048]{1,0:T(8,128)(2,1)S(1)}, u32[]{:S(2)}, u32[]{:S(2)}) collective-permute-start(bf16[32,2048]{1,0:T(8,128)(2,1)} %bitcast.6), channel_id=1, source_target_pairs={{0,2},{1,3},{2,0},{3,1},{4,6},{5,7},{6,4},{7,5},{8,10},{9,11},{10,... | collective-permute-start | bytes 393224 | tf_op jit(solution)/shard_map/ppermute | solution.py:168
  12.6 11.8 %collective-permute-start.10 = (bf16[64,2048]{1,0:T(8,128)(2,1)S(1)}, bf16[64,2048]{1,0:T(8,128)(2,1)S(1)}, u32[]{:S(2)}, u32[]{:S(2)}) collective-permute-start(bf16[64,2048]{1,0:T(8,128)(2,1)S(1)} %pad_maximum_fusion.refs_5_), channel_id=1, source_target_pairs={{0,1},{1,0},{2,3},{3,2},{4,5},{5,4},{6,7},{7,6},{8,9},{9,8},{10,11... | collective-permute-start | bytes 786440 | tf_op jit(solution)/shard_map/ppermute | solution.py:168
  15.2 5.1 %collective-permute-start.13 = (bf16[32,2048]{1,0:T(8,128)(2,1)S(1)}, bf16[32,2048]{1,0:T(8,128)(2,1)S(1)}, u32[]{:S(2)}, u32[]{:S(2)}) collective-permute-start(bf16[32,2048]{1,0:T(8,128)(2,1)S(1)} %collective-permute-done.12), channel_id=1, source_target_pairs={{0,4},{4,0},{8,12},{12,8},{16,20},{20,16},{24,28},{28,24},{1,5},{5... | collective-permute-start | bytes 393224 | tf_op jit(solution)/shard_map/ppermute | solution.py:168
  20.3 4.1 %collective-permute-start.14 = (bf16[128,2048]{1,0:T(8,128)(2,1)S(1)}, bf16[128,2048]{1,0:T(8,128)(2,1)S(1)}, u32[]{:S(2)}, u32[]{:S(2)}) collective-permute-start(bf16[128,2048]{1,0:T(8,128)(2,1)S(1)} %constant_dynamic-update-slice_fusion.5.refs_7_), channel_id=1, source_target_pairs={{0,1},{1,0},{2,3},{3,2},{4,5},{5,4},{6,7},{7,6},{8,9},{9,8},{10,11... | collective-permute-start | bytes 1572872 | tf_op jit(solution)/shard_map/ppermute | solution.py:168
  21.3 8.0 %collective-permute-start.7 = (bf16[64,2048]{1,0:T(8,128)(2,1)S(1)}, bf16[64,2048]{1,0:T(8,128)(2,1)S(1)}, u32[]{:S(2)}, u32[]{:S(2)}) collective-permute-start(bf16[64,2048]{1,0:T(8,128)(2,1)S(1)} %get-tuple-element.32), channel_id=1, source_target_pairs={{0,4},{4,0},{8,12},{12,8},{16,20},{20,16},{24,28},{28,24},{1,5},{5... | collective-permute-start | bytes 786440 | tf_op jit(solution)/shard_map/ppermute | solution.py:168
  21.6 7.7 %collective-permute-start.8 = (bf16[64,2048]{1,0:T(8,128)(2,1)S(1)}, bf16[64,2048]{1,0:T(8,128)(2,1)S(1)}, u32[]{:S(2)}, u32[]{:S(2)}) collective-permute-start(bf16[64,2048]{1,0:T(8,128)(2,1)S(1)} %get-tuple-element.32), channel_id=1, source_target_pairs={{0,2},{1,3},{2,0},{3,1},{4,6},{5,7},{6,4},{7,5},{8,10},{9,11},{10,... | collective-permute-start | bytes 786440 | tf_op jit(solution)/shard_map/ppermute | solution.py:168
  23.6 13.4 %collective-permute-start.2 = (bf16[32,2048]{1,0:T(8,128)(2,1)S(1)}, bf16[32,2048]{1,0:T(8,128)(2,1)S(1)}, u32[]{:S(2)}, u32[]{:S(2)}) collective-permute-start(bf16[32,2048]{1,0:T(8,128)(2,1)S(1)} %copy-done.2), channel_id=1, source_target_pairs={{0,16},{4,20},{8,24},{12,28},{16,0},{20,4},{24,8},{28,12},{1,17},{... | collective-permute-start | bytes 393224 | tf_op jit(solution)/shard_map/ppermute | solution.py:184
  29.4 3.9 %collective-permute-start.15 = (bf16[32,2048]{1,0:T(8,128)(2,1)S(1)}, bf16[32,2048]{1,0:T(8,128)(2,1)S(1)}, u32[]{:S(2)}, u32[]{:S(2)}) collective-permute-start(bf16[32,2048]{1,0:T(8,128)(2,1)S(1)} %slice.6), channel_id=1, source_target_pairs={{0,4},{4,0},{8,12},{12,8},{16,20},{20,16},{24,28},{28,24},{1,5},{5... | collective-permute-start | bytes 393224 | tf_op jit(solution)/shard_map/ppermute | solution.py:168
  30.6 4.1 %collective-permute-start.16 = (bf16[32,2048]{1,0:T(8,128)(2,1)S(1)}, bf16[32,2048]{1,0:T(8,128)(2,1)S(1)}, u32[]{:S(2)}, u32[]{:S(2)}) collective-permute-start(bf16[32,2048]{1,0:T(8,128)(2,1)S(1)} %slice.7), channel_id=1, source_target_pairs={{0,2},{1,3},{2,0},{3,1},{4,6},{5,7},{6,4},{7,5},{8,10},{9,11},{10,... | collective-permute-start | bytes 393224 | tf_op jit(solution)/shard_map/ppermute | solution.py:168
  34.7 8.7 %collective-permute-start.17 = (bf16[256,2048]{1,0:T(8,128)(2,1)S(1)}, bf16[256,2048]{1,0:T(8,128)(2,1)S(1)}, u32[]{:S(2)}, u32[]{:S(2)}) collective-permute-start(bf16[256,2048]{1,0:T(8,128)(2,1)S(1)} %constant_dynamic-update-slice_fusion.9.refs_5_), channel_id=1, source_target_pairs={{0,1},{1,0},{2,3},{3,2},{4,5},{5,4},{6,7},{7,6},{8,9},{9,8},{10,11... | collective-permute-start | bytes 3145736 | tf_op jit(solution)/shard_map/ppermute | solution.py:168
  37.0 5.1 %collective-permute-start.3 = (bf16[32,2048]{1,0:T(8,128)(2,1)S(1)}, bf16[32,2048]{1,0:T(8,128)(2,1)S(1)}, u32[]{:S(2)}, u32[]{:S(2)}) collective-permute-start(bf16[32,2048]{1,0:T(8,128)(2,1)S(1)} %collective-permute-done.2), channel_id=1, source_target_pairs={{0,4},{4,0},{8,12},{12,8},{16,20},{20,16},{24,28},{28,24},{1,5},{5... | collective-permute-start | bytes 393224 | tf_op jit(solution)/shard_map/ppermute | solution.py:168
  37.3 4.8 %collective-permute-start.4 = (bf16[32,2048]{1,0:T(8,128)(2,1)S(1)}, bf16[32,2048]{1,0:T(8,128)(2,1)S(1)}, u32[]{:S(2)}, u32[]{:S(2)}) collective-permute-start(bf16[32,2048]{1,0:T(8,128)(2,1)S(1)} %collective-permute-done.2), channel_id=1, source_target_pairs={{0,2},{1,3},{2,0},{3,1},{4,6},{5,7},{6,4},{7,5},{8,10},{9,11},{10,... | collective-permute-start | bytes 393224 | tf_op jit(solution)/shard_map/ppermute | solution.py:168
  42.1 6.2 %collective-permute-start.6 = (bf16[96,2048]{1,0:T(8,128)(2,1)S(1)}, bf16[96,2048]{1,0:T(8,128)(2,1)S(1)}, u32[]{:S(2)}, u32[]{:S(2)}) collective-permute-start(bf16[96,2048]{1,0:T(8,128)(2,1)S(1)} %constant_dynamic-update-slice_fusion.refs_5_), channel_id=1, source_target_pairs={{0,1},{1,0},{2,3},{3,2},{4,5},{5,4},{6,7},{7,6},{8,9},{9,8},{10,11... | collective-permute-start | bytes 1179656 | tf_op jit(solution)/shard_map/ppermute | solution.py:168
  43.3 5.1 %collective-permute-start.5 = (bf16[32,2048]{1,0:T(8,128)(2,1)S(1)}, bf16[32,2048]{1,0:T(8,128)(2,1)S(1)}, u32[]{:S(2)}, u32[]{:S(2)}) collective-permute-start(bf16[32,2048]{1,0:T(8,128)(2,1)S(1)} %collective-permute-done.3), channel_id=1, source_target_pairs={{0,2},{1,3},{2,0},{3,1},{4,6},{5,7},{6,4},{7,5},{8,10},{9,11},{10,... | collective-permute-start | bytes 393224 | tf_op jit(solution)/shard_map/ppermute | solution.py:168
  48.4 1.8 %collective-permute-start.18 = (bf16[32,2048]{1,0:T(8,128)(2,1)S(1)}, bf16[32,2048]{1,0:T(8,128)(2,1)S(1)}, u32[]{:S(2)}, u32[]{:S(2)}) collective-permute-start(bf16[32,2048]{1,0:T(8,128)(2,1)S(1)} %collective-permute-done.5.refs_7_), channel_id=1, source_target_pairs={{0,1},{1,0},{2,3},{3,2},{4,5},{5,4},{6,7},{7,6},{8,9},{9,8},{10,11... | collective-permute-start | bytes 393224 | tf_op jit(solution)/shard_map/ppermute | solution.py:168

commit v2 on v1

v2 whole, which is shorter than its diff:
```python
import functools

import jax
import jax.numpy as jnp
from jax import lax
from jax.experimental import pallas as pl
from jax.experimental.pallas import tpu as pltpu
from jax.sharding import PartitionSpec as P

QUERY_HEADS = 40
KEY_VALUE_HEADS = 8
HEAD_SIZE = 128
GROUP = QUERY_HEADS // KEY_VALUE_HEADS
PAIR = 2 * HEAD_SIZE
LOG2E = 1.4426950408889634
SCALE = HEAD_SIZE ** (-0.5) * LOG2E
MASKED = -1e30
CHUNK_ROWS = 1024
OWN_ORDER = (0, 2, 1, 3)


def dot_t(a, b):
    return lax.dot_general(a, b, (((1,), (1,)), ((), ())), preferred_element_type=jnp.float32)


def dot(a, b):
    return lax.dot_general(a, b, (((1,), (0,)), ((), ())), preferred_element_type=jnp.float32)


def attend_kernel(slots, own_order, own_count, tp_size, first_call, last_call, *refs):
    refs = list(refs)
    prefix_ref, del_start_ref, del_end_ref, tq, sq = refs[:5]
    del refs[:5]
    k_aug_ref, refs = refs[-1], refs[:-1]
    out_a, out_b = refs[-2:]
    del refs[-2:]
    if not first_call:
        stats_in, sum_in = refs[-2:]
        del refs[-2:]
    own_pieces, pieces = refs[:own_count], refs[own_count:]

    rows = tq.shape[0]
    ctx = lax.axis_index("ctx").astype(jnp.int32)
    tp = lax.axis_index("tp").astype(jnp.int32)
    first_position = (ctx * tp_size + tp) * rows
    prefix, del_start, del_end = prefix_ref[0], del_start_ref[0], del_end_ref[0]
    lanes = HEAD_SIZE
    lane = lax.broadcasted_iota(jnp.int32, (rows, lanes), 1)
    row = lax.broadcasted_iota(jnp.int32, (rows, lanes), 0)
    q_trace_aug = jnp.where(lane == row, 1.0, 0.0).astype(jnp.bfloat16)
    q_suffix_aug = jnp.where((lane == rows) | (lane == rows + 1 + row), 1.0, 0.0).astype(jnp.bfloat16)
    q_aug = jnp.concatenate([q_trace_aug] * GROUP + [q_suffix_aug] * GROUP, axis=0)
    for index, slot in enumerate(slots):
        position = slot(ctx, tp) * rows + row
        hidden_trace = (lane < rows) & (position > first_position + lane)
        hidden_suffix = (lane == rows) & (
            (position >= prefix) | ((position >= del_start) & (position < del_end))
        )
        bias = jnp.where(hidden_trace | hidden_suffix, MASKED, 0.0).astype(jnp.bfloat16)
        k_aug_ref[index * rows:(index + 1) * rows, :] = bias
    total = rows * len(slots)
    if first_call:
        for index, flip in enumerate(own_order):
            position = (tp ^ flip) * rows + row
            hidden = (lane > rows) & (position > tp * rows + (lane - rows - 1))
            bias = jnp.where(hidden, MASKED, 0.0).astype(jnp.bfloat16)
            k_aug_ref[total + index * rows:total + (index + 1) * rows, :] = bias
        own_total = rows * len(own_order)
        own_ones = jnp.ones((own_total, HEAD_SIZE), jnp.bfloat16)
    ones = jnp.ones((total, HEAD_SIZE), jnp.bfloat16)
    half = GROUP * rows
    lane_out = lax.broadcasted_iota(jnp.int32, (2 * half, HEAD_SIZE), 1)

    def one_head(g, _):
        def columns(index):
            return pl.ds(pl.multiple_of(index * HEAD_SIZE, HEAD_SIZE), HEAD_SIZE)

        def stacked(parts, index):
            return jnp.concatenate([part[:, columns(index)] for part in parts], axis=0)

        query = jnp.concatenate(
            [ref[:, columns(g * GROUP + j)] for ref in (tq, sq) for j in range(GROUP)], axis=0
        )
        query = jnp.concatenate([query, q_aug], axis=1)
        scores = dot_t(query, jnp.concatenate([stacked(pieces, 2 * g), k_aug_ref[0:total]], axis=1))
        top = jnp.max(scores, axis=1, keepdims=True)
        if first_call:
            own_key = jnp.concatenate(
                [stacked(own_pieces, 2 * g), k_aug_ref[total:total + own_total]], axis=1
            )
            own_scores = dot_t(query[half:], own_key)
            own_top = jnp.maximum(top[half:], jnp.max(own_scores, axis=1, keepdims=True))
            top = jnp.concatenate([top[:half], own_top], axis=0)
        else:
            old_top = stats_in[g, :, 0:1]
            top = jnp.maximum(old_top, top)
        weights = jnp.exp2((scores - top) * SCALE).astype(jnp.bfloat16)
        both = dot(weights, jnp.concatenate([stacked(pieces, 2 * g + 1), ones], axis=1))
        summed, denominator = both[:, :HEAD_SIZE], both[:, HEAD_SIZE:]
        if first_call:
            own_weights = jnp.exp2((own_scores - top[half:]) * SCALE).astype(jnp.bfloat16)
            own_both = dot(own_weights, jnp.concatenate([stacked(own_pieces, 2 * g + 1), own_ones], axis=1))
            summed = jnp.concatenate([summed[:half], summed[half:] + own_both[:, :HEAD_SIZE]], axis=0)
            denominator = jnp.concatenate(
                [denominator[:half], denominator[half:] + own_both[:, HEAD_SIZE:]], axis=0
            )
        else:
            rescale = jnp.exp2((old_top - top) * SCALE)
            summed = summed + sum_in[g] * rescale
            denominator = denominator + stats_in[g, :, 1:2] * rescale
        if last_call:
            inverse = pl.reciprocal(denominator, approx=True)
            inverse = inverse * (2.0 - denominator * inverse)
            result = (summed * inverse).astype(jnp.bfloat16)
            for j in range(GROUP):
                out_a[:, columns(g * GROUP + j)] = result[j * rows:(j + 1) * rows]
                out_b[:, columns(g * GROUP + j)] = result[half + j * rows:half + (j + 1) * rows]
        else:
            out_a[g] = jnp.where(lane_out == 0, top, denominator)
            out_b[g] = summed
        return 0

    lax.fori_loop(0, KEY_VALUE_HEADS, one_head, 0)


def attend(spans, tq, sq, own_pieces, pieces, slots, tp_size, carry, last_call):
    first_call = carry is None
    rows = tq.shape[0]
    own_pieces = list(own_pieces) if first_call else []
    smem = pl.BlockSpec(memory_space=pltpu.SMEM)
    vmem = pl.BlockSpec(memory_space=pltpu.VMEM)
    operands = [*spans, tq, sq, *own_pieces, *pieces]
    if not first_call:
        operands += list(carry)
    if last_call:
        out_shape = [jax.ShapeDtypeStruct(tq.shape, jnp.bfloat16)] * 2
    else:
        state = (KEY_VALUE_HEADS, 2 * GROUP * rows, HEAD_SIZE)
        out_shape = [jax.ShapeDtypeStruct(state, jnp.float32)] * 2
    all_rows = sum(p.shape[0] for p in pieces) + sum(p.shape[0] for p in own_pieces)
    flops = 2 * 2 * QUERY_HEADS * rows * all_rows * PAIR * 2
    return pl.pallas_call(
        functools.partial(
            attend_kernel, slots, OWN_ORDER, len(own_pieces), tp_size, first_call, last_call
        ),
        out_shape=out_shape,
        in_specs=[smem] * 3 + [vmem] * (len(operands) - 3),
        out_specs=[vmem] * len(out_shape),
        scratch_shapes=[pltpu.VMEM((all_rows, HEAD_SIZE), jnp.bfloat16)],
        compiler_params=pltpu.CompilerParams(vmem_limit_bytes=32 * 1024 * 1024),
        cost_estimate=pl.CostEstimate(
            flops=flops, bytes_accessed=all_rows * 4096, transcendentals=2 * QUERY_HEADS * rows * all_rows
        ),
    )(*operands)


def swap(array, axis, bit, size):
    return lax.ppermute(array, axis, [(i, i ^ bit) for i in range(size)])


def after(array, *others):
    return lax.optimization_barrier((array, *others))[0]


def local(ctx_size, tp_size, trace_q, trace_key_value, suffix_q, suffix_key_value, prefix_len, del_start, del_end):
    rows = trace_q.shape[0]
    spans = (prefix_len, del_start, del_end)
    sq = suffix_q[0]
    suffix_own = suffix_key_value[0]

    core = lambda a: swap(a, "tp", 1, tp_size)
    across_y = lambda a: swap(a, "tp", 2, tp_size)
    across_x = lambda a: swap(a, "ctx", 1, ctx_size)
    along_z = lambda a, shift: lax.ppermute(
        a, "ctx", [(i, (i + 2 * shift) % ctx_size) for i in range(ctx_size)]
    )

    across_both = lambda a: lax.ppermute(
        a,
        ("ctx", "tp"),
        [(i * tp_size + j, (i ^ 1) * tp_size + (j ^ 2)) for i in range(ctx_size) for j in range(tp_size)],
    )

    def slot(shift, x, y, c=0):
        return lambda ctx, tp: (((ctx + ctx_size - 2 * shift) % ctx_size) ^ x) * tp_size + (tp ^ (2 * y + c))

    def absorb(pieces, slots, state, last_call):
        return attend(spans, trace_q, sq, suffix_pieces, pieces, slots, tp_size, state, last_call)

    def with_core(names):
        return [slot(*n) for n in names] + [slot(*n, 1) for n in names]

    if ctx_size == 8 and tp_size == 4:
        own = trace_key_value
        up, down = along_z(own, 1), along_z(own, 3)
        own_x, own_y = across_x(own), across_y(own)
        far = along_z(own, 2)
        own_d = across_x(own_y)
        suffix_y = across_y(after(suffix_own, own_y))
        plane = jnp.concatenate([own, own_x, own_y, own_d, suffix_own, suffix_y], axis=0)
        plane_core = core(plane)
        here = 4 * rows
        suffix_pieces = [plane[here:], plane_core[here:]]
        first = [plane[:here], plane_core[:here]]
        first_slots = with_core([(0, 0, 0), (0, 1, 0), (0, 0, 1), (0, 1, 1)])

        near = jnp.concatenate([up, down], axis=0)
        near_x, near_y, near_d = across_x(near), across_y(near), across_both(near)
        state = absorb(first, first_slots, None, False)
        far_x, far_y, far_d = across_x(far), across_y(far), across_both(far)
        near_x, near_y, near_d, state = lax.optimization_barrier((near_x, near_y, near_d, state))
        planes = jnp.concatenate([near, near_x, near_y, near_d, far], axis=0)
        second = [planes, core(planes)]
        second_slots = with_core(
            [(z, x, y) for x, y in ((0, 0), (1, 0), (0, 1), (1, 1)) for z in (1, 3)] + [(2, 0, 0)]
        )
        state = absorb(second, second_slots, state, False)
        far_rest = jnp.concatenate([far_x, far_y, far_d], axis=0)
        third = [far_rest, core(far_rest)]
        third_slots = with_core([(2, 1, 0), (2, 0, 1), (2, 1, 1)])
        trace_out, suffix_out = absorb(third, third_slots, state, True)
    else:
        gathered = lax.all_gather(trace_key_value, ("ctx", "tp"), axis=0, tiled=True)
        own_parts = lax.all_gather(suffix_own, "tp", axis=0, tiled=False)
        tp = lax.axis_index("tp")
        suffix_pieces = [own_parts[tp ^ flip] for flip in OWN_ORDER]
        groups = [
            (
                [gathered[at:at + CHUNK_ROWS]],
                [lambda ctx, tp, number=number: number for number in range(at // rows, (at + CHUNK_ROWS) // rows)],
            )
            for at in range(0, gathered.shape[0], CHUNK_ROWS)
        ]

        state = None
        for index, (pieces, slots) in enumerate(groups):
            state = absorb(pieces, slots, state, index == len(groups) - 1)
        trace_out, suffix_out = state
    return trace_out, suffix_out[None]


def solution(mesh):
    return jax.shard_map(
        functools.partial(local, mesh.shape["ctx"], mesh.shape["tp"]),
        mesh=mesh,
        in_specs=(
            P(("ctx", "tp"), None),
            P(("ctx", "tp"), None),
            P("ctx", "tp", None),
            P("ctx", "tp", None),
            P("ctx"),
            P("ctx"),
            P("ctx"),
        ),
        out_specs=(P(("ctx", "tp"), None), P("ctx", "tp", None)),
        check_vma=False,
    )
```

time: 57.6 us -> 58.7 us (1.019)
  waiting for transfers between devices: 19.4 us -> 14 us
  Pallas kernels: 14.9 us -> 19.6 us
  local copies, waits for them, and re-layouts: 1.1 us -> 3.15 us
  other arithmetic: 0.92 us -> 0.06 us
  starting transfers between devices: 18.1 us -> 18.9 us
    ppermute x16 -> x11, waiting for transfers between devices: 19.4 us -> 6.14 us  [swap(): return lax.ppermute(array, axis, [(i, i ^ bit) for i in range(size)])]
    ppermute x0 -> x2, waiting for transfers between devices: none -> 7.82 us  [local(): lax.ppermute(a, ('ctx', 'tp'), [(i * tp_size + j, (i ^ 1) * tp_size + (j...]
    pallas_call x3, Pallas kernels: 14.9 us -> 19.6 us  [attend(): pl.pallas_call(functools.partial(attend_kernel, slots, OWN_ORDER, len(own...]
    ppermute x0 -> x2, starting transfers between devices: none -> 2.05 us  [local(): lax.ppermute(a, ('ctx', 'tp'), [(i * tp_size + j, (i ^ 1) * tp_size + (j...]
    unnamed x15 -> x19, local copies, waits for them, and re-layouts: 1.03 us -> 3.04 us
    ppermute x16 -> x11, starting transfers between devices: 14 us -> 13 us  [swap(): return lax.ppermute(array, axis, [(i, i ^ bit) for i in range(size)])]
    concatenate x1 -> x2, other arithmetic: 0.92 us -> 0.06 us  [local(): jnp.concatenate([own, own_x, own_y, own_d, suffix_own, suffix_y], axis=0)]
  transfers between devices with their start and end apart: 19 -> 16, of which waited for: 8 -> 5; matrix products, arithmetic and copies ran while one was open for 4% -> 4% of each run, Pallas kernels for 14% -> 23%
where the time goes in v2:
time: 58.7 us; the launch traced here: 58.5 us
  Pallas kernels  19.6 us (33%)
  starting transfers between devices  18.9 us (32%)
  waiting for transfers between devices  14 us (24%)
  local copies, waits for them, and re-layouts  3.15 us (5%)
  between operations  2.79 us (5%)
    pallas_call x3, Pallas kernels, attend(): pl.pallas_call(functools.partial(attend_kernel, slots, OWN_ORDER, len(own...  19.6 us
    ppermute x11, starting transfers between devices, swap(): return lax.ppermute(array, axis, [(i, i ^ bit) for i in range(size)])  13 us
    ppermute x2, waiting for transfers between devices, local(): lax.ppermute(a, ('ctx', 'tp'), [(i * tp_size + j, (i ^ 1) * tp_size + (j...  7.82 us
    ppermute x11, waiting for transfers between devices, swap(): return lax.ppermute(array, axis, [(i, i ^ bit) for i in range(size)])  6.14 us
    ppermute x3, starting transfers between devices, local(): lax.ppermute(a, 'ctx', [(i, (i + 2 * shift) % ctx_size) for i in range(ct...  3.77 us
    unnamed x19, local copies, waits for them, and re-layouts  3.04 us
    ppermute x2, starting transfers between devices, local(): lax.ppermute(a, ('ctx', 'tp'), [(i * tp_size + j, (i ^ 1) * tp_size + (j...  2.05 us
  transfers between devices with their start and end apart: 16, of which 5 were waited for; matrix products, arithmetic and copies ran while one was open for 4% of the time, Pallas kernels for 23%

profile of v2, /device:TPU:1, one launch (start us, length us, event | category | flops | bytes accessed | tf_op | source)
XLA Modules:
  0.0 58.5 jit_solution(10497320000015246461)
XLA Ops:
  0.6 2.1 %collective-permute-start.10 = (bf16[32,2048]{1,0:T(8,128)(2,1)}, bf16[32,2048]{1,0:T(8,128)(2,1)S(1)}, u32[]{:S(2)}, u32[]{:S(2)}) collective-permute-start(bf16[32,2048]{1,0:T(8,128)(2,1)} %param.8), channel_id=1, source_target_pairs={{0,2},{1,3},{2,0},{3,1},{4,6},{5,7},{6,4},{7,5},{8,10},{9,11},{10,... | collective-permute-start | bytes 393224 | tf_op jit(solution)/shard_map/ppermute | solution.py:158
  2.8 1.2 %collective-permute-start.12 = (bf16[32,2048]{1,0:T(8,128)(2,1)}, bf16[32,2048]{1,0:T(8,128)(2,1)S(1)}, u32[]{:S(2)}, u32[]{:S(2)}) collective-permute-start(bf16[32,2048]{1,0:T(8,128)(2,1)} %param.8), channel_id=1, source_target_pairs={{0,4},{4,0},{8,12},{12,8},{16,20},{20,16},{24,28},{28,24},{1,5},{5... | collective-permute-start | bytes 393224 | tf_op jit(solution)/shard_map/ppermute | solution.py:158
  4.0 1.3 %collective-permute-start.5 = (bf16[32,2048]{1,0:T(8,128)(2,1)}, bf16[32,2048]{1,0:T(8,128)(2,1)S(1)}, u32[]{:S(2)}, u32[]{:S(2)}) collective-permute-start(bf16[32,2048]{1,0:T(8,128)(2,1)} %param.8), channel_id=1, source_target_pairs={{0,8},{4,12},{8,16},{12,20},{16,24},{20,28},{24,0},{28,4},{1,9},{5... | collective-permute-start | bytes 393224 | tf_op jit(solution)/shard_map/ppermute | solution.py:174
  5.3 2.0 %collective-permute-start.6 = (bf16[32,2048]{1,0:T(8,128)(2,1)}, bf16[32,2048]{1,0:T(8,128)(2,1)S(1)}, u32[]{:S(2)}, u32[]{:S(2)}) collective-permute-start(bf16[32,2048]{1,0:T(8,128)(2,1)} %param.8), channel_id=1, source_target_pairs={{0,24},{4,28},{8,0},{12,4},{16,8},{20,12},{24,16},{28,20},{1,25},{... | collective-permute-start | bytes 393224 | tf_op jit(solution)/shard_map/ppermute | solution.py:174
  7.3 0.5 collective-permute-start
  9.7 1.0 %constant_dynamic-update-slice_fusion.10 = bf16[192,2048]{1,0:T(8,128)(2,1)S(1)} fusion(bf16[32,2048]{1,0:T(8,128)(2,1)} %param.8), kind=kLoop, calls=%fused_computation.12 | loop fusion | bytes 262144
  11.3 3.5 %collective-permute-done.13 = bf16[32,2048]{1,0:T(8,128)(2,1)S(1)} collective-permute-done((bf16[32,2048]{1,0:T(8,128)(2,1)S(1)}, bf16[32,2048]{1,0:T(8,128)(2,1)S(1)}, u32[]{:S(2)}, u32[]{:S(2)}) %collective-permute-start.13) | collective-permute-done | bytes 131104 | tf_op jit(solution)/shard_map/ppermute | solution.py:158
  14.8 1.0 %constant_dynamic-update-slice_fusion.6 = bf16[192,2048]{1,0:T(8,128)(2,1)S(1)} fusion(bf16[192,2048]{1,0:T(8,128)(2,1)S(1)} %constant_dynamic-update-slice_fusion.7, bf16[1,32,2048]{2,1,0:T(8,128)(2,1)} %param.10), kind=kLoop, calls=%fused_computation.8 | loop fusion | bytes 262144
  15.8 3.6 %collective-permute-start.14 = (bf16[192,2048]{1,0:T(8,128)(2,1)S(1)}, bf16[192,2048]{1,0:T(8,128)(2,1)S(1)}, u32[]{:S(2)}, u32[]{:S(2)}) collective-permute-start(bf16[192,2048]{1,0:T(8,128)(2,1)S(1)} %constant_dynamic-update-slice_fusion.5), channel_id=1, source_target_pairs={{0,1},{1,0},{2,3},{3,2},{4,5},{5,4},{6,7},{7,6},{8,9},{9,8},{10,11... | collective-permute-start | bytes 2359304 | tf_op jit(solution)/shard_map/ppermute | solution.py:158
  19.5 0.3 collective-permute-start.7
  19.8 1.2 %collective-permute-start.8 = (bf16[64,2048]{1,0:T(8,128)(2,1)S(1)}, bf16[64,2048]{1,0:T(8,128)(2,1)S(1)}, u32[]{:S(2)}, u32[]{:S(2)}) collective-permute-start(bf16[64,2048]{1,0:T(8,128)(2,1)S(1)} %get-tuple-element.26), channel_id=1, source_target_pairs={{0,2},{1,3},{2,0},{3,1},{4,6},{5,7},{6,4},{7,5},{8,10},{9,11},{10,... | collective-permute-start | bytes 786440 | tf_op jit(solution)/shard_map/ppermute | solution.py:158
  21.0 1.2 %collective-permute-start.9 = (bf16[64,2048]{1,0:T(8,128)(2,1)S(1)}, bf16[64,2048]{1,0:T(8,128)(2,1)S(1)}, u32[]{:S(2)}, u32[]{:S(2)}) collective-permute-start(bf16[64,2048]{1,0:T(8,128)(2,1)S(1)} %get-tuple-element.26), channel_id=1, source_target_pairs={{0,6},{1,7},{2,4},{3,5},{4,2},{5,3},{6,0},{7,1},{8,14},{9,15},{10,... | collective-permute-start | bytes 786440 | tf_op jit(solution)/shard_map/ppermute | solution.py:178
  22.4 0.8 %copy-done = bf16[32,5120]{1,0:T(8,128)(2,1)S(1)} copy-done((bf16[32,5120]{1,0:T(8,128)(2,1)S(1)}, bf16[32,5120]{1,0:T(8,128)(2,1)}, u32[]{:S(2)}) %copy-start) | copy-done | bytes 327704
  23.3 5.6 %shard_map.86 = (f32[8,320,128]{2,1,0:T(8,128)S(1)}, f32[8,320,128]{2,1,0:T(8,128)S(1)}) custom-call(s32[1]{0:T(128)S(6)} %copy.22.refs_0_, s32[1]{0:T(128)S(6)} %copy.23.refs_1_, s32[1]{0:T(128)S(6)} %copy.24.refs_2_, bf16[32,5120]{1,0:T(8,128)(2,1)S(1)} %copy-done, bf16[32,5120]{1,0:T(8,128)(2,1)S(1)} %bitcast.4, ...), custom_call_target="tpu_custom_call" | custom-call | flops 1006632960 | bytes 1572864 | tf_op jit(solution)/shard_map/pallas_call | solution.py:142
  28.9 5.1 %collective-permute-done.9 = bf16[64,2048]{1,0:T(8,128)(2,1)S(1)} collective-permute-done((bf16[64,2048]{1,0:T(8,128)(2,1)S(1)}, bf16[64,2048]{1,0:T(8,128)(2,1)S(1)}, u32[]{:S(2)}, u32[]{:S(2)}) %collective-permute-start.9) | collective-permute-done | bytes 262176 | tf_op jit(solution)/shard_map/ppermute | solution.py:178
  34.1 0.9 %collective-permute-start.15 = (bf16[288,2048]{1,0:T(8,128)(2,1)S(1)}, bf16[288,2048]{1,0:T(8,128)(2,1)S(1)}, u32[]{:S(2)}, u32[]{:S(2)}) collective-permute-start(bf16[288,2048]{1,0:T(8,128)(2,1)S(1)} %constant_dynamic-update-slice_fusion.11.refs_5_), channel_id=1, source_target_pairs={{0,1},{1,0},{2,3},{3,2},{4,5},{5,4},{6,7},{7,6},{8,9},{9,8},{10,11... | collective-permute-start | bytes 3538952 | tf_op jit(solution)/shard_map/ppermute | solution.py:158
  35.0 0.5 collective-permute-start.1
  35.5 1.2 %collective-permute-start.2 = (bf16[32,2048]{1,0:T(8,128)(2,1)S(1)}, bf16[32,2048]{1,0:T(8,128)(2,1)S(1)}, u32[]{:S(2)}, u32[]{:S(2)}) collective-permute-start(bf16[32,2048]{1,0:T(8,128)(2,1)S(1)} %collective-permute-done), channel_id=1, source_target_pairs={{0,2},{1,3},{2,0},{3,1},{4,6},{5,7},{6,4},{7,5},{8,10},{9,11},{10,... | collective-permute-start | bytes 393224 | tf_op jit(solution)/shard_map/ppermute | solution.py:158
  36.8 0.9 %collective-permute-start.3 = (bf16[32,2048]{1,0:T(8,128)(2,1)S(1)}, bf16[32,2048]{1,0:T(8,128)(2,1)S(1)}, u32[]{:S(2)}, u32[]{:S(2)}) collective-permute-start(bf16[32,2048]{1,0:T(8,128)(2,1)S(1)} %collective-permute-done), channel_id=1, source_target_pairs={{0,6},{1,7},{2,4},{3,5},{4,2},{5,3},{6,0},{7,1},{8,14},{9,15},{10,... | collective-permute-start | bytes 393224 | tf_op jit(solution)/shard_map/ppermute | solution.py:178
  37.7 2.4 %collective-permute-done.1 = bf16[32,2048]{1,0:T(8,128)(2,1)S(1)} collective-permute-done((bf16[32,2048]{1,0:T(8,128)(2,1)S(1)}, bf16[32,2048]{1,0:T(8,128)(2,1)S(1)}, u32[]{:S(2)}, u32[]{:S(2)}) %collective-permute-start.1) | collective-permute-done | bytes 131104 | tf_op jit(solution)/shard_map/ppermute | solution.py:158
  40.3 2.7 %collective-permute-done.3 = bf16[32,2048]{1,0:T(8,128)(2,1)S(1)} collective-permute-done((bf16[32,2048]{1,0:T(8,128)(2,1)S(1)}, bf16[32,2048]{1,0:T(8,128)(2,1)S(1)}, u32[]{:S(2)}, u32[]{:S(2)}) %collective-permute-start.3) | collective-permute-done | bytes 131104 | tf_op jit(solution)/shard_map/ppermute | solution.py:178
  43.0 1.4 %collective-permute-start.4 = (bf16[96,2048]{1,0:T(8,128)(2,1)S(1)}, bf16[96,2048]{1,0:T(8,128)(2,1)S(1)}, u32[]{:S(2)}, u32[]{:S(2)}) collective-permute-start(bf16[96,2048]{1,0:T(8,128)(2,1)S(1)} %constant_dynamic-update-slice_fusion.refs_5_), channel_id=1, source_target_pairs={{0,1},{1,0},{2,3},{3,2},{4,5},{5,4},{6,7},{7,6},{8,9},{9,8},{10,11... | collective-permute-start | bytes 1179656 | tf_op jit(solution)/shard_map/ppermute | solution.py:158
  44.4 8.2 %shard_map.87 = (f32[8,320,128]{2,1,0:T(8,128)S(1)}, f32[8,320,128]{2,1,0:T(8,128)S(1)}) custom-call(s32[1]{0:T(128)S(6)} %copy.22.refs_0_, s32[1]{0:T(128)S(6)} %copy.23.refs_1_, s32[1]{0:T(128)S(6)} %copy.24.refs_2_, bf16[32,5120]{1,0:T(8,128)(2,1)S(1)} %copy-done, bf16[32,5120]{1,0:T(8,128)(2,1)S(1)} %bitcast.5, ...), custom_call_target="tpu_custom_call" | custom-call | flops 1509949440 | bytes 2359296 | tf_op jit(solution)/shard_map/pallas_call | solution.py:142
  52.5 5.9 %shard_map.88 = (bf16[32,5120]{1,0:T(8,128)(2,1)}, bf16[32,5120]{1,0:T(8,128)(2,1)}) custom-call(s32[1]{0:T(128)S(6)} %copy.22.refs_0_, s32[1]{0:T(128)S(6)} %copy.23.refs_1_, s32[1]{0:T(128)S(6)} %copy.24.refs_2_, bf16[32,5120]{1,0:T(8,128)(2,1)S(1)} %copy-done, bf16[32,5120]{1,0:T(8,128)(2,1)S(1)} %bitcast.6, ...), custom_call_target="tpu_custom_call" | custom-call | flops 503316480 | bytes 786432 | tf_op jit(solution)/shard_map/pallas_call | solution.py:142
  (38 shorter events, 1.2 us)
Async XLA Ops:
  0.6 10.1 %collective-permute-start.10 = (bf16[32,2048]{1,0:T(8,128)(2,1)}, bf16[32,2048]{1,0:T(8,128)(2,1)S(1)}, u32[]{:S(2)}, u32[]{:S(2)}) collective-permute-start(bf16[32,2048]{1,0:T(8,128)(2,1)} %param.8), channel_id=1, source_target_pairs={{0,2},{1,3},{2,0},{3,1},{4,6},{5,7},{6,4},{7,5},{8,10},{9,11},{10,... | collective-permute-start | bytes 393224 | tf_op jit(solution)/shard_map/ppermute | solution.py:158
  2.8 8.2 %collective-permute-start.12 = (bf16[32,2048]{1,0:T(8,128)(2,1)}, bf16[32,2048]{1,0:T(8,128)(2,1)S(1)}, u32[]{:S(2)}, u32[]{:S(2)}) collective-permute-start(bf16[32,2048]{1,0:T(8,128)(2,1)} %param.8), channel_id=1, source_target_pairs={{0,4},{4,0},{8,12},{12,8},{16,20},{20,16},{24,28},{28,24},{1,5},{5... | collective-permute-start | bytes 393224 | tf_op jit(solution)/shard_map/ppermute | solution.py:158
  4.0 15.4 %collective-permute-start.5 = (bf16[32,2048]{1,0:T(8,128)(2,1)}, bf16[32,2048]{1,0:T(8,128)(2,1)S(1)}, u32[]{:S(2)}, u32[]{:S(2)}) collective-permute-start(bf16[32,2048]{1,0:T(8,128)(2,1)} %param.8), channel_id=1, source_target_pairs={{0,8},{4,12},{8,16},{12,20},{16,24},{20,28},{24,0},{28,4},{1,9},{5... | collective-permute-start | bytes 393224 | tf_op jit(solution)/shard_map/ppermute | solution.py:174
  5.3 14.2 %collective-permute-start.6 = (bf16[32,2048]{1,0:T(8,128)(2,1)}, bf16[32,2048]{1,0:T(8,128)(2,1)S(1)}, u32[]{:S(2)}, u32[]{:S(2)}) collective-permute-start(bf16[32,2048]{1,0:T(8,128)(2,1)} %param.8), channel_id=1, source_target_pairs={{0,24},{4,28},{8,0},{12,4},{16,8},{20,12},{24,16},{28,20},{1,25},{... | collective-permute-start | bytes 393224 | tf_op jit(solution)/shard_map/ppermute | solution.py:174
  7.3 26.8 %collective-permute-start = (bf16[32,2048]{1,0:T(8,128)(2,1)}, bf16[32,2048]{1,0:T(8,128)(2,1)S(1)}, u32[]{:S(2)}, u32[]{:S(2)}) collective-permute-start(bf16[32,2048]{1,0:T(8,128)(2,1)} %param.8), channel_id=1, source_target_pairs={{0,16},{4,20},{8,24},{12,28},{16,0},{20,4},{24,8},{28,12},{1,17},{... | collective-permute-start | bytes 393224 | tf_op jit(solution)/shard_map/ppermute | solution.py:174
  9.7 12.5 %copy-start.3 = (bf16[32,2048]{1,0:T(8,128)(2,1)S(1)}, bf16[32,2048]{1,0:T(8,128)(2,1)}, u32[]{:S(2)}) copy-start(bf16[32,2048]{1,0:T(8,128)(2,1)} %param.8) | copy-start | bytes 393220
  10.7 5.1 %collective-permute-start.11 = (bf16[32,2048]{1,0:T(8,128)(2,1)}, bf16[32,2048]{1,0:T(8,128)(2,1)S(1)}, u32[]{:S(2)}, u32[]{:S(2)}) collective-permute-start(bf16[32,2048]{1,0:T(8,128)(2,1)} %bitcast.7), channel_id=1, source_target_pairs={{0,2},{1,3},{2,0},{3,1},{4,6},{5,7},{6,4},{7,5},{8,10},{9,11},{10,... | collective-permute-start | bytes 393224 | tf_op jit(solution)/shard_map/ppermute | solution.py:158
  11.0 3.8 %collective-permute-start.13 = (bf16[32,2048]{1,0:T(8,128)(2,1)S(1)}, bf16[32,2048]{1,0:T(8,128)(2,1)S(1)}, u32[]{:S(2)}, u32[]{:S(2)}) collective-permute-start(bf16[32,2048]{1,0:T(8,128)(2,1)S(1)} %collective-permute-done.10), channel_id=1, source_target_pairs={{0,4},{4,0},{8,12},{12,8},{16,20},{20,16},{24,28},{28,24},{1,5},{5... | collective-permute-start | bytes 393224 | tf_op jit(solution)/shard_map/ppermute | solution.py:158
  14.8 7.4 %copy-start.2 = (bf16[1,32,2048]{2,1,0:T(8,128)(2,1)S(1)}, bf16[1,32,2048]{2,1,0:T(8,128)(2,1)}, u32[]{:S(2)}) copy-start(bf16[1,32,2048]{2,1,0:T(8,128)(2,1)} %param.10) | copy-start | bytes 393220
  15.8 6.5 %collective-permute-start.14 = (bf16[192,2048]{1,0:T(8,128)(2,1)S(1)}, bf16[192,2048]{1,0:T(8,128)(2,1)S(1)}, u32[]{:S(2)}, u32[]{:S(2)}) collective-permute-start(bf16[192,2048]{1,0:T(8,128)(2,1)S(1)} %constant_dynamic-update-slice_fusion.5), channel_id=1, source_target_pairs={{0,1},{1,0},{2,3},{3,2},{4,5},{5,4},{6,7},{7,6},{8,9},{9,8},{10,11... | collective-permute-start | bytes 2359304 | tf_op jit(solution)/shard_map/ppermute | solution.py:158
  19.5 9.4 %collective-permute-start.7 = (bf16[64,2048]{1,0:T(8,128)(2,1)S(1)}, bf16[64,2048]{1,0:T(8,128)(2,1)S(1)}, u32[]{:S(2)}, u32[]{:S(2)}) collective-permute-start(bf16[64,2048]{1,0:T(8,128)(2,1)S(1)} %get-tuple-element.26), channel_id=1, source_target_pairs={{0,4},{4,0},{8,12},{12,8},{16,20},{20,16},{24,28},{28,24},{1,5},{5... | collective-permute-start | bytes 786440 | tf_op jit(solution)/shard_map/ppermute | solution.py:158
  19.8 9.1 %collective-permute-start.8 = (bf16[64,2048]{1,0:T(8,128)(2,1)S(1)}, bf16[64,2048]{1,0:T(8,128)(2,1)S(1)}, u32[]{:S(2)}, u32[]{:S(2)}) collective-permute-start(bf16[64,2048]{1,0:T(8,128)(2,1)S(1)} %get-tuple-element.26), channel_id=1, source_target_pairs={{0,2},{1,3},{2,0},{3,1},{4,6},{5,7},{6,4},{7,5},{8,10},{9,11},{10,... | collective-permute-start | bytes 786440 | tf_op jit(solution)/shard_map/ppermute | solution.py:158
  21.0 13.0 %collective-permute-start.9 = (bf16[64,2048]{1,0:T(8,128)(2,1)S(1)}, bf16[64,2048]{1,0:T(8,128)(2,1)S(1)}, u32[]{:S(2)}, u32[]{:S(2)}) collective-permute-start(bf16[64,2048]{1,0:T(8,128)(2,1)S(1)} %get-tuple-element.26), channel_id=1, source_target_pairs={{0,6},{1,7},{2,4},{3,5},{4,2},{5,3},{6,0},{7,1},{8,14},{9,15},{10,... | collective-permute-start | bytes 786440 | tf_op jit(solution)/shard_map/ppermute | solution.py:178
  22.3 1.0 %copy-start = (bf16[32,5120]{1,0:T(8,128)(2,1)S(1)}, bf16[32,5120]{1,0:T(8,128)(2,1)}, u32[]{:S(2)}) copy-start(bf16[32,5120]{1,0:T(8,128)(2,1)} %refs_3_.5) | copy-start | bytes 983044
  22.3 1.1 %copy-start.1 = (bf16[1,32,5120]{2,1,0:T(8,128)(2,1)S(1)}, bf16[1,32,5120]{2,1,0:T(8,128)(2,1)}, u32[]{:S(2)}) copy-start(bf16[1,32,5120]{2,1,0:T(8,128)(2,1)} %param.9) | copy-start | bytes 983044
  34.1 10.2 %collective-permute-start.15 = (bf16[288,2048]{1,0:T(8,128)(2,1)S(1)}, bf16[288,2048]{1,0:T(8,128)(2,1)S(1)}, u32[]{:S(2)}, u32[]{:S(2)}) collective-permute-start(bf16[288,2048]{1,0:T(8,128)(2,1)S(1)} %constant_dynamic-update-slice_fusion.11.refs_5_), channel_id=1, source_target_pairs={{0,1},{1,0},{2,3},{3,2},{4,5},{5,4},{6,7},{7,6},{8,9},{9,8},{10,11... | collective-permute-start | bytes 3538952 | tf_op jit(solution)/shard_map/ppermute | solution.py:158
  35.0 5.1 %collective-permute-start.1 = (bf16[32,2048]{1,0:T(8,128)(2,1)S(1)}, bf16[32,2048]{1,0:T(8,128)(2,1)S(1)}, u32[]{:S(2)}, u32[]{:S(2)}) collective-permute-start(bf16[32,2048]{1,0:T(8,128)(2,1)S(1)} %collective-permute-done), channel_id=1, source_target_pairs={{0,4},{4,0},{8,12},{12,8},{16,20},{20,16},{24,28},{28,24},{1,5},{5... | collective-permute-start | bytes 393224 | tf_op jit(solution)/shard_map/ppermute | solution.py:158
  35.5 4.7 %collective-permute-start.2 = (bf16[32,2048]{1,0:T(8,128)(2,1)S(1)}, bf16[32,2048]{1,0:T(8,128)(2,1)S(1)}, u32[]{:S(2)}, u32[]{:S(2)}) collective-permute-start(bf16[32,2048]{1,0:T(8,128)(2,1)S(1)} %collective-permute-done), channel_id=1, source_target_pairs={{0,2},{1,3},{2,0},{3,1},{4,6},{5,7},{6,4},{7,5},{8,10},{9,11},{10,... | collective-permute-start | bytes 393224 | tf_op jit(solution)/shard_map/ppermute | solution.py:158
  36.8 6.2 %collective-permute-start.3 = (bf16[32,2048]{1,0:T(8,128)(2,1)S(1)}, bf16[32,2048]{1,0:T(8,128)(2,1)S(1)}, u32[]{:S(2)}, u32[]{:S(2)}) collective-permute-start(bf16[32,2048]{1,0:T(8,128)(2,1)S(1)} %collective-permute-done), channel_id=1, source_target_pairs={{0,6},{1,7},{2,4},{3,5},{4,2},{5,3},{6,0},{7,1},{8,14},{9,15},{10,... | collective-permute-start | bytes 393224 | tf_op jit(solution)/shard_map/ppermute | solution.py:178
  43.0 9.6 %collective-permute-start.4 = (bf16[96,2048]{1,0:T(8,128)(2,1)S(1)}, bf16[96,2048]{1,0:T(8,128)(2,1)S(1)}, u32[]{:S(2)}, u32[]{:S(2)}) collective-permute-start(bf16[96,2048]{1,0:T(8,128)(2,1)S(1)} %constant_dynamic-update-slice_fusion.refs_5_), channel_id=1, source_target_pairs={{0,1},{1,0},{2,3},{3,2},{4,5},{5,4},{6,7},{7,6},{8,9},{9,8},{10,11... | collective-permute-start | bytes 1179656 | tf_op jit(solution)/shard_map/ppermute | solution.py:158

commit v3 on v2

--- a/solution.py
+++ b/solution.py
@@ -59,7 +59,7 @@
         bias = jnp.where(hidden_trace | hidden_suffix, MASKED, 0.0).astype(jnp.bfloat16)
         k_aug_ref[index * rows:(index + 1) * rows, :] = bias
     total = rows * len(slots)
-    if first_call:
+    if own_count:
         for index, flip in enumerate(own_order):
             position = (tp ^ flip) * rows + row
             hidden = (lane > rows) & (position > tp * rows + (lane - rows - 1))
@@ -71,40 +71,42 @@
     half = GROUP * rows
     lane_out = lax.broadcasted_iota(jnp.int32, (2 * half, HEAD_SIZE), 1)
 
-    def one_head(g, _):
-        def columns(index):
-            return pl.ds(pl.multiple_of(index * HEAD_SIZE, HEAD_SIZE), HEAD_SIZE)
-
-        def stacked(parts, index):
-            return jnp.concatenate([part[:, columns(index)] for part in parts], axis=0)
-
+    def columns(index):
+        return slice(index * HEAD_SIZE, (index + 1) * HEAD_SIZE)
+
+    def stacked(parts, index):
+        return jnp.concatenate([part[:, columns(index)] for part in parts], axis=0)
+
+    def scores_of(g):
         query = jnp.concatenate(
             [ref[:, columns(g * GROUP + j)] for ref in (tq, sq) for j in range(GROUP)], axis=0
         )
         query = jnp.concatenate([query, q_aug], axis=1)
         scores = dot_t(query, jnp.concatenate([stacked(pieces, 2 * g), k_aug_ref[0:total]], axis=1))
+        if not own_count:
+            return scores, None
+        own_key = jnp.concatenate([stacked(own_pieces, 2 * g), k_aug_ref[total:total + own_total]], axis=1)
+        return scores, dot_t(query[half:], own_key)
+
+    def absorb_head(g, scores, own_scores):
         top = jnp.max(scores, axis=1, keepdims=True)
-        if first_call:
-            own_key = jnp.concatenate(
-                [stacked(own_pieces, 2 * g), k_aug_ref[total:total + own_total]], axis=1
-            )
-            own_scores = dot_t(query[half:], own_key)
+        if own_count:
             own_top = jnp.maximum(top[half:], jnp.max(own_scores, axis=1, keepdims=True))
             top = jnp.concatenate([top[:half], own_top], axis=0)
-        else:
+        if not first_call:
             old_top = stats_in[g, :, 0:1]
             top = jnp.maximum(old_top, top)
         weights = jnp.exp2((scores - top) * SCALE).astype(jnp.bfloat16)
         both = dot(weights, jnp.concatenate([stacked(pieces, 2 * g + 1), ones], axis=1))
         summed, denominator = both[:, :HEAD_SIZE], both[:, HEAD_SIZE:]
-        if first_call:
+        if own_count:
             own_weights = jnp.exp2((own_scores - top[half:]) * SCALE).astype(jnp.bfloat16)
             own_both = dot(own_weights, jnp.concatenate([stacked(own_pieces, 2 * g + 1), own_ones], axis=1))
             summed = jnp.concatenate([summed[:half], summed[half:] + own_both[:, :HEAD_SIZE]], axis=0)
             denominator = jnp.concatenate(
                 [denominator[:half], denominator[half:] + own_both[:, HEAD_SIZE:]], axis=0
             )
-        else:
+        if not first_call:
             rescale = jnp.exp2((old_top - top) * SCALE)
             summed = summed + sum_in[g] * rescale
             denominator = denominator + stats_in[g, :, 1:2] * rescale
@@ -118,15 +120,16 @@
         else:
             out_a[g] = jnp.where(lane_out == 0, top, denominator)
             out_b[g] = summed
-        return 0
-
-    lax.fori_loop(0, KEY_VALUE_HEADS, one_head, 0)
+
+    ahead = scores_of(0)
+    for g in range(KEY_VALUE_HEADS):
+        now, ahead = ahead, scores_of(g + 1) if g + 1 < KEY_VALUE_HEADS else None
+        absorb_head(g, *now)
 
 
 def attend(spans, tq, sq, own_pieces, pieces, slots, tp_size, carry, last_call):
     first_call = carry is None
     rows = tq.shape[0]
-    own_pieces = list(own_pieces) if first_call else []
     smem = pl.BlockSpec(memory_space=pltpu.SMEM)
     vmem = pl.BlockSpec(memory_space=pltpu.VMEM)
     operands = [*spans, tq, sq, *own_pieces, *pieces]
@@ -184,40 +187,39 @@
     def slot(shift, x, y, c=0):
         return lambda ctx, tp: (((ctx + ctx_size - 2 * shift) % ctx_size) ^ x) * tp_size + (tp ^ (2 * y + c))
 
-    def absorb(pieces, slots, state, last_call):
+    def absorb(pieces, slots, state, last_call, suffix_pieces=()):
         return attend(spans, trace_q, sq, suffix_pieces, pieces, slots, tp_size, state, last_call)
 
     def with_core(names):
         return [slot(*n) for n in names] + [slot(*n, 1) for n in names]
 
     if ctx_size == 8 and tp_size == 4:
-        own = trace_key_value
-        up, down = along_z(own, 1), along_z(own, 3)
-        own_x, own_y = across_x(own), across_y(own)
-        far = along_z(own, 2)
-        own_d = across_x(own_y)
-        suffix_y = across_y(after(suffix_own, own_y))
-        plane = jnp.concatenate([own, own_x, own_y, own_d, suffix_own, suffix_y], axis=0)
-        plane_core = core(plane)
-        here = 4 * rows
-        suffix_pieces = [plane[here:], plane_core[here:]]
-        first = [plane[:here], plane_core[:here]]
+        up, down = along_z(trace_key_value, 1), along_z(trace_key_value, 3)
+        own_x, own_y = across_x(trace_key_value), across_y(trace_key_value)
+        own_d = across_both(trace_key_value)
+        own, suffix_own, own_x, own_y = lax.optimization_barrier((trace_key_value, suffix_own, own_x, own_y))
+        suffix_y = across_y(suffix_own)
+        plane = jnp.concatenate([own, own_x, own_y, own_d], axis=0)
+        first = [plane, core(plane)]
         first_slots = with_core([(0, 0, 0), (0, 1, 0), (0, 0, 1), (0, 1, 1)])
 
+        far = along_z(up, 1)
         near = jnp.concatenate([up, down], axis=0)
-        near_x, near_y, near_d = across_x(near), across_y(near), across_both(near)
+        near_x, near_y = across_x(near), across_y(near)
+        far_x, far_y = across_x(far), across_y(far)
+        rest_d = across_both(jnp.concatenate([near, far], axis=0))
+        far, first[0] = lax.optimization_barrier((far, first[0]))
         state = absorb(first, first_slots, None, False)
-        far_x, far_y, far_d = across_x(far), across_y(far), across_both(far)
-        near_x, near_y, near_d, state = lax.optimization_barrier((near_x, near_y, near_d, state))
-        planes = jnp.concatenate([near, near_x, near_y, near_d, far], axis=0)
-        second = [planes, core(planes)]
-        second_slots = with_core(
-            [(z, x, y) for x, y in ((0, 0), (1, 0), (0, 1), (1, 1)) for z in (1, 3)] + [(2, 0, 0)]
-        )
-        state = absorb(second, second_slots, state, False)
-        far_rest = jnp.concatenate([far_x, far_y, far_d], axis=0)
-        third = [far_rest, core(far_rest)]
-        third_slots = with_core([(2, 1, 0), (2, 0, 1), (2, 1, 1)])
+        near_x, near_y, suffix_y, state = lax.optimization_barrier((near_x, near_y, suffix_y, state))
+        planes = jnp.concatenate([near, near_x, near_y, far, suffix_own, suffix_y], axis=0)
+        planes_core = core(planes)
+        here = 7 * rows
+        second = [planes[:here], planes_core[:here]]
+        second_slots = with_core([(z, x, y) for x, y in ((0, 0), (1, 0), (0, 1)) for z in (1, 3)] + [(2, 0, 0)])
+        state = absorb(second, second_slots, state, False, [planes[here:], planes_core[here:]])
+        rest = jnp.concatenate([far_x, far_y, rest_d], axis=0)
+        third = [rest, core(rest)]
+        third_slots = with_core([(2, 1, 0), (2, 0, 1), (1, 1, 1), (3, 1, 1), (2, 1, 1)])
         trace_out, suffix_out = absorb(third, third_slots, state, True)
     else:
         gathered = lax.all_gather(trace_key_value, ("ctx", "tp"), axis=0, tiled=True)
@@ -234,7 +236,8 @@
 
         state = None
         for index, (pieces, slots) in enumerate(groups):
-            state = absorb(pieces, slots, state, index == len(groups) - 1)
+            own_here = suffix_pieces if index == 0 else ()
+            state = absorb(pieces, slots, state, index == len(groups) - 1, own_here)
         trace_out, suffix_out = state
     return trace_out, suffix_out[None]
 

time: 58.7 us -> 50.1 us (0.85)
  Pallas kernels: 19.6 us -> 11.1 us
  local copies, waits for them, and re-layouts: 3.15 us -> 1.31 us
  starting transfers between devices: 18.9 us -> 20.3 us
    pallas_call x3, Pallas kernels: 19.6 us -> 11.1 us  [attend(): pl.pallas_call(functools.partial(attend_kernel, slots, OWN_ORDER, len(own...]
    ppermute x2, waiting for transfers between devices: 7.82 us -> 0.01 us  [local(): lax.ppermute(a, ('ctx', 'tp'), [(i * tp_size + j, (i ^ 1) * tp_size + (j...]
    ppermute x11 -> x10, waiting for transfers between devices: 6.14 us -> 10.8 us  [swap(): return lax.ppermute(array, axis, [(i, i ^ bit) for i in range(size)])]
    ppermute x3, waiting for transfers between devices: 0.01 us -> 3.04 us  [local(): lax.ppermute(a, 'ctx', [(i, (i + 2 * shift) % ctx_size) for i in range(ct...]
    unnamed x19 -> x16, local copies, waits for them, and re-layouts: 3.04 us -> 1.13 us
    ppermute x3, starting transfers between devices: 3.77 us -> 4.8 us  [local(): lax.ppermute(a, 'ctx', [(i, (i + 2 * shift) % ctx_size) for i in range(ct...]
    ppermute x11 -> x10, starting transfers between devices: 13 us -> 13.9 us  [swap(): return lax.ppermute(array, axis, [(i, i ^ bit) for i in range(size)])]
  transfers between devices with their start and end apart: 16 -> 15, of which waited for: 5 -> 3; matrix products, arithmetic and copies ran while one was open for 4% -> 3% of each run, Pallas kernels for 23% -> 14%
where the time goes in v3:
time: 50.1 us; the launch traced here: 49.4 us
  starting transfers between devices  20.3 us (41%)
  waiting for transfers between devices  13.8 us (28%)
  Pallas kernels  11.1 us (22%)
  between operations  2.8 us (6%)
  local copies, waits for them, and re-layouts  1.31 us (3%)
    ppermute x10, starting transfers between devices, swap(): return lax.ppermute(array, axis, [(i, i ^ bit) for i in range(size)])  13.9 us
    pallas_call x3, Pallas kernels, attend(): pl.pallas_call(functools.partial(attend_kernel, slots, OWN_ORDER, len(own...  11.1 us
    ppermute x10, waiting for transfers between devices, swap(): return lax.ppermute(array, axis, [(i, i ^ bit) for i in range(size)])  10.8 us
    ppermute x3, starting transfers between devices, local(): lax.ppermute(a, 'ctx', [(i, (i + 2 * shift) % ctx_size) for i in range(ct...  4.8 us
    ppermute x3, waiting for transfers between devices, local(): lax.ppermute(a, 'ctx', [(i, (i + 2 * shift) % ctx_size) for i in range(ct...  3.04 us
    ppermute x2, starting transfers between devices, local(): lax.ppermute(a, ('ctx', 'tp'), [(i * tp_size + j, (i ^ 1) * tp_size + (j...  1.63 us
    unnamed x16, local copies, waits for them, and re-layouts  1.13 us
  transfers between devices with their start and end apart: 15, of which 3 were waited for; matrix products, arithmetic and copies ran while one was open for 3% of the time, Pallas kernels for 14%

profile of v3, /device:TPU:1, one launch (start us, length us, event | category | flops | bytes accessed | tf_op | source)
XLA Modules:
  0.0 49.4 jit_solution(9348356648427777779)
XLA Ops:
  0.6 2.1 %collective-permute-start.7 = (bf16[32,2048]{1,0:T(8,128)(2,1)}, bf16[32,2048]{1,0:T(8,128)(2,1)S(1)}, u32[]{:S(2)}, u32[]{:S(2)}) collective-permute-start(bf16[32,2048]{1,0:T(8,128)(2,1)} %param.8), channel_id=1, source_target_pairs={{0,4},{4,0},{8,12},{12,8},{16,20},{20,16},{24,28},{28,24},{1,5},{5... | collective-permute-start | bytes 393224 | tf_op jit(solution)/shard_map/ppermute | solution.py:161
  2.7 1.2 %collective-permute-start.8 = (bf16[32,2048]{1,0:T(8,128)(2,1)}, bf16[32,2048]{1,0:T(8,128)(2,1)S(1)}, u32[]{:S(2)}, u32[]{:S(2)}) collective-permute-start(bf16[32,2048]{1,0:T(8,128)(2,1)} %param.8), channel_id=1, source_target_pairs={{0,2},{1,3},{2,0},{3,1},{4,6},{5,7},{6,4},{7,5},{8,10},{9,11},{10,... | collective-permute-start | bytes 393224 | tf_op jit(solution)/shard_map/ppermute | solution.py:161
  4.0 0.0 collective-permute-start.12
  4.0 1.5 %collective-permute-start = (bf16[32,2048]{1,0:T(8,128)(2,1)}, bf16[32,2048]{1,0:T(8,128)(2,1)S(1)}, u32[]{:S(2)}, u32[]{:S(2)}) collective-permute-start(bf16[32,2048]{1,0:T(8,128)(2,1)} %param.8), channel_id=1, source_target_pairs={{0,8},{4,12},{8,16},{12,20},{16,24},{20,28},{24,0},{28,4},{1,9},{5... | collective-permute-start | bytes 393224 | tf_op jit(solution)/shard_map/ppermute | solution.py:177
  5.5 2.0 %collective-permute-start.4 = (bf16[32,2048]{1,0:T(8,128)(2,1)}, bf16[32,2048]{1,0:T(8,128)(2,1)S(1)}, u32[]{:S(2)}, u32[]{:S(2)}) collective-permute-start(bf16[32,2048]{1,0:T(8,128)(2,1)} %param.8), channel_id=1, source_target_pairs={{0,24},{4,28},{8,0},{12,4},{16,8},{20,12},{24,16},{28,20},{1,25},{... | collective-permute-start | bytes 393224 | tf_op jit(solution)/shard_map/ppermute | solution.py:177
  9.5 0.9 %constant_dynamic-update-slice_fusion.8 = bf16[128,2048]{1,0:T(8,128)(2,1)S(1)} fusion(bf16[32,2048]{1,0:T(8,128)(2,1)} %param.8), kind=kLoop, calls=%fused_computation.10 | loop fusion | bytes 262144
  10.4 0.0 copy-start
  10.5 2.3 %collective-permute-start.13 = (bf16[128,2048]{1,0:T(8,128)(2,1)S(1)}, bf16[128,2048]{1,0:T(8,128)(2,1)S(1)}, u32[]{:S(2)}, u32[]{:S(2)}) collective-permute-start(bf16[128,2048]{1,0:T(8,128)(2,1)S(1)} %constant_dynamic-update-slice_fusion.5.refs_5_), channel_id=1, source_target_pairs={{0,1},{1,0},{2,3},{3,2},{4,5},{5,4},{6,7},{7,6},{8,9},{9,8},{10,11... | collective-permute-start | bytes 1572872 | tf_op jit(solution)/shard_map/ppermute | solution.py:161
  12.8 1.3 %collective-permute-start.1 = (bf16[32,2048]{1,0:T(8,128)(2,1)S(1)}, bf16[32,2048]{1,0:T(8,128)(2,1)S(1)}, u32[]{:S(2)}, u32[]{:S(2)}) collective-permute-start(bf16[32,2048]{1,0:T(8,128)(2,1)S(1)} %collective-permute-done), channel_id=1, source_target_pairs={{0,8},{4,12},{8,16},{12,20},{16,24},{20,28},{24,0},{28,4},{1,9},{5... | collective-permute-start | bytes 393224 | tf_op jit(solution)/shard_map/ppermute | solution.py:177
  14.1 1.3 %collective-permute-start.10 = (bf16[64,2048]{1,0:T(8,128)(2,1)S(1)}, bf16[64,2048]{1,0:T(8,128)(2,1)S(1)}, u32[]{:S(2)}, u32[]{:S(2)}) collective-permute-start(bf16[64,2048]{1,0:T(8,128)(2,1)S(1)} %get-tuple-element.44), channel_id=1, source_target_pairs={{0,2},{1,3},{2,0},{3,1},{4,6},{5,7},{6,4},{7,5},{8,10},{9,11},{10,... | collective-permute-start | bytes 786440 | tf_op jit(solution)/shard_map/ppermute | solution.py:161
  15.4 0.3 collective-permute-start.9
  15.7 0.1 collective-permute-start.11
  15.8 3.0 %collective-permute-done.1 = bf16[32,2048]{1,0:T(8,128)(2,1)S(1)} collective-permute-done((bf16[32,2048]{1,0:T(8,128)(2,1)S(1)}, bf16[32,2048]{1,0:T(8,128)(2,1)S(1)}, u32[]{:S(2)}, u32[]{:S(2)}) %collective-permute-start.1) | collective-permute-done | bytes 131104 | tf_op jit(solution)/shard_map/ppermute | solution.py:177
  18.8 1.6 %collective-permute-start.5 = (bf16[96,2048]{1,0:T(8,128)(2,1)S(1)}, bf16[96,2048]{1,0:T(8,128)(2,1)S(1)}, u32[]{:S(2)}, u32[]{:S(2)}) collective-permute-start(bf16[96,2048]{1,0:T(8,128)(2,1)S(1)} %pad_maximum_fusion), channel_id=1, source_target_pairs={{0,6},{1,7},{2,4},{3,5},{4,2},{5,3},{6,0},{7,1},{8,14},{9,15},{10,... | collective-permute-start | bytes 1179656 | tf_op jit(solution)/shard_map/ppermute | solution.py:181
  20.5 0.8 %collective-permute-start.2 = (bf16[32,2048]{1,0:T(8,128)(2,1)S(1)}, bf16[32,2048]{1,0:T(8,128)(2,1)S(1)}, u32[]{:S(2)}, u32[]{:S(2)}) collective-permute-start(bf16[32,2048]{1,0:T(8,128)(2,1)S(1)} %collective-permute-done.1), channel_id=1, source_target_pairs={{0,4},{4,0},{8,12},{12,8},{16,20},{20,16},{24,28},{28,24},{1,5},{5... | collective-permute-start | bytes 393224 | tf_op jit(solution)/shard_map/ppermute | solution.py:161
  21.3 1.1 %shard_map.86 = (f32[8,320,128]{2,1,0:T(8,128)S(1)}, f32[8,320,128]{2,1,0:T(8,128)S(1)}) custom-call(s32[1]{0:T(128)S(6)} %copy.25.refs_0_, s32[1]{0:T(128)S(6)} %copy.26.refs_1_, s32[1]{0:T(128)S(6)} %copy.27.refs_2_, bf16[32,5120]{1,0:T(8,128)(2,1)S(1)} %copy-done, bf16[32,5120]{1,0:T(8,128)(2,1)S(1)} %bitcast.3, ...), custom_call_target="tpu_custom_call" | custom-call | flops 671088640 | bytes 1048576 | tf_op jit(solution)/shard_map/pallas_call | solution.py:145
  22.4 10.2 %collective-permute-done.11 = bf16[32,2048]{1,0:T(8,128)(2,1)S(1)} collective-permute-done((bf16[32,2048]{1,0:T(8,128)(2,1)S(1)}, bf16[32,2048]{1,0:T(8,128)(2,1)S(1)}, u32[]{:S(2)}, u32[]{:S(2)}) %collective-permute-start.11) | collective-permute-done | bytes 131104 | tf_op jit(solution)/shard_map/ppermute | solution.py:161
  32.7 1.2 %collective-permute-start.3 = (bf16[32,2048]{1,0:T(8,128)(2,1)S(1)}, bf16[32,2048]{1,0:T(8,128)(2,1)S(1)}, u32[]{:S(2)}, u32[]{:S(2)}) collective-permute-start(bf16[32,2048]{1,0:T(8,128)(2,1)S(1)} %collective-permute-done.1), channel_id=1, source_target_pairs={{0,2},{1,3},{2,0},{3,1},{4,6},{5,7},{6,4},{7,5},{8,10},{9,11},{10,... | collective-permute-start | bytes 393224 | tf_op jit(solution)/shard_map/ppermute | solution.py:161
  34.1 1.8 %collective-permute-start.14 = (bf16[288,2048]{1,0:T(8,128)(2,1)S(1)}, bf16[288,2048]{1,0:T(8,128)(2,1)S(1)}, u32[]{:S(2)}, u32[]{:S(2)}) collective-permute-start(bf16[288,2048]{1,0:T(8,128)(2,1)S(1)} %constant_dynamic-update-slice_fusion.9), channel_id=1, source_target_pairs={{0,1},{1,0},{2,3},{3,2},{4,5},{5,4},{6,7},{7,6},{8,9},{9,8},{10,11... | collective-permute-start | bytes 3538952 | tf_op jit(solution)/shard_map/ppermute | solution.py:161
  35.9 0.5 %collective-permute-done.3 = bf16[32,2048]{1,0:T(8,128)(2,1)S(1)} collective-permute-done((bf16[32,2048]{1,0:T(8,128)(2,1)S(1)}, bf16[32,2048]{1,0:T(8,128)(2,1)S(1)}, u32[]{:S(2)}, u32[]{:S(2)}) %collective-permute-start.3) | collective-permute-done | bytes 131104 | tf_op jit(solution)/shard_map/ppermute | solution.py:161
  36.5 2.7 %collective-permute-start.6 = (bf16[160,2048]{1,0:T(8,128)(2,1)S(1)}, bf16[160,2048]{1,0:T(8,128)(2,1)S(1)}, u32[]{:S(2)}, u32[]{:S(2)}) collective-permute-start(bf16[160,2048]{1,0:T(8,128)(2,1)S(1)} %constant_dynamic-update-slice_fusion.refs_5_), channel_id=1, source_target_pairs={{0,1},{1,0},{2,3},{3,2},{4,5},{5,4},{6,7},{7,6},{8,9},{9,8},{10,11... | collective-permute-start | bytes 1966088 | tf_op jit(solution)/shard_map/ppermute | solution.py:161
  39.3 0.1 slice.13.refs_8_
  39.4 5.8 %shard_map.87 = (f32[8,320,128]{2,1,0:T(8,128)S(1)}, f32[8,320,128]{2,1,0:T(8,128)S(1)}) custom-call(s32[1]{0:T(128)S(6)} %copy.25.refs_0_, s32[1]{0:T(128)S(6)} %copy.26.refs_1_, s32[1]{0:T(128)S(6)} %copy.27.refs_2_, bf16[32,5120]{1,0:T(8,128)(2,1)S(1)} %copy-done, bf16[32,5120]{1,0:T(8,128)(2,1)S(1)} %bitcast.4, ...), custom_call_target="tpu_custom_call" | custom-call | flops 1509949440 | bytes 2359296 | tf_op jit(solution)/shard_map/pallas_call | solution.py:145
  45.2 4.2 %shard_map.88 = (bf16[32,5120]{1,0:T(8,128)(2,1)}, bf16[32,5120]{1,0:T(8,128)(2,1)}) custom-call(s32[1]{0:T(128)S(6)} %copy.25.refs_0_, s32[1]{0:T(128)S(6)} %copy.26.refs_1_, s32[1]{0:T(128)S(6)} %copy.27.refs_2_, bf16[32,5120]{1,0:T(8,128)(2,1)S(1)} %copy-done, bf16[32,5120]{1,0:T(8,128)(2,1)S(1)} %bitcast.5, ...), custom_call_target="tpu_custom_call" | custom-call | flops 838860800 | bytes 1310720 | tf_op jit(solution)/shard_map/pallas_call | solution.py:145
  (33 shorter events, 0.4 us)
Async XLA Ops:
  0.6 15.1 %copy-start.2 = (bf16[1,32,2048]{2,1,0:T(8,128)(2,1)S(1)}, bf16[1,32,2048]{2,1,0:T(8,128)(2,1)}, u32[]{:S(2)}) copy-start(bf16[1,32,2048]{2,1,0:T(8,128)(2,1)} %param.10) | copy-start | bytes 393220
  0.6 8.8 %collective-permute-start.7 = (bf16[32,2048]{1,0:T(8,128)(2,1)}, bf16[32,2048]{1,0:T(8,128)(2,1)S(1)}, u32[]{:S(2)}, u32[]{:S(2)}) collective-permute-start(bf16[32,2048]{1,0:T(8,128)(2,1)} %param.8), channel_id=1, source_target_pairs={{0,4},{4,0},{8,12},{12,8},{16,20},{20,16},{24,28},{28,24},{1,5},{5... | collective-permute-start | bytes 393224 | tf_op jit(solution)/shard_map/ppermute | solution.py:161
  2.7 6.7 %collective-permute-start.8 = (bf16[32,2048]{1,0:T(8,128)(2,1)}, bf16[32,2048]{1,0:T(8,128)(2,1)S(1)}, u32[]{:S(2)}, u32[]{:S(2)}) collective-permute-start(bf16[32,2048]{1,0:T(8,128)(2,1)} %param.8), channel_id=1, source_target_pairs={{0,2},{1,3},{2,0},{3,1},{4,6},{5,7},{6,4},{7,5},{8,10},{9,11},{10,... | collective-permute-start | bytes 393224 | tf_op jit(solution)/shard_map/ppermute | solution.py:161
  4.0 6.5 %collective-permute-start.12 = (bf16[32,2048]{1,0:T(8,128)(2,1)}, bf16[32,2048]{1,0:T(8,128)(2,1)S(1)}, u32[]{:S(2)}, u32[]{:S(2)}) collective-permute-start(bf16[32,2048]{1,0:T(8,128)(2,1)} %param.8), channel_id=1, source_target_pairs={{0,6},{1,7},{2,4},{3,5},{4,2},{5,3},{6,0},{7,1},{8,14},{9,15},{10,... | collective-permute-start | bytes 393224 | tf_op jit(solution)/shard_map/ppermute | solution.py:181
  4.0 8.8 %collective-permute-start = (bf16[32,2048]{1,0:T(8,128)(2,1)}, bf16[32,2048]{1,0:T(8,128)(2,1)S(1)}, u32[]{:S(2)}, u32[]{:S(2)}) collective-permute-start(bf16[32,2048]{1,0:T(8,128)(2,1)} %param.8), channel_id=1, source_target_pairs={{0,8},{4,12},{8,16},{12,20},{16,24},{20,28},{24,0},{28,4},{1,9},{5... | collective-permute-start | bytes 393224 | tf_op jit(solution)/shard_map/ppermute | solution.py:177
  5.5 8.6 %collective-permute-start.4 = (bf16[32,2048]{1,0:T(8,128)(2,1)}, bf16[32,2048]{1,0:T(8,128)(2,1)S(1)}, u32[]{:S(2)}, u32[]{:S(2)}) collective-permute-start(bf16[32,2048]{1,0:T(8,128)(2,1)} %param.8), channel_id=1, source_target_pairs={{0,24},{4,28},{8,0},{12,4},{16,8},{20,12},{24,16},{28,20},{1,25},{... | collective-permute-start | bytes 393224 | tf_op jit(solution)/shard_map/ppermute | solution.py:177
  10.4 10.9 %copy-start = (bf16[32,5120]{1,0:T(8,128)(2,1)S(1)}, bf16[32,5120]{1,0:T(8,128)(2,1)}, u32[]{:S(2)}) copy-start(bf16[32,5120]{1,0:T(8,128)(2,1)} %refs_3_.5) | copy-start | bytes 983044
  10.4 10.9 %copy-start.1 = (bf16[1,32,5120]{2,1,0:T(8,128)(2,1)S(1)}, bf16[1,32,5120]{2,1,0:T(8,128)(2,1)}, u32[]{:S(2)}) copy-start(bf16[1,32,5120]{2,1,0:T(8,128)(2,1)} %param.9) | copy-start | bytes 983044
  10.5 10.0 %collective-permute-start.13 = (bf16[128,2048]{1,0:T(8,128)(2,1)S(1)}, bf16[128,2048]{1,0:T(8,128)(2,1)S(1)}, u32[]{:S(2)}, u32[]{:S(2)}) collective-permute-start(bf16[128,2048]{1,0:T(8,128)(2,1)S(1)} %constant_dynamic-update-slice_fusion.5.refs_5_), channel_id=1, source_target_pairs={{0,1},{1,0},{2,3},{3,2},{4,5},{5,4},{6,7},{7,6},{8,9},{9,8},{10,11... | collective-permute-start | bytes 1572872 | tf_op jit(solution)/shard_map/ppermute | solution.py:161
  12.8 6.0 %collective-permute-start.1 = (bf16[32,2048]{1,0:T(8,128)(2,1)S(1)}, bf16[32,2048]{1,0:T(8,128)(2,1)S(1)}, u32[]{:S(2)}, u32[]{:S(2)}) collective-permute-start(bf16[32,2048]{1,0:T(8,128)(2,1)S(1)} %collective-permute-done), channel_id=1, source_target_pairs={{0,8},{4,12},{8,16},{12,20},{16,24},{20,28},{24,0},{28,4},{1,9},{5... | collective-permute-start | bytes 393224 | tf_op jit(solution)/shard_map/ppermute | solution.py:177
  14.1 19.8 %collective-permute-start.10 = (bf16[64,2048]{1,0:T(8,128)(2,1)S(1)}, bf16[64,2048]{1,0:T(8,128)(2,1)S(1)}, u32[]{:S(2)}, u32[]{:S(2)}) collective-permute-start(bf16[64,2048]{1,0:T(8,128)(2,1)S(1)} %get-tuple-element.44), channel_id=1, source_target_pairs={{0,2},{1,3},{2,0},{3,1},{4,6},{5,7},{6,4},{7,5},{8,10},{9,11},{10,... | collective-permute-start | bytes 786440 | tf_op jit(solution)/shard_map/ppermute | solution.py:161
  15.4 18.5 %collective-permute-start.9 = (bf16[64,2048]{1,0:T(8,128)(2,1)S(1)}, bf16[64,2048]{1,0:T(8,128)(2,1)S(1)}, u32[]{:S(2)}, u32[]{:S(2)}) collective-permute-start(bf16[64,2048]{1,0:T(8,128)(2,1)S(1)} %get-tuple-element.44), channel_id=1, source_target_pairs={{0,4},{4,0},{8,12},{12,8},{16,20},{20,16},{24,28},{28,24},{1,5},{5... | collective-permute-start | bytes 786440 | tf_op jit(solution)/shard_map/ppermute | solution.py:161
  15.7 17.0 %collective-permute-start.11 = (bf16[32,2048]{1,0:T(8,128)(2,1)S(1)}, bf16[32,2048]{1,0:T(8,128)(2,1)S(1)}, u32[]{:S(2)}, u32[]{:S(2)}) collective-permute-start(bf16[32,2048]{1,0:T(8,128)(2,1)S(1)} %bitcast.6), channel_id=1, source_target_pairs={{0,2},{1,3},{2,0},{3,1},{4,6},{5,7},{6,4},{7,5},{8,10},{9,11},{10,... | collective-permute-start | bytes 393224 | tf_op jit(solution)/shard_map/ppermute | solution.py:161
  18.8 17.7 %collective-permute-start.5 = (bf16[96,2048]{1,0:T(8,128)(2,1)S(1)}, bf16[96,2048]{1,0:T(8,128)(2,1)S(1)}, u32[]{:S(2)}, u32[]{:S(2)}) collective-permute-start(bf16[96,2048]{1,0:T(8,128)(2,1)S(1)} %pad_maximum_fusion), channel_id=1, source_target_pairs={{0,6},{1,7},{2,4},{3,5},{4,2},{5,3},{6,0},{7,1},{8,14},{9,15},{10,... | collective-permute-start | bytes 1179656 | tf_op jit(solution)/shard_map/ppermute | solution.py:181
  20.5 15.5 %collective-permute-start.2 = (bf16[32,2048]{1,0:T(8,128)(2,1)S(1)}, bf16[32,2048]{1,0:T(8,128)(2,1)S(1)}, u32[]{:S(2)}, u32[]{:S(2)}) collective-permute-start(bf16[32,2048]{1,0:T(8,128)(2,1)S(1)} %collective-permute-done.1), channel_id=1, source_target_pairs={{0,4},{4,0},{8,12},{12,8},{16,20},{20,16},{24,28},{28,24},{1,5},{5... | collective-permute-start | bytes 393224 | tf_op jit(solution)/shard_map/ppermute | solution.py:161
  32.7 3.8 %collective-permute-start.3 = (bf16[32,2048]{1,0:T(8,128)(2,1)S(1)}, bf16[32,2048]{1,0:T(8,128)(2,1)S(1)}, u32[]{:S(2)}, u32[]{:S(2)}) collective-permute-start(bf16[32,2048]{1,0:T(8,128)(2,1)S(1)} %collective-permute-done.1), channel_id=1, source_target_pairs={{0,2},{1,3},{2,0},{3,1},{4,6},{5,7},{6,4},{7,5},{8,10},{9,11},{10,... | collective-permute-start | bytes 393224 | tf_op jit(solution)/shard_map/ppermute | solution.py:161
  34.1 5.2 %collective-permute-start.14 = (bf16[288,2048]{1,0:T(8,128)(2,1)S(1)}, bf16[288,2048]{1,0:T(8,128)(2,1)S(1)}, u32[]{:S(2)}, u32[]{:S(2)}) collective-permute-start(bf16[288,2048]{1,0:T(8,128)(2,1)S(1)} %constant_dynamic-update-slice_fusion.9), channel_id=1, source_target_pairs={{0,1},{1,0},{2,3},{3,2},{4,5},{5,4},{6,7},{7,6},{8,9},{9,8},{10,11... | collective-permute-start | bytes 3538952 | tf_op jit(solution)/shard_map/ppermute | solution.py:161
  36.5 8.7 %collective-permute-start.6 = (bf16[160,2048]{1,0:T(8,128)(2,1)S(1)}, bf16[160,2048]{1,0:T(8,128)(2,1)S(1)}, u32[]{:S(2)}, u32[]{:S(2)}) collective-permute-start(bf16[160,2048]{1,0:T(8,128)(2,1)S(1)} %constant_dynamic-update-slice_fusion.refs_5_), channel_id=1, source_target_pairs={{0,1},{1,0},{2,3},{3,2},{4,5},{5,4},{6,7},{7,6},{8,9},{9,8},{10,11... | collective-permute-start | bytes 1966088 | tf_op jit(solution)/shard_map/ppermute | solution.py:161

commit v4 on v3

v4 whole, which is shorter than its diff:
```python
import functools

import jax
import jax.numpy as jnp
from jax import lax
from jax.experimental import pallas as pl
from jax.experimental.pallas import tpu as pltpu
from jax.sharding import PartitionSpec as P

QUERY_HEADS = 40
KEY_VALUE_HEADS = 8
HEAD_SIZE = 128
GROUP = QUERY_HEADS // KEY_VALUE_HEADS
PAIR = 2 * HEAD_SIZE
LOG2E = 1.4426950408889634
SCALE = HEAD_SIZE ** (-0.5) * LOG2E
MASKED = -1e30
CHUNK_ROWS = 1024


def dot_t(a, b):
    return lax.dot_general(a, b, (((1,), (1,)), ((), ())), preferred_element_type=jnp.float32)


def dot(a, b):
    return lax.dot_general(a, b, (((1,), (0,)), ((), ())), preferred_element_type=jnp.float32)


def attend_kernel(slots, tp_size, first_call, last_call, *refs):
    refs = list(refs)
    prefix_ref, del_start_ref, del_end_ref, tq, sq = refs[:5]
    del refs[:5]
    k_aug_ref = refs.pop()
    outs, refs = (refs[-2:], refs[:-2]) if last_call else (refs[-3:], refs[:-3])
    if not first_call:
        top_in, denominator_in, sum_in = refs[-3:]
        del refs[-3:]
    pieces = refs

    rows = tq.shape[0]
    half = GROUP * rows
    ctx = lax.axis_index("ctx").astype(jnp.int32)
    tp = lax.axis_index("tp").astype(jnp.int32)
    first_position = (ctx * tp_size + tp) * rows
    prefix, del_start, del_end = prefix_ref[0], del_start_ref[0], del_end_ref[0]
    lane = lax.broadcasted_iota(jnp.int32, (rows, HEAD_SIZE), 1)
    row = lax.broadcasted_iota(jnp.int32, (rows, HEAD_SIZE), 0)
    q_trace_aug = jnp.where(lane == row, 1.0, 0.0).astype(jnp.bfloat16)
    q_suffix_aug = jnp.where((lane == rows) | (lane == rows + 1 + row), 1.0, 0.0).astype(jnp.bfloat16)
    q_aug = jnp.concatenate([q_trace_aug] * GROUP + [q_suffix_aug] * GROUP, axis=0)
    for index, slot in enumerate(slots):
        kind, block = slot(ctx, tp)
        position = block * rows + row
        if kind == "trace":
            hidden_trace = (lane < rows) & (position > first_position + lane)
            hidden_suffix = (lane == rows) & (
                (position >= prefix) | ((position >= del_start) & (position < del_end))
            )
            hidden = hidden_trace | hidden_suffix
        else:
            hidden = (lane < rows) | ((lane > rows) & (position > tp * rows + (lane - rows - 1)))
        k_aug_ref[index * rows:(index + 1) * rows, :] = jnp.where(hidden, MASKED, 0.0).astype(jnp.bfloat16)
    total = rows * len(slots)
    ones = jnp.ones((total, HEAD_SIZE), jnp.bfloat16)

    def columns(index):
        return slice(index * HEAD_SIZE, (index + 1) * HEAD_SIZE)

    def stacked(index):
        return jnp.concatenate([piece[:, columns(index)] for piece in pieces], axis=0)

    def scores_of(g):
        query = jnp.concatenate(
            [ref[:, columns(g * GROUP + j)] for ref in (tq, sq) for j in range(GROUP)], axis=0
        )
        query = jnp.concatenate([query, q_aug], axis=1)
        return dot_t(query, jnp.concatenate([stacked(2 * g), k_aug_ref[...]], axis=1))

    def absorb_head(g, scores):
        top = jnp.broadcast_to(jnp.max(scores, axis=1, keepdims=True), (2 * half, HEAD_SIZE))
        if not first_call:
            old_top = top_in[g]
            top = jnp.maximum(old_top, top)
        shifted = scores - jnp.concatenate([top] * (total // HEAD_SIZE), axis=1)
        weights = jnp.exp2(shifted * SCALE).astype(jnp.bfloat16)
        both = dot(weights, jnp.concatenate([stacked(2 * g + 1), ones], axis=1))
        summed, denominator = both[:, :HEAD_SIZE], both[:, HEAD_SIZE:]
        if not first_call:
            rescale = jnp.exp2((old_top - top) * SCALE)
            summed = summed + sum_in[g] * rescale
            denominator = denominator + denominator_in[g] * rescale
        if last_call:
            inverse = pl.reciprocal(denominator, approx=True)
            inverse = inverse * (2.0 - denominator * inverse)
            result = (summed * inverse).astype(jnp.bfloat16)
            for j in range(GROUP):
                outs[0][:, columns(g * GROUP + j)] = result[j * rows:(j + 1) * rows]
                outs[1][:, columns(g * GROUP + j)] = result[half + j * rows:half + (j + 1) * rows]
        else:
            for out, state in zip(outs, (top, denominator, summed)):
                out[g] = state

    ahead = scores_of(0)
    for g in range(KEY_VALUE_HEADS):
        now, ahead = ahead, scores_of(g + 1) if g + 1 < KEY_VALUE_HEADS else None
        absorb_head(g, now)


def attend(spans, tq, sq, pieces, slots, tp_size, carry, last_call):
    first_call = carry is None
    rows = tq.shape[0]
    smem = pl.BlockSpec(memory_space=pltpu.SMEM)
    vmem = pl.BlockSpec(memory_space=pltpu.VMEM)
    operands = [*spans, tq, sq, *pieces]
    if not first_call:
        operands += list(carry)
    if last_call:
        out_shape = [jax.ShapeDtypeStruct(tq.shape, jnp.bfloat16)] * 2
    else:
        state = (KEY_VALUE_HEADS, 2 * GROUP * rows, HEAD_SIZE)
        out_shape = [jax.ShapeDtypeStruct(state, jnp.float32)] * 3
    all_rows = sum(p.shape[0] for p in pieces)
    flops = 2 * 2 * QUERY_HEADS * rows * all_rows * PAIR * 2
    return pl.pallas_call(
        functools.partial(attend_kernel, slots, tp_size, first_call, last_call),
        out_shape=out_shape,
        in_specs=[smem] * 3 + [vmem] * (len(operands) - 3),
        out_specs=[vmem] * len(out_shape),
        scratch_shapes=[pltpu.VMEM((all_rows, HEAD_SIZE), jnp.bfloat16)],
        compiler_params=pltpu.CompilerParams(vmem_limit_bytes=32 * 1024 * 1024),
        cost_estimate=pl.CostEstimate(
            flops=flops, bytes_accessed=all_rows * 4096, transcendentals=2 * QUERY_HEADS * rows * all_rows
        ),
    )(*operands)


def swap(array, axis, bit, size):
    return lax.ppermute(array, axis, [(i, i ^ bit) for i in range(size)])


def after(array, *others):
    return lax.optimization_barrier((array, *others))[0]


def local(ctx_size, tp_size, trace_q, trace_key_value, suffix_q, suffix_key_value, prefix_len, del_start, del_end):
    rows = trace_q.shape[0]
    spans = (prefix_len, del_start, del_end)
    sq = suffix_q[0]
    suffix_own = suffix_key_value[0]

    core = lambda a: swap(a, "tp", 1, tp_size)
    across_y = lambda a: swap(a, "tp", 2, tp_size)
    across_x = lambda a: swap(a, "ctx", 1, ctx_size)
    along_z = lambda a, shift: lax.ppermute(
        a, "ctx", [(i, (i + 2 * shift) % ctx_size) for i in range(ctx_size)]
    )

    across_both = lambda a: lax.ppermute(
        a,
        ("ctx", "tp"),
        [(i * tp_size + j, (i ^ 1) * tp_size + (j ^ 2)) for i in range(ctx_size) for j in range(tp_size)],
    )

    def slot(place, c):
        if isinstance(place, int):
            return lambda ctx, tp: ("suffix", tp ^ place ^ c)
        shift, x, y = place
        return lambda ctx, tp: (
            "trace",
            (((ctx + ctx_size - 2 * shift) % ctx_size) ^ x) * tp_size + (tp ^ (2 * y + c)),
        )

    def absorb(pieces, slots, state, last_call=False):
        return attend(spans, trace_q, sq, pieces, slots, tp_size, state, last_call)

    def absorb_both(mine, sibling, places, state, last_call=False):
        slots = [slot(place, c) for c in (0, 1) for place in places]
        return absorb(mine + sibling, slots, state, last_call)

    if ctx_size == 8 and tp_size == 4:
        barrier = lax.optimization_barrier
        up, down = along_z(trace_key_value, 1), along_z(trace_key_value, 3)
        own_x, own_d = across_x(trace_key_value), across_both(trace_key_value)
        own = jnp.concatenate([trace_key_value, suffix_own], axis=0)
        own_y = across_y(own)
        up, down, own_x, own_d = barrier((up, down, own_x, own_d))

        up_two = along_z(jnp.concatenate([up, own_d], axis=0), 1)
        down_d = along_z(own_d, 3)
        near = jnp.concatenate([up, down], axis=0)
        near_x, near_y = across_x(near), across_y(near)
        plane = jnp.concatenate([own, own_y, own_x, own_d], axis=0)
        here = [(0, 0, 0), 0, (0, 0, 1), 2, (0, 1, 0), (0, 1, 1)]
        state = absorb_both([plane], [core(plane)], here, None)

        near_x, near_y, state = barrier((near_x, near_y, state))
        sides = jnp.concatenate([near, near_x, near_y], axis=0)
        sides_core = core(sides)
        far, up_d = up_two[:rows], up_two[rows:]
        far_x, far_y, far_d = across_x(far), across_y(far), along_z(up_d, 1)
        mixed = jnp.concatenate([up_two, down_d], axis=0)
        mixed_core = core(mixed)
        here = [(z, x, y) for x, y in ((0, 0), (1, 0), (0, 1)) for z in (1, 3)]
        state = absorb_both([sides], [sides_core], here, state)

        far_x, far_y, far_d, state = barrier((far_x, far_y, far_d, state))
        rest = jnp.concatenate([far_x, far_y, far_d], axis=0)
        here = [(2, 0, 0), (1, 1, 1), (3, 1, 1), (2, 1, 0), (2, 0, 1), (2, 1, 1)]
        trace_out, suffix_out = absorb_both([mixed, rest], [mixed_core, core(rest)], here, state, True)
    else:
        gathered = lax.all_gather(trace_key_value, ("ctx", "tp"), axis=0, tiled=True)
        suffix_all = lax.all_gather(suffix_own, "tp", axis=0, tiled=True)
        state = None
        for at in range(0, gathered.shape[0], CHUNK_ROWS):
            last_call = at + CHUNK_ROWS >= gathered.shape[0]
            pieces = [gathered[at:at + CHUNK_ROWS]]
            slots = [
                lambda ctx, tp, block=block: ("trace", block)
                for block in range(at // rows, min(at + CHUNK_ROWS, gathered.shape[0]) // rows)
            ]
            if at == 0:
                pieces.append(suffix_all)
                slots += [lambda ctx, tp, block=block: ("suffix", block) for block in range(tp_size)]
            state = absorb(pieces, slots, state, last_call)
        trace_out, suffix_out = state
    return trace_out, suffix_out[None]


def solution(mesh):
    return jax.shard_map(
        functools.partial(local, mesh.shape["ctx"], mesh.shape["tp"]),
        mesh=mesh,
        in_specs=(
            P(("ctx", "tp"), None),
            P(("ctx", "tp"), None),
            P("ctx", "tp", None),
            P("ctx", "tp", None),
            P("ctx"),
            P("ctx"),
            P("ctx"),
        ),
        out_specs=(P(("ctx", "tp"), None), P("ctx", "tp", None)),
        check_vma=False,
    )
```

time: 50.1 us -> 48.6 us (0.970)
  Pallas kernels: 11.1 us -> 6.55 us
  starting transfers between devices: 20.3 us -> 21.5 us
  other arithmetic: 0.04 us -> 1.01 us
  local copies, waits for them, and re-layouts: 1.31 us -> 2.1 us
    pallas_call x3, Pallas kernels: 11.1 us -> 6.55 us  [attend(): pl.pallas_call(functools.partial(attend_kernel, slots, tp_size, first_cal...]
    ppermute x3 -> x5, starting transfers between devices: 4.8 us -> 7.14 us  [local(): lax.ppermute(a, 'ctx', [(i, (i + 2 * shift) % ctx_size) for i in range(ct...]
    ppermute x2 -> x1, waiting for transfers between devices: 0.01 us -> 1.84 us  [local(): lax.ppermute(a, ('ctx', 'tp'), [(i * tp_size + j, (i ^ 1) * tp_size + (j...]
    concatenate x2, other arithmetic: 0.04 us -> 1.01 us  [the longest x1 0.99 us: local(): own = jnp.concatenate([trace_key_value, suffix_own], axis=0)]
    unnamed x16 -> x13, local copies, waits for them, and re-layouts: 1.13 us -> 2.01 us
    ppermute x3 -> x5, waiting for transfers between devices: 3.04 us -> 2.16 us  [local(): lax.ppermute(a, 'ctx', [(i, (i + 2 * shift) % ctx_size) for i in range(ct...]
    ppermute x10, starting transfers between devices: 13.9 us -> 13.2 us  [swap(): return lax.ppermute(array, axis, [(i, i ^ bit) for i in range(size)])]
    ppermute x10, waiting for transfers between devices: 10.8 us -> 10.1 us  [swap(): return lax.ppermute(array, axis, [(i, i ^ bit) for i in range(size)])]
  transfers between devices with their start and end apart: 15 -> 16, of which waited for: 3 -> 7; matrix products, arithmetic and copies ran while one was open for 3% -> 6% of each run, Pallas kernels for 14% -> 8%
where the time goes in v4:
time: 48.6 us; the launch traced here: 48.1 us
  starting transfers between devices  21.5 us (44%)
  waiting for transfers between devices  14.1 us (29%)
  Pallas kernels  6.55 us (13%)
  between operations  2.76 us (6%)
  local copies, waits for them, and re-layouts  2.1 us (4%)
  other arithmetic  1.01 us (2%)
    ppermute x10, starting transfers between devices, swap(): return lax.ppermute(array, axis, [(i, i ^ bit) for i in range(size)])  13.2 us
    ppermute x10, waiting for transfers between devices, swap(): return lax.ppermute(array, axis, [(i, i ^ bit) for i in range(size)])  10.1 us
    ppermute x5, starting transfers between devices, local(): lax.ppermute(a, 'ctx', [(i, (i + 2 * shift) % ctx_size) for i in range(ct...  7.14 us
    pallas_call x3, Pallas kernels, attend(): pl.pallas_call(functools.partial(attend_kernel, slots, tp_size, first_cal...  6.55 us
    ppermute x5, waiting for transfers between devices, local(): lax.ppermute(a, 'ctx', [(i, (i + 2 * shift) % ctx_size) for i in range(ct...  2.16 us
    unnamed x13, local copies, waits for them, and re-layouts  2.01 us
    ppermute x1, waiting for transfers between devices, local(): lax.ppermute(a, ('ctx', 'tp'), [(i * tp_size + j, (i ^ 1) * tp_size + (j...  1.84 us
    ppermute x1, starting transfers between devices, local(): lax.ppermute(a, ('ctx', 'tp'), [(i * tp_size + j, (i ^ 1) * tp_size + (j...  1.21 us
  transfers between devices with their start and end apart: 16, of which 7 were waited for; matrix products, arithmetic and copies ran while one was open for 6% of the time, Pallas kernels for 8%

profile of v4, /device:TPU:1, one launch (start us, length us, event | category | flops | bytes accessed | tf_op | source)
XLA Modules:
  0.0 48.1 jit_solution(10321570755929109912)
XLA Ops:
  0.6 2.2 %collective-permute-start = (bf16[32,2048]{1,0:T(8,128)(2,1)}, bf16[32,2048]{1,0:T(8,128)(2,1)S(1)}, u32[]{:S(2)}, u32[]{:S(2)}) collective-permute-start(bf16[32,2048]{1,0:T(8,128)(2,1)} %param.8), channel_id=1, source_target_pairs={{0,8},{4,12},{8,16},{12,20},{16,24},{20,28},{24,0},{28,4},{1,9},{5... | collective-permute-start | bytes 393224 | tf_op jit(solution)/shard_map/ppermute | solution.py:154
  2.8 2.1 %collective-permute-start.1 = (bf16[32,2048]{1,0:T(8,128)(2,1)}, bf16[32,2048]{1,0:T(8,128)(2,1)S(1)}, u32[]{:S(2)}, u32[]{:S(2)}) collective-permute-start(bf16[32,2048]{1,0:T(8,128)(2,1)} %param.8), channel_id=1, source_target_pairs={{0,24},{4,28},{8,0},{12,4},{16,8},{20,12},{24,16},{28,20},{1,25},{... | collective-permute-start | bytes 393224 | tf_op jit(solution)/shard_map/ppermute | solution.py:154
  4.9 1.2 %collective-permute-start.2 = (bf16[32,2048]{1,0:T(8,128)(2,1)}, bf16[32,2048]{1,0:T(8,128)(2,1)S(1)}, u32[]{:S(2)}, u32[]{:S(2)}) collective-permute-start(bf16[32,2048]{1,0:T(8,128)(2,1)} %param.8), channel_id=1, source_target_pairs={{0,4},{4,0},{8,12},{12,8},{16,20},{20,16},{24,28},{28,24},{1,5},{5... | collective-permute-start | bytes 393224 | tf_op jit(solution)/shard_map/ppermute | solution.py:138
  6.1 1.2 %collective-permute-start.3 = (bf16[32,2048]{1,0:T(8,128)(2,1)}, bf16[32,2048]{1,0:T(8,128)(2,1)S(1)}, u32[]{:S(2)}, u32[]{:S(2)}) collective-permute-start(bf16[32,2048]{1,0:T(8,128)(2,1)} %param.8), channel_id=1, source_target_pairs={{0,6},{1,7},{2,4},{3,5},{4,2},{5,3},{6,0},{7,1},{8,14},{9,15},{10,... | collective-permute-start | bytes 393224 | tf_op jit(solution)/shard_map/ppermute | solution.py:158
  7.3 1.0 %pad_maximum_fusion.1 = bf16[64,2048]{1,0:T(8,128)(2,1)S(1)} fusion(bf16[32,2048]{1,0:T(8,128)(2,1)} %bitcast.7, bf16[32,2048]{1,0:T(8,128)(2,1)} %param.8), kind=kLoop, calls=%fused_computation.1 | loop fusion | flops 524288 | bytes 524288 | tf_op jit(solution)/shard_map/concatenate | solution.py:184
  8.6 0.9 %constant_dynamic-update-slice_fusion.8 = bf16[192,2048]{1,0:T(8,128)(2,1)S(1)} fusion(bf16[32,2048]{1,0:T(8,128)(2,1)} %param.8), kind=kLoop, calls=%fused_computation.10 | loop fusion | bytes 262144
  9.6 1.0 %constant_dynamic-update-slice_fusion.7 = bf16[192,2048]{1,0:T(8,128)(2,1)S(1)} fusion(bf16[192,2048]{1,0:T(8,128)(2,1)S(1)} %constant_dynamic-update-slice_fusion.8, bf16[1,32,2048]{2,1,0:T(8,128)(2,1)} %param.10), kind=kLoop, calls=%fused_computation.9 | loop fusion | bytes 262144
  10.6 1.8 %collective-permute-done.3 = bf16[32,2048]{1,0:T(8,128)(2,1)S(1)} collective-permute-done((bf16[32,2048]{1,0:T(8,128)(2,1)}, bf16[32,2048]{1,0:T(8,128)(2,1)S(1)}, u32[]{:S(2)}, u32[]{:S(2)}) %collective-permute-start.3) | collective-permute-done | bytes 131104 | tf_op jit(solution)/shard_map/ppermute | solution.py:158
  12.5 5.3 %collective-permute-done.11 = bf16[64,2048]{1,0:T(8,128)(2,1)S(1)} collective-permute-done((bf16[64,2048]{1,0:T(8,128)(2,1)S(1)}, bf16[64,2048]{1,0:T(8,128)(2,1)S(1)}, u32[]{:S(2)}, u32[]{:S(2)}) %collective-permute-start.11) | collective-permute-done | bytes 262176 | tf_op jit(solution)/shard_map/ppermute | solution.py:138
  17.8 1.7 %collective-permute-start.12 = (bf16[192,2048]{1,0:T(8,128)(2,1)S(1)}, bf16[192,2048]{1,0:T(8,128)(2,1)S(1)}, u32[]{:S(2)}, u32[]{:S(2)}) collective-permute-start(bf16[192,2048]{1,0:T(8,128)(2,1)S(1)} %constant_dynamic-update-slice_fusion.4.refs_5_), channel_id=1, source_target_pairs={{0,1},{1,0},{2,3},{3,2},{4,5},{5,4},{6,7},{7,6},{8,9},{9,8},{10,11... | collective-permute-start | bytes 2359304 | tf_op jit(solution)/shard_map/ppermute | solution.py:138
  21.5 0.8 %collective-permute-start.10 = (bf16[64,2048]{1,0:T(8,128)(2,1)S(1)}, bf16[64,2048]{1,0:T(8,128)(2,1)S(1)}, u32[]{:S(2)}, u32[]{:S(2)}) collective-permute-start(bf16[64,2048]{1,0:T(8,128)(2,1)S(1)} %get-tuple-element.50), channel_id=1, source_target_pairs={{0,2},{1,3},{2,0},{3,1},{4,6},{5,7},{6,4},{7,5},{8,10},{9,11},{10,... | collective-permute-start | bytes 786440 | tf_op jit(solution)/shard_map/ppermute | solution.py:138
  22.2 0.7 %collective-permute-start.9 = (bf16[64,2048]{1,0:T(8,128)(2,1)S(1)}, bf16[64,2048]{1,0:T(8,128)(2,1)S(1)}, u32[]{:S(2)}, u32[]{:S(2)}) collective-permute-start(bf16[64,2048]{1,0:T(8,128)(2,1)S(1)} %get-tuple-element.50), channel_id=1, source_target_pairs={{0,4},{4,0},{8,12},{12,8},{16,20},{20,16},{24,28},{28,24},{1,5},{5... | collective-permute-start | bytes 786440 | tf_op jit(solution)/shard_map/ppermute | solution.py:138
  23.0 1.3 %collective-permute-start.5 = (bf16[32,2048]{1,0:T(8,128)(2,1)S(1)}, bf16[32,2048]{1,0:T(8,128)(2,1)S(1)}, u32[]{:S(2)}, u32[]{:S(2)}) collective-permute-start(bf16[32,2048]{1,0:T(8,128)(2,1)S(1)} %collective-permute-done.3), channel_id=1, source_target_pairs={{0,24},{4,28},{8,0},{12,4},{16,8},{20,12},{24,16},{28,20},{1,25},{... | collective-permute-start | bytes 393224 | tf_op jit(solution)/shard_map/ppermute | solution.py:154
  24.5 1.8 %shard_map.86 = (f32[8,320,128]{2,1,0:T(8,128)S(1)}, f32[8,320,128]{2,1,0:T(8,128)S(1)}, f32[8,320,128]{2,1,0:T(8,128)S(1)}) custom-call(s32[1]{0:T(128)S(6)} %copy.20.refs_0_, s32[1]{0:T(128)S(6)} %copy.21.refs_1_, s32[1]{0:T(128)S(6)} %copy.22.refs_2_, bf16[32,5120]{1,0:T(8,128)(2,1)S(1)} %copy-done, bf16[32,5120]{1,0:T(8,128)(2,1)S(1)} %bitcast.4, ...), custom_call_target="tpu_custom_call" | custom-call | flops 1006632960 | bytes 1572864 | tf_op jit(solution)/shard_map/pallas_call | solution.py:124
  26.4 3.1 %collective-permute-done.10 = bf16[64,2048]{1,0:T(8,128)(2,1)S(1)} collective-permute-done((bf16[64,2048]{1,0:T(8,128)(2,1)S(1)}, bf16[64,2048]{1,0:T(8,128)(2,1)S(1)}, u32[]{:S(2)}, u32[]{:S(2)}) %collective-permute-start.10) | collective-permute-done | bytes 262176 | tf_op jit(solution)/shard_map/ppermute | solution.py:138
  29.9 1.2 %collective-permute-start.13 = (bf16[192,2048]{1,0:T(8,128)(2,1)S(1)}, bf16[192,2048]{1,0:T(8,128)(2,1)S(1)}, u32[]{:S(2)}, u32[]{:S(2)}) collective-permute-start(bf16[192,2048]{1,0:T(8,128)(2,1)S(1)} %constant_dynamic-update-slice_fusion.9.refs_5_), channel_id=1, source_target_pairs={{0,1},{1,0},{2,3},{3,2},{4,5},{5,4},{6,7},{7,6},{8,9},{9,8},{10,11... | collective-permute-start | bytes 2359304 | tf_op jit(solution)/shard_map/ppermute | solution.py:138
  31.1 2.1 %collective-permute-done.4 = bf16[64,2048]{1,0:T(8,128)(2,1)S(1)} collective-permute-done((bf16[64,2048]{1,0:T(8,128)(2,1)S(1)}, bf16[64,2048]{1,0:T(8,128)(2,1)S(1)}, u32[]{:S(2)}, u32[]{:S(2)}) %collective-permute-start.4) | collective-permute-done | bytes 262176 | tf_op jit(solution)/shard_map/ppermute | solution.py:154
  33.2 0.8 %collective-permute-start.6 = (bf16[32,2048]{1,0:T(8,128)(2,1)S(1)}, bf16[32,2048]{1,0:T(8,128)(2,1)S(1)}, u32[]{:S(2)}, u32[]{:S(2)}) collective-permute-start(bf16[32,2048]{1,0:T(8,128)(2,1)S(1)} %get-tuple-element.49), channel_id=1, source_target_pairs={{0,4},{4,0},{8,12},{12,8},{16,20},{20,16},{24,28},{28,24},{1,5},{5... | collective-permute-start | bytes 393224 | tf_op jit(solution)/shard_map/ppermute | solution.py:138
  34.7 1.4 %collective-permute-start.8 = (bf16[32,2048]{1,0:T(8,128)(2,1)S(1)}, bf16[32,2048]{1,0:T(8,128)(2,1)S(1)}, u32[]{:S(2)}, u32[]{:S(2)}) collective-permute-start(bf16[32,2048]{1,0:T(8,128)(2,1)S(1)} %get-tuple-element.48), channel_id=1, source_target_pairs={{0,8},{4,12},{8,16},{12,20},{16,24},{20,28},{24,0},{28,4},{1,9},{5... | collective-permute-start | bytes 393224 | tf_op jit(solution)/shard_map/ppermute | solution.py:154
  36.1 2.3 %collective-permute-start.14 = (bf16[96,2048]{1,0:T(8,128)(2,1)S(1)}, bf16[96,2048]{1,0:T(8,128)(2,1)S(1)}, u32[]{:S(2)}, u32[]{:S(2)}) collective-permute-start(bf16[96,2048]{1,0:T(8,128)(2,1)S(1)} %constant_dynamic-update-slice_fusion.refs_5_), channel_id=1, source_target_pairs={{0,1},{1,0},{2,3},{3,2},{4,5},{5,4},{6,7},{7,6},{8,9},{9,8},{10,11... | collective-permute-start | bytes 1179656 | tf_op jit(solution)/shard_map/ppermute | solution.py:138
  38.4 1.9 %shard_map.87 = (f32[8,320,128]{2,1,0:T(8,128)S(1)}, f32[8,320,128]{2,1,0:T(8,128)S(1)}, f32[8,320,128]{2,1,0:T(8,128)S(1)}) custom-call(s32[1]{0:T(128)S(6)} %copy.20.refs_0_, s32[1]{0:T(128)S(6)} %copy.21.refs_1_, s32[1]{0:T(128)S(6)} %copy.22.refs_2_, bf16[32,5120]{1,0:T(8,128)(2,1)S(1)} %copy-done, bf16[32,5120]{1,0:T(8,128)(2,1)S(1)} %bitcast.5, ...), custom_call_target="tpu_custom_call" | custom-call | flops 1006632960 | bytes 1572864 | tf_op jit(solution)/shard_map/pallas_call | solution.py:124
  40.5 3.5 %collective-permute-start.15 = (bf16[96,2048]{1,0:T(8,128)(2,1)S(1)}, bf16[96,2048]{1,0:T(8,128)(2,1)S(1)}, u32[]{:S(2)}, u32[]{:S(2)}) collective-permute-start(bf16[96,2048]{1,0:T(8,128)(2,1)S(1)} %constant_dynamic-update-slice_fusion.13.refs_6_), channel_id=1, source_target_pairs={{0,1},{1,0},{2,3},{3,2},{4,5},{5,4},{6,7},{7,6},{8,9},{9,8},{10,11... | collective-permute-start | bytes 1179656 | tf_op jit(solution)/shard_map/ppermute | solution.py:138
  43.9 1.3 %collective-permute-done.15.refs_8_ = bf16[96,2048]{1,0:T(8,128)(2,1)S(1)} collective-permute-done((bf16[96,2048]{1,0:T(8,128)(2,1)S(1)}, bf16[96,2048]{1,0:T(8,128)(2,1)S(1)}, u32[]{:S(2)}, u32[]{:S(2)}) %collective-permute-start.15) | collective-permute-done | bytes 393248 | tf_op jit(solution)/shard_map/ppermute | solution.py:138
  45.3 2.8 %shard_map.88 = (bf16[32,5120]{1,0:T(8,128)(2,1)}, bf16[32,5120]{1,0:T(8,128)(2,1)}) custom-call(s32[1]{0:T(128)S(6)} %copy.20.refs_0_, s32[1]{0:T(128)S(6)} %copy.21.refs_1_, s32[1]{0:T(128)S(6)} %copy.22.refs_2_, bf16[32,5120]{1,0:T(8,128)(2,1)S(1)} %copy-done, bf16[32,5120]{1,0:T(8,128)(2,1)S(1)} %bitcast.6, ...), custom_call_target="tpu_custom_call" | custom-call | flops 1006632960 | bytes 1572864 | tf_op jit(solution)/shard_map/pallas_call | solution.py:124
  (32 shorter events, 1.9 us)
Async XLA Ops:
  0.6 9.9 %collective-permute-start = (bf16[32,2048]{1,0:T(8,128)(2,1)}, bf16[32,2048]{1,0:T(8,128)(2,1)S(1)}, u32[]{:S(2)}, u32[]{:S(2)}) collective-permute-start(bf16[32,2048]{1,0:T(8,128)(2,1)} %param.8), channel_id=1, source_target_pairs={{0,8},{4,12},{8,16},{12,20},{16,24},{20,28},{24,0},{28,4},{1,9},{5... | collective-permute-start | bytes 393224 | tf_op jit(solution)/shard_map/ppermute | solution.py:154
  2.8 7.8 %collective-permute-start.1 = (bf16[32,2048]{1,0:T(8,128)(2,1)}, bf16[32,2048]{1,0:T(8,128)(2,1)S(1)}, u32[]{:S(2)}, u32[]{:S(2)}) collective-permute-start(bf16[32,2048]{1,0:T(8,128)(2,1)} %param.8), channel_id=1, source_target_pairs={{0,24},{4,28},{8,0},{12,4},{16,8},{20,12},{24,16},{28,20},{1,25},{... | collective-permute-start | bytes 393224 | tf_op jit(solution)/shard_map/ppermute | solution.py:154
  4.9 5.7 %collective-permute-start.2 = (bf16[32,2048]{1,0:T(8,128)(2,1)}, bf16[32,2048]{1,0:T(8,128)(2,1)S(1)}, u32[]{:S(2)}, u32[]{:S(2)}) collective-permute-start(bf16[32,2048]{1,0:T(8,128)(2,1)} %param.8), channel_id=1, source_target_pairs={{0,4},{4,0},{8,12},{12,8},{16,20},{20,16},{24,28},{28,24},{1,5},{5... | collective-permute-start | bytes 393224 | tf_op jit(solution)/shard_map/ppermute | solution.py:138
  6.1 6.3 %collective-permute-start.3 = (bf16[32,2048]{1,0:T(8,128)(2,1)}, bf16[32,2048]{1,0:T(8,128)(2,1)S(1)}, u32[]{:S(2)}, u32[]{:S(2)}) collective-permute-start(bf16[32,2048]{1,0:T(8,128)(2,1)} %param.8), channel_id=1, source_target_pairs={{0,6},{1,7},{2,4},{3,5},{4,2},{5,3},{6,0},{7,1},{8,14},{9,15},{10,... | collective-permute-start | bytes 393224 | tf_op jit(solution)/shard_map/ppermute | solution.py:158
  8.3 9.4 %collective-permute-start.11 = (bf16[64,2048]{1,0:T(8,128)(2,1)S(1)}, bf16[64,2048]{1,0:T(8,128)(2,1)S(1)}, u32[]{:S(2)}, u32[]{:S(2)}) collective-permute-start(bf16[64,2048]{1,0:T(8,128)(2,1)S(1)} %pad_maximum_fusion.1), channel_id=1, source_target_pairs={{0,2},{1,3},{2,0},{3,1},{4,6},{5,7},{6,4},{7,5},{8,10},{9,11},{10,... | collective-permute-start | bytes 786440 | tf_op jit(solution)/shard_map/ppermute | solution.py:138
  9.5 15.0 %copy-start = (bf16[32,5120]{1,0:T(8,128)(2,1)S(1)}, bf16[32,5120]{1,0:T(8,128)(2,1)}, u32[]{:S(2)}) copy-start(bf16[32,5120]{1,0:T(8,128)(2,1)} %refs_3_.5) | copy-start | bytes 983044
  9.5 15.0 %copy-start.1 = (bf16[1,32,5120]{2,1,0:T(8,128)(2,1)S(1)}, bf16[1,32,5120]{2,1,0:T(8,128)(2,1)}, u32[]{:S(2)}) copy-start(bf16[1,32,5120]{2,1,0:T(8,128)(2,1)} %param.9) | copy-start | bytes 983044
  17.8 6.7 %collective-permute-start.12 = (bf16[192,2048]{1,0:T(8,128)(2,1)S(1)}, bf16[192,2048]{1,0:T(8,128)(2,1)S(1)}, u32[]{:S(2)}, u32[]{:S(2)}) collective-permute-start(bf16[192,2048]{1,0:T(8,128)(2,1)S(1)} %constant_dynamic-update-slice_fusion.4.refs_5_), channel_id=1, source_target_pairs={{0,1},{1,0},{2,3},{3,2},{4,5},{5,4},{6,7},{7,6},{8,9},{9,8},{10,11... | collective-permute-start | bytes 2359304 | tf_op jit(solution)/shard_map/ppermute | solution.py:138
  21.5 8.0 %collective-permute-start.10 = (bf16[64,2048]{1,0:T(8,128)(2,1)S(1)}, bf16[64,2048]{1,0:T(8,128)(2,1)S(1)}, u32[]{:S(2)}, u32[]{:S(2)}) collective-permute-start(bf16[64,2048]{1,0:T(8,128)(2,1)S(1)} %get-tuple-element.50), channel_id=1, source_target_pairs={{0,2},{1,3},{2,0},{3,1},{4,6},{5,7},{6,4},{7,5},{8,10},{9,11},{10,... | collective-permute-start | bytes 786440 | tf_op jit(solution)/shard_map/ppermute | solution.py:138
  22.2 7.6 %collective-permute-start.9 = (bf16[64,2048]{1,0:T(8,128)(2,1)S(1)}, bf16[64,2048]{1,0:T(8,128)(2,1)S(1)}, u32[]{:S(2)}, u32[]{:S(2)}) collective-permute-start(bf16[64,2048]{1,0:T(8,128)(2,1)S(1)} %get-tuple-element.50), channel_id=1, source_target_pairs={{0,4},{4,0},{8,12},{12,8},{16,20},{20,16},{24,28},{28,24},{1,5},{5... | collective-permute-start | bytes 786440 | tf_op jit(solution)/shard_map/ppermute | solution.py:138
  23.0 13.1 %collective-permute-start.5 = (bf16[32,2048]{1,0:T(8,128)(2,1)S(1)}, bf16[32,2048]{1,0:T(8,128)(2,1)S(1)}, u32[]{:S(2)}, u32[]{:S(2)}) collective-permute-start(bf16[32,2048]{1,0:T(8,128)(2,1)S(1)} %collective-permute-done.3), channel_id=1, source_target_pairs={{0,24},{4,28},{8,0},{12,4},{16,8},{20,12},{24,16},{28,20},{1,25},{... | collective-permute-start | bytes 393224 | tf_op jit(solution)/shard_map/ppermute | solution.py:154
  24.3 8.8 %collective-permute-start.4 = (bf16[64,2048]{1,0:T(8,128)(2,1)S(1)}, bf16[64,2048]{1,0:T(8,128)(2,1)S(1)}, u32[]{:S(2)}, u32[]{:S(2)}) collective-permute-start(bf16[64,2048]{1,0:T(8,128)(2,1)S(1)} %pad_maximum_fusion), channel_id=1, source_target_pairs={{0,8},{4,12},{8,16},{12,20},{16,24},{20,28},{24,0},{28,4},{1,9},{5... | collective-permute-start | bytes 786440 | tf_op jit(solution)/shard_map/ppermute | solution.py:154
  29.9 8.5 %collective-permute-start.13 = (bf16[192,2048]{1,0:T(8,128)(2,1)S(1)}, bf16[192,2048]{1,0:T(8,128)(2,1)S(1)}, u32[]{:S(2)}, u32[]{:S(2)}) collective-permute-start(bf16[192,2048]{1,0:T(8,128)(2,1)S(1)} %constant_dynamic-update-slice_fusion.9.refs_5_), channel_id=1, source_target_pairs={{0,1},{1,0},{2,3},{3,2},{4,5},{5,4},{6,7},{7,6},{8,9},{9,8},{10,11... | collective-permute-start | bytes 2359304 | tf_op jit(solution)/shard_map/ppermute | solution.py:138
  33.2 7.2 %collective-permute-start.6 = (bf16[32,2048]{1,0:T(8,128)(2,1)S(1)}, bf16[32,2048]{1,0:T(8,128)(2,1)S(1)}, u32[]{:S(2)}, u32[]{:S(2)}) collective-permute-start(bf16[32,2048]{1,0:T(8,128)(2,1)S(1)} %get-tuple-element.49), channel_id=1, source_target_pairs={{0,4},{4,0},{8,12},{12,8},{16,20},{20,16},{24,28},{28,24},{1,5},{5... | collective-permute-start | bytes 393224 | tf_op jit(solution)/shard_map/ppermute | solution.py:138
  34.0 6.4 %collective-permute-start.7 = (bf16[32,2048]{1,0:T(8,128)(2,1)S(1)}, bf16[32,2048]{1,0:T(8,128)(2,1)S(1)}, u32[]{:S(2)}, u32[]{:S(2)}) collective-permute-start(bf16[32,2048]{1,0:T(8,128)(2,1)S(1)} %get-tuple-element.49), channel_id=1, source_target_pairs={{0,2},{1,3},{2,0},{3,1},{4,6},{5,7},{6,4},{7,5},{8,10},{9,11},{10,... | collective-permute-start | bytes 393224 | tf_op jit(solution)/shard_map/ppermute | solution.py:138
  34.7 5.7 %collective-permute-start.8 = (bf16[32,2048]{1,0:T(8,128)(2,1)S(1)}, bf16[32,2048]{1,0:T(8,128)(2,1)S(1)}, u32[]{:S(2)}, u32[]{:S(2)}) collective-permute-start(bf16[32,2048]{1,0:T(8,128)(2,1)S(1)} %get-tuple-element.48), channel_id=1, source_target_pairs={{0,8},{4,12},{8,16},{12,20},{16,24},{20,28},{24,0},{28,4},{1,9},{5... | collective-permute-start | bytes 393224 | tf_op jit(solution)/shard_map/ppermute | solution.py:154
  36.1 7.8 %collective-permute-start.14 = (bf16[96,2048]{1,0:T(8,128)(2,1)S(1)}, bf16[96,2048]{1,0:T(8,128)(2,1)S(1)}, u32[]{:S(2)}, u32[]{:S(2)}) collective-permute-start(bf16[96,2048]{1,0:T(8,128)(2,1)S(1)} %constant_dynamic-update-slice_fusion.refs_5_), channel_id=1, source_target_pairs={{0,1},{1,0},{2,3},{3,2},{4,5},{5,4},{6,7},{7,6},{8,9},{9,8},{10,11... | collective-permute-start | bytes 1179656 | tf_op jit(solution)/shard_map/ppermute | solution.py:138
  40.5 4.8 %collective-permute-start.15 = (bf16[96,2048]{1,0:T(8,128)(2,1)S(1)}, bf16[96,2048]{1,0:T(8,128)(2,1)S(1)}, u32[]{:S(2)}, u32[]{:S(2)}) collective-permute-start(bf16[96,2048]{1,0:T(8,128)(2,1)S(1)} %constant_dynamic-update-slice_fusion.13.refs_6_), channel_id=1, source_target_pairs={{0,1},{1,0},{2,3},{3,2},{4,5},{5,4},{6,7},{7,6},{8,9},{9,8},{10,11... | collective-permute-start | bytes 1179656 | tf_op jit(solution)/shard_map/ppermute | solution.py:138

commit v5 on v4

--- a/solution.py
+++ b/solution.py
@@ -28,8 +28,8 @@
 
 def attend_kernel(slots, tp_size, first_call, last_call, *refs):
     refs = list(refs)
-    prefix_ref, del_start_ref, del_end_ref, tq, sq = refs[:5]
-    del refs[:5]
+    spans, tq, sq = refs[:3]
+    del refs[:3]
     k_aug_ref = refs.pop()
     outs, refs = (refs[-2:], refs[:-2]) if last_call else (refs[-3:], refs[:-3])
     if not first_call:
@@ -42,7 +42,7 @@
     ctx = lax.axis_index("ctx").astype(jnp.int32)
     tp = lax.axis_index("tp").astype(jnp.int32)
     first_position = (ctx * tp_size + tp) * rows
-    prefix, del_start, del_end = prefix_ref[0], del_start_ref[0], del_end_ref[0]
+    prefix, del_start, del_end = spans[0:1], spans[1:2], spans[2:3]
     lane = lax.broadcasted_iota(jnp.int32, (rows, HEAD_SIZE), 1)
     row = lax.broadcasted_iota(jnp.int32, (rows, HEAD_SIZE), 0)
     q_trace_aug = jnp.where(lane == row, 1.0, 0.0).astype(jnp.bfloat16)
@@ -109,9 +109,8 @@
 def attend(spans, tq, sq, pieces, slots, tp_size, carry, last_call):
     first_call = carry is None
     rows = tq.shape[0]
-    smem = pl.BlockSpec(memory_space=pltpu.SMEM)
     vmem = pl.BlockSpec(memory_space=pltpu.VMEM)
-    operands = [*spans, tq, sq, *pieces]
+    operands = [spans, tq, sq, *pieces]
     if not first_call:
         operands += list(carry)
     if last_call:
@@ -124,7 +123,7 @@
     return pl.pallas_call(
         functools.partial(attend_kernel, slots, tp_size, first_call, last_call),
         out_shape=out_shape,
-        in_specs=[smem] * 3 + [vmem] * (len(operands) - 3),
+        in_specs=[vmem] * len(operands),
         out_specs=[vmem] * len(out_shape),
         scratch_shapes=[pltpu.VMEM((all_rows, HEAD_SIZE), jnp.bfloat16)],
         compiler_params=pltpu.CompilerParams(vmem_limit_bytes=32 * 1024 * 1024),
@@ -144,7 +143,7 @@
 
 def local(ctx_size, tp_size, trace_q, trace_key_value, suffix_q, suffix_key_value, prefix_len, del_start, del_end):
     rows = trace_q.shape[0]
-    spans = (prefix_len, del_start, del_end)
+    spans = jnp.broadcast_to(jnp.stack([prefix_len, del_start, del_end]), (3, HEAD_SIZE))
     sq = suffix_q[0]
     suffix_own = suffix_key_value[0]
 
@@ -180,28 +179,29 @@
     if ctx_size == 8 and tp_size == 4:
         barrier = lax.optimization_barrier
         up, down = along_z(trace_key_value, 1), along_z(trace_key_value, 3)
-        own_x, own_d = across_x(trace_key_value), across_both(trace_key_value)
-        own = jnp.concatenate([trace_key_value, suffix_own], axis=0)
-        own_y = across_y(own)
-        up, down, own_x, own_d = barrier((up, down, own_x, own_d))
-
+        own_x, own_y = across_x(trace_key_value), across_y(trace_key_value)
+        own_d = across_both(trace_key_value)
+        up, down, own_x, own_y, own_d, spans = barrier((up, down, own_x, own_y, own_d, spans))
+
+        near_x = across_x(jnp.concatenate([up, down], axis=0))
+        near_y = across_y(jnp.concatenate([up, down, suffix_own], axis=0))
         up_two = along_z(jnp.concatenate([up, own_d], axis=0), 1)
         down_d = along_z(own_d, 3)
-        near = jnp.concatenate([up, down], axis=0)
-        near_x, near_y = across_x(near), across_y(near)
-        plane = jnp.concatenate([own, own_y, own_x, own_d], axis=0)
-        here = [(0, 0, 0), 0, (0, 0, 1), 2, (0, 1, 0), (0, 1, 1)]
-        state = absorb_both([plane], [core(plane)], here, None)
+        plane = jnp.concatenate([trace_key_value, own_x, own_y, own_d, up, down, suffix_own], axis=0)
+        plane_core = core(plane)
+        cut = 6 * rows
+        here = [(0, 0, 0), (0, 1, 0), (0, 0, 1), (0, 1, 1), (1, 0, 0), (3, 0, 0)]
+        state = absorb_both([plane[:cut]], [plane_core[:cut]], here, None)
 
         near_x, near_y, state = barrier((near_x, near_y, state))
-        sides = jnp.concatenate([near, near_x, near_y], axis=0)
+        sides = jnp.concatenate([near_x, near_y], axis=0)
         sides_core = core(sides)
         far, up_d = up_two[:rows], up_two[rows:]
         far_x, far_y, far_d = across_x(far), across_y(far), along_z(up_d, 1)
         mixed = jnp.concatenate([up_two, down_d], axis=0)
         mixed_core = core(mixed)
-        here = [(z, x, y) for x, y in ((0, 0), (1, 0), (0, 1)) for z in (1, 3)]
-        state = absorb_both([sides], [sides_core], here, state)
+        here = [0, (1, 1, 0), (3, 1, 0), (1, 0, 1), (3, 0, 1), 2]
+        state = absorb_both([plane[cut:], sides], [plane_core[cut:], sides_core], here, state)
 
         far_x, far_y, far_d, state = barrier((far_x, far_y, far_d, state))
         rest = jnp.concatenate([far_x, far_y, far_d], axis=0)

time: 48.6 us -> 43.4 us (0.89)
  waiting for transfers between devices: 14.1 us -> 9.81 us
  other arithmetic: 1.01 us -> 0.14 us
  local copies, waits for them, and re-layouts: 2.1 us -> 1.35 us
  Pallas kernels: 6.55 us -> 7.04 us
    ppermute x10, waiting for transfers between devices: 10.1 us -> 7.41 us  [swap(): return lax.ppermute(array, axis, [(i, i ^ bit) for i in range(size)])]
    ppermute x5, waiting for transfers between devices: 2.16 us -> 0.11 us  [local(): lax.ppermute(a, 'ctx', [(i, (i + 2 * shift) % ctx_size) for i in range(ct...]
    ppermute x10, starting transfers between devices: 13.2 us -> 14.4 us  [swap(): return lax.ppermute(array, axis, [(i, i ^ bit) for i in range(size)])]
    ppermute x1, starting transfers between devices: 1.21 us -> 0.2 us  [local(): lax.ppermute(a, ('ctx', 'tp'), [(i * tp_size + j, (i ^ 1) * tp_size + (j...]
    concatenate x2, other arithmetic: 1.01 us -> 0.07 us  [the longest x1 0.04 us: local(): near_x = across_x(jnp.concatenate([up, down], axis=0))]
    unnamed x13 -> x16, local copies, waits for them, and re-layouts: 2.01 us -> 1.13 us
    pallas_call x3, Pallas kernels: 6.55 us -> 7.04 us  [attend(): pl.pallas_call(functools.partial(attend_kernel, slots, tp_size, first_cal...]
  transfers between devices with their start and end apart: 16 -> 16, of which waited for: 7 -> 5; matrix products, arithmetic and copies ran while one was open for 6% -> 3% of each run, Pallas kernels for 8% -> 9%
where the time goes in v5:
time: 43.4 us; the launch traced here: 42.9 us
  starting transfers between devices  21.7 us (50%)
  waiting for transfers between devices  9.81 us (23%)
  Pallas kernels  7.04 us (16%)
  between operations  2.81 us (6%)
  local copies, waits for them, and re-layouts  1.35 us (3%)
    ppermute x10, starting transfers between devices, swap(): return lax.ppermute(array, axis, [(i, i ^ bit) for i in range(size)])  14.4 us
    ppermute x10, waiting for transfers between devices, swap(): return lax.ppermute(array, axis, [(i, i ^ bit) for i in range(size)])  7.41 us
    ppermute x5, starting transfers between devices, local(): lax.ppermute(a, 'ctx', [(i, (i + 2 * shift) % ctx_size) for i in range(ct...  7.15 us
    pallas_call x3, Pallas kernels, attend(): pl.pallas_call(functools.partial(attend_kernel, slots, tp_size, first_cal...  7.04 us
    ppermute x1, waiting for transfers between devices, local(): lax.ppermute(a, ('ctx', 'tp'), [(i * tp_size + j, (i ^ 1) * tp_size + (j...  2.29 us
    unnamed x16, local copies, waits for them, and re-layouts  1.13 us
  transfers between devices with their start and end apart: 16, of which 5 were waited for; matrix products, arithmetic and copies ran while one was open for 3% of the time, Pallas kernels for 9%

profile of v5, /device:TPU:1, one launch (start us, length us, event | category | flops | bytes accessed | tf_op | source)
XLA Modules:
  0.0 42.9 jit_solution(8836335865367731475)
XLA Ops:
  0.6 2.2 %collective-permute-start = (bf16[32,2048]{1,0:T(8,128)(2,1)}, bf16[32,2048]{1,0:T(8,128)(2,1)S(1)}, u32[]{:S(2)}, u32[]{:S(2)}) collective-permute-start(bf16[32,2048]{1,0:T(8,128)(2,1)} %param.8), channel_id=1, source_target_pairs={{0,8},{4,12},{8,16},{12,20},{16,24},{20,28},{24,0},{28,4},{1,9},{5... | collective-permute-start | bytes 393224 | tf_op jit(solution)/shard_map/ppermute | solution.py:153
  2.8 2.1 %collective-permute-start.1 = (bf16[32,2048]{1,0:T(8,128)(2,1)}, bf16[32,2048]{1,0:T(8,128)(2,1)S(1)}, u32[]{:S(2)}, u32[]{:S(2)}) collective-permute-start(bf16[32,2048]{1,0:T(8,128)(2,1)} %param.8), channel_id=1, source_target_pairs={{0,24},{4,28},{8,0},{12,4},{16,8},{20,12},{24,16},{28,20},{1,25},{... | collective-permute-start | bytes 393224 | tf_op jit(solution)/shard_map/ppermute | solution.py:153
  4.9 1.2 %collective-permute-start.2 = (bf16[32,2048]{1,0:T(8,128)(2,1)}, bf16[32,2048]{1,0:T(8,128)(2,1)S(1)}, u32[]{:S(2)}, u32[]{:S(2)}) collective-permute-start(bf16[32,2048]{1,0:T(8,128)(2,1)} %param.8), channel_id=1, source_target_pairs={{0,4},{4,0},{8,12},{12,8},{16,20},{20,16},{24,28},{28,24},{1,5},{5... | collective-permute-start | bytes 393224 | tf_op jit(solution)/shard_map/ppermute | solution.py:137
  6.1 1.2 %collective-permute-start.3 = (bf16[32,2048]{1,0:T(8,128)(2,1)}, bf16[32,2048]{1,0:T(8,128)(2,1)S(1)}, u32[]{:S(2)}, u32[]{:S(2)}) collective-permute-start(bf16[32,2048]{1,0:T(8,128)(2,1)} %param.8), channel_id=1, source_target_pairs={{0,2},{1,3},{2,0},{3,1},{4,6},{5,7},{6,4},{7,5},{8,10},{9,11},{10,... | collective-permute-start | bytes 393224 | tf_op jit(solution)/shard_map/ppermute | solution.py:137
  7.4 0.2 collective-permute-start.4
  7.6 1.0 %constant_dynamic-update-slice_fusion.14 = (bf16[224,2048]{1,0:T(8,128)(2,1)S(1)}, bf16[192,2048]{1,0:T(8,128)(2,1)S(1)}) fusion(bf16[32,2048]{1,0:T(8,128)(2,1)} %param.8), kind=kLoop, calls=%fused_computation.17 | loop fusion | bytes 393216
  10.5 0.1 collective-permute-done.1
  10.6 2.3 %collective-permute-done.4 = bf16[32,2048]{1,0:T(8,128)(2,1)S(1)} collective-permute-done((bf16[32,2048]{1,0:T(8,128)(2,1)}, bf16[32,2048]{1,0:T(8,128)(2,1)S(1)}, u32[]{:S(2)}, u32[]{:S(2)}) %collective-permute-start.4) | collective-permute-done | bytes 131104 | tf_op jit(solution)/shard_map/ppermute | solution.py:157
  13.2 2.6 %collective-permute-start.12 = (bf16[224,2048]{1,0:T(8,128)(2,1)S(1)}, bf16[224,2048]{1,0:T(8,128)(2,1)S(1)}, u32[]{:S(2)}, u32[]{:S(2)}) collective-permute-start(bf16[224,2048]{1,0:T(8,128)(2,1)S(1)} %constant_dynamic-update-slice_fusion.8), channel_id=1, source_target_pairs={{0,1},{1,0},{2,3},{3,2},{4,5},{5,4},{6,7},{7,6},{8,9},{9,8},{10,11... | collective-permute-start | bytes 2752520 | tf_op jit(solution)/shard_map/ppermute | solution.py:137
  15.9 0.9 %collective-permute-start.11 = (bf16[96,2048]{1,0:T(8,128)(2,1)S(1)}, bf16[96,2048]{1,0:T(8,128)(2,1)S(1)}, u32[]{:S(2)}, u32[]{:S(2)}) collective-permute-start(bf16[96,2048]{1,0:T(8,128)(2,1)S(1)} %pad_maximum_fusion), channel_id=1, source_target_pairs={{0,2},{1,3},{2,0},{3,1},{4,6},{5,7},{6,4},{7,5},{8,10},{9,11},{10,... | collective-permute-start | bytes 1179656 | tf_op jit(solution)/shard_map/ppermute | solution.py:137
  16.8 0.3 collective-permute-start.10
  17.1 1.4 %collective-permute-start.6 = (bf16[32,2048]{1,0:T(8,128)(2,1)S(1)}, bf16[32,2048]{1,0:T(8,128)(2,1)S(1)}, u32[]{:S(2)}, u32[]{:S(2)}) collective-permute-start(bf16[32,2048]{1,0:T(8,128)(2,1)S(1)} %collective-permute-done.4), channel_id=1, source_target_pairs={{0,24},{4,28},{8,0},{12,4},{16,8},{20,12},{24,16},{28,20},{1,25},{... | collective-permute-start | bytes 393224 | tf_op jit(solution)/shard_map/ppermute | solution.py:153
  18.7 1.9 %shard_map.86 = (f32[8,320,128]{2,1,0:T(8,128)S(1)}, f32[8,320,128]{2,1,0:T(8,128)S(1)}, f32[8,320,128]{2,1,0:T(8,128)S(1)}) custom-call(s32[3,128]{1,0:T(4,128)S(1)} %broadcast_in_dim.11.refs_0_, bf16[32,5120]{1,0:T(8,128)(2,1)S(1)} %copy-done, bf16[32,5120]{1,0:T(8,128)(2,1)S(1)} %bitcast.12, bf16[192,2048]{1,0:T(8,128)(2,1)S(1)} %get-tuple-element.55.refs_3_, ...), custom_call_target="tpu_custom_call" | custom-call | flops 1006632960 | bytes 1572864 | tf_op jit(solution)/shard_map/pallas_call | solution.py:123
  20.6 3.9 %collective-permute-done.10 = bf16[64,2048]{1,0:T(8,128)(2,1)S(1)} collective-permute-done((bf16[64,2048]{1,0:T(8,128)(2,1)S(1)}, bf16[64,2048]{1,0:T(8,128)(2,1)S(1)}, u32[]{:S(2)}, u32[]{:S(2)}) %collective-permute-start.10) | collective-permute-done | bytes 262176 | tf_op jit(solution)/shard_map/ppermute | solution.py:137
  24.5 2.1 %collective-permute-done.11 = bf16[96,2048]{1,0:T(8,128)(2,1)S(1)} collective-permute-done((bf16[96,2048]{1,0:T(8,128)(2,1)S(1)}, bf16[96,2048]{1,0:T(8,128)(2,1)S(1)}, u32[]{:S(2)}, u32[]{:S(2)}) %collective-permute-start.11) | collective-permute-done | bytes 393248 | tf_op jit(solution)/shard_map/ppermute | solution.py:137
  26.7 0.9 %collective-permute-start.13 = (bf16[160,2048]{1,0:T(8,128)(2,1)S(1)}, bf16[160,2048]{1,0:T(8,128)(2,1)S(1)}, u32[]{:S(2)}, u32[]{:S(2)}) collective-permute-start(bf16[160,2048]{1,0:T(8,128)(2,1)S(1)} %constant_dynamic-update-slice_fusion.15.refs_4_), channel_id=1, source_target_pairs={{0,1},{1,0},{2,3},{3,2},{4,5},{5,4},{6,7},{7,6},{8,9},{9,8},{10,11... | collective-permute-start | bytes 1966088 | tf_op jit(solution)/shard_map/ppermute | solution.py:137
  27.6 1.1 %collective-permute-start.7 = (bf16[32,2048]{1,0:T(8,128)(2,1)S(1)}, bf16[32,2048]{1,0:T(8,128)(2,1)S(1)}, u32[]{:S(2)}, u32[]{:S(2)}) collective-permute-start(bf16[32,2048]{1,0:T(8,128)(2,1)S(1)} %get-tuple-element.53), channel_id=1, source_target_pairs={{0,4},{4,0},{8,12},{12,8},{16,20},{20,16},{24,28},{28,24},{1,5},{5... | collective-permute-start | bytes 393224 | tf_op jit(solution)/shard_map/ppermute | solution.py:137
  28.7 0.7 %collective-permute-start.8 = (bf16[32,2048]{1,0:T(8,128)(2,1)S(1)}, bf16[32,2048]{1,0:T(8,128)(2,1)S(1)}, u32[]{:S(2)}, u32[]{:S(2)}) collective-permute-start(bf16[32,2048]{1,0:T(8,128)(2,1)S(1)} %get-tuple-element.53), channel_id=1, source_target_pairs={{0,2},{1,3},{2,0},{3,1},{4,6},{5,7},{6,4},{7,5},{8,10},{9,11},{10,... | collective-permute-start | bytes 393224 | tf_op jit(solution)/shard_map/ppermute | solution.py:137
  29.3 1.4 %collective-permute-start.9 = (bf16[32,2048]{1,0:T(8,128)(2,1)S(1)}, bf16[32,2048]{1,0:T(8,128)(2,1)S(1)}, u32[]{:S(2)}, u32[]{:S(2)}) collective-permute-start(bf16[32,2048]{1,0:T(8,128)(2,1)S(1)} %get-tuple-element.52), channel_id=1, source_target_pairs={{0,8},{4,12},{8,16},{12,20},{16,24},{20,28},{24,0},{28,4},{1,9},{5... | collective-permute-start | bytes 393224 | tf_op jit(solution)/shard_map/ppermute | solution.py:153
  30.8 2.3 %collective-permute-start.14 = (bf16[96,2048]{1,0:T(8,128)(2,1)S(1)}, bf16[96,2048]{1,0:T(8,128)(2,1)S(1)}, u32[]{:S(2)}, u32[]{:S(2)}) collective-permute-start(bf16[96,2048]{1,0:T(8,128)(2,1)S(1)} %constant_dynamic-update-slice_fusion.refs_3_), channel_id=1, source_target_pairs={{0,1},{1,0},{2,3},{3,2},{4,5},{5,4},{6,7},{7,6},{8,9},{9,8},{10,11... | collective-permute-start | bytes 1179656 | tf_op jit(solution)/shard_map/ppermute | solution.py:137
  33.1 2.1 %shard_map.87 = (f32[8,320,128]{2,1,0:T(8,128)S(1)}, f32[8,320,128]{2,1,0:T(8,128)S(1)}, f32[8,320,128]{2,1,0:T(8,128)S(1)}) custom-call(s32[3,128]{1,0:T(4,128)S(1)} %broadcast_in_dim.11.refs_0_, bf16[32,5120]{1,0:T(8,128)(2,1)S(1)} %copy-done, bf16[32,5120]{1,0:T(8,128)(2,1)S(1)} %bitcast.13, bf16[32,2048]{1,0:T(8,128)(2,1)S(1)} %bitcast.16, ...), custom_call_target="tpu_custom_call" | custom-call | flops 1006632960 | bytes 1572864 | tf_op jit(solution)/shard_map/pallas_call | solution.py:123
  35.4 3.2 %collective-permute-start.15 = (bf16[96,2048]{1,0:T(8,128)(2,1)S(1)}, bf16[96,2048]{1,0:T(8,128)(2,1)S(1)}, u32[]{:S(2)}, u32[]{:S(2)}) collective-permute-start(bf16[96,2048]{1,0:T(8,128)(2,1)S(1)} %constant_dynamic-update-slice_fusion.17.refs_4_), channel_id=1, source_target_pairs={{0,1},{1,0},{2,3},{3,2},{4,5},{5,4},{6,7},{7,6},{8,9},{9,8},{10,11... | collective-permute-start | bytes 1179656 | tf_op jit(solution)/shard_map/ppermute | solution.py:137
  38.5 1.3 %collective-permute-done.15.refs_6_ = bf16[96,2048]{1,0:T(8,128)(2,1)S(1)} collective-permute-done((bf16[96,2048]{1,0:T(8,128)(2,1)S(1)}, bf16[96,2048]{1,0:T(8,128)(2,1)S(1)}, u32[]{:S(2)}, u32[]{:S(2)}) %collective-permute-start.15) | collective-permute-done | bytes 393248 | tf_op jit(solution)/shard_map/ppermute | solution.py:137
  39.9 3.0 %shard_map.88 = (bf16[32,5120]{1,0:T(8,128)(2,1)}, bf16[32,5120]{1,0:T(8,128)(2,1)}) custom-call(s32[3,128]{1,0:T(4,128)S(1)} %broadcast_in_dim.11.refs_0_, bf16[32,5120]{1,0:T(8,128)(2,1)S(1)} %copy-done, bf16[32,5120]{1,0:T(8,128)(2,1)S(1)} %bitcast.14, bf16[96,2048]{1,0:T(8,128)(2,1)S(1)} %constant_dynamic-update-slice_fusion.refs_3_, ...), custom_call_target="tpu_custom_call" | custom-call | flops 1006632960 | bytes 1572864 | tf_op jit(solution)/shard_map/pallas_call | solution.py:123
  (38 shorter events, 0.6 us)
Async XLA Ops:
  0.6 12.5 %copy-start.2 = (bf16[1,32,2048]{2,1,0:T(8,128)(2,1)S(1)}, bf16[1,32,2048]{2,1,0:T(8,128)(2,1)}, u32[]{:S(2)}) copy-start(bf16[1,32,2048]{2,1,0:T(8,128)(2,1)} %param.10) | copy-start | bytes 393220
  0.6 9.9 %collective-permute-start = (bf16[32,2048]{1,0:T(8,128)(2,1)}, bf16[32,2048]{1,0:T(8,128)(2,1)S(1)}, u32[]{:S(2)}, u32[]{:S(2)}) collective-permute-start(bf16[32,2048]{1,0:T(8,128)(2,1)} %param.8), channel_id=1, source_target_pairs={{0,8},{4,12},{8,16},{12,20},{16,24},{20,28},{24,0},{28,4},{1,9},{5... | collective-permute-start | bytes 393224 | tf_op jit(solution)/shard_map/ppermute | solution.py:153
  2.8 7.8 %collective-permute-start.1 = (bf16[32,2048]{1,0:T(8,128)(2,1)}, bf16[32,2048]{1,0:T(8,128)(2,1)S(1)}, u32[]{:S(2)}, u32[]{:S(2)}) collective-permute-start(bf16[32,2048]{1,0:T(8,128)(2,1)} %param.8), channel_id=1, source_target_pairs={{0,24},{4,28},{8,0},{12,4},{16,8},{20,12},{24,16},{28,20},{1,25},{... | collective-permute-start | bytes 393224 | tf_op jit(solution)/shard_map/ppermute | solution.py:153
  4.9 5.7 %collective-permute-start.2 = (bf16[32,2048]{1,0:T(8,128)(2,1)}, bf16[32,2048]{1,0:T(8,128)(2,1)S(1)}, u32[]{:S(2)}, u32[]{:S(2)}) collective-permute-start(bf16[32,2048]{1,0:T(8,128)(2,1)} %param.8), channel_id=1, source_target_pairs={{0,4},{4,0},{8,12},{12,8},{16,20},{20,16},{24,28},{28,24},{1,5},{5... | collective-permute-start | bytes 393224 | tf_op jit(solution)/shard_map/ppermute | solution.py:137
  6.1 4.5 %collective-permute-start.3 = (bf16[32,2048]{1,0:T(8,128)(2,1)}, bf16[32,2048]{1,0:T(8,128)(2,1)S(1)}, u32[]{:S(2)}, u32[]{:S(2)}) collective-permute-start(bf16[32,2048]{1,0:T(8,128)(2,1)} %param.8), channel_id=1, source_target_pairs={{0,2},{1,3},{2,0},{3,1},{4,6},{5,7},{6,4},{7,5},{8,10},{9,11},{10,... | collective-permute-start | bytes 393224 | tf_op jit(solution)/shard_map/ppermute | solution.py:137
  7.4 5.6 %collective-permute-start.4 = (bf16[32,2048]{1,0:T(8,128)(2,1)}, bf16[32,2048]{1,0:T(8,128)(2,1)S(1)}, u32[]{:S(2)}, u32[]{:S(2)}) collective-permute-start(bf16[32,2048]{1,0:T(8,128)(2,1)} %param.8), channel_id=1, source_target_pairs={{0,6},{1,7},{2,4},{3,5},{4,2},{5,3},{6,0},{7,1},{8,14},{9,15},{10,... | collective-permute-start | bytes 393224 | tf_op jit(solution)/shard_map/ppermute | solution.py:157
  13.2 5.4 %collective-permute-start.12 = (bf16[224,2048]{1,0:T(8,128)(2,1)S(1)}, bf16[224,2048]{1,0:T(8,128)(2,1)S(1)}, u32[]{:S(2)}, u32[]{:S(2)}) collective-permute-start(bf16[224,2048]{1,0:T(8,128)(2,1)S(1)} %constant_dynamic-update-slice_fusion.8), channel_id=1, source_target_pairs={{0,1},{1,0},{2,3},{3,2},{4,5},{5,4},{6,7},{7,6},{8,9},{9,8},{10,11... | collective-permute-start | bytes 2752520 | tf_op jit(solution)/shard_map/ppermute | solution.py:137
  15.8 2.8 %copy-start = (bf16[32,5120]{1,0:T(8,128)(2,1)S(1)}, bf16[32,5120]{1,0:T(8,128)(2,1)}, u32[]{:S(2)}) copy-start(bf16[32,5120]{1,0:T(8,128)(2,1)} %refs_1_.5) | copy-start | bytes 983044
  15.8 2.8 %copy-start.1 = (bf16[1,32,5120]{2,1,0:T(8,128)(2,1)S(1)}, bf16[1,32,5120]{2,1,0:T(8,128)(2,1)}, u32[]{:S(2)}) copy-start(bf16[1,32,5120]{2,1,0:T(8,128)(2,1)} %param.9) | copy-start | bytes 983044
  15.9 10.8 %collective-permute-start.11 = (bf16[96,2048]{1,0:T(8,128)(2,1)S(1)}, bf16[96,2048]{1,0:T(8,128)(2,1)S(1)}, u32[]{:S(2)}, u32[]{:S(2)}) collective-permute-start(bf16[96,2048]{1,0:T(8,128)(2,1)S(1)} %pad_maximum_fusion), channel_id=1, source_target_pairs={{0,2},{1,3},{2,0},{3,1},{4,6},{5,7},{6,4},{7,5},{8,10},{9,11},{10,... | collective-permute-start | bytes 1179656 | tf_op jit(solution)/shard_map/ppermute | solution.py:137
  16.8 7.7 %collective-permute-start.10 = (bf16[64,2048]{1,0:T(8,128)(2,1)S(1)}, bf16[64,2048]{1,0:T(8,128)(2,1)S(1)}, u32[]{:S(2)}, u32[]{:S(2)}) collective-permute-start(bf16[64,2048]{1,0:T(8,128)(2,1)S(1)} %get-tuple-element.66), channel_id=1, source_target_pairs={{0,4},{4,0},{8,12},{12,8},{16,20},{20,16},{24,28},{28,24},{1,5},{5... | collective-permute-start | bytes 786440 | tf_op jit(solution)/shard_map/ppermute | solution.py:137
  17.1 13.7 %collective-permute-start.6 = (bf16[32,2048]{1,0:T(8,128)(2,1)S(1)}, bf16[32,2048]{1,0:T(8,128)(2,1)S(1)}, u32[]{:S(2)}, u32[]{:S(2)}) collective-permute-start(bf16[32,2048]{1,0:T(8,128)(2,1)S(1)} %collective-permute-done.4), channel_id=1, source_target_pairs={{0,24},{4,28},{8,0},{12,4},{16,8},{20,12},{24,16},{28,20},{1,25},{... | collective-permute-start | bytes 393224 | tf_op jit(solution)/shard_map/ppermute | solution.py:153
  18.5 9.1 %collective-permute-start.5 = (bf16[64,2048]{1,0:T(8,128)(2,1)S(1)}, bf16[64,2048]{1,0:T(8,128)(2,1)S(1)}, u32[]{:S(2)}, u32[]{:S(2)}) collective-permute-start(bf16[64,2048]{1,0:T(8,128)(2,1)S(1)} %get-tuple-element.67), channel_id=1, source_target_pairs={{0,8},{4,12},{8,16},{12,20},{16,24},{20,28},{24,0},{28,4},{1,9},{5... | collective-permute-start | bytes 786440 | tf_op jit(solution)/shard_map/ppermute | solution.py:153
  26.7 6.4 %collective-permute-start.13 = (bf16[160,2048]{1,0:T(8,128)(2,1)S(1)}, bf16[160,2048]{1,0:T(8,128)(2,1)S(1)}, u32[]{:S(2)}, u32[]{:S(2)}) collective-permute-start(bf16[160,2048]{1,0:T(8,128)(2,1)S(1)} %constant_dynamic-update-slice_fusion.15.refs_4_), channel_id=1, source_target_pairs={{0,1},{1,0},{2,3},{3,2},{4,5},{5,4},{6,7},{7,6},{8,9},{9,8},{10,11... | collective-permute-start | bytes 1966088 | tf_op jit(solution)/shard_map/ppermute | solution.py:137
  27.6 7.7 %collective-permute-start.7 = (bf16[32,2048]{1,0:T(8,128)(2,1)S(1)}, bf16[32,2048]{1,0:T(8,128)(2,1)S(1)}, u32[]{:S(2)}, u32[]{:S(2)}) collective-permute-start(bf16[32,2048]{1,0:T(8,128)(2,1)S(1)} %get-tuple-element.53), channel_id=1, source_target_pairs={{0,4},{4,0},{8,12},{12,8},{16,20},{20,16},{24,28},{28,24},{1,5},{5... | collective-permute-start | bytes 393224 | tf_op jit(solution)/shard_map/ppermute | solution.py:137
  28.7 6.6 %collective-permute-start.8 = (bf16[32,2048]{1,0:T(8,128)(2,1)S(1)}, bf16[32,2048]{1,0:T(8,128)(2,1)S(1)}, u32[]{:S(2)}, u32[]{:S(2)}) collective-permute-start(bf16[32,2048]{1,0:T(8,128)(2,1)S(1)} %get-tuple-element.53), channel_id=1, source_target_pairs={{0,2},{1,3},{2,0},{3,1},{4,6},{5,7},{6,4},{7,5},{8,10},{9,11},{10,... | collective-permute-start | bytes 393224 | tf_op jit(solution)/shard_map/ppermute | solution.py:137
  29.3 6.0 %collective-permute-start.9 = (bf16[32,2048]{1,0:T(8,128)(2,1)S(1)}, bf16[32,2048]{1,0:T(8,128)(2,1)S(1)}, u32[]{:S(2)}, u32[]{:S(2)}) collective-permute-start(bf16[32,2048]{1,0:T(8,128)(2,1)S(1)} %get-tuple-element.52), channel_id=1, source_target_pairs={{0,8},{4,12},{8,16},{12,20},{16,24},{20,28},{24,0},{28,4},{1,9},{5... | collective-permute-start | bytes 393224 | tf_op jit(solution)/shard_map/ppermute | solution.py:153
  30.8 7.7 %collective-permute-start.14 = (bf16[96,2048]{1,0:T(8,128)(2,1)S(1)}, bf16[96,2048]{1,0:T(8,128)(2,1)S(1)}, u32[]{:S(2)}, u32[]{:S(2)}) collective-permute-start(bf16[96,2048]{1,0:T(8,128)(2,1)S(1)} %constant_dynamic-update-slice_fusion.refs_3_), channel_id=1, source_target_pairs={{0,1},{1,0},{2,3},{3,2},{4,5},{5,4},{6,7},{7,6},{8,9},{9,8},{10,11... | collective-permute-start | bytes 1179656 | tf_op jit(solution)/shard_map/ppermute | solution.py:137
  35.4 4.5 %collective-permute-start.15 = (bf16[96,2048]{1,0:T(8,128)(2,1)S(1)}, bf16[96,2048]{1,0:T(8,128)(2,1)S(1)}, u32[]{:S(2)}, u32[]{:S(2)}) collective-permute-start(bf16[96,2048]{1,0:T(8,128)(2,1)S(1)} %constant_dynamic-update-slice_fusion.17.refs_4_), channel_id=1, source_target_pairs={{0,1},{1,0},{2,3},{3,2},{4,5},{5,4},{6,7},{7,6},{8,9},{9,8},{10,11... | collective-permute-start | bytes 1179656 | tf_op jit(solution)/shard_map/ppermute | solution.py:137

commit v6 on v5

--- a/solution.py
+++ b/solution.py
@@ -189,17 +189,16 @@
         down_d = along_z(own_d, 3)
         plane = jnp.concatenate([trace_key_value, own_x, own_y, own_d, up, down, suffix_own], axis=0)
         plane_core = core(plane)
-        cut = 6 * rows
-        here = [(0, 0, 0), (0, 1, 0), (0, 0, 1), (0, 1, 1), (1, 0, 0), (3, 0, 0)]
-        state = absorb_both([plane[:cut]], [plane_core[:cut]], here, None)
-
-        near_x, near_y, state = barrier((near_x, near_y, state))
+        near_x, near_y, up_two, plane, plane_core = barrier((near_x, near_y, up_two, plane, plane_core))
         sides = jnp.concatenate([near_x, near_y], axis=0)
         sides_core = core(sides)
         far, up_d = up_two[:rows], up_two[rows:]
         far_x, far_y, far_d = across_x(far), across_y(far), along_z(up_d, 1)
         mixed = jnp.concatenate([up_two, down_d], axis=0)
         mixed_core = core(mixed)
+        cut = 6 * rows
+        here = [(0, 0, 0), (0, 1, 0), (0, 0, 1), (0, 1, 1), (1, 0, 0), (3, 0, 0)]
+        state = absorb_both([plane[:cut]], [plane_core[:cut]], here, None)
         here = [0, (1, 1, 0), (3, 1, 0), (1, 0, 1), (3, 0, 1), 2]
         state = absorb_both([plane[cut:], sides], [plane_core[cut:], sides_core], here, state)
 

time: 43.4 us -> 43.6 us (level)
  starting transfers between devices: 21.7 us -> 20.2 us
  waiting for transfers between devices: 9.81 us -> 11.3 us
    ppermute x5, waiting for transfers between devices: 0.11 us -> 3.08 us  [local(): lax.ppermute(a, 'ctx', [(i, (i + 2 * shift) % ctx_size) for i in range(ct...]
    ppermute x10, starting transfers between devices: 14.4 us -> 12.5 us  [swap(): return lax.ppermute(array, axis, [(i, i ^ bit) for i in range(size)])]
    ppermute x10, waiting for transfers between devices: 7.41 us -> 5.89 us  [swap(): return lax.ppermute(array, axis, [(i, i ^ bit) for i in range(size)])]
    ppermute x5, starting transfers between devices: 7.15 us -> 7.59 us  [local(): lax.ppermute(a, 'ctx', [(i, (i + 2 * shift) % ctx_size) for i in range(ct...]
  transfers between devices with their start and end apart: 16 -> 16, of which waited for: 5 -> 7; matrix products, arithmetic and copies ran while one was open for 3% -> 3% of each run, Pallas kernels for 9% -> 9%
where the time goes in v6:
time: 43.6 us; the launch traced here: 43.1 us
  starting transfers between devices  20.2 us (46%)
  waiting for transfers between devices  11.3 us (26%)
  Pallas kernels  7.03 us (16%)
  between operations  2.81 us (6%)
  local copies, waits for them, and re-layouts  1.58 us (4%)
    ppermute x10, starting transfers between devices, swap(): return lax.ppermute(array, axis, [(i, i ^ bit) for i in range(size)])  12.5 us
    ppermute x5, starting transfers between devices, local(): lax.ppermute(a, 'ctx', [(i, (i + 2 * shift) % ctx_size) for i in range(ct...  7.59 us
    pallas_call x3, Pallas kernels, attend(): pl.pallas_call(functools.partial(attend_kernel, slots, tp_size, first_cal...  7.03 us
    ppermute x10, waiting for transfers between devices, swap(): return lax.ppermute(array, axis, [(i, i ^ bit) for i in range(size)])  5.89 us
    ppermute x5, waiting for transfers between devices, local(): lax.ppermute(a, 'ctx', [(i, (i + 2 * shift) % ctx_size) for i in range(ct...  3.08 us
    ppermute x1, waiting for transfers between devices, local(): lax.ppermute(a, ('ctx', 'tp'), [(i * tp_size + j, (i ^ 1) * tp_size + (j...  2.29 us
    unnamed x16, local copies, waits for them, and re-layouts  1.28 us
  transfers between devices with their start and end apart: 16, of which 7 were waited for; matrix products, arithmetic and copies ran while one was open for 3% of the time, Pallas kernels for 9%

profile of v6, /device:TPU:1, one launch (start us, length us, event | category | flops | bytes accessed | tf_op | source)
XLA Modules:
  0.0 43.1 jit_solution(8998966380528189854)
XLA Ops:
  0.6 2.2 %collective-permute-start = (bf16[32,2048]{1,0:T(8,128)(2,1)}, bf16[32,2048]{1,0:T(8,128)(2,1)S(1)}, u32[]{:S(2)}, u32[]{:S(2)}) collective-permute-start(bf16[32,2048]{1,0:T(8,128)(2,1)} %param.8), channel_id=1, source_target_pairs={{0,8},{4,12},{8,16},{12,20},{16,24},{20,28},{24,0},{28,4},{1,9},{5... | collective-permute-start | bytes 393224 | tf_op jit(solution)/shard_map/ppermute | solution.py:153
  2.8 2.1 %collective-permute-start.1 = (bf16[32,2048]{1,0:T(8,128)(2,1)}, bf16[32,2048]{1,0:T(8,128)(2,1)S(1)}, u32[]{:S(2)}, u32[]{:S(2)}) collective-permute-start(bf16[32,2048]{1,0:T(8,128)(2,1)} %param.8), channel_id=1, source_target_pairs={{0,24},{4,28},{8,0},{12,4},{16,8},{20,12},{24,16},{28,20},{1,25},{... | collective-permute-start | bytes 393224 | tf_op jit(solution)/shard_map/ppermute | solution.py:153
  4.9 1.2 %collective-permute-start.2 = (bf16[32,2048]{1,0:T(8,128)(2,1)}, bf16[32,2048]{1,0:T(8,128)(2,1)S(1)}, u32[]{:S(2)}, u32[]{:S(2)}) collective-permute-start(bf16[32,2048]{1,0:T(8,128)(2,1)} %param.8), channel_id=1, source_target_pairs={{0,4},{4,0},{8,12},{12,8},{16,20},{20,16},{24,28},{28,24},{1,5},{5... | collective-permute-start | bytes 393224 | tf_op jit(solution)/shard_map/ppermute | solution.py:137
  6.1 1.2 %collective-permute-start.3 = (bf16[32,2048]{1,0:T(8,128)(2,1)}, bf16[32,2048]{1,0:T(8,128)(2,1)S(1)}, u32[]{:S(2)}, u32[]{:S(2)}) collective-permute-start(bf16[32,2048]{1,0:T(8,128)(2,1)} %param.8), channel_id=1, source_target_pairs={{0,2},{1,3},{2,0},{3,1},{4,6},{5,7},{6,4},{7,5},{8,10},{9,11},{10,... | collective-permute-start | bytes 393224 | tf_op jit(solution)/shard_map/ppermute | solution.py:137
  7.4 0.2 collective-permute-start.4
  7.6 0.9 %constant_dynamic-update-slice_fusion.6 = bf16[224,2048]{1,0:T(8,128)(2,1)S(1)} fusion(bf16[32,2048]{1,0:T(8,128)(2,1)} %param.8), kind=kLoop, calls=%fused_computation.9 | loop fusion | bytes 262144
  10.6 2.3 %collective-permute-done.4 = bf16[32,2048]{1,0:T(8,128)(2,1)S(1)} collective-permute-done((bf16[32,2048]{1,0:T(8,128)(2,1)}, bf16[32,2048]{1,0:T(8,128)(2,1)S(1)}, u32[]{:S(2)}, u32[]{:S(2)}) %collective-permute-start.4) | collective-permute-done | bytes 131104 | tf_op jit(solution)/shard_map/ppermute | solution.py:157
  13.1 2.6 %collective-permute-start.8 = (bf16[224,2048]{1,0:T(8,128)(2,1)S(1)}, bf16[224,2048]{1,0:T(8,128)(2,1)S(1)}, u32[]{:S(2)}, u32[]{:S(2)}) collective-permute-start(bf16[224,2048]{1,0:T(8,128)(2,1)S(1)} %constant_dynamic-update-slice_fusion), channel_id=1, source_target_pairs={{0,1},{1,0},{2,3},{3,2},{4,5},{5,4},{6,7},{7,6},{8,9},{9,8},{10,11... | collective-permute-start | bytes 2752520 | tf_op jit(solution)/shard_map/ppermute | solution.py:137
  15.8 0.9 %collective-permute-start.6 = (bf16[96,2048]{1,0:T(8,128)(2,1)S(1)}, bf16[96,2048]{1,0:T(8,128)(2,1)S(1)}, u32[]{:S(2)}, u32[]{:S(2)}) collective-permute-start(bf16[96,2048]{1,0:T(8,128)(2,1)S(1)} %pad_maximum_fusion), channel_id=1, source_target_pairs={{0,2},{1,3},{2,0},{3,1},{4,6},{5,7},{6,4},{7,5},{8,10},{9,11},{10,... | collective-permute-start | bytes 1179656 | tf_op jit(solution)/shard_map/ppermute | solution.py:137
  16.8 0.3 collective-permute-start.5
  17.0 3.3 %collective-permute-start.9 = (bf16[32,2048]{1,0:T(8,128)(2,1)S(1)}, bf16[32,2048]{1,0:T(8,128)(2,1)S(1)}, u32[]{:S(2)}, u32[]{:S(2)}) collective-permute-start(bf16[32,2048]{1,0:T(8,128)(2,1)S(1)} %collective-permute-done.4), channel_id=1, source_target_pairs={{0,24},{4,28},{8,0},{12,4},{16,8},{20,12},{24,16},{28,20},{1,25},{... | collective-permute-start | bytes 393224 | tf_op jit(solution)/shard_map/ppermute | solution.py:153
  20.3 4.1 %collective-permute-done.5 = bf16[64,2048]{1,0:T(8,128)(2,1)S(1)} collective-permute-done((bf16[64,2048]{1,0:T(8,128)(2,1)S(1)}, bf16[64,2048]{1,0:T(8,128)(2,1)S(1)}, u32[]{:S(2)}, u32[]{:S(2)}) %collective-permute-start.5) | collective-permute-done | bytes 262176 | tf_op jit(solution)/shard_map/ppermute | solution.py:137
  24.4 1.8 %collective-permute-done.7 = bf16[64,2048]{1,0:T(8,128)(2,1)S(1)} collective-permute-done((bf16[64,2048]{1,0:T(8,128)(2,1)S(1)}, bf16[64,2048]{1,0:T(8,128)(2,1)S(1)}, u32[]{:S(2)}, u32[]{:S(2)}) %collective-permute-start.7) | collective-permute-done | bytes 262176 | tf_op jit(solution)/shard_map/ppermute | solution.py:153
  26.2 0.4 collective-permute-done.6
  26.6 2.1 %collective-permute-start.13 = (bf16[160,2048]{1,0:T(8,128)(2,1)S(1)}, bf16[160,2048]{1,0:T(8,128)(2,1)S(1)}, u32[]{:S(2)}, u32[]{:S(2)}) collective-permute-start(bf16[160,2048]{1,0:T(8,128)(2,1)S(1)} %constant_dynamic-update-slice_fusion.9.refs_4_), channel_id=1, source_target_pairs={{0,1},{1,0},{2,3},{3,2},{4,5},{5,4},{6,7},{7,6},{8,9},{9,8},{10,11... | collective-permute-start | bytes 1966088 | tf_op jit(solution)/shard_map/ppermute | solution.py:137
  28.8 1.3 %collective-permute-start.10 = (bf16[32,2048]{1,0:T(8,128)(2,1)S(1)}, bf16[32,2048]{1,0:T(8,128)(2,1)S(1)}, u32[]{:S(2)}, u32[]{:S(2)}) collective-permute-start(bf16[32,2048]{1,0:T(8,128)(2,1)S(1)} %get-tuple-element.53), channel_id=1, source_target_pairs={{0,4},{4,0},{8,12},{12,8},{16,20},{20,16},{24,28},{28,24},{1,5},{5... | collective-permute-start | bytes 393224 | tf_op jit(solution)/shard_map/ppermute | solution.py:137
  30.1 0.6 %collective-permute-start.11 = (bf16[32,2048]{1,0:T(8,128)(2,1)S(1)}, bf16[32,2048]{1,0:T(8,128)(2,1)S(1)}, u32[]{:S(2)}, u32[]{:S(2)}) collective-permute-start(bf16[32,2048]{1,0:T(8,128)(2,1)S(1)} %get-tuple-element.53), channel_id=1, source_target_pairs={{0,2},{1,3},{2,0},{3,1},{4,6},{5,7},{6,4},{7,5},{8,10},{9,11},{10,... | collective-permute-start | bytes 393224 | tf_op jit(solution)/shard_map/ppermute | solution.py:137
  31.0 0.6 %collective-permute-start.14 = (bf16[96,2048]{1,0:T(8,128)(2,1)S(1)}, bf16[96,2048]{1,0:T(8,128)(2,1)S(1)}, u32[]{:S(2)}, u32[]{:S(2)}) collective-permute-start(bf16[96,2048]{1,0:T(8,128)(2,1)S(1)} %constant_dynamic-update-slice_fusion.7.refs_3_), channel_id=1, source_target_pairs={{0,1},{1,0},{2,3},{3,2},{4,5},{5,4},{6,7},{7,6},{8,9},{9,8},{10,11... | collective-permute-start | bytes 1179656 | tf_op jit(solution)/shard_map/ppermute | solution.py:137
  31.8 1.9 %shard_map.86 = (f32[8,320,128]{2,1,0:T(8,128)S(1)}, f32[8,320,128]{2,1,0:T(8,128)S(1)}, f32[8,320,128]{2,1,0:T(8,128)S(1)}) custom-call(s32[3,128]{1,0:T(4,128)S(1)} %broadcast_in_dim.11.refs_0_, bf16[32,5120]{1,0:T(8,128)(2,1)S(1)} %copy-done, bf16[32,5120]{1,0:T(8,128)(2,1)S(1)} %bitcast.12, bf16[192,2048]{1,0:T(8,128)(2,1)S(1)} %slice.22.refs_3_, ...), custom_call_target="tpu_custom_call" | custom-call | flops 1006632960 | bytes 1572864 | tf_op jit(solution)/shard_map/pallas_call | solution.py:123
  33.8 2.1 %shard_map.87 = (f32[8,320,128]{2,1,0:T(8,128)S(1)}, f32[8,320,128]{2,1,0:T(8,128)S(1)}, f32[8,320,128]{2,1,0:T(8,128)S(1)}) custom-call(s32[3,128]{1,0:T(4,128)S(1)} %broadcast_in_dim.11.refs_0_, bf16[32,5120]{1,0:T(8,128)(2,1)S(1)} %copy-done, bf16[32,5120]{1,0:T(8,128)(2,1)S(1)} %bitcast.13, bf16[32,2048]{1,0:T(8,128)(2,1)S(1)} %slice.20.refs_3_, ...), custom_call_target="tpu_custom_call" | custom-call | flops 1006632960 | bytes 1572864 | tf_op jit(solution)/shard_map/pallas_call | solution.py:123
  36.0 1.2 %collective-permute-done.12 = bf16[32,2048]{1,0:T(8,128)(2,1)S(1)} collective-permute-done((bf16[32,2048]{1,0:T(8,128)(2,1)S(1)}, bf16[32,2048]{1,0:T(8,128)(2,1)S(1)}, u32[]{:S(2)}, u32[]{:S(2)}) %collective-permute-start.12) | collective-permute-done | bytes 131104 | tf_op jit(solution)/shard_map/ppermute | solution.py:153
  37.2 1.5 %collective-permute-start.15 = (bf16[96,2048]{1,0:T(8,128)(2,1)S(1)}, bf16[96,2048]{1,0:T(8,128)(2,1)S(1)}, u32[]{:S(2)}, u32[]{:S(2)}) collective-permute-start(bf16[96,2048]{1,0:T(8,128)(2,1)S(1)} %constant_dynamic-update-slice_fusion.11.refs_4_), channel_id=1, source_target_pairs={{0,1},{1,0},{2,3},{3,2},{4,5},{5,4},{6,7},{7,6},{8,9},{9,8},{10,11... | collective-permute-start | bytes 1179656 | tf_op jit(solution)/shard_map/ppermute | solution.py:137
  38.7 1.3 %collective-permute-done.15.refs_6_ = bf16[96,2048]{1,0:T(8,128)(2,1)S(1)} collective-permute-done((bf16[96,2048]{1,0:T(8,128)(2,1)S(1)}, bf16[96,2048]{1,0:T(8,128)(2,1)S(1)}, u32[]{:S(2)}, u32[]{:S(2)}) %collective-permute-start.15) | collective-permute-done | bytes 393248 | tf_op jit(solution)/shard_map/ppermute | solution.py:137
  40.1 3.0 %shard_map.88 = (bf16[32,5120]{1,0:T(8,128)(2,1)}, bf16[32,5120]{1,0:T(8,128)(2,1)}) custom-call(s32[3,128]{1,0:T(4,128)S(1)} %broadcast_in_dim.11.refs_0_, bf16[32,5120]{1,0:T(8,128)(2,1)S(1)} %copy-done, bf16[32,5120]{1,0:T(8,128)(2,1)S(1)} %bitcast.14, bf16[96,2048]{1,0:T(8,128)(2,1)S(1)} %constant_dynamic-update-slice_fusion.7.refs_3_, ...), custom_call_target="tpu_custom_call" | custom-call | flops 1006632960 | bytes 1572864 | tf_op jit(solution)/shard_map/pallas_call | solution.py:123
  (40 shorter events, 1.0 us)
Async XLA Ops:
  0.6 12.5 %copy-start.2 = (bf16[1,32,2048]{2,1,0:T(8,128)(2,1)S(1)}, bf16[1,32,2048]{2,1,0:T(8,128)(2,1)}, u32[]{:S(2)}) copy-start(bf16[1,32,2048]{2,1,0:T(8,128)(2,1)} %param.10) | copy-start | bytes 393220
  0.6 9.9 %collective-permute-start = (bf16[32,2048]{1,0:T(8,128)(2,1)}, bf16[32,2048]{1,0:T(8,128)(2,1)S(1)}, u32[]{:S(2)}, u32[]{:S(2)}) collective-permute-start(bf16[32,2048]{1,0:T(8,128)(2,1)} %param.8), channel_id=1, source_target_pairs={{0,8},{4,12},{8,16},{12,20},{16,24},{20,28},{24,0},{28,4},{1,9},{5... | collective-permute-start | bytes 393224 | tf_op jit(solution)/shard_map/ppermute | solution.py:153
  2.8 7.8 %collective-permute-start.1 = (bf16[32,2048]{1,0:T(8,128)(2,1)}, bf16[32,2048]{1,0:T(8,128)(2,1)S(1)}, u32[]{:S(2)}, u32[]{:S(2)}) collective-permute-start(bf16[32,2048]{1,0:T(8,128)(2,1)} %param.8), channel_id=1, source_target_pairs={{0,24},{4,28},{8,0},{12,4},{16,8},{20,12},{24,16},{28,20},{1,25},{... | collective-permute-start | bytes 393224 | tf_op jit(solution)/shard_map/ppermute | solution.py:153
  4.9 5.7 %collective-permute-start.2 = (bf16[32,2048]{1,0:T(8,128)(2,1)}, bf16[32,2048]{1,0:T(8,128)(2,1)S(1)}, u32[]{:S(2)}, u32[]{:S(2)}) collective-permute-start(bf16[32,2048]{1,0:T(8,128)(2,1)} %param.8), channel_id=1, source_target_pairs={{0,4},{4,0},{8,12},{12,8},{16,20},{20,16},{24,28},{28,24},{1,5},{5... | collective-permute-start | bytes 393224 | tf_op jit(solution)/shard_map/ppermute | solution.py:137
  6.1 4.5 %collective-permute-start.3 = (bf16[32,2048]{1,0:T(8,128)(2,1)}, bf16[32,2048]{1,0:T(8,128)(2,1)S(1)}, u32[]{:S(2)}, u32[]{:S(2)}) collective-permute-start(bf16[32,2048]{1,0:T(8,128)(2,1)} %param.8), channel_id=1, source_target_pairs={{0,2},{1,3},{2,0},{3,1},{4,6},{5,7},{6,4},{7,5},{8,10},{9,11},{10,... | collective-permute-start | bytes 393224 | tf_op jit(solution)/shard_map/ppermute | solution.py:137
  7.4 5.6 %collective-permute-start.4 = (bf16[32,2048]{1,0:T(8,128)(2,1)}, bf16[32,2048]{1,0:T(8,128)(2,1)S(1)}, u32[]{:S(2)}, u32[]{:S(2)}) collective-permute-start(bf16[32,2048]{1,0:T(8,128)(2,1)} %param.8), channel_id=1, source_target_pairs={{0,6},{1,7},{2,4},{3,5},{4,2},{5,3},{6,0},{7,1},{8,14},{9,15},{10,... | collective-permute-start | bytes 393224 | tf_op jit(solution)/shard_map/ppermute | solution.py:157
  13.1 13.5 %collective-permute-start.8 = (bf16[224,2048]{1,0:T(8,128)(2,1)S(1)}, bf16[224,2048]{1,0:T(8,128)(2,1)S(1)}, u32[]{:S(2)}, u32[]{:S(2)}) collective-permute-start(bf16[224,2048]{1,0:T(8,128)(2,1)S(1)} %constant_dynamic-update-slice_fusion), channel_id=1, source_target_pairs={{0,1},{1,0},{2,3},{3,2},{4,5},{5,4},{6,7},{7,6},{8,9},{9,8},{10,11... | collective-permute-start | bytes 2752520 | tf_op jit(solution)/shard_map/ppermute | solution.py:137
  15.8 10.8 %collective-permute-start.6 = (bf16[96,2048]{1,0:T(8,128)(2,1)S(1)}, bf16[96,2048]{1,0:T(8,128)(2,1)S(1)}, u32[]{:S(2)}, u32[]{:S(2)}) collective-permute-start(bf16[96,2048]{1,0:T(8,128)(2,1)S(1)} %pad_maximum_fusion), channel_id=1, source_target_pairs={{0,2},{1,3},{2,0},{3,1},{4,6},{5,7},{6,4},{7,5},{8,10},{9,11},{10,... | collective-permute-start | bytes 1179656 | tf_op jit(solution)/shard_map/ppermute | solution.py:137
  16.8 7.7 %collective-permute-start.5 = (bf16[64,2048]{1,0:T(8,128)(2,1)S(1)}, bf16[64,2048]{1,0:T(8,128)(2,1)S(1)}, u32[]{:S(2)}, u32[]{:S(2)}) collective-permute-start(bf16[64,2048]{1,0:T(8,128)(2,1)S(1)} %get-tuple-element.55), channel_id=1, source_target_pairs={{0,4},{4,0},{8,12},{12,8},{16,20},{20,16},{24,28},{28,24},{1,5},{5... | collective-permute-start | bytes 786440 | tf_op jit(solution)/shard_map/ppermute | solution.py:137
  17.0 9.2 %collective-permute-start.7 = (bf16[64,2048]{1,0:T(8,128)(2,1)S(1)}, bf16[64,2048]{1,0:T(8,128)(2,1)S(1)}, u32[]{:S(2)}, u32[]{:S(2)}) collective-permute-start(bf16[64,2048]{1,0:T(8,128)(2,1)S(1)} %get-tuple-element.54), channel_id=1, source_target_pairs={{0,8},{4,12},{8,16},{12,20},{16,24},{20,28},{24,0},{28,4},{1,9},{5... | collective-permute-start | bytes 786440 | tf_op jit(solution)/shard_map/ppermute | solution.py:153
  17.0 13.9 %collective-permute-start.9 = (bf16[32,2048]{1,0:T(8,128)(2,1)S(1)}, bf16[32,2048]{1,0:T(8,128)(2,1)S(1)}, u32[]{:S(2)}, u32[]{:S(2)}) collective-permute-start(bf16[32,2048]{1,0:T(8,128)(2,1)S(1)} %collective-permute-done.4), channel_id=1, source_target_pairs={{0,24},{4,28},{8,0},{12,4},{16,8},{20,12},{24,16},{28,20},{1,25},{... | collective-permute-start | bytes 393224 | tf_op jit(solution)/shard_map/ppermute | solution.py:153
  26.6 7.2 %collective-permute-start.13 = (bf16[160,2048]{1,0:T(8,128)(2,1)S(1)}, bf16[160,2048]{1,0:T(8,128)(2,1)S(1)}, u32[]{:S(2)}, u32[]{:S(2)}) collective-permute-start(bf16[160,2048]{1,0:T(8,128)(2,1)S(1)} %constant_dynamic-update-slice_fusion.9.refs_4_), channel_id=1, source_target_pairs={{0,1},{1,0},{2,3},{3,2},{4,5},{5,4},{6,7},{7,6},{8,9},{9,8},{10,11... | collective-permute-start | bytes 1966088 | tf_op jit(solution)/shard_map/ppermute | solution.py:137
  28.8 7.2 %collective-permute-start.10 = (bf16[32,2048]{1,0:T(8,128)(2,1)S(1)}, bf16[32,2048]{1,0:T(8,128)(2,1)S(1)}, u32[]{:S(2)}, u32[]{:S(2)}) collective-permute-start(bf16[32,2048]{1,0:T(8,128)(2,1)S(1)} %get-tuple-element.53), channel_id=1, source_target_pairs={{0,4},{4,0},{8,12},{12,8},{16,20},{20,16},{24,28},{28,24},{1,5},{5... | collective-permute-start | bytes 393224 | tf_op jit(solution)/shard_map/ppermute | solution.py:137
  30.1 5.9 %collective-permute-start.11 = (bf16[32,2048]{1,0:T(8,128)(2,1)S(1)}, bf16[32,2048]{1,0:T(8,128)(2,1)S(1)}, u32[]{:S(2)}, u32[]{:S(2)}) collective-permute-start(bf16[32,2048]{1,0:T(8,128)(2,1)S(1)} %get-tuple-element.53), channel_id=1, source_target_pairs={{0,2},{1,3},{2,0},{3,1},{4,6},{5,7},{6,4},{7,5},{8,10},{9,11},{10,... | collective-permute-start | bytes 393224 | tf_op jit(solution)/shard_map/ppermute | solution.py:137
  30.8 1.0 %copy-start = (bf16[32,5120]{1,0:T(8,128)(2,1)S(1)}, bf16[32,5120]{1,0:T(8,128)(2,1)}, u32[]{:S(2)}) copy-start(bf16[32,5120]{1,0:T(8,128)(2,1)} %refs_1_.5) | copy-start | bytes 983044
  30.8 1.1 %copy-start.1 = (bf16[1,32,5120]{2,1,0:T(8,128)(2,1)S(1)}, bf16[1,32,5120]{2,1,0:T(8,128)(2,1)}, u32[]{:S(2)}) copy-start(bf16[1,32,5120]{2,1,0:T(8,128)(2,1)} %param.9) | copy-start | bytes 983044
  30.9 6.3 %collective-permute-start.12 = (bf16[32,2048]{1,0:T(8,128)(2,1)S(1)}, bf16[32,2048]{1,0:T(8,128)(2,1)S(1)}, u32[]{:S(2)}, u32[]{:S(2)}) collective-permute-start(bf16[32,2048]{1,0:T(8,128)(2,1)S(1)} %get-tuple-element.52), channel_id=1, source_target_pairs={{0,8},{4,12},{8,16},{12,20},{16,24},{20,28},{24,0},{28,4},{1,9},{5... | collective-permute-start | bytes 393224 | tf_op jit(solution)/shard_map/ppermute | solution.py:153
  31.0 7.8 %collective-permute-start.14 = (bf16[96,2048]{1,0:T(8,128)(2,1)S(1)}, bf16[96,2048]{1,0:T(8,128)(2,1)S(1)}, u32[]{:S(2)}, u32[]{:S(2)}) collective-permute-start(bf16[96,2048]{1,0:T(8,128)(2,1)S(1)} %constant_dynamic-update-slice_fusion.7.refs_3_), channel_id=1, source_target_pairs={{0,1},{1,0},{2,3},{3,2},{4,5},{5,4},{6,7},{7,6},{8,9},{9,8},{10,11... | collective-permute-start | bytes 1179656 | tf_op jit(solution)/shard_map/ppermute | solution.py:137
  37.2 2.9 %collective-permute-start.15 = (bf16[96,2048]{1,0:T(8,128)(2,1)S(1)}, bf16[96,2048]{1,0:T(8,128)(2,1)S(1)}, u32[]{:S(2)}, u32[]{:S(2)}) collective-permute-start(bf16[96,2048]{1,0:T(8,128)(2,1)S(1)} %constant_dynamic-update-slice_fusion.11.refs_4_), channel_id=1, source_target_pairs={{0,1},{1,0},{2,3},{3,2},{4,5},{5,4},{6,7},{7,6},{8,9},{9,8},{10,11... | collective-permute-start | bytes 1179656 | tf_op jit(solution)/shard_map/ppermute | solution.py:137

commit v7 on v5

--- a/solution.py
+++ b/solution.py
@@ -26,7 +26,7 @@
     return lax.dot_general(a, b, (((1,), (0,)), ((), ())), preferred_element_type=jnp.float32)
 
 
-def attend_kernel(slots, tp_size, first_call, last_call, *refs):
+def attend_kernel(slots, ranges, tp_size, first_call, last_call, *refs):
     refs = list(refs)
     spans, tq, sq = refs[:3]
     del refs[:3]
@@ -60,14 +60,20 @@
         else:
             hidden = (lane < rows) | ((lane > rows) & (position > tp * rows + (lane - rows - 1)))
         k_aug_ref[index * rows:(index + 1) * rows, :] = jnp.where(hidden, MASKED, 0.0).astype(jnp.bfloat16)
-    total = rows * len(slots)
+    filled, total = rows * len(slots), k_aug_ref.shape[0]
+    if filled < total:
+        k_aug_ref[filled:total, :] = jnp.full((total - filled, HEAD_SIZE), MASKED, jnp.bfloat16)
+        padding = [jnp.zeros((total - filled, HEAD_SIZE), jnp.bfloat16)]
+    else:
+        padding = []
     ones = jnp.ones((total, HEAD_SIZE), jnp.bfloat16)
 
     def columns(index):
         return slice(index * HEAD_SIZE, (index + 1) * HEAD_SIZE)
 
     def stacked(index):
-        return jnp.concatenate([piece[:, columns(index)] for piece in pieces], axis=0)
+        parts = [piece[start:stop, columns(index)] for piece, (start, stop) in zip(pieces, ranges)]
+        return jnp.concatenate(parts + padding, axis=0)
 
     def scores_of(g):
         query = jnp.concatenate(
@@ -110,7 +116,7 @@
     first_call = carry is None
     rows = tq.shape[0]
     vmem = pl.BlockSpec(memory_space=pltpu.VMEM)
-    operands = [spans, tq, sq, *pieces]
+    operands = [spans, tq, sq, *(piece for piece, _, _ in pieces)]
     if not first_call:
         operands += list(carry)
     if last_call:
@@ -118,10 +124,11 @@
     else:
         state = (KEY_VALUE_HEADS, 2 * GROUP * rows, HEAD_SIZE)
         out_shape = [jax.ShapeDtypeStruct(state, jnp.float32)] * 3
-    all_rows = sum(p.shape[0] for p in pieces)
+    ranges = tuple((first * rows, last * rows) for _, first, last in pieces)
+    all_rows = pl.cdiv(sum(stop - start for start, stop in ranges), HEAD_SIZE) * HEAD_SIZE
     flops = 2 * 2 * QUERY_HEADS * rows * all_rows * PAIR * 2
     return pl.pallas_call(
-        functools.partial(attend_kernel, slots, tp_size, first_call, last_call),
+        functools.partial(attend_kernel, slots, ranges, tp_size, first_call, last_call),
         out_shape=out_shape,
         in_specs=[vmem] * len(operands),
         out_specs=[vmem] * len(out_shape),
@@ -169,12 +176,11 @@
             (((ctx + ctx_size - 2 * shift) % ctx_size) ^ x) * tp_size + (tp ^ (2 * y + c)),
         )
 
+    def slots_of(places, c=0):
+        return [slot(place, c) for place in places]
+
     def absorb(pieces, slots, state, last_call=False):
         return attend(spans, trace_q, sq, pieces, slots, tp_size, state, last_call)
-
-    def absorb_both(mine, sibling, places, state, last_call=False):
-        slots = [slot(place, c) for c in (0, 1) for place in places]
-        return absorb(mine + sibling, slots, state, last_call)
 
     if ctx_size == 8 and tp_size == 4:
         barrier = lax.optimization_barrier
@@ -183,43 +189,48 @@
         own_d = across_both(trace_key_value)
         up, down, own_x, own_y, own_d, spans = barrier((up, down, own_x, own_y, own_d, spans))
 
-        near_x = across_x(jnp.concatenate([up, down], axis=0))
-        near_y = across_y(jnp.concatenate([up, down, suffix_own], axis=0))
-        up_two = along_z(jnp.concatenate([up, own_d], axis=0), 1)
-        down_d = along_z(own_d, 3)
+        near = jnp.concatenate([up, down], axis=0)
+        up_two, down_d = along_z(jnp.concatenate([up, own_d], axis=0), 1), along_z(own_d, 3)
+        near_x, near_y = across_x(near), across_y(near)
         plane = jnp.concatenate([trace_key_value, own_x, own_y, own_d, up, down, suffix_own], axis=0)
-        plane_core = core(plane)
-        cut = 6 * rows
         here = [(0, 0, 0), (0, 1, 0), (0, 0, 1), (0, 1, 1), (1, 0, 0), (3, 0, 0)]
-        state = absorb_both([plane[:cut]], [plane_core[:cut]], here, None)
-
-        near_x, near_y, state = barrier((near_x, near_y, state))
-        sides = jnp.concatenate([near_x, near_y], axis=0)
-        sides_core = core(sides)
+        state = absorb([(plane, 0, 7)], slots_of(here + [0]), None)
+
+        near_x, near_y, up_two, down_d, state = barrier((near_x, near_y, up_two, down_d, state))
         far, up_d = up_two[:rows], up_two[rows:]
-        far_x, far_y, far_d = across_x(far), across_y(far), along_z(up_d, 1)
-        mixed = jnp.concatenate([up_two, down_d], axis=0)
-        mixed_core = core(mixed)
-        here = [0, (1, 1, 0), (3, 1, 0), (1, 0, 1), (3, 0, 1), 2]
-        state = absorb_both([plane[cut:], sides], [plane_core[cut:], sides_core], here, state)
+        far_y = across_y(jnp.concatenate([far, suffix_own], axis=0))
+        far_x, far_d = across_x(far), along_z(up_d, 1)
+        sides = jnp.concatenate([plane, near_x, near_y, up_d, down_d, far], axis=0)
+        sibling = core(sides)
+        near_here = [(1, 1, 0), (3, 1, 0), (1, 0, 1), (3, 0, 1), (1, 1, 1), (3, 1, 1)]
+        state = absorb([(sides, 7, 13), (sibling, 0, 6)], slots_of(near_here) + slots_of(here, 1), state)
 
         far_x, far_y, far_d, state = barrier((far_x, far_y, far_d, state))
         rest = jnp.concatenate([far_x, far_y, far_d], axis=0)
-        here = [(2, 0, 0), (1, 1, 1), (3, 1, 1), (2, 1, 0), (2, 0, 1), (2, 1, 1)]
-        trace_out, suffix_out = absorb_both([mixed, rest], [mixed_core, core(rest)], here, state, True)
+        rest_sibling = core(rest)
+        state = absorb(
+            [(sides, 13, 14), (sibling, 7, 14)], slots_of([(2, 0, 0)]) + slots_of(near_here + [(2, 0, 0)], 1), state
+        )
+        here = [(2, 1, 0), (2, 0, 1), 2, (2, 1, 1)]
+        trace_out, suffix_out = absorb(
+            [(rest, 0, 4), (rest_sibling, 0, 4), (sibling, 6, 7)],
+            slots_of(here) + slots_of(here + [0], 1),
+            state,
+            True,
+        )
     else:
         gathered = lax.all_gather(trace_key_value, ("ctx", "tp"), axis=0, tiled=True)
         suffix_all = lax.all_gather(suffix_own, "tp", axis=0, tiled=True)
         state = None
         for at in range(0, gathered.shape[0], CHUNK_ROWS):
             last_call = at + CHUNK_ROWS >= gathered.shape[0]
-            pieces = [gathered[at:at + CHUNK_ROWS]]
+            pieces = [(gathered[at:at + CHUNK_ROWS], 0, min(CHUNK_ROWS, gathered.shape[0] - at) // rows)]
             slots = [
                 lambda ctx, tp, block=block: ("trace", block)
                 for block in range(at // rows, min(at + CHUNK_ROWS, gathered.shape[0]) // rows)
             ]
             if at == 0:
-                pieces.append(suffix_all)
+                pieces.append((suffix_all, 0, tp_size))
                 slots += [lambda ctx, tp, block=block: ("suffix", block) for block in range(tp_size)]
             state = absorb(pieces, slots, state, last_call)
         trace_out, suffix_out = state

time: 43.4 us -> 42.1 us (0.970)
  starting transfers between devices: 21.7 us -> 15.3 us
  waiting for transfers between devices: 9.81 us -> 14.4 us
  Pallas kernels: 7.04 us -> 7.7 us
    ppermute x5, waiting for transfers between devices: 0.11 us -> 8.79 us  [local(): lax.ppermute(a, 'ctx', [(i, (i + 2 * shift) % ctx_size) for i in range(ct...]
    ppermute x10 -> x8, starting transfers between devices: 14.4 us -> 9.25 us  [swap(): return lax.ppermute(array, axis, [(i, i ^ bit) for i in range(size)])]
    ppermute x10 -> x8, waiting for transfers between devices: 7.41 us -> 3.33 us  [swap(): return lax.ppermute(array, axis, [(i, i ^ bit) for i in range(size)])]
    ppermute x5, starting transfers between devices: 7.15 us -> 5.89 us  [local(): lax.ppermute(a, 'ctx', [(i, (i + 2 * shift) % ctx_size) for i in range(ct...]
    pallas_call x3 -> x4, Pallas kernels: 7.04 us -> 7.7 us  [attend(): pl.pallas_call(functools.partial(attend_kernel, slots, ranges, tp_size, f...]
    unnamed x16 -> x19, local copies, waits for them, and re-layouts: 1.13 us -> 1.19 us
  transfers between devices with their start and end apart: 16 -> 14, of which waited for: 5 -> 9; matrix products, arithmetic and copies ran while one was open for 3% -> 3% of each run, Pallas kernels for 9% -> 12%
where the time goes in v7:
time: 42.1 us; the launch traced here: 41.6 us
  starting transfers between devices  15.3 us (36%)
  waiting for transfers between devices  14.4 us (34%)
  Pallas kernels  7.7 us (18%)
  between operations  2.75 us (7%)
  local copies, waits for them, and re-layouts  1.3 us (3%)
    ppermute x8, starting transfers between devices, swap(): return lax.ppermute(array, axis, [(i, i ^ bit) for i in range(size)])  9.25 us
    ppermute x5, waiting for transfers between devices, local(): lax.ppermute(a, 'ctx', [(i, (i + 2 * shift) % ctx_size) for i in range(ct...  8.79 us
    pallas_call x4, Pallas kernels, attend(): pl.pallas_call(functools.partial(attend_kernel, slots, ranges, tp_size, f...  7.7 us
    ppermute x5, starting transfers between devices, local(): lax.ppermute(a, 'ctx', [(i, (i + 2 * shift) % ctx_size) for i in range(ct...  5.89 us
    ppermute x8, waiting for transfers between devices, swap(): return lax.ppermute(array, axis, [(i, i ^ bit) for i in range(size)])  3.33 us
    ppermute x1, waiting for transfers between devices, local(): lax.ppermute(a, ('ctx', 'tp'), [(i * tp_size + j, (i ^ 1) * tp_size + (j...  2.29 us
    unnamed x19, local copies, waits for them, and re-layouts  1.19 us
  transfers between devices with their start and end apart: 14, of which 9 were waited for; matrix products, arithmetic and copies ran while one was open for 3% of the time, Pallas kernels for 12%

profile of v7, /device:TPU:1, one launch (start us, length us, event | category | flops | bytes accessed | tf_op | source)
XLA Modules:
  0.0 41.6 jit_solution(9785841655687230746)
XLA Ops:
  0.7 2.2 %collective-permute-start = (bf16[32,2048]{1,0:T(8,128)(2,1)}, bf16[32,2048]{1,0:T(8,128)(2,1)S(1)}, u32[]{:S(2)}, u32[]{:S(2)}) collective-permute-start(bf16[32,2048]{1,0:T(8,128)(2,1)} %param.8), channel_id=1, source_target_pairs={{0,8},{4,12},{8,16},{12,20},{16,24},{20,28},{24,0},{28,4},{1,9},{5... | collective-permute-start | bytes 393224 | tf_op jit(solution)/shard_map/ppermute | solution.py:160
  2.8 2.1 %collective-permute-start.1 = (bf16[32,2048]{1,0:T(8,128)(2,1)}, bf16[32,2048]{1,0:T(8,128)(2,1)S(1)}, u32[]{:S(2)}, u32[]{:S(2)}) collective-permute-start(bf16[32,2048]{1,0:T(8,128)(2,1)} %param.8), channel_id=1, source_target_pairs={{0,24},{4,28},{8,0},{12,4},{16,8},{20,12},{24,16},{28,20},{1,25},{... | collective-permute-start | bytes 393224 | tf_op jit(solution)/shard_map/ppermute | solution.py:160
  4.9 1.2 %collective-permute-start.2 = (bf16[32,2048]{1,0:T(8,128)(2,1)}, bf16[32,2048]{1,0:T(8,128)(2,1)S(1)}, u32[]{:S(2)}, u32[]{:S(2)}) collective-permute-start(bf16[32,2048]{1,0:T(8,128)(2,1)} %param.8), channel_id=1, source_target_pairs={{0,4},{4,0},{8,12},{12,8},{16,20},{20,16},{24,28},{28,24},{1,5},{5... | collective-permute-start | bytes 393224 | tf_op jit(solution)/shard_map/ppermute | solution.py:144
  6.1 1.2 %collective-permute-start.3 = (bf16[32,2048]{1,0:T(8,128)(2,1)}, bf16[32,2048]{1,0:T(8,128)(2,1)S(1)}, u32[]{:S(2)}, u32[]{:S(2)}) collective-permute-start(bf16[32,2048]{1,0:T(8,128)(2,1)} %param.8), channel_id=1, source_target_pairs={{0,2},{1,3},{2,0},{3,1},{4,6},{5,7},{6,4},{7,5},{8,10},{9,11},{10,... | collective-permute-start | bytes 393224 | tf_op jit(solution)/shard_map/ppermute | solution.py:144
  7.6 1.0 %constant_dynamic-update-slice_fusion.20 = (bf16[448,2048]{1,0:T(8,128)(2,1)S(1)}, bf16[224,2048]{1,0:T(8,128)(2,1)S(1)}) fusion(bf16[32,2048]{1,0:T(8,128)(2,1)} %param.8), kind=kLoop, calls=%fused_computation.22 | loop fusion | bytes 393216
  10.7 2.3 %collective-permute-done.4 = bf16[32,2048]{1,0:T(8,128)(2,1)S(1)} collective-permute-done((bf16[32,2048]{1,0:T(8,128)(2,1)}, bf16[32,2048]{1,0:T(8,128)(2,1)S(1)}, u32[]{:S(2)}, u32[]{:S(2)}) %collective-permute-start.4) | collective-permute-done | bytes 131104 | tf_op jit(solution)/shard_map/ppermute | solution.py:164
  13.2 0.9 %collective-permute-start.5 = (bf16[64,2048]{1,0:T(8,128)(2,1)S(1)}, bf16[64,2048]{1,0:T(8,128)(2,1)S(1)}, u32[]{:S(2)}, u32[]{:S(2)}) collective-permute-start(bf16[64,2048]{1,0:T(8,128)(2,1)S(1)} %get-tuple-element.69), channel_id=1, source_target_pairs={{0,4},{4,0},{8,12},{12,8},{16,20},{20,16},{24,28},{28,24},{1,5},{5... | collective-permute-start | bytes 786440 | tf_op jit(solution)/shard_map/ppermute | solution.py:144
  14.1 0.2 collective-permute-start.6
  14.4 1.6 %collective-permute-start.8 = (bf16[32,2048]{1,0:T(8,128)(2,1)S(1)}, bf16[32,2048]{1,0:T(8,128)(2,1)S(1)}, u32[]{:S(2)}, u32[]{:S(2)}) collective-permute-start(bf16[32,2048]{1,0:T(8,128)(2,1)S(1)} %collective-permute-done.4), channel_id=1, source_target_pairs={{0,24},{4,28},{8,0},{12,4},{16,8},{20,12},{24,16},{28,20},{1,25},{... | collective-permute-start | bytes 393224 | tf_op jit(solution)/shard_map/ppermute | solution.py:160
  16.0 1.1 %shard_map.86 = (f32[8,320,128]{2,1,0:T(8,128)S(1)}, f32[8,320,128]{2,1,0:T(8,128)S(1)}, f32[8,320,128]{2,1,0:T(8,128)S(1)}) custom-call(s32[3,128]{1,0:T(4,128)S(1)} %broadcast_in_dim.11.refs_0_, bf16[32,5120]{1,0:T(8,128)(2,1)S(1)} %copy-done, bf16[32,5120]{1,0:T(8,128)(2,1)S(1)} %bitcast.13, bf16[224,2048]{1,0:T(8,128)(2,1)S(1)} %get-tuple-element.66.refs_3_), custom_call_target="tpu_custom_call" | custom-call | flops 671088640 | bytes 1048576 | tf_op jit(solution)/shard_map/pallas_call | solution.py:130
  17.2 1.1 %collective-permute-done.8 = bf16[32,2048]{1,0:T(8,128)(2,1)S(1)} collective-permute-done((bf16[32,2048]{1,0:T(8,128)(2,1)S(1)}, bf16[32,2048]{1,0:T(8,128)(2,1)S(1)}, u32[]{:S(2)}, u32[]{:S(2)}) %collective-permute-start.8) | collective-permute-done | bytes 131104 | tf_op jit(solution)/shard_map/ppermute | solution.py:160
  18.2 0.2 collective-permute-done.5
  18.5 1.2 %collective-permute-done.6 = bf16[64,2048]{1,0:T(8,128)(2,1)S(1)} collective-permute-done((bf16[64,2048]{1,0:T(8,128)(2,1)S(1)}, bf16[64,2048]{1,0:T(8,128)(2,1)S(1)}, u32[]{:S(2)}, u32[]{:S(2)}) %collective-permute-start.6) | collective-permute-done | bytes 262176 | tf_op jit(solution)/shard_map/ppermute | solution.py:144
  19.6 5.5 %collective-permute-done.7 = bf16[64,2048]{1,0:T(8,128)(2,1)S(1)} collective-permute-done((bf16[64,2048]{1,0:T(8,128)(2,1)S(1)}, bf16[64,2048]{1,0:T(8,128)(2,1)S(1)}, u32[]{:S(2)}, u32[]{:S(2)}) %collective-permute-start.7) | collective-permute-done | bytes 262176 | tf_op jit(solution)/shard_map/ppermute | solution.py:160
  25.3 2.9 %collective-permute-start.12 = (bf16[448,2048]{1,0:T(8,128)(2,1)S(1)}, bf16[448,2048]{1,0:T(8,128)(2,1)S(1)}, u32[]{:S(2)}, u32[]{:S(2)}) collective-permute-start(bf16[448,2048]{1,0:T(8,128)(2,1)S(1)} %get-tuple-element.62.refs_3_), channel_id=1, source_target_pairs={{0,1},{1,0},{2,3},{3,2},{4,5},{5,4},{6,7},{7,6},{8,9},{9,8},{10,11... | collective-permute-start | bytes 5505032 | tf_op jit(solution)/shard_map/ppermute | solution.py:144
  28.2 1.0 %collective-permute-start.10 = (bf16[64,2048]{1,0:T(8,128)(2,1)S(1)}, bf16[64,2048]{1,0:T(8,128)(2,1)S(1)}, u32[]{:S(2)}, u32[]{:S(2)}) collective-permute-start(bf16[64,2048]{1,0:T(8,128)(2,1)S(1)} %pad_maximum_fusion.1), channel_id=1, source_target_pairs={{0,2},{1,3},{2,0},{3,1},{4,6},{5,7},{6,4},{7,5},{8,10},{9,11},{10,... | collective-permute-start | bytes 786440 | tf_op jit(solution)/shard_map/ppermute | solution.py:144
  29.3 0.8 %collective-permute-start.9 = (bf16[32,2048]{1,0:T(8,128)(2,1)S(1)}, bf16[32,2048]{1,0:T(8,128)(2,1)S(1)}, u32[]{:S(2)}, u32[]{:S(2)}) collective-permute-start(bf16[32,2048]{1,0:T(8,128)(2,1)S(1)} %get-tuple-element.64), channel_id=1, source_target_pairs={{0,4},{4,0},{8,12},{12,8},{16,20},{20,16},{24,28},{28,24},{1,5},{5... | collective-permute-start | bytes 393224 | tf_op jit(solution)/shard_map/ppermute | solution.py:144
  30.1 1.5 %collective-permute-done.12.refs_4_.refs_5_ = bf16[448,2048]{1,0:T(8,128)(2,1)S(1)} collective-permute-done((bf16[448,2048]{1,0:T(8,128)(2,1)S(1)}, bf16[448,2048]{1,0:T(8,128)(2,1)S(1)}, u32[]{:S(2)}, u32[]{:S(2)}) %collective-permute-start.12) | collective-permute-done | bytes 1835040 | tf_op jit(solution)/shard_map/ppermute | solution.py:144
  31.6 2.1 %shard_map.87 = (f32[8,320,128]{2,1,0:T(8,128)S(1)}, f32[8,320,128]{2,1,0:T(8,128)S(1)}, f32[8,320,128]{2,1,0:T(8,128)S(1)}) custom-call(s32[3,128]{1,0:T(4,128)S(1)} %broadcast_in_dim.11.refs_0_, bf16[32,5120]{1,0:T(8,128)(2,1)S(1)} %copy-done, bf16[32,5120]{1,0:T(8,128)(2,1)S(1)} %bitcast.14, bf16[448,2048]{1,0:T(8,128)(2,1)S(1)} %get-tuple-element.62.refs_3_, ...), custom_call_target="tpu_custom_call" | custom-call | flops 1006632960 | bytes 1572864 | tf_op jit(solution)/shard_map/pallas_call | solution.py:130
  33.8 2.1 %collective-permute-done.11 = bf16[32,2048]{1,0:T(8,128)(2,1)S(1)} collective-permute-done((bf16[32,2048]{1,0:T(8,128)(2,1)S(1)}, bf16[32,2048]{1,0:T(8,128)(2,1)S(1)}, u32[]{:S(2)}, u32[]{:S(2)}) %collective-permute-start.11) | collective-permute-done | bytes 131104 | tf_op jit(solution)/shard_map/ppermute | solution.py:160
  35.9 0.4 collective-permute-done.10
  36.3 0.9 %collective-permute-start.13 = (bf16[128,2048]{1,0:T(8,128)(2,1)S(1)}, bf16[128,2048]{1,0:T(8,128)(2,1)S(1)}, u32[]{:S(2)}, u32[]{:S(2)}) collective-permute-start(bf16[128,2048]{1,0:T(8,128)(2,1)S(1)} %constant_dynamic-update-slice_fusion.21.refs_3_), channel_id=1, source_target_pairs={{0,1},{1,0},{2,3},{3,2},{4,5},{5,4},{6,7},{7,6},{8,9},{9,8},{10,11... | collective-permute-start | bytes 1572872 | tf_op jit(solution)/shard_map/ppermute | solution.py:144
  37.2 1.5 %shard_map.88 = (f32[8,320,128]{2,1,0:T(8,128)S(1)}, f32[8,320,128]{2,1,0:T(8,128)S(1)}, f32[8,320,128]{2,1,0:T(8,128)S(1)}) custom-call(s32[3,128]{1,0:T(4,128)S(1)} %broadcast_in_dim.11.refs_0_, bf16[32,5120]{1,0:T(8,128)(2,1)S(1)} %copy-done, bf16[32,5120]{1,0:T(8,128)(2,1)S(1)} %bitcast.15, bf16[448,2048]{1,0:T(8,128)(2,1)S(1)} %get-tuple-element.62.refs_3_, ...), custom_call_target="tpu_custom_call" | custom-call | flops 671088640 | bytes 1048576 | tf_op jit(solution)/shard_map/pallas_call | solution.py:130
  38.7 2.9 %shard_map.89 = (bf16[32,5120]{1,0:T(8,128)(2,1)}, bf16[32,5120]{1,0:T(8,128)(2,1)}) custom-call(s32[3,128]{1,0:T(4,128)S(1)} %broadcast_in_dim.11.refs_0_, bf16[32,5120]{1,0:T(8,128)(2,1)S(1)} %copy-done, bf16[32,5120]{1,0:T(8,128)(2,1)S(1)} %bitcast.16, bf16[128,2048]{1,0:T(8,128)(2,1)S(1)} %constant_dynamic-update-slice_fusion.21.refs_3_, ...), custom_call_target="tpu_custom_call" | custom-call | flops 1006632960 | bytes 1572864 | tf_op jit(solution)/shard_map/pallas_call | solution.py:130
  (33 shorter events, 0.8 us)
Async XLA Ops:
  0.6 15.4 %copy-start.2 = (bf16[1,32,2048]{2,1,0:T(8,128)(2,1)S(1)}, bf16[1,32,2048]{2,1,0:T(8,128)(2,1)}, u32[]{:S(2)}) copy-start(bf16[1,32,2048]{2,1,0:T(8,128)(2,1)} %param.10) | copy-start | bytes 393220
  0.6 15.4 %copy-start.1 = (bf16[1,32,5120]{2,1,0:T(8,128)(2,1)S(1)}, bf16[1,32,5120]{2,1,0:T(8,128)(2,1)}, u32[]{:S(2)}) copy-start(bf16[1,32,5120]{2,1,0:T(8,128)(2,1)} %param.9) | copy-start | bytes 983044
  0.7 15.4 %copy-start = (bf16[32,5120]{1,0:T(8,128)(2,1)S(1)}, bf16[32,5120]{1,0:T(8,128)(2,1)}, u32[]{:S(2)}) copy-start(bf16[32,5120]{1,0:T(8,128)(2,1)} %refs_1_.7) | copy-start | bytes 983044
  0.7 9.9 %collective-permute-start = (bf16[32,2048]{1,0:T(8,128)(2,1)}, bf16[32,2048]{1,0:T(8,128)(2,1)S(1)}, u32[]{:S(2)}, u32[]{:S(2)}) collective-permute-start(bf16[32,2048]{1,0:T(8,128)(2,1)} %param.8), channel_id=1, source_target_pairs={{0,8},{4,12},{8,16},{12,20},{16,24},{20,28},{24,0},{28,4},{1,9},{5... | collective-permute-start | bytes 393224 | tf_op jit(solution)/shard_map/ppermute | solution.py:160
  2.8 7.8 %collective-permute-start.1 = (bf16[32,2048]{1,0:T(8,128)(2,1)}, bf16[32,2048]{1,0:T(8,128)(2,1)S(1)}, u32[]{:S(2)}, u32[]{:S(2)}) collective-permute-start(bf16[32,2048]{1,0:T(8,128)(2,1)} %param.8), channel_id=1, source_target_pairs={{0,24},{4,28},{8,0},{12,4},{16,8},{20,12},{24,16},{28,20},{1,25},{... | collective-permute-start | bytes 393224 | tf_op jit(solution)/shard_map/ppermute | solution.py:160
  4.9 5.7 %collective-permute-start.2 = (bf16[32,2048]{1,0:T(8,128)(2,1)}, bf16[32,2048]{1,0:T(8,128)(2,1)S(1)}, u32[]{:S(2)}, u32[]{:S(2)}) collective-permute-start(bf16[32,2048]{1,0:T(8,128)(2,1)} %param.8), channel_id=1, source_target_pairs={{0,4},{4,0},{8,12},{12,8},{16,20},{20,16},{24,28},{28,24},{1,5},{5... | collective-permute-start | bytes 393224 | tf_op jit(solution)/shard_map/ppermute | solution.py:144
  6.1 4.5 %collective-permute-start.3 = (bf16[32,2048]{1,0:T(8,128)(2,1)}, bf16[32,2048]{1,0:T(8,128)(2,1)S(1)}, u32[]{:S(2)}, u32[]{:S(2)}) collective-permute-start(bf16[32,2048]{1,0:T(8,128)(2,1)} %param.8), channel_id=1, source_target_pairs={{0,2},{1,3},{2,0},{3,1},{4,6},{5,7},{6,4},{7,5},{8,10},{9,11},{10,... | collective-permute-start | bytes 393224 | tf_op jit(solution)/shard_map/ppermute | solution.py:144
  7.4 5.6 %collective-permute-start.4 = (bf16[32,2048]{1,0:T(8,128)(2,1)}, bf16[32,2048]{1,0:T(8,128)(2,1)S(1)}, u32[]{:S(2)}, u32[]{:S(2)}) collective-permute-start(bf16[32,2048]{1,0:T(8,128)(2,1)} %param.8), channel_id=1, source_target_pairs={{0,6},{1,7},{2,4},{3,5},{4,2},{5,3},{6,0},{7,1},{8,14},{9,15},{10,... | collective-permute-start | bytes 393224 | tf_op jit(solution)/shard_map/ppermute | solution.py:164
  13.2 5.3 %collective-permute-start.5 = (bf16[64,2048]{1,0:T(8,128)(2,1)S(1)}, bf16[64,2048]{1,0:T(8,128)(2,1)S(1)}, u32[]{:S(2)}, u32[]{:S(2)}) collective-permute-start(bf16[64,2048]{1,0:T(8,128)(2,1)S(1)} %get-tuple-element.69), channel_id=1, source_target_pairs={{0,4},{4,0},{8,12},{12,8},{16,20},{20,16},{24,28},{28,24},{1,5},{5... | collective-permute-start | bytes 786440 | tf_op jit(solution)/shard_map/ppermute | solution.py:144
  14.1 5.5 %collective-permute-start.6 = (bf16[64,2048]{1,0:T(8,128)(2,1)S(1)}, bf16[64,2048]{1,0:T(8,128)(2,1)S(1)}, u32[]{:S(2)}, u32[]{:S(2)}) collective-permute-start(bf16[64,2048]{1,0:T(8,128)(2,1)S(1)} %get-tuple-element.69), channel_id=1, source_target_pairs={{0,2},{1,3},{2,0},{3,1},{4,6},{5,7},{6,4},{7,5},{8,10},{9,11},{10,... | collective-permute-start | bytes 786440 | tf_op jit(solution)/shard_map/ppermute | solution.py:144
  14.4 3.9 %collective-permute-start.8 = (bf16[32,2048]{1,0:T(8,128)(2,1)S(1)}, bf16[32,2048]{1,0:T(8,128)(2,1)S(1)}, u32[]{:S(2)}, u32[]{:S(2)}) collective-permute-start(bf16[32,2048]{1,0:T(8,128)(2,1)S(1)} %collective-permute-done.4), channel_id=1, source_target_pairs={{0,24},{4,28},{8,0},{12,4},{16,8},{20,12},{24,16},{28,20},{1,25},{... | collective-permute-start | bytes 393224 | tf_op jit(solution)/shard_map/ppermute | solution.py:160
  16.0 9.2 %collective-permute-start.7 = (bf16[64,2048]{1,0:T(8,128)(2,1)S(1)}, bf16[64,2048]{1,0:T(8,128)(2,1)S(1)}, u32[]{:S(2)}, u32[]{:S(2)}) collective-permute-start(bf16[64,2048]{1,0:T(8,128)(2,1)S(1)} %pad_maximum_fusion), channel_id=1, source_target_pairs={{0,8},{4,12},{8,16},{12,20},{16,24},{20,28},{24,0},{28,4},{1,9},{5... | collective-permute-start | bytes 786440 | tf_op jit(solution)/shard_map/ppermute | solution.py:160
  25.3 6.3 %collective-permute-start.12 = (bf16[448,2048]{1,0:T(8,128)(2,1)S(1)}, bf16[448,2048]{1,0:T(8,128)(2,1)S(1)}, u32[]{:S(2)}, u32[]{:S(2)}) collective-permute-start(bf16[448,2048]{1,0:T(8,128)(2,1)S(1)} %get-tuple-element.62.refs_3_), channel_id=1, source_target_pairs={{0,1},{1,0},{2,3},{3,2},{4,5},{5,4},{6,7},{7,6},{8,9},{9,8},{10,11... | collective-permute-start | bytes 5505032 | tf_op jit(solution)/shard_map/ppermute | solution.py:144
  28.2 8.0 %collective-permute-start.10 = (bf16[64,2048]{1,0:T(8,128)(2,1)S(1)}, bf16[64,2048]{1,0:T(8,128)(2,1)S(1)}, u32[]{:S(2)}, u32[]{:S(2)}) collective-permute-start(bf16[64,2048]{1,0:T(8,128)(2,1)S(1)} %pad_maximum_fusion.1), channel_id=1, source_target_pairs={{0,2},{1,3},{2,0},{3,1},{4,6},{5,7},{6,4},{7,5},{8,10},{9,11},{10,... | collective-permute-start | bytes 786440 | tf_op jit(solution)/shard_map/ppermute | solution.py:144
  29.3 6.6 %collective-permute-start.11 = (bf16[32,2048]{1,0:T(8,128)(2,1)S(1)}, bf16[32,2048]{1,0:T(8,128)(2,1)S(1)}, u32[]{:S(2)}, u32[]{:S(2)}) collective-permute-start(bf16[32,2048]{1,0:T(8,128)(2,1)S(1)} %get-tuple-element.63), channel_id=1, source_target_pairs={{0,8},{4,12},{8,16},{12,20},{16,24},{20,28},{24,0},{28,4},{1,9},{5... | collective-permute-start | bytes 393224 | tf_op jit(solution)/shard_map/ppermute | solution.py:160
  29.3 6.6 %collective-permute-start.9 = (bf16[32,2048]{1,0:T(8,128)(2,1)S(1)}, bf16[32,2048]{1,0:T(8,128)(2,1)S(1)}, u32[]{:S(2)}, u32[]{:S(2)}) collective-permute-start(bf16[32,2048]{1,0:T(8,128)(2,1)S(1)} %get-tuple-element.64), channel_id=1, source_target_pairs={{0,4},{4,0},{8,12},{12,8},{16,20},{20,16},{24,28},{28,24},{1,5},{5... | collective-permute-start | bytes 393224 | tf_op jit(solution)/shard_map/ppermute | solution.py:144
  36.3 2.4 %collective-permute-start.13 = (bf16[128,2048]{1,0:T(8,128)(2,1)S(1)}, bf16[128,2048]{1,0:T(8,128)(2,1)S(1)}, u32[]{:S(2)}, u32[]{:S(2)}) collective-permute-start(bf16[128,2048]{1,0:T(8,128)(2,1)S(1)} %constant_dynamic-update-slice_fusion.21.refs_3_), channel_id=1, source_target_pairs={{0,1},{1,0},{2,3},{3,2},{4,5},{5,4},{6,7},{7,6},{8,9},{9,8},{10,11... | collective-permute-start | bytes 1572872 | tf_op jit(solution)/shard_map/ppermute | solution.py:144

commit v8 on v7

--- a/solution.py
+++ b/solution.py
@@ -157,9 +157,7 @@
     core = lambda a: swap(a, "tp", 1, tp_size)
     across_y = lambda a: swap(a, "tp", 2, tp_size)
     across_x = lambda a: swap(a, "ctx", 1, ctx_size)
-    along_z = lambda a, shift: lax.ppermute(
-        a, "ctx", [(i, (i + 2 * shift) % ctx_size) for i in range(ctx_size)]
-    )
+    along_z = lambda a, flip: swap(a, "ctx", 2 * flip, ctx_size)
 
     across_both = lambda a: lax.ppermute(
         a,
@@ -170,10 +168,10 @@
     def slot(place, c):
         if isinstance(place, int):
             return lambda ctx, tp: ("suffix", tp ^ place ^ c)
-        shift, x, y = place
+        z, x, y = place
         return lambda ctx, tp: (
             "trace",
-            (((ctx + ctx_size - 2 * shift) % ctx_size) ^ x) * tp_size + (tp ^ (2 * y + c)),
+            (ctx ^ (2 * z + x)) * tp_size + (tp ^ (2 * y + c)),
         )
 
     def slots_of(places, c=0):
@@ -184,39 +182,34 @@
 
     if ctx_size == 8 and tp_size == 4:
         barrier = lax.optimization_barrier
-        up, down = along_z(trace_key_value, 1), along_z(trace_key_value, 3)
+        next_z, third_z = along_z(trace_key_value, 1), along_z(trace_key_value, 3)
         own_x, own_y = across_x(trace_key_value), across_y(trace_key_value)
         own_d = across_both(trace_key_value)
-        up, down, own_x, own_y, own_d, spans = barrier((up, down, own_x, own_y, own_d, spans))
-
-        near = jnp.concatenate([up, down], axis=0)
-        up_two, down_d = along_z(jnp.concatenate([up, own_d], axis=0), 1), along_z(own_d, 3)
+        next_z, third_z, own_x, own_y, own_d, spans = barrier((next_z, third_z, own_x, own_y, own_d, spans))
+
+        near = jnp.concatenate([next_z, third_z], axis=0)
+        far_and_next_d, third_d = along_z(jnp.concatenate([third_z, own_d], axis=0), 1), along_z(own_d, 3)
         near_x, near_y = across_x(near), across_y(near)
-        plane = jnp.concatenate([trace_key_value, own_x, own_y, own_d, up, down, suffix_own], axis=0)
-        here = [(0, 0, 0), (0, 1, 0), (0, 0, 1), (0, 1, 1), (1, 0, 0), (3, 0, 0)]
-        state = absorb([(plane, 0, 7)], slots_of(here + [0]), None)
-
-        near_x, near_y, up_two, down_d, state = barrier((near_x, near_y, up_two, down_d, state))
-        far, up_d = up_two[:rows], up_two[rows:]
+        plane = jnp.concatenate([trace_key_value, own_x, own_y, own_d, near, suffix_own], axis=0)
+        here = [(0, 0, 0), (0, 1, 0), (0, 0, 1), (0, 1, 1), (1, 0, 0), (3, 0, 0), 0]
+        state = absorb([(plane, 0, 7)], slots_of(here), None)
+
+        near_x, near_y, far_and_next_d, third_d, state = barrier((near_x, near_y, far_and_next_d, third_d, state))
+        far = far_and_next_d[:rows]
         far_y = across_y(jnp.concatenate([far, suffix_own], axis=0))
-        far_x, far_d = across_x(far), along_z(up_d, 1)
-        sides = jnp.concatenate([plane, near_x, near_y, up_d, down_d, far], axis=0)
+        far_x, far_d = across_x(far), along_z(third_d, 1)
+        sides = jnp.concatenate([plane, near_x, near_y, far_and_next_d, third_d], axis=0)
         sibling = core(sides)
-        near_here = [(1, 1, 0), (3, 1, 0), (1, 0, 1), (3, 0, 1), (1, 1, 1), (3, 1, 1)]
-        state = absorb([(sides, 7, 13), (sibling, 0, 6)], slots_of(near_here) + slots_of(here, 1), state)
+        near_here = [(1, 1, 0), (3, 1, 0), (1, 0, 1), (3, 0, 1), (2, 0, 0), (1, 1, 1), (3, 1, 1)]
+        state = absorb([(sides, 7, 14), (sibling, 0, 5)], slots_of(near_here) + slots_of(here[:5], 1), state)
 
         far_x, far_y, far_d, state = barrier((far_x, far_y, far_d, state))
         rest = jnp.concatenate([far_x, far_y, far_d], axis=0)
         rest_sibling = core(rest)
-        state = absorb(
-            [(sides, 13, 14), (sibling, 7, 14)], slots_of([(2, 0, 0)]) + slots_of(near_here + [(2, 0, 0)], 1), state
-        )
+        state = absorb([(sibling, 5, 14)], slots_of(here[5:] + near_here, 1), state)
         here = [(2, 1, 0), (2, 0, 1), 2, (2, 1, 1)]
         trace_out, suffix_out = absorb(
-            [(rest, 0, 4), (rest_sibling, 0, 4), (sibling, 6, 7)],
-            slots_of(here) + slots_of(here + [0], 1),
-            state,
-            True,
+            [(rest, 0, 4), (rest_sibling, 0, 4)], slots_of(here) + slots_of(here, 1), state, True
         )
     else:
         gathered = lax.all_gather(trace_key_value, ("ctx", "tp"), axis=0, tiled=True)

time: 42.1 us -> 41.1 us (0.976)
  waiting for transfers between devices: 14.4 us -> 13.3 us
  starting transfers between devices: 15.3 us -> 15.8 us
    ppermute x5 -> x0, waiting for transfers between devices: 8.79 us -> none  [local(): lax.ppermute(a, 'ctx', [(i, (i + 2 * shift) % ctx_size) for i in range(ct...]
    ppermute x8 -> x13, waiting for transfers between devices: 3.33 us -> 11 us  [swap(): return lax.ppermute(array, axis, [(i, i ^ bit) for i in range(size)])]
    ppermute x8 -> x13, starting transfers between devices: 9.25 us -> 15.6 us  [swap(): return lax.ppermute(array, axis, [(i, i ^ bit) for i in range(size)])]
    ppermute x5 -> x0, starting transfers between devices: 5.89 us -> none  [local(): lax.ppermute(a, 'ctx', [(i, (i + 2 * shift) % ctx_size) for i in range(ct...]
    unnamed x19 -> x18, local copies, waits for them, and re-layouts: 1.19 us -> 1.19 us
  transfers between devices with their start and end apart: 14 -> 14, of which waited for: 9 -> 8; matrix products, arithmetic and copies ran while one was open for 3% -> 3% of each run, Pallas kernels for 12% -> 13%
where the time goes in v8:
time: 41.1 us; the launch traced here: 40.9 us
  starting transfers between devices  15.8 us (38%)
  waiting for transfers between devices  13.3 us (32%)
  Pallas kernels  7.7 us (19%)
  between operations  2.76 us (7%)
  local copies, waits for them, and re-layouts  1.29 us (3%)
    ppermute x13, starting transfers between devices, swap(): return lax.ppermute(array, axis, [(i, i ^ bit) for i in range(size)])  15.6 us
    ppermute x13, waiting for transfers between devices, swap(): return lax.ppermute(array, axis, [(i, i ^ bit) for i in range(size)])  11 us
    pallas_call x4, Pallas kernels, attend(): pl.pallas_call(functools.partial(attend_kernel, slots, ranges, tp_size, f...  7.7 us
    ppermute x1, waiting for transfers between devices, local(): lax.ppermute(a, ('ctx', 'tp'), [(i * tp_size + j, (i ^ 1) * tp_size + (j...  2.22 us
    unnamed x18, local copies, waits for them, and re-layouts  1.19 us
  transfers between devices with their start and end apart: 14, of which 8 were waited for; matrix products, arithmetic and copies ran while one was open for 3% of the time, Pallas kernels for 13%

profile of v8, /device:TPU:1, one launch (start us, length us, event | category | flops | bytes accessed | tf_op | source)
XLA Modules:
  0.0 40.9 jit_solution(17229543284939488052)
XLA Ops:
  0.7 2.2 %collective-permute-start = (bf16[32,2048]{1,0:T(8,128)(2,1)}, bf16[32,2048]{1,0:T(8,128)(2,1)S(1)}, u32[]{:S(2)}, u32[]{:S(2)}) collective-permute-start(bf16[32,2048]{1,0:T(8,128)(2,1)} %param.8), channel_id=1, source_target_pairs={{0,8},{4,12},{8,0},{12,4},{16,24},{20,28},{24,16},{28,20},{1,9},{5... | collective-permute-start | bytes 393224 | tf_op jit(solution)/shard_map/ppermute | solution.py:144
  2.9 2.2 %collective-permute-start.1 = (bf16[32,2048]{1,0:T(8,128)(2,1)}, bf16[32,2048]{1,0:T(8,128)(2,1)S(1)}, u32[]{:S(2)}, u32[]{:S(2)}) collective-permute-start(bf16[32,2048]{1,0:T(8,128)(2,1)} %param.8), channel_id=1, source_target_pairs={{0,24},{4,28},{8,16},{12,20},{16,8},{20,12},{24,0},{28,4},{1,25},{... | collective-permute-start | bytes 393224 | tf_op jit(solution)/shard_map/ppermute | solution.py:144
  5.0 1.2 %collective-permute-start.2 = (bf16[32,2048]{1,0:T(8,128)(2,1)}, bf16[32,2048]{1,0:T(8,128)(2,1)S(1)}, u32[]{:S(2)}, u32[]{:S(2)}) collective-permute-start(bf16[32,2048]{1,0:T(8,128)(2,1)} %param.8), channel_id=1, source_target_pairs={{0,4},{4,0},{8,12},{12,8},{16,20},{20,16},{24,28},{28,24},{1,5},{5... | collective-permute-start | bytes 393224 | tf_op jit(solution)/shard_map/ppermute | solution.py:144
  6.3 1.2 %collective-permute-start.3 = (bf16[32,2048]{1,0:T(8,128)(2,1)}, bf16[32,2048]{1,0:T(8,128)(2,1)S(1)}, u32[]{:S(2)}, u32[]{:S(2)}) collective-permute-start(bf16[32,2048]{1,0:T(8,128)(2,1)} %param.8), channel_id=1, source_target_pairs={{0,2},{1,3},{2,0},{3,1},{4,6},{5,7},{6,4},{7,5},{8,10},{9,11},{10,... | collective-permute-start | bytes 393224 | tf_op jit(solution)/shard_map/ppermute | solution.py:144
  7.7 1.0 %constant_dynamic-update-slice_fusion.19 = (bf16[448,2048]{1,0:T(8,128)(2,1)S(1)}, bf16[224,2048]{1,0:T(8,128)(2,1)S(1)}) fusion(bf16[32,2048]{1,0:T(8,128)(2,1)} %param.8), kind=kLoop, calls=%fused_computation.21 | loop fusion | bytes 393216
  10.7 0.3 collective-permute-done.1
  11.0 2.2 %collective-permute-done.4 = bf16[32,2048]{1,0:T(8,128)(2,1)S(1)} collective-permute-done((bf16[32,2048]{1,0:T(8,128)(2,1)}, bf16[32,2048]{1,0:T(8,128)(2,1)S(1)}, u32[]{:S(2)}, u32[]{:S(2)}) %collective-permute-start.4) | collective-permute-done | bytes 131104 | tf_op jit(solution)/shard_map/ppermute | solution.py:162
  13.4 0.7 %collective-permute-start.5 = (bf16[64,2048]{1,0:T(8,128)(2,1)S(1)}, bf16[64,2048]{1,0:T(8,128)(2,1)S(1)}, u32[]{:S(2)}, u32[]{:S(2)}) collective-permute-start(bf16[64,2048]{1,0:T(8,128)(2,1)S(1)} %get-tuple-element.66), channel_id=1, source_target_pairs={{0,4},{4,0},{8,12},{12,8},{16,20},{20,16},{24,28},{28,24},{1,5},{5... | collective-permute-start | bytes 786440 | tf_op jit(solution)/shard_map/ppermute | solution.py:144
  14.1 0.5 %collective-permute-start.6 = (bf16[64,2048]{1,0:T(8,128)(2,1)S(1)}, bf16[64,2048]{1,0:T(8,128)(2,1)S(1)}, u32[]{:S(2)}, u32[]{:S(2)}) collective-permute-start(bf16[64,2048]{1,0:T(8,128)(2,1)S(1)} %get-tuple-element.66), channel_id=1, source_target_pairs={{0,2},{1,3},{2,0},{3,1},{4,6},{5,7},{6,4},{7,5},{8,10},{9,11},{10,... | collective-permute-start | bytes 786440 | tf_op jit(solution)/shard_map/ppermute | solution.py:144
  14.7 1.1 %collective-permute-start.8 = (bf16[32,2048]{1,0:T(8,128)(2,1)S(1)}, bf16[32,2048]{1,0:T(8,128)(2,1)S(1)}, u32[]{:S(2)}, u32[]{:S(2)}) collective-permute-start(bf16[32,2048]{1,0:T(8,128)(2,1)S(1)} %collective-permute-done.4), channel_id=1, source_target_pairs={{0,24},{4,28},{8,16},{12,20},{16,8},{20,12},{24,0},{28,4},{1,25},{... | collective-permute-start | bytes 393224 | tf_op jit(solution)/shard_map/ppermute | solution.py:144
  15.8 1.1 %shard_map.86 = (f32[8,320,128]{2,1,0:T(8,128)S(1)}, f32[8,320,128]{2,1,0:T(8,128)S(1)}, f32[8,320,128]{2,1,0:T(8,128)S(1)}) custom-call(s32[3,128]{1,0:T(4,128)S(1)} %broadcast_in_dim.11.refs_0_, bf16[32,5120]{1,0:T(8,128)(2,1)S(1)} %copy-done, bf16[32,5120]{1,0:T(8,128)(2,1)S(1)} %bitcast.13, bf16[224,2048]{1,0:T(8,128)(2,1)S(1)} %get-tuple-element.63.refs_3_), custom_call_target="tpu_custom_call" | custom-call | flops 671088640 | bytes 1048576 | tf_op jit(solution)/shard_map/pallas_call | solution.py:130
  17.0 3.4 %collective-permute-done.8 = bf16[32,2048]{1,0:T(8,128)(2,1)S(1)} collective-permute-done((bf16[32,2048]{1,0:T(8,128)(2,1)S(1)}, bf16[32,2048]{1,0:T(8,128)(2,1)S(1)}, u32[]{:S(2)}, u32[]{:S(2)}) %collective-permute-start.8) | collective-permute-done | bytes 131104 | tf_op jit(solution)/shard_map/ppermute | solution.py:144
  20.5 3.3 %collective-permute-done.7 = bf16[64,2048]{1,0:T(8,128)(2,1)S(1)} collective-permute-done((bf16[64,2048]{1,0:T(8,128)(2,1)S(1)}, bf16[64,2048]{1,0:T(8,128)(2,1)S(1)}, u32[]{:S(2)}, u32[]{:S(2)}) %collective-permute-start.7) | collective-permute-done | bytes 262176 | tf_op jit(solution)/shard_map/ppermute | solution.py:144
  23.8 3.7 %collective-permute-start.12 = (bf16[448,2048]{1,0:T(8,128)(2,1)S(1)}, bf16[448,2048]{1,0:T(8,128)(2,1)S(1)}, u32[]{:S(2)}, u32[]{:S(2)}) collective-permute-start(bf16[448,2048]{1,0:T(8,128)(2,1)S(1)} %constant_dynamic-update-slice_fusion.9.refs_3_), channel_id=1, source_target_pairs={{0,1},{1,0},{2,3},{3,2},{4,5},{5,4},{6,7},{7,6},{8,9},{9,8},{10,11... | collective-permute-start | bytes 5505032 | tf_op jit(solution)/shard_map/ppermute | solution.py:144
  27.5 1.0 %collective-permute-start.10 = (bf16[64,2048]{1,0:T(8,128)(2,1)S(1)}, bf16[64,2048]{1,0:T(8,128)(2,1)S(1)}, u32[]{:S(2)}, u32[]{:S(2)}) collective-permute-start(bf16[64,2048]{1,0:T(8,128)(2,1)S(1)} %pad_maximum_fusion.1), channel_id=1, source_target_pairs={{0,2},{1,3},{2,0},{3,1},{4,6},{5,7},{6,4},{7,5},{8,10},{9,11},{10,... | collective-permute-start | bytes 786440 | tf_op jit(solution)/shard_map/ppermute | solution.py:144
  28.5 0.8 %collective-permute-start.9 = (bf16[32,2048]{1,0:T(8,128)(2,1)S(1)}, bf16[32,2048]{1,0:T(8,128)(2,1)S(1)}, u32[]{:S(2)}, u32[]{:S(2)}) collective-permute-start(bf16[32,2048]{1,0:T(8,128)(2,1)S(1)} %slice.3), channel_id=1, source_target_pairs={{0,4},{4,0},{8,12},{12,8},{16,20},{20,16},{24,28},{28,24},{1,5},{5... | collective-permute-start | bytes 393224 | tf_op jit(solution)/shard_map/ppermute | solution.py:144
  29.4 1.5 %collective-permute-done.12.refs_4_.refs_3_ = bf16[448,2048]{1,0:T(8,128)(2,1)S(1)} collective-permute-done((bf16[448,2048]{1,0:T(8,128)(2,1)S(1)}, bf16[448,2048]{1,0:T(8,128)(2,1)S(1)}, u32[]{:S(2)}, u32[]{:S(2)}) %collective-permute-start.12) | collective-permute-done | bytes 1835040 | tf_op jit(solution)/shard_map/ppermute | solution.py:144
  30.9 2.1 %shard_map.87 = (f32[8,320,128]{2,1,0:T(8,128)S(1)}, f32[8,320,128]{2,1,0:T(8,128)S(1)}, f32[8,320,128]{2,1,0:T(8,128)S(1)}) custom-call(s32[3,128]{1,0:T(4,128)S(1)} %broadcast_in_dim.11.refs_0_, bf16[32,5120]{1,0:T(8,128)(2,1)S(1)} %copy-done, bf16[32,5120]{1,0:T(8,128)(2,1)S(1)} %bitcast.14, ...), custom_call_target="tpu_custom_call" | custom-call | flops 1006632960 | bytes 1572864 | tf_op jit(solution)/shard_map/pallas_call | solution.py:130
  33.0 0.3 collective-permute-done.9
  33.3 0.5 %collective-permute-done.11 = bf16[32,2048]{1,0:T(8,128)(2,1)S(1)} collective-permute-done((bf16[32,2048]{1,0:T(8,128)(2,1)S(1)}, bf16[32,2048]{1,0:T(8,128)(2,1)S(1)}, u32[]{:S(2)}, u32[]{:S(2)}) %collective-permute-start.11) | collective-permute-done | bytes 131104 | tf_op jit(solution)/shard_map/ppermute | solution.py:144
  33.8 1.7 %collective-permute-done.10 = bf16[64,2048]{1,0:T(8,128)(2,1)S(1)} collective-permute-done((bf16[64,2048]{1,0:T(8,128)(2,1)S(1)}, bf16[64,2048]{1,0:T(8,128)(2,1)S(1)}, u32[]{:S(2)}, u32[]{:S(2)}) %collective-permute-start.10) | collective-permute-done | bytes 262176 | tf_op jit(solution)/shard_map/ppermute | solution.py:144
  35.6 0.9 %collective-permute-start.13 = (bf16[128,2048]{1,0:T(8,128)(2,1)S(1)}, bf16[128,2048]{1,0:T(8,128)(2,1)S(1)}, u32[]{:S(2)}, u32[]{:S(2)}) collective-permute-start(bf16[128,2048]{1,0:T(8,128)(2,1)S(1)} %constant_dynamic-update-slice_fusion.20.refs_3_), channel_id=1, source_target_pairs={{0,1},{1,0},{2,3},{3,2},{4,5},{5,4},{6,7},{7,6},{8,9},{9,8},{10,11... | collective-permute-start | bytes 1572872 | tf_op jit(solution)/shard_map/ppermute | solution.py:144
  36.4 2.0 %shard_map.88 = (f32[8,320,128]{2,1,0:T(8,128)S(1)}, f32[8,320,128]{2,1,0:T(8,128)S(1)}, f32[8,320,128]{2,1,0:T(8,128)S(1)}) custom-call(s32[3,128]{1,0:T(4,128)S(1)} %broadcast_in_dim.11.refs_0_, bf16[32,5120]{1,0:T(8,128)(2,1)S(1)} %copy-done, bf16[32,5120]{1,0:T(8,128)(2,1)S(1)} %bitcast.15, ...), custom_call_target="tpu_custom_call" | custom-call | flops 1006632960 | bytes 1572864 | tf_op jit(solution)/shard_map/pallas_call | solution.py:130
  38.5 2.4 %shard_map.89 = (bf16[32,5120]{1,0:T(8,128)(2,1)}, bf16[32,5120]{1,0:T(8,128)(2,1)}) custom-call(s32[3,128]{1,0:T(4,128)S(1)} %broadcast_in_dim.11.refs_0_, bf16[32,5120]{1,0:T(8,128)(2,1)S(1)} %copy-done, bf16[32,5120]{1,0:T(8,128)(2,1)S(1)} %bitcast.16, bf16[128,2048]{1,0:T(8,128)(2,1)S(1)} %constant_dynamic-update-slice_fusion.20.refs_3_, ...), custom_call_target="tpu_custom_call" | custom-call | flops 671088640 | bytes 1048576 | tf_op jit(solution)/shard_map/pallas_call | solution.py:130
  (33 shorter events, 0.7 us)
Async XLA Ops:
  0.6 15.2 %copy-start.2 = (bf16[1,32,2048]{2,1,0:T(8,128)(2,1)S(1)}, bf16[1,32,2048]{2,1,0:T(8,128)(2,1)}, u32[]{:S(2)}) copy-start(bf16[1,32,2048]{2,1,0:T(8,128)(2,1)} %param.10) | copy-start | bytes 393220
  0.6 15.2 %copy-start.1 = (bf16[1,32,5120]{2,1,0:T(8,128)(2,1)S(1)}, bf16[1,32,5120]{2,1,0:T(8,128)(2,1)}, u32[]{:S(2)}) copy-start(bf16[1,32,5120]{2,1,0:T(8,128)(2,1)} %param.9) | copy-start | bytes 983044
  0.7 15.2 %copy-start = (bf16[32,5120]{1,0:T(8,128)(2,1)S(1)}, bf16[32,5120]{1,0:T(8,128)(2,1)}, u32[]{:S(2)}) copy-start(bf16[32,5120]{1,0:T(8,128)(2,1)} %refs_1_.7) | copy-start | bytes 983044
  0.7 10.0 %collective-permute-start = (bf16[32,2048]{1,0:T(8,128)(2,1)}, bf16[32,2048]{1,0:T(8,128)(2,1)S(1)}, u32[]{:S(2)}, u32[]{:S(2)}) collective-permute-start(bf16[32,2048]{1,0:T(8,128)(2,1)} %param.8), channel_id=1, source_target_pairs={{0,8},{4,12},{8,0},{12,4},{16,24},{20,28},{24,16},{28,20},{1,9},{5... | collective-permute-start | bytes 393224 | tf_op jit(solution)/shard_map/ppermute | solution.py:144
  2.9 8.1 %collective-permute-start.1 = (bf16[32,2048]{1,0:T(8,128)(2,1)}, bf16[32,2048]{1,0:T(8,128)(2,1)S(1)}, u32[]{:S(2)}, u32[]{:S(2)}) collective-permute-start(bf16[32,2048]{1,0:T(8,128)(2,1)} %param.8), channel_id=1, source_target_pairs={{0,24},{4,28},{8,16},{12,20},{16,8},{20,12},{24,0},{28,4},{1,25},{... | collective-permute-start | bytes 393224 | tf_op jit(solution)/shard_map/ppermute | solution.py:144
  5.0 5.9 %collective-permute-start.2 = (bf16[32,2048]{1,0:T(8,128)(2,1)}, bf16[32,2048]{1,0:T(8,128)(2,1)S(1)}, u32[]{:S(2)}, u32[]{:S(2)}) collective-permute-start(bf16[32,2048]{1,0:T(8,128)(2,1)} %param.8), channel_id=1, source_target_pairs={{0,4},{4,0},{8,12},{12,8},{16,20},{20,16},{24,28},{28,24},{1,5},{5... | collective-permute-start | bytes 393224 | tf_op jit(solution)/shard_map/ppermute | solution.py:144
  6.3 4.7 %collective-permute-start.3 = (bf16[32,2048]{1,0:T(8,128)(2,1)}, bf16[32,2048]{1,0:T(8,128)(2,1)S(1)}, u32[]{:S(2)}, u32[]{:S(2)}) collective-permute-start(bf16[32,2048]{1,0:T(8,128)(2,1)} %param.8), channel_id=1, source_target_pairs={{0,2},{1,3},{2,0},{3,1},{4,6},{5,7},{6,4},{7,5},{8,10},{9,11},{10,... | collective-permute-start | bytes 393224 | tf_op jit(solution)/shard_map/ppermute | solution.py:144
  7.5 5.7 %collective-permute-start.4 = (bf16[32,2048]{1,0:T(8,128)(2,1)}, bf16[32,2048]{1,0:T(8,128)(2,1)S(1)}, u32[]{:S(2)}, u32[]{:S(2)}) collective-permute-start(bf16[32,2048]{1,0:T(8,128)(2,1)} %param.8), channel_id=1, source_target_pairs={{0,6},{1,7},{2,4},{3,5},{4,2},{5,3},{6,0},{7,1},{8,14},{9,15},{10,... | collective-permute-start | bytes 393224 | tf_op jit(solution)/shard_map/ppermute | solution.py:162
  13.4 7.0 %collective-permute-start.5 = (bf16[64,2048]{1,0:T(8,128)(2,1)S(1)}, bf16[64,2048]{1,0:T(8,128)(2,1)S(1)}, u32[]{:S(2)}, u32[]{:S(2)}) collective-permute-start(bf16[64,2048]{1,0:T(8,128)(2,1)S(1)} %get-tuple-element.66), channel_id=1, source_target_pairs={{0,4},{4,0},{8,12},{12,8},{16,20},{20,16},{24,28},{28,24},{1,5},{5... | collective-permute-start | bytes 786440 | tf_op jit(solution)/shard_map/ppermute | solution.py:144
  14.1 6.3 %collective-permute-start.6 = (bf16[64,2048]{1,0:T(8,128)(2,1)S(1)}, bf16[64,2048]{1,0:T(8,128)(2,1)S(1)}, u32[]{:S(2)}, u32[]{:S(2)}) collective-permute-start(bf16[64,2048]{1,0:T(8,128)(2,1)S(1)} %get-tuple-element.66), channel_id=1, source_target_pairs={{0,2},{1,3},{2,0},{3,1},{4,6},{5,7},{6,4},{7,5},{8,10},{9,11},{10,... | collective-permute-start | bytes 786440 | tf_op jit(solution)/shard_map/ppermute | solution.py:144
  14.7 5.8 %collective-permute-start.8 = (bf16[32,2048]{1,0:T(8,128)(2,1)S(1)}, bf16[32,2048]{1,0:T(8,128)(2,1)S(1)}, u32[]{:S(2)}, u32[]{:S(2)}) collective-permute-start(bf16[32,2048]{1,0:T(8,128)(2,1)S(1)} %collective-permute-done.4), channel_id=1, source_target_pairs={{0,24},{4,28},{8,16},{12,20},{16,8},{20,12},{24,0},{28,4},{1,25},{... | collective-permute-start | bytes 393224 | tf_op jit(solution)/shard_map/ppermute | solution.py:144
  15.8 7.9 %collective-permute-start.7 = (bf16[64,2048]{1,0:T(8,128)(2,1)S(1)}, bf16[64,2048]{1,0:T(8,128)(2,1)S(1)}, u32[]{:S(2)}, u32[]{:S(2)}) collective-permute-start(bf16[64,2048]{1,0:T(8,128)(2,1)S(1)} %pad_maximum_fusion), channel_id=1, source_target_pairs={{0,8},{4,12},{8,0},{12,4},{16,24},{20,28},{24,16},{28,20},{1,9},{5... | collective-permute-start | bytes 786440 | tf_op jit(solution)/shard_map/ppermute | solution.py:144
  23.8 7.1 %collective-permute-start.12 = (bf16[448,2048]{1,0:T(8,128)(2,1)S(1)}, bf16[448,2048]{1,0:T(8,128)(2,1)S(1)}, u32[]{:S(2)}, u32[]{:S(2)}) collective-permute-start(bf16[448,2048]{1,0:T(8,128)(2,1)S(1)} %constant_dynamic-update-slice_fusion.9.refs_3_), channel_id=1, source_target_pairs={{0,1},{1,0},{2,3},{3,2},{4,5},{5,4},{6,7},{7,6},{8,9},{9,8},{10,11... | collective-permute-start | bytes 5505032 | tf_op jit(solution)/shard_map/ppermute | solution.py:144
  27.5 8.0 %collective-permute-start.10 = (bf16[64,2048]{1,0:T(8,128)(2,1)S(1)}, bf16[64,2048]{1,0:T(8,128)(2,1)S(1)}, u32[]{:S(2)}, u32[]{:S(2)}) collective-permute-start(bf16[64,2048]{1,0:T(8,128)(2,1)S(1)} %pad_maximum_fusion.1), channel_id=1, source_target_pairs={{0,2},{1,3},{2,0},{3,1},{4,6},{5,7},{6,4},{7,5},{8,10},{9,11},{10,... | collective-permute-start | bytes 786440 | tf_op jit(solution)/shard_map/ppermute | solution.py:144
  28.5 4.8 %collective-permute-start.9 = (bf16[32,2048]{1,0:T(8,128)(2,1)S(1)}, bf16[32,2048]{1,0:T(8,128)(2,1)S(1)}, u32[]{:S(2)}, u32[]{:S(2)}) collective-permute-start(bf16[32,2048]{1,0:T(8,128)(2,1)S(1)} %slice.3), channel_id=1, source_target_pairs={{0,4},{4,0},{8,12},{12,8},{16,20},{20,16},{24,28},{28,24},{1,5},{5... | collective-permute-start | bytes 393224 | tf_op jit(solution)/shard_map/ppermute | solution.py:144
  29.4 4.5 %collective-permute-start.11 = (bf16[32,2048]{1,0:T(8,128)(2,1)S(1)}, bf16[32,2048]{1,0:T(8,128)(2,1)S(1)}, u32[]{:S(2)}, u32[]{:S(2)}) collective-permute-start(bf16[32,2048]{1,0:T(8,128)(2,1)S(1)} %collective-permute-done.8), channel_id=1, source_target_pairs={{0,8},{4,12},{8,0},{12,4},{16,24},{20,28},{24,16},{28,20},{1,9},{5... | collective-permute-start | bytes 393224 | tf_op jit(solution)/shard_map/ppermute | solution.py:144
  35.6 2.9 %collective-permute-start.13 = (bf16[128,2048]{1,0:T(8,128)(2,1)S(1)}, bf16[128,2048]{1,0:T(8,128)(2,1)S(1)}, u32[]{:S(2)}, u32[]{:S(2)}) collective-permute-start(bf16[128,2048]{1,0:T(8,128)(2,1)S(1)} %constant_dynamic-update-slice_fusion.20.refs_3_), channel_id=1, source_target_pairs={{0,1},{1,0},{2,3},{3,2},{4,5},{5,4},{6,7},{7,6},{8,9},{9,8},{10,11... | collective-permute-start | bytes 1572872 | tf_op jit(solution)/shard_map/ppermute | solution.py:144

commit v9 on v8

--- a/solution.py
+++ b/solution.py
@@ -188,29 +188,29 @@
         next_z, third_z, own_x, own_y, own_d, spans = barrier((next_z, third_z, own_x, own_y, own_d, spans))
 
         near = jnp.concatenate([next_z, third_z], axis=0)
-        far_and_next_d, third_d = along_z(jnp.concatenate([third_z, own_d], axis=0), 1), along_z(own_d, 3)
+        far, third_d = along_z(third_z, 1), along_z(own_d, 3)
         near_x, near_y = across_x(near), across_y(near)
         plane = jnp.concatenate([trace_key_value, own_x, own_y, own_d, near, suffix_own], axis=0)
         here = [(0, 0, 0), (0, 1, 0), (0, 0, 1), (0, 1, 1), (1, 0, 0), (3, 0, 0), 0]
         state = absorb([(plane, 0, 7)], slots_of(here), None)
 
-        near_x, near_y, far_and_next_d, third_d, state = barrier((near_x, near_y, far_and_next_d, third_d, state))
-        far = far_and_next_d[:rows]
+        near_x, near_y, far, third_d, state = barrier((near_x, near_y, far, third_d, state))
         far_y = across_y(jnp.concatenate([far, suffix_own], axis=0))
-        far_x, far_d = across_x(far), along_z(third_d, 1)
-        sides = jnp.concatenate([plane, near_x, near_y, far_and_next_d, third_d], axis=0)
+        far_and_next_d = along_z(jnp.concatenate([third_d, own_d], axis=0), 1)
+        far_x = across_x(far)
+        sides = jnp.concatenate([plane, near_x, near_y, far, third_d], axis=0)
         sibling = core(sides)
-        near_here = [(1, 1, 0), (3, 1, 0), (1, 0, 1), (3, 0, 1), (2, 0, 0), (1, 1, 1), (3, 1, 1)]
-        state = absorb([(sides, 7, 14), (sibling, 0, 5)], slots_of(near_here) + slots_of(here[:5], 1), state)
-
-        far_x, far_y, far_d, state = barrier((far_x, far_y, far_d, state))
-        rest = jnp.concatenate([far_x, far_y, far_d], axis=0)
+        near_here = [(1, 1, 0), (3, 1, 0), (1, 0, 1), (3, 0, 1), (2, 0, 0), (3, 1, 1)]
+        state = absorb([(sides, 7, 13), (sibling, 0, 6)], slots_of(near_here) + slots_of(here[:6], 1), state)
+
+        far_x, far_y, far_and_next_d, state = barrier((far_x, far_y, far_and_next_d, state))
+        rest = jnp.concatenate([far_x, far_y, far_and_next_d], axis=0)
         rest_sibling = core(rest)
-        state = absorb([(sibling, 5, 14)], slots_of(here[5:] + near_here, 1), state)
-        here = [(2, 1, 0), (2, 0, 1), 2, (2, 1, 1)]
-        trace_out, suffix_out = absorb(
-            [(rest, 0, 4), (rest_sibling, 0, 4)], slots_of(here) + slots_of(here, 1), state, True
+        rest_here = [(2, 1, 0), (2, 0, 1), 2, (2, 1, 1), (1, 1, 1)]
+        state = absorb(
+            [(sibling, 6, 13), (rest, 0, 5)], slots_of(here[6:] + near_here, 1) + slots_of(rest_here), state
         )
+        trace_out, suffix_out = absorb([(rest_sibling, 0, 5)], slots_of(rest_here, 1), state, True)
     else:
         gathered = lax.all_gather(trace_key_value, ("ctx", "tp"), axis=0, tiled=True)
         suffix_all = lax.all_gather(suffix_own, "tp", axis=0, tiled=True)

time: 41.1 us -> 39.2 us (0.954)
  waiting for transfers between devices: 13.3 us -> 10.6 us
  starting transfers between devices: 15.8 us -> 16.4 us
    ppermute x13, waiting for transfers between devices: 11 us -> 8.41 us  [swap(): return lax.ppermute(array, axis, [(i, i ^ bit) for i in range(size)])]
    ppermute x13, starting transfers between devices: 15.6 us -> 16.2 us  [swap(): return lax.ppermute(array, axis, [(i, i ^ bit) for i in range(size)])]
  transfers between devices with their start and end apart: 14 -> 14, of which waited for: 8 -> 8; matrix products, arithmetic and copies ran while one was open for 3% -> 3% of each run, Pallas kernels for 13% -> 14%
where the time goes in v9:
time: 39.2 us; the launch traced here: 39 us
  starting transfers between devices  16.4 us (42%)
  waiting for transfers between devices  10.6 us (27%)
  Pallas kernels  7.76 us (20%)
  between operations  2.77 us (7%)
  local copies, waits for them, and re-layouts  1.28 us (3%)
    ppermute x13, starting transfers between devices, swap(): return lax.ppermute(array, axis, [(i, i ^ bit) for i in range(size)])  16.2 us
    ppermute x13, waiting for transfers between devices, swap(): return lax.ppermute(array, axis, [(i, i ^ bit) for i in range(size)])  8.41 us
    pallas_call x4, Pallas kernels, attend(): pl.pallas_call(functools.partial(attend_kernel, slots, ranges, tp_size, f...  7.76 us
    ppermute x1, waiting for transfers between devices, local(): lax.ppermute(a, ('ctx', 'tp'), [(i * tp_size + j, (i ^ 1) * tp_size + (j...  2.22 us
    unnamed x18, local copies, waits for them, and re-layouts  1.18 us
  transfers between devices with their start and end apart: 14, of which 8 were waited for; matrix products, arithmetic and copies ran while one was open for 3% of the time, Pallas kernels for 14%

profile of v9, /device:TPU:1, one launch (start us, length us, event | category | flops | bytes accessed | tf_op | source)
XLA Modules:
  0.0 39.0 jit_solution(2360193963624179184)
XLA Ops:
  0.7 2.2 %collective-permute-start = (bf16[32,2048]{1,0:T(8,128)(2,1)}, bf16[32,2048]{1,0:T(8,128)(2,1)S(1)}, u32[]{:S(2)}, u32[]{:S(2)}) collective-permute-start(bf16[32,2048]{1,0:T(8,128)(2,1)} %param.8), channel_id=1, source_target_pairs={{0,8},{4,12},{8,0},{12,4},{16,24},{20,28},{24,16},{28,20},{1,9},{5... | collective-permute-start | bytes 393224 | tf_op jit(solution)/shard_map/ppermute | solution.py:144
  2.9 2.2 %collective-permute-start.1 = (bf16[32,2048]{1,0:T(8,128)(2,1)}, bf16[32,2048]{1,0:T(8,128)(2,1)S(1)}, u32[]{:S(2)}, u32[]{:S(2)}) collective-permute-start(bf16[32,2048]{1,0:T(8,128)(2,1)} %param.8), channel_id=1, source_target_pairs={{0,24},{4,28},{8,16},{12,20},{16,8},{20,12},{24,0},{28,4},{1,25},{... | collective-permute-start | bytes 393224 | tf_op jit(solution)/shard_map/ppermute | solution.py:144
  5.0 1.2 %collective-permute-start.2 = (bf16[32,2048]{1,0:T(8,128)(2,1)}, bf16[32,2048]{1,0:T(8,128)(2,1)S(1)}, u32[]{:S(2)}, u32[]{:S(2)}) collective-permute-start(bf16[32,2048]{1,0:T(8,128)(2,1)} %param.8), channel_id=1, source_target_pairs={{0,4},{4,0},{8,12},{12,8},{16,20},{20,16},{24,28},{28,24},{1,5},{5... | collective-permute-start | bytes 393224 | tf_op jit(solution)/shard_map/ppermute | solution.py:144
  6.3 1.2 %collective-permute-start.3 = (bf16[32,2048]{1,0:T(8,128)(2,1)}, bf16[32,2048]{1,0:T(8,128)(2,1)S(1)}, u32[]{:S(2)}, u32[]{:S(2)}) collective-permute-start(bf16[32,2048]{1,0:T(8,128)(2,1)} %param.8), channel_id=1, source_target_pairs={{0,2},{1,3},{2,0},{3,1},{4,6},{5,7},{6,4},{7,5},{8,10},{9,11},{10,... | collective-permute-start | bytes 393224 | tf_op jit(solution)/shard_map/ppermute | solution.py:144
  7.5 0.2 collective-permute-start.4
  7.7 1.0 %constant_dynamic-update-slice_fusion.19 = (bf16[416,2048]{1,0:T(8,128)(2,1)S(1)}, bf16[224,2048]{1,0:T(8,128)(2,1)S(1)}) fusion(bf16[32,2048]{1,0:T(8,128)(2,1)} %param.8), kind=kLoop, calls=%fused_computation.21 | loop fusion | bytes 393216
  10.7 0.3 collective-permute-done.1
  11.0 2.2 %collective-permute-done.4 = bf16[32,2048]{1,0:T(8,128)(2,1)S(1)} collective-permute-done((bf16[32,2048]{1,0:T(8,128)(2,1)}, bf16[32,2048]{1,0:T(8,128)(2,1)S(1)}, u32[]{:S(2)}, u32[]{:S(2)}) %collective-permute-start.4) | collective-permute-done | bytes 131104 | tf_op jit(solution)/shard_map/ppermute | solution.py:162
  13.4 0.7 %collective-permute-start.5 = (bf16[64,2048]{1,0:T(8,128)(2,1)S(1)}, bf16[64,2048]{1,0:T(8,128)(2,1)S(1)}, u32[]{:S(2)}, u32[]{:S(2)}) collective-permute-start(bf16[64,2048]{1,0:T(8,128)(2,1)S(1)} %get-tuple-element.66), channel_id=1, source_target_pairs={{0,4},{4,0},{8,12},{12,8},{16,20},{20,16},{24,28},{28,24},{1,5},{5... | collective-permute-start | bytes 786440 | tf_op jit(solution)/shard_map/ppermute | solution.py:144
  14.1 0.5 %collective-permute-start.6 = (bf16[64,2048]{1,0:T(8,128)(2,1)S(1)}, bf16[64,2048]{1,0:T(8,128)(2,1)S(1)}, u32[]{:S(2)}, u32[]{:S(2)}) collective-permute-start(bf16[64,2048]{1,0:T(8,128)(2,1)S(1)} %get-tuple-element.66), channel_id=1, source_target_pairs={{0,2},{1,3},{2,0},{3,1},{4,6},{5,7},{6,4},{7,5},{8,10},{9,11},{10,... | collective-permute-start | bytes 786440 | tf_op jit(solution)/shard_map/ppermute | solution.py:144
  14.6 1.1 %collective-permute-start.8 = (bf16[32,2048]{1,0:T(8,128)(2,1)S(1)}, bf16[32,2048]{1,0:T(8,128)(2,1)S(1)}, u32[]{:S(2)}, u32[]{:S(2)}) collective-permute-start(bf16[32,2048]{1,0:T(8,128)(2,1)S(1)} %collective-permute-done.4), channel_id=1, source_target_pairs={{0,24},{4,28},{8,16},{12,20},{16,8},{20,12},{24,0},{28,4},{1,25},{... | collective-permute-start | bytes 393224 | tf_op jit(solution)/shard_map/ppermute | solution.py:144
  15.8 1.1 %shard_map.86 = (f32[8,320,128]{2,1,0:T(8,128)S(1)}, f32[8,320,128]{2,1,0:T(8,128)S(1)}, f32[8,320,128]{2,1,0:T(8,128)S(1)}) custom-call(s32[3,128]{1,0:T(4,128)S(1)} %broadcast_in_dim.11.refs_0_, bf16[32,5120]{1,0:T(8,128)(2,1)S(1)} %copy-done, bf16[32,5120]{1,0:T(8,128)(2,1)S(1)} %bitcast.13, bf16[224,2048]{1,0:T(8,128)(2,1)S(1)} %get-tuple-element.63.refs_3_), custom_call_target="tpu_custom_call" | custom-call | flops 671088640 | bytes 1048576 | tf_op jit(solution)/shard_map/pallas_call | solution.py:130
  16.9 3.5 %collective-permute-done.8 = bf16[32,2048]{1,0:T(8,128)(2,1)S(1)} collective-permute-done((bf16[32,2048]{1,0:T(8,128)(2,1)S(1)}, bf16[32,2048]{1,0:T(8,128)(2,1)S(1)}, u32[]{:S(2)}, u32[]{:S(2)}) %collective-permute-start.8) | collective-permute-done | bytes 131104 | tf_op jit(solution)/shard_map/ppermute | solution.py:144
  20.4 0.9 %collective-permute-done.7 = bf16[32,2048]{1,0:T(8,128)(2,1)S(1)} collective-permute-done((bf16[32,2048]{1,0:T(8,128)(2,1)S(1)}, bf16[32,2048]{1,0:T(8,128)(2,1)S(1)}, u32[]{:S(2)}, u32[]{:S(2)}) %collective-permute-start.7) | collective-permute-done | bytes 131104 | tf_op jit(solution)/shard_map/ppermute | solution.py:144
  21.3 4.1 %collective-permute-start.12 = (bf16[416,2048]{1,0:T(8,128)(2,1)S(1)}, bf16[416,2048]{1,0:T(8,128)(2,1)S(1)}, u32[]{:S(2)}, u32[]{:S(2)}) collective-permute-start(bf16[416,2048]{1,0:T(8,128)(2,1)S(1)} %constant_dynamic-update-slice_fusion.9.refs_3_), channel_id=1, source_target_pairs={{0,1},{1,0},{2,3},{3,2},{4,5},{5,4},{6,7},{7,6},{8,9},{9,8},{10,11... | collective-permute-start | bytes 5111816 | tf_op jit(solution)/shard_map/ppermute | solution.py:144
  25.6 1.0 %collective-permute-start.10 = (bf16[64,2048]{1,0:T(8,128)(2,1)S(1)}, bf16[64,2048]{1,0:T(8,128)(2,1)S(1)}, u32[]{:S(2)}, u32[]{:S(2)}) collective-permute-start(bf16[64,2048]{1,0:T(8,128)(2,1)S(1)} %pad_maximum_fusion), channel_id=1, source_target_pairs={{0,2},{1,3},{2,0},{3,1},{4,6},{5,7},{6,4},{7,5},{8,10},{9,11},{10,... | collective-permute-start | bytes 786440 | tf_op jit(solution)/shard_map/ppermute | solution.py:144
  26.6 1.1 %collective-permute-start.9 = (bf16[32,2048]{1,0:T(8,128)(2,1)S(1)}, bf16[32,2048]{1,0:T(8,128)(2,1)S(1)}, u32[]{:S(2)}, u32[]{:S(2)}) collective-permute-start(bf16[32,2048]{1,0:T(8,128)(2,1)S(1)} %collective-permute-done.7), channel_id=1, source_target_pairs={{0,4},{4,0},{8,12},{12,8},{16,20},{20,16},{24,28},{28,24},{1,5},{5... | collective-permute-start | bytes 393224 | tf_op jit(solution)/shard_map/ppermute | solution.py:144
  27.6 1.0 %collective-permute-done.12.refs_4_.refs_3_ = bf16[416,2048]{1,0:T(8,128)(2,1)S(1)} collective-permute-done((bf16[416,2048]{1,0:T(8,128)(2,1)S(1)}, bf16[416,2048]{1,0:T(8,128)(2,1)S(1)}, u32[]{:S(2)}, u32[]{:S(2)}) %collective-permute-start.12) | collective-permute-done | bytes 1703968 | tf_op jit(solution)/shard_map/ppermute | solution.py:144
  28.7 2.1 %shard_map.87 = (f32[8,320,128]{2,1,0:T(8,128)S(1)}, f32[8,320,128]{2,1,0:T(8,128)S(1)}, f32[8,320,128]{2,1,0:T(8,128)S(1)}) custom-call(s32[3,128]{1,0:T(4,128)S(1)} %broadcast_in_dim.11.refs_0_, bf16[32,5120]{1,0:T(8,128)(2,1)S(1)} %copy-done, bf16[32,5120]{1,0:T(8,128)(2,1)S(1)} %bitcast.14, ...), custom_call_target="tpu_custom_call" | custom-call | flops 1006632960 | bytes 1572864 | tf_op jit(solution)/shard_map/pallas_call | solution.py:130
  30.8 0.6 %collective-permute-done.9 = bf16[32,2048]{1,0:T(8,128)(2,1)S(1)} collective-permute-done((bf16[32,2048]{1,0:T(8,128)(2,1)S(1)}, bf16[32,2048]{1,0:T(8,128)(2,1)S(1)}, u32[]{:S(2)}, u32[]{:S(2)}) %collective-permute-start.9) | collective-permute-done | bytes 131104 | tf_op jit(solution)/shard_map/ppermute | solution.py:144
  31.4 2.1 %collective-permute-done.11 = bf16[64,2048]{1,0:T(8,128)(2,1)S(1)} collective-permute-done((bf16[64,2048]{1,0:T(8,128)(2,1)S(1)}, bf16[64,2048]{1,0:T(8,128)(2,1)S(1)}, u32[]{:S(2)}, u32[]{:S(2)}) %collective-permute-start.11) | collective-permute-done | bytes 262176 | tf_op jit(solution)/shard_map/ppermute | solution.py:144
  33.6 0.9 %collective-permute-start.13 = (bf16[160,2048]{1,0:T(8,128)(2,1)S(1)}, bf16[160,2048]{1,0:T(8,128)(2,1)S(1)}, u32[]{:S(2)}, u32[]{:S(2)}) collective-permute-start(bf16[160,2048]{1,0:T(8,128)(2,1)S(1)} %constant_dynamic-update-slice_fusion.20.refs_4_), channel_id=1, source_target_pairs={{0,1},{1,0},{2,3},{3,2},{4,5},{5,4},{6,7},{7,6},{8,9},{9,8},{10,11... | collective-permute-start | bytes 1966088 | tf_op jit(solution)/shard_map/ppermute | solution.py:144
  34.5 2.1 %shard_map.88 = (f32[8,320,128]{2,1,0:T(8,128)S(1)}, f32[8,320,128]{2,1,0:T(8,128)S(1)}, f32[8,320,128]{2,1,0:T(8,128)S(1)}) custom-call(s32[3,128]{1,0:T(4,128)S(1)} %broadcast_in_dim.11.refs_0_, bf16[32,5120]{1,0:T(8,128)(2,1)S(1)} %copy-done, bf16[32,5120]{1,0:T(8,128)(2,1)S(1)} %bitcast.15, ...), custom_call_target="tpu_custom_call" | custom-call | flops 1006632960 | bytes 1572864 | tf_op jit(solution)/shard_map/pallas_call | solution.py:130
  36.6 2.4 %shard_map.89 = (bf16[32,5120]{1,0:T(8,128)(2,1)}, bf16[32,5120]{1,0:T(8,128)(2,1)}) custom-call(s32[3,128]{1,0:T(4,128)S(1)} %broadcast_in_dim.11.refs_0_, bf16[32,5120]{1,0:T(8,128)(2,1)S(1)} %copy-done, bf16[32,5120]{1,0:T(8,128)(2,1)S(1)} %bitcast.16, bf16[160,2048]{1,0:T(8,128)(2,1)S(1)} %collective-permute-done.13.refs_3_, ...), custom_call_target="tpu_custom_call" | custom-call | flops 671088640 | bytes 1048576 | tf_op jit(solution)/shard_map/pallas_call | solution.py:130
  (32 shorter events, 0.6 us)
Async XLA Ops:
  0.6 15.1 %copy-start.2 = (bf16[1,32,2048]{2,1,0:T(8,128)(2,1)S(1)}, bf16[1,32,2048]{2,1,0:T(8,128)(2,1)}, u32[]{:S(2)}) copy-start(bf16[1,32,2048]{2,1,0:T(8,128)(2,1)} %param.10) | copy-start | bytes 393220
  0.6 15.1 %copy-start.1 = (bf16[1,32,5120]{2,1,0:T(8,128)(2,1)S(1)}, bf16[1,32,5120]{2,1,0:T(8,128)(2,1)}, u32[]{:S(2)}) copy-start(bf16[1,32,5120]{2,1,0:T(8,128)(2,1)} %param.9) | copy-start | bytes 983044
  0.7 15.1 %copy-start = (bf16[32,5120]{1,0:T(8,128)(2,1)S(1)}, bf16[32,5120]{1,0:T(8,128)(2,1)}, u32[]{:S(2)}) copy-start(bf16[32,5120]{1,0:T(8,128)(2,1)} %refs_1_.7) | copy-start | bytes 983044
  0.7 10.0 %collective-permute-start = (bf16[32,2048]{1,0:T(8,128)(2,1)}, bf16[32,2048]{1,0:T(8,128)(2,1)S(1)}, u32[]{:S(2)}, u32[]{:S(2)}) collective-permute-start(bf16[32,2048]{1,0:T(8,128)(2,1)} %param.8), channel_id=1, source_target_pairs={{0,8},{4,12},{8,0},{12,4},{16,24},{20,28},{24,16},{28,20},{1,9},{5... | collective-permute-start | bytes 393224 | tf_op jit(solution)/shard_map/ppermute | solution.py:144
  2.9 8.1 %collective-permute-start.1 = (bf16[32,2048]{1,0:T(8,128)(2,1)}, bf16[32,2048]{1,0:T(8,128)(2,1)S(1)}, u32[]{:S(2)}, u32[]{:S(2)}) collective-permute-start(bf16[32,2048]{1,0:T(8,128)(2,1)} %param.8), channel_id=1, source_target_pairs={{0,24},{4,28},{8,16},{12,20},{16,8},{20,12},{24,0},{28,4},{1,25},{... | collective-permute-start | bytes 393224 | tf_op jit(solution)/shard_map/ppermute | solution.py:144
  5.0 5.9 %collective-permute-start.2 = (bf16[32,2048]{1,0:T(8,128)(2,1)}, bf16[32,2048]{1,0:T(8,128)(2,1)S(1)}, u32[]{:S(2)}, u32[]{:S(2)}) collective-permute-start(bf16[32,2048]{1,0:T(8,128)(2,1)} %param.8), channel_id=1, source_target_pairs={{0,4},{4,0},{8,12},{12,8},{16,20},{20,16},{24,28},{28,24},{1,5},{5... | collective-permute-start | bytes 393224 | tf_op jit(solution)/shard_map/ppermute | solution.py:144
  6.3 4.7 %collective-permute-start.3 = (bf16[32,2048]{1,0:T(8,128)(2,1)}, bf16[32,2048]{1,0:T(8,128)(2,1)S(1)}, u32[]{:S(2)}, u32[]{:S(2)}) collective-permute-start(bf16[32,2048]{1,0:T(8,128)(2,1)} %param.8), channel_id=1, source_target_pairs={{0,2},{1,3},{2,0},{3,1},{4,6},{5,7},{6,4},{7,5},{8,10},{9,11},{10,... | collective-permute-start | bytes 393224 | tf_op jit(solution)/shard_map/ppermute | solution.py:144
  7.5 5.7 %collective-permute-start.4 = (bf16[32,2048]{1,0:T(8,128)(2,1)}, bf16[32,2048]{1,0:T(8,128)(2,1)S(1)}, u32[]{:S(2)}, u32[]{:S(2)}) collective-permute-start(bf16[32,2048]{1,0:T(8,128)(2,1)} %param.8), channel_id=1, source_target_pairs={{0,6},{1,7},{2,4},{3,5},{4,2},{5,3},{6,0},{7,1},{8,14},{9,15},{10,... | collective-permute-start | bytes 393224 | tf_op jit(solution)/shard_map/ppermute | solution.py:162
  13.4 7.8 %collective-permute-start.5 = (bf16[64,2048]{1,0:T(8,128)(2,1)S(1)}, bf16[64,2048]{1,0:T(8,128)(2,1)S(1)}, u32[]{:S(2)}, u32[]{:S(2)}) collective-permute-start(bf16[64,2048]{1,0:T(8,128)(2,1)S(1)} %get-tuple-element.66), channel_id=1, source_target_pairs={{0,4},{4,0},{8,12},{12,8},{16,20},{20,16},{24,28},{28,24},{1,5},{5... | collective-permute-start | bytes 786440 | tf_op jit(solution)/shard_map/ppermute | solution.py:144
  14.1 7.1 %collective-permute-start.6 = (bf16[64,2048]{1,0:T(8,128)(2,1)S(1)}, bf16[64,2048]{1,0:T(8,128)(2,1)S(1)}, u32[]{:S(2)}, u32[]{:S(2)}) collective-permute-start(bf16[64,2048]{1,0:T(8,128)(2,1)S(1)} %get-tuple-element.66), channel_id=1, source_target_pairs={{0,2},{1,3},{2,0},{3,1},{4,6},{5,7},{6,4},{7,5},{8,10},{9,11},{10,... | collective-permute-start | bytes 786440 | tf_op jit(solution)/shard_map/ppermute | solution.py:144
  14.6 5.7 %collective-permute-start.8 = (bf16[32,2048]{1,0:T(8,128)(2,1)S(1)}, bf16[32,2048]{1,0:T(8,128)(2,1)S(1)}, u32[]{:S(2)}, u32[]{:S(2)}) collective-permute-start(bf16[32,2048]{1,0:T(8,128)(2,1)S(1)} %collective-permute-done.4), channel_id=1, source_target_pairs={{0,24},{4,28},{8,16},{12,20},{16,8},{20,12},{24,0},{28,4},{1,25},{... | collective-permute-start | bytes 393224 | tf_op jit(solution)/shard_map/ppermute | solution.py:144
  15.7 5.5 %collective-permute-start.7 = (bf16[32,2048]{1,0:T(8,128)(2,1)S(1)}, bf16[32,2048]{1,0:T(8,128)(2,1)S(1)}, u32[]{:S(2)}, u32[]{:S(2)}) collective-permute-start(bf16[32,2048]{1,0:T(8,128)(2,1)S(1)} %collective-permute-done.1), channel_id=1, source_target_pairs={{0,8},{4,12},{8,0},{12,4},{16,24},{20,28},{24,16},{28,20},{1,9},{5... | collective-permute-start | bytes 393224 | tf_op jit(solution)/shard_map/ppermute | solution.py:144
  21.3 7.3 %collective-permute-start.12 = (bf16[416,2048]{1,0:T(8,128)(2,1)S(1)}, bf16[416,2048]{1,0:T(8,128)(2,1)S(1)}, u32[]{:S(2)}, u32[]{:S(2)}) collective-permute-start(bf16[416,2048]{1,0:T(8,128)(2,1)S(1)} %constant_dynamic-update-slice_fusion.9.refs_3_), channel_id=1, source_target_pairs={{0,1},{1,0},{2,3},{3,2},{4,5},{5,4},{6,7},{7,6},{8,9},{9,8},{10,11... | collective-permute-start | bytes 5111816 | tf_op jit(solution)/shard_map/ppermute | solution.py:144
  25.5 8.0 %collective-permute-start.11 = (bf16[64,2048]{1,0:T(8,128)(2,1)S(1)}, bf16[64,2048]{1,0:T(8,128)(2,1)S(1)}, u32[]{:S(2)}, u32[]{:S(2)}) collective-permute-start(bf16[64,2048]{1,0:T(8,128)(2,1)S(1)} %pad_maximum_fusion.1), channel_id=1, source_target_pairs={{0,8},{4,12},{8,0},{12,4},{16,24},{20,28},{24,16},{28,20},{1,9},{5... | collective-permute-start | bytes 786440 | tf_op jit(solution)/shard_map/ppermute | solution.py:144
  25.6 8.0 %collective-permute-start.10 = (bf16[64,2048]{1,0:T(8,128)(2,1)S(1)}, bf16[64,2048]{1,0:T(8,128)(2,1)S(1)}, u32[]{:S(2)}, u32[]{:S(2)}) collective-permute-start(bf16[64,2048]{1,0:T(8,128)(2,1)S(1)} %pad_maximum_fusion), channel_id=1, source_target_pairs={{0,2},{1,3},{2,0},{3,1},{4,6},{5,7},{6,4},{7,5},{8,10},{9,11},{10,... | collective-permute-start | bytes 786440 | tf_op jit(solution)/shard_map/ppermute | solution.py:144
  26.6 4.8 %collective-permute-start.9 = (bf16[32,2048]{1,0:T(8,128)(2,1)S(1)}, bf16[32,2048]{1,0:T(8,128)(2,1)S(1)}, u32[]{:S(2)}, u32[]{:S(2)}) collective-permute-start(bf16[32,2048]{1,0:T(8,128)(2,1)S(1)} %collective-permute-done.7), channel_id=1, source_target_pairs={{0,4},{4,0},{8,12},{12,8},{16,20},{20,16},{24,28},{28,24},{1,5},{5... | collective-permute-start | bytes 393224 | tf_op jit(solution)/shard_map/ppermute | solution.py:144
  33.6 3.0 %collective-permute-start.13 = (bf16[160,2048]{1,0:T(8,128)(2,1)S(1)}, bf16[160,2048]{1,0:T(8,128)(2,1)S(1)}, u32[]{:S(2)}, u32[]{:S(2)}) collective-permute-start(bf16[160,2048]{1,0:T(8,128)(2,1)S(1)} %constant_dynamic-update-slice_fusion.20.refs_4_), channel_id=1, source_target_pairs={{0,1},{1,0},{2,3},{3,2},{4,5},{5,4},{6,7},{7,6},{8,9},{9,8},{10,11... | collective-permute-start | bytes 1966088 | tf_op jit(solution)/shard_map/ppermute | solution.py:144

commit v10 on v9

--- a/solution.py
+++ b/solution.py
@@ -16,6 +16,7 @@
 SCALE = HEAD_SIZE ** (-0.5) * LOG2E
 MASKED = -1e30
 CHUNK_ROWS = 1024
+COST_FACTOR = 10
 
 
 def dot_t(a, b):
@@ -135,7 +136,7 @@
         scratch_shapes=[pltpu.VMEM((all_rows, HEAD_SIZE), jnp.bfloat16)],
         compiler_params=pltpu.CompilerParams(vmem_limit_bytes=32 * 1024 * 1024),
         cost_estimate=pl.CostEstimate(
-            flops=flops, bytes_accessed=all_rows * 4096, transcendentals=2 * QUERY_HEADS * rows * all_rows
+            flops=COST_FACTOR * flops, bytes_accessed=all_rows * 4096, transcendentals=2 * QUERY_HEADS * rows * all_rows
         ),
     )(*operands)
 
@@ -193,22 +194,27 @@
         plane = jnp.concatenate([trace_key_value, own_x, own_y, own_d, near, suffix_own], axis=0)
         here = [(0, 0, 0), (0, 1, 0), (0, 0, 1), (0, 1, 1), (1, 0, 0), (3, 0, 0), 0]
         state = absorb([(plane, 0, 7)], slots_of(here), None)
+        plane, state = barrier((plane, state))
+        plane_sibling = core(plane)
 
         near_x, near_y, far, third_d, state = barrier((near_x, near_y, far, third_d, state))
         far_y = across_y(jnp.concatenate([far, suffix_own], axis=0))
         far_and_next_d = along_z(jnp.concatenate([third_d, own_d], axis=0), 1)
         far_x = across_x(far)
-        sides = jnp.concatenate([plane, near_x, near_y, far, third_d], axis=0)
-        sibling = core(sides)
+        sides = jnp.concatenate([near_x, near_y, far, third_d], axis=0)
         near_here = [(1, 1, 0), (3, 1, 0), (1, 0, 1), (3, 0, 1), (2, 0, 0), (3, 1, 1)]
-        state = absorb([(sides, 7, 13), (sibling, 0, 6)], slots_of(near_here) + slots_of(here[:6], 1), state)
+        state = absorb([(sides, 0, 6), (plane_sibling, 0, 6)], slots_of(near_here) + slots_of(here[:6], 1), state)
+        sides, state = barrier((sides, state))
+        sides_sibling = core(sides)
 
         far_x, far_y, far_and_next_d, state = barrier((far_x, far_y, far_and_next_d, state))
         rest = jnp.concatenate([far_x, far_y, far_and_next_d], axis=0)
         rest_sibling = core(rest)
         rest_here = [(2, 1, 0), (2, 0, 1), 2, (2, 1, 1), (1, 1, 1)]
         state = absorb(
-            [(sibling, 6, 13), (rest, 0, 5)], slots_of(here[6:] + near_here, 1) + slots_of(rest_here), state
+            [(plane_sibling, 6, 7), (sides_sibling, 0, 6), (rest, 0, 5)],
+            slots_of(here[6:] + near_here, 1) + slots_of(rest_here),
+            state,
         )
         trace_out, suffix_out = absorb([(rest_sibling, 0, 5)], slots_of(rest_here, 1), state, True)
     else:

time: 39.2 us -> 39.1 us (level)
  starting transfers between devices: 16.4 us -> 23.5 us
  waiting for transfers between devices: 10.6 us -> 3.61 us
    ppermute x13 -> x14, starting transfers between devices: 16.2 us -> 23.4 us  [swap(): return lax.ppermute(array, axis, [(i, i ^ bit) for i in range(size)])]
    ppermute x13 -> x14, waiting for transfers between devices: 8.41 us -> 1.39 us  [swap(): return lax.ppermute(array, axis, [(i, i ^ bit) for i in range(size)])]
    unnamed x18 -> x17, local copies, waits for them, and re-layouts: 1.18 us -> 1.11 us
  transfers between devices with their start and end apart: 14 -> 15, of which waited for: 8 -> 4; matrix products, arithmetic and copies ran while one was open for 3% -> 3% of each run, Pallas kernels for 14% -> 14%
where the time goes in v10:
time: 39.1 us; the launch traced here: 39 us
  starting transfers between devices  23.5 us (60%)
  Pallas kernels  7.71 us (20%)
  waiting for transfers between devices  3.61 us (9%)
  between operations  2.77 us (7%)
  local copies, waits for them, and re-layouts  1.22 us (3%)
    ppermute x14, starting transfers between devices, swap(): return lax.ppermute(array, axis, [(i, i ^ bit) for i in range(size)])  23.4 us
    pallas_call x4, Pallas kernels, attend(): pl.pallas_call(functools.partial(attend_kernel, slots, ranges, tp_size, f...  7.71 us
    ppermute x1, waiting for transfers between devices, local(): lax.ppermute(a, ('ctx', 'tp'), [(i * tp_size + j, (i ^ 1) * tp_size + (j...  2.22 us
    ppermute x14, waiting for transfers between devices, swap(): return lax.ppermute(array, axis, [(i, i ^ bit) for i in range(size)])  1.39 us
    unnamed x17, local copies, waits for them, and re-layouts  1.11 us
  transfers between devices with their start and end apart: 15, of which 4 were waited for; matrix products, arithmetic and copies ran while one was open for 3% of the time, Pallas kernels for 14%

profile of v10, /device:TPU:1, one launch (start us, length us, event | category | flops | bytes accessed | tf_op | source)
XLA Modules:
  0.0 39.0 jit_solution(2269463005273378253)
XLA Ops:
  0.7 2.2 %collective-permute-start = (bf16[32,2048]{1,0:T(8,128)(2,1)}, bf16[32,2048]{1,0:T(8,128)(2,1)S(1)}, u32[]{:S(2)}, u32[]{:S(2)}) collective-permute-start(bf16[32,2048]{1,0:T(8,128)(2,1)} %param.8), channel_id=1, source_target_pairs={{0,8},{4,12},{8,0},{12,4},{16,24},{20,28},{24,16},{28,20},{1,9},{5... | collective-permute-start | bytes 393224 | tf_op jit(solution)/shard_map/ppermute | solution.py:145
  2.9 2.2 %collective-permute-start.1 = (bf16[32,2048]{1,0:T(8,128)(2,1)}, bf16[32,2048]{1,0:T(8,128)(2,1)S(1)}, u32[]{:S(2)}, u32[]{:S(2)}) collective-permute-start(bf16[32,2048]{1,0:T(8,128)(2,1)} %param.8), channel_id=1, source_target_pairs={{0,24},{4,28},{8,16},{12,20},{16,8},{20,12},{24,0},{28,4},{1,25},{... | collective-permute-start | bytes 393224 | tf_op jit(solution)/shard_map/ppermute | solution.py:145
  5.0 1.2 %collective-permute-start.2 = (bf16[32,2048]{1,0:T(8,128)(2,1)}, bf16[32,2048]{1,0:T(8,128)(2,1)S(1)}, u32[]{:S(2)}, u32[]{:S(2)}) collective-permute-start(bf16[32,2048]{1,0:T(8,128)(2,1)} %param.8), channel_id=1, source_target_pairs={{0,4},{4,0},{8,12},{12,8},{16,20},{20,16},{24,28},{28,24},{1,5},{5... | collective-permute-start | bytes 393224 | tf_op jit(solution)/shard_map/ppermute | solution.py:145
  6.3 1.2 %collective-permute-start.3 = (bf16[32,2048]{1,0:T(8,128)(2,1)}, bf16[32,2048]{1,0:T(8,128)(2,1)S(1)}, u32[]{:S(2)}, u32[]{:S(2)}) collective-permute-start(bf16[32,2048]{1,0:T(8,128)(2,1)} %param.8), channel_id=1, source_target_pairs={{0,2},{1,3},{2,0},{3,1},{4,6},{5,7},{6,4},{7,5},{8,10},{9,11},{10,... | collective-permute-start | bytes 393224 | tf_op jit(solution)/shard_map/ppermute | solution.py:145
  7.5 0.2 collective-permute-start.4
  7.7 0.9 %constant_dynamic-update-slice_fusion.8 = bf16[224,2048]{1,0:T(8,128)(2,1)S(1)} fusion(bf16[32,2048]{1,0:T(8,128)(2,1)} %param.8), kind=kLoop, calls=%fused_computation.10 | loop fusion | bytes 262144
  10.6 0.1 add_bitcast_fusion
  10.7 0.3 collective-permute-done.1
  11.0 2.2 %collective-permute-done.4 = bf16[32,2048]{1,0:T(8,128)(2,1)S(1)} collective-permute-done((bf16[32,2048]{1,0:T(8,128)(2,1)}, bf16[32,2048]{1,0:T(8,128)(2,1)S(1)}, u32[]{:S(2)}, u32[]{:S(2)}) %collective-permute-start.4) | collective-permute-done | bytes 131104 | tf_op jit(solution)/shard_map/ppermute | solution.py:163
  13.4 0.7 %collective-permute-start.5 = (bf16[64,2048]{1,0:T(8,128)(2,1)S(1)}, bf16[64,2048]{1,0:T(8,128)(2,1)S(1)}, u32[]{:S(2)}, u32[]{:S(2)}) collective-permute-start(bf16[64,2048]{1,0:T(8,128)(2,1)S(1)} %get-tuple-element.79), channel_id=1, source_target_pairs={{0,4},{4,0},{8,12},{12,8},{16,20},{20,16},{24,28},{28,24},{1,5},{5... | collective-permute-start | bytes 786440 | tf_op jit(solution)/shard_map/ppermute | solution.py:145
  14.1 0.5 %collective-permute-start.6 = (bf16[64,2048]{1,0:T(8,128)(2,1)S(1)}, bf16[64,2048]{1,0:T(8,128)(2,1)S(1)}, u32[]{:S(2)}, u32[]{:S(2)}) collective-permute-start(bf16[64,2048]{1,0:T(8,128)(2,1)S(1)} %get-tuple-element.79), channel_id=1, source_target_pairs={{0,2},{1,3},{2,0},{3,1},{4,6},{5,7},{6,4},{7,5},{8,10},{9,11},{10,... | collective-permute-start | bytes 786440 | tf_op jit(solution)/shard_map/ppermute | solution.py:145
  14.6 1.1 %collective-permute-start.8 = (bf16[32,2048]{1,0:T(8,128)(2,1)S(1)}, bf16[32,2048]{1,0:T(8,128)(2,1)S(1)}, u32[]{:S(2)}, u32[]{:S(2)}) collective-permute-start(bf16[32,2048]{1,0:T(8,128)(2,1)S(1)} %collective-permute-done.4), channel_id=1, source_target_pairs={{0,24},{4,28},{8,16},{12,20},{16,8},{20,12},{24,0},{28,4},{1,25},{... | collective-permute-start | bytes 393224 | tf_op jit(solution)/shard_map/ppermute | solution.py:145
  15.7 1.1 %shard_map.86 = (f32[8,320,128]{2,1,0:T(8,128)S(1)}, f32[8,320,128]{2,1,0:T(8,128)S(1)}, f32[8,320,128]{2,1,0:T(8,128)S(1)}) custom-call(s32[3,128]{1,0:T(4,128)S(1)} %broadcast_in_dim.11.refs_0_, bf16[32,5120]{1,0:T(8,128)(2,1)S(1)} %copy-done, bf16[32,5120]{1,0:T(8,128)(2,1)S(1)} %bitcast.12, bf16[224,2048]{1,0:T(8,128)(2,1)S(1)} %constant_dynamic-update-slice_fusion.2.refs_3_), custom_call_target="tpu_custom_call" | custom-call | flops 6710886400 | bytes 1048576 | tf_op jit(solution)/shard_map/pallas_call | solution.py:131
  16.9 3.3 %collective-permute-start.12 = (bf16[224,2048]{1,0:T(8,128)(2,1)S(1)}, bf16[224,2048]{1,0:T(8,128)(2,1)S(1)}, u32[]{:S(2)}, u32[]{:S(2)}) collective-permute-start(bf16[224,2048]{1,0:T(8,128)(2,1)S(1)} %constant_dynamic-update-slice_fusion.2.refs_3_), channel_id=1, source_target_pairs={{0,1},{1,0},{2,3},{3,2},{4,5},{5,4},{6,7},{7,6},{8,9},{9,8},{10,11... | collective-permute-start | bytes 2752520 | tf_op jit(solution)/shard_map/ppermute | solution.py:145
  20.1 0.2 collective-permute-done.8
  20.3 0.9 %collective-permute-done.7 = bf16[32,2048]{1,0:T(8,128)(2,1)S(1)} collective-permute-done((bf16[32,2048]{1,0:T(8,128)(2,1)S(1)}, bf16[32,2048]{1,0:T(8,128)(2,1)S(1)}, u32[]{:S(2)}, u32[]{:S(2)}) %collective-permute-start.7) | collective-permute-done | bytes 131104 | tf_op jit(solution)/shard_map/ppermute | solution.py:145
  21.2 0.8 %collective-permute-start.11 = (bf16[64,2048]{1,0:T(8,128)(2,1)S(1)}, bf16[64,2048]{1,0:T(8,128)(2,1)S(1)}, u32[]{:S(2)}, u32[]{:S(2)}) collective-permute-start(bf16[64,2048]{1,0:T(8,128)(2,1)S(1)} %pad_maximum_fusion.1), channel_id=1, source_target_pairs={{0,8},{4,12},{8,0},{12,4},{16,24},{20,28},{24,16},{28,20},{1,9},{5... | collective-permute-start | bytes 786440 | tf_op jit(solution)/shard_map/ppermute | solution.py:145
  22.0 1.3 %collective-permute-start.9 = (bf16[32,2048]{1,0:T(8,128)(2,1)S(1)}, bf16[32,2048]{1,0:T(8,128)(2,1)S(1)}, u32[]{:S(2)}, u32[]{:S(2)}) collective-permute-start(bf16[32,2048]{1,0:T(8,128)(2,1)S(1)} %collective-permute-done.7), channel_id=1, source_target_pairs={{0,4},{4,0},{8,12},{12,8},{16,20},{20,16},{24,28},{28,24},{1,5},{5... | collective-permute-start | bytes 393224 | tf_op jit(solution)/shard_map/ppermute | solution.py:145
  23.3 0.7 %collective-permute-start.10 = (bf16[64,2048]{1,0:T(8,128)(2,1)S(1)}, bf16[64,2048]{1,0:T(8,128)(2,1)S(1)}, u32[]{:S(2)}, u32[]{:S(2)}) collective-permute-start(bf16[64,2048]{1,0:T(8,128)(2,1)S(1)} %pad_maximum_fusion), channel_id=1, source_target_pairs={{0,2},{1,3},{2,0},{3,1},{4,6},{5,7},{6,4},{7,5},{8,10},{9,11},{10,... | collective-permute-start | bytes 786440 | tf_op jit(solution)/shard_map/ppermute | solution.py:145
  24.1 2.0 %shard_map.87 = (f32[8,320,128]{2,1,0:T(8,128)S(1)}, f32[8,320,128]{2,1,0:T(8,128)S(1)}, f32[8,320,128]{2,1,0:T(8,128)S(1)}) custom-call(s32[3,128]{1,0:T(4,128)S(1)} %broadcast_in_dim.11.refs_0_, bf16[32,5120]{1,0:T(8,128)(2,1)S(1)} %copy-done, bf16[32,5120]{1,0:T(8,128)(2,1)S(1)} %bitcast.13, ...), custom_call_target="tpu_custom_call" | custom-call | flops 10066329600 | bytes 1572864 | tf_op jit(solution)/shard_map/pallas_call | solution.py:131
  26.2 4.8 %collective-permute-start.14 = (bf16[192,2048]{1,0:T(8,128)(2,1)S(1)}, bf16[192,2048]{1,0:T(8,128)(2,1)S(1)}, u32[]{:S(2)}, u32[]{:S(2)}) collective-permute-start(bf16[192,2048]{1,0:T(8,128)(2,1)S(1)} %constant_dynamic-update-slice_fusion.9.refs_3_), channel_id=1, source_target_pairs={{0,1},{1,0},{2,3},{3,2},{4,5},{5,4},{6,7},{7,6},{8,9},{9,8},{10,11... | collective-permute-start | bytes 2359304 | tf_op jit(solution)/shard_map/ppermute | solution.py:145
  31.1 3.3 %collective-permute-start.13 = (bf16[160,2048]{1,0:T(8,128)(2,1)S(1)}, bf16[160,2048]{1,0:T(8,128)(2,1)S(1)}, u32[]{:S(2)}, u32[]{:S(2)}) collective-permute-start(bf16[160,2048]{1,0:T(8,128)(2,1)S(1)} %constant_dynamic-update-slice_fusion.13.refs_5_), channel_id=1, source_target_pairs={{0,1},{1,0},{2,3},{3,2},{4,5},{5,4},{6,7},{7,6},{8,9},{9,8},{10,11... | collective-permute-start | bytes 1966088 | tf_op jit(solution)/shard_map/ppermute | solution.py:145
  34.4 2.2 %shard_map.88 = (f32[8,320,128]{2,1,0:T(8,128)S(1)}, f32[8,320,128]{2,1,0:T(8,128)S(1)}, f32[8,320,128]{2,1,0:T(8,128)S(1)}) custom-call(s32[3,128]{1,0:T(4,128)S(1)} %broadcast_in_dim.11.refs_0_, bf16[32,5120]{1,0:T(8,128)(2,1)S(1)} %copy-done, bf16[32,5120]{1,0:T(8,128)(2,1)S(1)} %bitcast.14, ...), custom_call_target="tpu_custom_call" | custom-call | flops 10066329600 | bytes 1572864 | tf_op jit(solution)/shard_map/pallas_call | solution.py:131
  36.6 2.4 %shard_map.89 = (bf16[32,5120]{1,0:T(8,128)(2,1)}, bf16[32,5120]{1,0:T(8,128)(2,1)}) custom-call(s32[3,128]{1,0:T(4,128)S(1)} %broadcast_in_dim.11.refs_0_, bf16[32,5120]{1,0:T(8,128)(2,1)S(1)} %copy-done, bf16[32,5120]{1,0:T(8,128)(2,1)S(1)} %bitcast.15, bf16[160,2048]{1,0:T(8,128)(2,1)S(1)} %collective-permute-done.13.refs_3_, ...), custom_call_target="tpu_custom_call" | custom-call | flops 6710886400 | bytes 1048576 | tf_op jit(solution)/shard_map/pallas_call | solution.py:131
  (34 shorter events, 0.3 us)
Async XLA Ops:
  0.6 15.0 %copy-start.2 = (bf16[1,32,2048]{2,1,0:T(8,128)(2,1)S(1)}, bf16[1,32,2048]{2,1,0:T(8,128)(2,1)}, u32[]{:S(2)}) copy-start(bf16[1,32,2048]{2,1,0:T(8,128)(2,1)} %param.10) | copy-start | bytes 393220
  0.6 15.0 %copy-start.1 = (bf16[1,32,5120]{2,1,0:T(8,128)(2,1)S(1)}, bf16[1,32,5120]{2,1,0:T(8,128)(2,1)}, u32[]{:S(2)}) copy-start(bf16[1,32,5120]{2,1,0:T(8,128)(2,1)} %param.9) | copy-start | bytes 983044
  0.7 15.0 %copy-start = (bf16[32,5120]{1,0:T(8,128)(2,1)S(1)}, bf16[32,5120]{1,0:T(8,128)(2,1)}, u32[]{:S(2)}) copy-start(bf16[32,5120]{1,0:T(8,128)(2,1)} %refs_1_.7) | copy-start | bytes 983044
  0.7 10.0 %collective-permute-start = (bf16[32,2048]{1,0:T(8,128)(2,1)}, bf16[32,2048]{1,0:T(8,128)(2,1)S(1)}, u32[]{:S(2)}, u32[]{:S(2)}) collective-permute-start(bf16[32,2048]{1,0:T(8,128)(2,1)} %param.8), channel_id=1, source_target_pairs={{0,8},{4,12},{8,0},{12,4},{16,24},{20,28},{24,16},{28,20},{1,9},{5... | collective-permute-start | bytes 393224 | tf_op jit(solution)/shard_map/ppermute | solution.py:145
  2.9 8.1 %collective-permute-start.1 = (bf16[32,2048]{1,0:T(8,128)(2,1)}, bf16[32,2048]{1,0:T(8,128)(2,1)S(1)}, u32[]{:S(2)}, u32[]{:S(2)}) collective-permute-start(bf16[32,2048]{1,0:T(8,128)(2,1)} %param.8), channel_id=1, source_target_pairs={{0,24},{4,28},{8,16},{12,20},{16,8},{20,12},{24,0},{28,4},{1,25},{... | collective-permute-start | bytes 393224 | tf_op jit(solution)/shard_map/ppermute | solution.py:145
  5.0 5.9 %collective-permute-start.2 = (bf16[32,2048]{1,0:T(8,128)(2,1)}, bf16[32,2048]{1,0:T(8,128)(2,1)S(1)}, u32[]{:S(2)}, u32[]{:S(2)}) collective-permute-start(bf16[32,2048]{1,0:T(8,128)(2,1)} %param.8), channel_id=1, source_target_pairs={{0,4},{4,0},{8,12},{12,8},{16,20},{20,16},{24,28},{28,24},{1,5},{5... | collective-permute-start | bytes 393224 | tf_op jit(solution)/shard_map/ppermute | solution.py:145
  6.3 4.7 %collective-permute-start.3 = (bf16[32,2048]{1,0:T(8,128)(2,1)}, bf16[32,2048]{1,0:T(8,128)(2,1)S(1)}, u32[]{:S(2)}, u32[]{:S(2)}) collective-permute-start(bf16[32,2048]{1,0:T(8,128)(2,1)} %param.8), channel_id=1, source_target_pairs={{0,2},{1,3},{2,0},{3,1},{4,6},{5,7},{6,4},{7,5},{8,10},{9,11},{10,... | collective-permute-start | bytes 393224 | tf_op jit(solution)/shard_map/ppermute | solution.py:145
  7.5 5.7 %collective-permute-start.4 = (bf16[32,2048]{1,0:T(8,128)(2,1)}, bf16[32,2048]{1,0:T(8,128)(2,1)S(1)}, u32[]{:S(2)}, u32[]{:S(2)}) collective-permute-start(bf16[32,2048]{1,0:T(8,128)(2,1)} %param.8), channel_id=1, source_target_pairs={{0,6},{1,7},{2,4},{3,5},{4,2},{5,3},{6,0},{7,1},{8,14},{9,15},{10,... | collective-permute-start | bytes 393224 | tf_op jit(solution)/shard_map/ppermute | solution.py:163
  13.4 7.8 %collective-permute-start.5 = (bf16[64,2048]{1,0:T(8,128)(2,1)S(1)}, bf16[64,2048]{1,0:T(8,128)(2,1)S(1)}, u32[]{:S(2)}, u32[]{:S(2)}) collective-permute-start(bf16[64,2048]{1,0:T(8,128)(2,1)S(1)} %get-tuple-element.79), channel_id=1, source_target_pairs={{0,4},{4,0},{8,12},{12,8},{16,20},{20,16},{24,28},{28,24},{1,5},{5... | collective-permute-start | bytes 786440 | tf_op jit(solution)/shard_map/ppermute | solution.py:145
  14.1 7.1 %collective-permute-start.6 = (bf16[64,2048]{1,0:T(8,128)(2,1)S(1)}, bf16[64,2048]{1,0:T(8,128)(2,1)S(1)}, u32[]{:S(2)}, u32[]{:S(2)}) collective-permute-start(bf16[64,2048]{1,0:T(8,128)(2,1)S(1)} %get-tuple-element.79), channel_id=1, source_target_pairs={{0,2},{1,3},{2,0},{3,1},{4,6},{5,7},{6,4},{7,5},{8,10},{9,11},{10,... | collective-permute-start | bytes 786440 | tf_op jit(solution)/shard_map/ppermute | solution.py:145
  14.6 5.7 %collective-permute-start.8 = (bf16[32,2048]{1,0:T(8,128)(2,1)S(1)}, bf16[32,2048]{1,0:T(8,128)(2,1)S(1)}, u32[]{:S(2)}, u32[]{:S(2)}) collective-permute-start(bf16[32,2048]{1,0:T(8,128)(2,1)S(1)} %collective-permute-done.4), channel_id=1, source_target_pairs={{0,24},{4,28},{8,16},{12,20},{16,8},{20,12},{24,0},{28,4},{1,25},{... | collective-permute-start | bytes 393224 | tf_op jit(solution)/shard_map/ppermute | solution.py:145
  15.7 5.5 %collective-permute-start.7 = (bf16[32,2048]{1,0:T(8,128)(2,1)S(1)}, bf16[32,2048]{1,0:T(8,128)(2,1)S(1)}, u32[]{:S(2)}, u32[]{:S(2)}) collective-permute-start(bf16[32,2048]{1,0:T(8,128)(2,1)S(1)} %collective-permute-done.1), channel_id=1, source_target_pairs={{0,8},{4,12},{8,0},{12,4},{16,24},{20,28},{24,16},{28,20},{1,9},{5... | collective-permute-start | bytes 393224 | tf_op jit(solution)/shard_map/ppermute | solution.py:145
  16.9 7.3 %collective-permute-start.12 = (bf16[224,2048]{1,0:T(8,128)(2,1)S(1)}, bf16[224,2048]{1,0:T(8,128)(2,1)S(1)}, u32[]{:S(2)}, u32[]{:S(2)}) collective-permute-start(bf16[224,2048]{1,0:T(8,128)(2,1)S(1)} %constant_dynamic-update-slice_fusion.2.refs_3_), channel_id=1, source_target_pairs={{0,1},{1,0},{2,3},{3,2},{4,5},{5,4},{6,7},{7,6},{8,9},{9,8},{10,11... | collective-permute-start | bytes 2752520 | tf_op jit(solution)/shard_map/ppermute | solution.py:145
  21.2 9.8 %collective-permute-start.11 = (bf16[64,2048]{1,0:T(8,128)(2,1)S(1)}, bf16[64,2048]{1,0:T(8,128)(2,1)S(1)}, u32[]{:S(2)}, u32[]{:S(2)}) collective-permute-start(bf16[64,2048]{1,0:T(8,128)(2,1)S(1)} %pad_maximum_fusion.1), channel_id=1, source_target_pairs={{0,8},{4,12},{8,0},{12,4},{16,24},{20,28},{24,16},{28,20},{1,9},{5... | collective-permute-start | bytes 786440 | tf_op jit(solution)/shard_map/ppermute | solution.py:145
  22.0 9.1 %collective-permute-start.9 = (bf16[32,2048]{1,0:T(8,128)(2,1)S(1)}, bf16[32,2048]{1,0:T(8,128)(2,1)S(1)}, u32[]{:S(2)}, u32[]{:S(2)}) collective-permute-start(bf16[32,2048]{1,0:T(8,128)(2,1)S(1)} %collective-permute-done.7), channel_id=1, source_target_pairs={{0,4},{4,0},{8,12},{12,8},{16,20},{20,16},{24,28},{28,24},{1,5},{5... | collective-permute-start | bytes 393224 | tf_op jit(solution)/shard_map/ppermute | solution.py:145
  23.3 7.7 %collective-permute-start.10 = (bf16[64,2048]{1,0:T(8,128)(2,1)S(1)}, bf16[64,2048]{1,0:T(8,128)(2,1)S(1)}, u32[]{:S(2)}, u32[]{:S(2)}) collective-permute-start(bf16[64,2048]{1,0:T(8,128)(2,1)S(1)} %pad_maximum_fusion), channel_id=1, source_target_pairs={{0,2},{1,3},{2,0},{3,1},{4,6},{5,7},{6,4},{7,5},{8,10},{9,11},{10,... | collective-permute-start | bytes 786440 | tf_op jit(solution)/shard_map/ppermute | solution.py:145
  26.2 8.2 %collective-permute-start.14 = (bf16[192,2048]{1,0:T(8,128)(2,1)S(1)}, bf16[192,2048]{1,0:T(8,128)(2,1)S(1)}, u32[]{:S(2)}, u32[]{:S(2)}) collective-permute-start(bf16[192,2048]{1,0:T(8,128)(2,1)S(1)} %constant_dynamic-update-slice_fusion.9.refs_3_), channel_id=1, source_target_pairs={{0,1},{1,0},{2,3},{3,2},{4,5},{5,4},{6,7},{7,6},{8,9},{9,8},{10,11... | collective-permute-start | bytes 2359304 | tf_op jit(solution)/shard_map/ppermute | solution.py:145
  31.1 5.5 %collective-permute-start.13 = (bf16[160,2048]{1,0:T(8,128)(2,1)S(1)}, bf16[160,2048]{1,0:T(8,128)(2,1)S(1)}, u32[]{:S(2)}, u32[]{:S(2)}) collective-permute-start(bf16[160,2048]{1,0:T(8,128)(2,1)S(1)} %constant_dynamic-update-slice_fusion.13.refs_5_), channel_id=1, source_target_pairs={{0,1},{1,0},{2,3},{3,2},{4,5},{5,4},{6,7},{7,6},{8,9},{9,8},{10,11... | collective-permute-start | bytes 1966088 | tf_op jit(solution)/shard_map/ppermute | solution.py:145

commit v11 on v10

--- a/solution.py
+++ b/solution.py
@@ -199,18 +199,18 @@
 
         near_x, near_y, far, third_d, state = barrier((near_x, near_y, far, third_d, state))
         far_y = across_y(jnp.concatenate([far, suffix_own], axis=0))
-        far_and_next_d = along_z(jnp.concatenate([third_d, own_d], axis=0), 1)
-        far_x = across_x(far)
+        far_x = across_x(jnp.concatenate([far, near_y[:rows]], axis=0))
+        far_d = along_z(third_d, 1)
         sides = jnp.concatenate([near_x, near_y, far, third_d], axis=0)
         near_here = [(1, 1, 0), (3, 1, 0), (1, 0, 1), (3, 0, 1), (2, 0, 0), (3, 1, 1)]
         state = absorb([(sides, 0, 6), (plane_sibling, 0, 6)], slots_of(near_here) + slots_of(here[:6], 1), state)
         sides, state = barrier((sides, state))
         sides_sibling = core(sides)
 
-        far_x, far_y, far_and_next_d, state = barrier((far_x, far_y, far_and_next_d, state))
-        rest = jnp.concatenate([far_x, far_y, far_and_next_d], axis=0)
+        far_x, far_y, far_d, state = barrier((far_x, far_y, far_d, state))
+        rest = jnp.concatenate([far_x, far_y, far_d], axis=0)
         rest_sibling = core(rest)
-        rest_here = [(2, 1, 0), (2, 0, 1), 2, (2, 1, 1), (1, 1, 1)]
+        rest_here = [(2, 1, 0), (1, 1, 1), (2, 0, 1), 2, (2, 1, 1)]
         state = absorb(
             [(plane_sibling, 6, 7), (sides_sibling, 0, 6), (rest, 0, 5)],
             slots_of(here[6:] + near_here, 1) + slots_of(rest_here),

time: 39.1 us -> 37.7 us (0.964)
  waiting for transfers between devices: 3.61 us -> 2.55 us
  starting transfers between devices: 23.5 us -> 23 us
    ppermute x14, waiting for transfers between devices: 1.39 us -> 0.33 us  [swap(): return lax.ppermute(array, axis, [(i, i ^ bit) for i in range(size)])]
    ppermute x14, starting transfers between devices: 23.4 us -> 22.8 us  [swap(): return lax.ppermute(array, axis, [(i, i ^ bit) for i in range(size)])]
  transfers between devices with their start and end apart: 15 -> 15, of which waited for: 4 -> 2; matrix products, arithmetic and copies ran while one was open for 3% -> 3% of each run, Pallas kernels for 14% -> 14%
where the time goes in v11:
time: 37.7 us; the launch traced here: 37.4 us
  starting transfers between devices  23 us (61%)
  Pallas kernels  7.71 us (20%)
  between operations  2.79 us (7%)
  waiting for transfers between devices  2.55 us (7%)
  local copies, waits for them, and re-layouts  1.23 us (3%)
    ppermute x14, starting transfers between devices, swap(): return lax.ppermute(array, axis, [(i, i ^ bit) for i in range(size)])  22.8 us
    pallas_call x4, Pallas kernels, attend(): pl.pallas_call(functools.partial(attend_kernel, slots, ranges, tp_size, f...  7.71 us
    ppermute x1, waiting for transfers between devices, local(): lax.ppermute(a, ('ctx', 'tp'), [(i * tp_size + j, (i ^ 1) * tp_size + (j...  2.22 us
    unnamed x17, local copies, waits for them, and re-layouts  1.12 us
  transfers between devices with their start and end apart: 15, of which 2 were waited for; matrix products, arithmetic and copies ran while one was open for 3% of the time, Pallas kernels for 14%

profile of v11, /device:TPU:1, one launch (start us, length us, event | category | flops | bytes accessed | tf_op | source)
XLA Modules:
  0.0 37.4 jit_solution(14003912933141342098)
XLA Ops:
  0.7 2.2 %collective-permute-start = (bf16[32,2048]{1,0:T(8,128)(2,1)}, bf16[32,2048]{1,0:T(8,128)(2,1)S(1)}, u32[]{:S(2)}, u32[]{:S(2)}) collective-permute-start(bf16[32,2048]{1,0:T(8,128)(2,1)} %param.8), channel_id=1, source_target_pairs={{0,8},{4,12},{8,0},{12,4},{16,24},{20,28},{24,16},{28,20},{1,9},{5... | collective-permute-start | bytes 393224 | tf_op jit(solution)/shard_map/ppermute | solution.py:145
  2.9 2.2 %collective-permute-start.1 = (bf16[32,2048]{1,0:T(8,128)(2,1)}, bf16[32,2048]{1,0:T(8,128)(2,1)S(1)}, u32[]{:S(2)}, u32[]{:S(2)}) collective-permute-start(bf16[32,2048]{1,0:T(8,128)(2,1)} %param.8), channel_id=1, source_target_pairs={{0,24},{4,28},{8,16},{12,20},{16,8},{20,12},{24,0},{28,4},{1,25},{... | collective-permute-start | bytes 393224 | tf_op jit(solution)/shard_map/ppermute | solution.py:145
  5.0 1.2 %collective-permute-start.2 = (bf16[32,2048]{1,0:T(8,128)(2,1)}, bf16[32,2048]{1,0:T(8,128)(2,1)S(1)}, u32[]{:S(2)}, u32[]{:S(2)}) collective-permute-start(bf16[32,2048]{1,0:T(8,128)(2,1)} %param.8), channel_id=1, source_target_pairs={{0,4},{4,0},{8,12},{12,8},{16,20},{20,16},{24,28},{28,24},{1,5},{5... | collective-permute-start | bytes 393224 | tf_op jit(solution)/shard_map/ppermute | solution.py:145
  6.3 1.2 %collective-permute-start.3 = (bf16[32,2048]{1,0:T(8,128)(2,1)}, bf16[32,2048]{1,0:T(8,128)(2,1)S(1)}, u32[]{:S(2)}, u32[]{:S(2)}) collective-permute-start(bf16[32,2048]{1,0:T(8,128)(2,1)} %param.8), channel_id=1, source_target_pairs={{0,2},{1,3},{2,0},{3,1},{4,6},{5,7},{6,4},{7,5},{8,10},{9,11},{10,... | collective-permute-start | bytes 393224 | tf_op jit(solution)/shard_map/ppermute | solution.py:145
  7.5 0.2 collective-permute-start.4
  7.7 0.9 %constant_dynamic-update-slice_fusion.8 = bf16[224,2048]{1,0:T(8,128)(2,1)S(1)} fusion(bf16[32,2048]{1,0:T(8,128)(2,1)} %param.8), kind=kLoop, calls=%fused_computation.10 | loop fusion | bytes 262144
  10.6 0.1 add_bitcast_fusion
  10.7 0.3 collective-permute-done.1
  11.0 2.2 %collective-permute-done.4 = bf16[32,2048]{1,0:T(8,128)(2,1)S(1)} collective-permute-done((bf16[32,2048]{1,0:T(8,128)(2,1)}, bf16[32,2048]{1,0:T(8,128)(2,1)S(1)}, u32[]{:S(2)}, u32[]{:S(2)}) %collective-permute-start.4) | collective-permute-done | bytes 131104 | tf_op jit(solution)/shard_map/ppermute | solution.py:163
  13.2 0.1 broadcast_in_dim.11.refs_0_
  13.4 0.7 %collective-permute-start.5 = (bf16[64,2048]{1,0:T(8,128)(2,1)S(1)}, bf16[64,2048]{1,0:T(8,128)(2,1)S(1)}, u32[]{:S(2)}, u32[]{:S(2)}) collective-permute-start(bf16[64,2048]{1,0:T(8,128)(2,1)S(1)} %get-tuple-element.81), channel_id=1, source_target_pairs={{0,4},{4,0},{8,12},{12,8},{16,20},{20,16},{24,28},{28,24},{1,5},{5... | collective-permute-start | bytes 786440 | tf_op jit(solution)/shard_map/ppermute | solution.py:145
  14.1 0.5 %collective-permute-start.6 = (bf16[64,2048]{1,0:T(8,128)(2,1)S(1)}, bf16[64,2048]{1,0:T(8,128)(2,1)S(1)}, u32[]{:S(2)}, u32[]{:S(2)}) collective-permute-start(bf16[64,2048]{1,0:T(8,128)(2,1)S(1)} %get-tuple-element.81), channel_id=1, source_target_pairs={{0,2},{1,3},{2,0},{3,1},{4,6},{5,7},{6,4},{7,5},{8,10},{9,11},{10,... | collective-permute-start | bytes 786440 | tf_op jit(solution)/shard_map/ppermute | solution.py:145
  14.6 0.1 collective-permute-start.7
  14.7 1.7 %collective-permute-start.8 = (bf16[32,2048]{1,0:T(8,128)(2,1)S(1)}, bf16[32,2048]{1,0:T(8,128)(2,1)S(1)}, u32[]{:S(2)}, u32[]{:S(2)}) collective-permute-start(bf16[32,2048]{1,0:T(8,128)(2,1)S(1)} %collective-permute-done.4), channel_id=1, source_target_pairs={{0,24},{4,28},{8,16},{12,20},{16,8},{20,12},{24,0},{28,4},{1,25},{... | collective-permute-start | bytes 393224 | tf_op jit(solution)/shard_map/ppermute | solution.py:145
  16.5 1.1 %shard_map.86 = (f32[8,320,128]{2,1,0:T(8,128)S(1)}, f32[8,320,128]{2,1,0:T(8,128)S(1)}, f32[8,320,128]{2,1,0:T(8,128)S(1)}) custom-call(s32[3,128]{1,0:T(4,128)S(1)} %broadcast_in_dim.11.refs_0_, bf16[32,5120]{1,0:T(8,128)(2,1)S(1)} %copy-done, bf16[32,5120]{1,0:T(8,128)(2,1)S(1)} %bitcast.12, bf16[224,2048]{1,0:T(8,128)(2,1)S(1)} %constant_dynamic-update-slice_fusion.2.refs_3_), custom_call_target="tpu_custom_call" | custom-call | flops 6710886400 | bytes 1048576 | tf_op jit(solution)/shard_map/pallas_call | solution.py:131
  17.6 3.0 %collective-permute-start.12 = (bf16[224,2048]{1,0:T(8,128)(2,1)S(1)}, bf16[224,2048]{1,0:T(8,128)(2,1)S(1)}, u32[]{:S(2)}, u32[]{:S(2)}) collective-permute-start(bf16[224,2048]{1,0:T(8,128)(2,1)S(1)} %constant_dynamic-update-slice_fusion.2.refs_3_), channel_id=1, source_target_pairs={{0,1},{1,0},{2,3},{3,2},{4,5},{5,4},{6,7},{7,6},{8,9},{9,8},{10,11... | collective-permute-start | bytes 2752520 | tf_op jit(solution)/shard_map/ppermute | solution.py:145
  20.7 1.5 %collective-permute-start.10 = (bf16[64,2048]{1,0:T(8,128)(2,1)S(1)}, bf16[64,2048]{1,0:T(8,128)(2,1)S(1)}, u32[]{:S(2)}, u32[]{:S(2)}) collective-permute-start(bf16[64,2048]{1,0:T(8,128)(2,1)S(1)} %get-tuple-element.78), channel_id=1, source_target_pairs={{0,2},{1,3},{2,0},{3,1},{4,6},{5,7},{6,4},{7,5},{8,10},{9,11},{10,... | collective-permute-start | bytes 786440 | tf_op jit(solution)/shard_map/ppermute | solution.py:145
  22.2 0.8 %collective-permute-start.9 = (bf16[64,2048]{1,0:T(8,128)(2,1)S(1)}, bf16[64,2048]{1,0:T(8,128)(2,1)S(1)}, u32[]{:S(2)}, u32[]{:S(2)}) collective-permute-start(bf16[64,2048]{1,0:T(8,128)(2,1)S(1)} %get-tuple-element.79), channel_id=1, source_target_pairs={{0,4},{4,0},{8,12},{12,8},{16,20},{20,16},{24,28},{28,24},{1,5},{5... | collective-permute-start | bytes 786440 | tf_op jit(solution)/shard_map/ppermute | solution.py:145
  23.0 0.4 %collective-permute-start.11 = (bf16[32,2048]{1,0:T(8,128)(2,1)S(1)}, bf16[32,2048]{1,0:T(8,128)(2,1)S(1)}, u32[]{:S(2)}, u32[]{:S(2)}) collective-permute-start(bf16[32,2048]{1,0:T(8,128)(2,1)S(1)} %collective-permute-done.8), channel_id=1, source_target_pairs={{0,8},{4,12},{8,0},{12,4},{16,24},{20,28},{24,16},{28,20},{1,9},{5... | collective-permute-start | bytes 393224 | tf_op jit(solution)/shard_map/ppermute | solution.py:145
  23.5 2.1 %shard_map.87 = (f32[8,320,128]{2,1,0:T(8,128)S(1)}, f32[8,320,128]{2,1,0:T(8,128)S(1)}, f32[8,320,128]{2,1,0:T(8,128)S(1)}) custom-call(s32[3,128]{1,0:T(4,128)S(1)} %broadcast_in_dim.11.refs_0_, bf16[32,5120]{1,0:T(8,128)(2,1)S(1)} %copy-done, bf16[32,5120]{1,0:T(8,128)(2,1)S(1)} %bitcast.13, ...), custom_call_target="tpu_custom_call" | custom-call | flops 10066329600 | bytes 1572864 | tf_op jit(solution)/shard_map/pallas_call | solution.py:131
  25.6 5.3 %collective-permute-start.14 = (bf16[192,2048]{1,0:T(8,128)(2,1)S(1)}, bf16[192,2048]{1,0:T(8,128)(2,1)S(1)}, u32[]{:S(2)}, u32[]{:S(2)}) collective-permute-start(bf16[192,2048]{1,0:T(8,128)(2,1)S(1)} %constant_dynamic-update-slice_fusion.9.refs_3_), channel_id=1, source_target_pairs={{0,1},{1,0},{2,3},{3,2},{4,5},{5,4},{6,7},{7,6},{8,9},{9,8},{10,11... | collective-permute-start | bytes 2359304 | tf_op jit(solution)/shard_map/ppermute | solution.py:145
  30.9 2.0 %collective-permute-start.13 = (bf16[160,2048]{1,0:T(8,128)(2,1)S(1)}, bf16[160,2048]{1,0:T(8,128)(2,1)S(1)}, u32[]{:S(2)}, u32[]{:S(2)}) collective-permute-start(bf16[160,2048]{1,0:T(8,128)(2,1)S(1)} %constant_dynamic-update-slice_fusion.13.refs_5_), channel_id=1, source_target_pairs={{0,1},{1,0},{2,3},{3,2},{4,5},{5,4},{6,7},{7,6},{8,9},{9,8},{10,11... | collective-permute-start | bytes 1966088 | tf_op jit(solution)/shard_map/ppermute | solution.py:145
  32.9 2.1 %shard_map.88 = (f32[8,320,128]{2,1,0:T(8,128)S(1)}, f32[8,320,128]{2,1,0:T(8,128)S(1)}, f32[8,320,128]{2,1,0:T(8,128)S(1)}) custom-call(s32[3,128]{1,0:T(4,128)S(1)} %broadcast_in_dim.11.refs_0_, bf16[32,5120]{1,0:T(8,128)(2,1)S(1)} %copy-done, bf16[32,5120]{1,0:T(8,128)(2,1)S(1)} %bitcast.14, ...), custom_call_target="tpu_custom_call" | custom-call | flops 10066329600 | bytes 1572864 | tf_op jit(solution)/shard_map/pallas_call | solution.py:131
  35.1 2.4 %shard_map.89 = (bf16[32,5120]{1,0:T(8,128)(2,1)}, bf16[32,5120]{1,0:T(8,128)(2,1)}) custom-call(s32[3,128]{1,0:T(4,128)S(1)} %broadcast_in_dim.11.refs_0_, bf16[32,5120]{1,0:T(8,128)(2,1)S(1)} %copy-done, bf16[32,5120]{1,0:T(8,128)(2,1)S(1)} %bitcast.15, bf16[160,2048]{1,0:T(8,128)(2,1)S(1)} %collective-permute-done.13.refs_3_, ...), custom_call_target="tpu_custom_call" | custom-call | flops 6710886400 | bytes 1048576 | tf_op jit(solution)/shard_map/pallas_call | solution.py:131
  (34 shorter events, 0.3 us)
Async XLA Ops:
  0.6 15.8 %copy-start.2 = (bf16[1,32,2048]{2,1,0:T(8,128)(2,1)S(1)}, bf16[1,32,2048]{2,1,0:T(8,128)(2,1)}, u32[]{:S(2)}) copy-start(bf16[1,32,2048]{2,1,0:T(8,128)(2,1)} %param.10) | copy-start | bytes 393220
  0.6 15.8 %copy-start.1 = (bf16[1,32,5120]{2,1,0:T(8,128)(2,1)S(1)}, bf16[1,32,5120]{2,1,0:T(8,128)(2,1)}, u32[]{:S(2)}) copy-start(bf16[1,32,5120]{2,1,0:T(8,128)(2,1)} %param.9) | copy-start | bytes 983044
  0.7 15.8 %copy-start = (bf16[32,5120]{1,0:T(8,128)(2,1)S(1)}, bf16[32,5120]{1,0:T(8,128)(2,1)}, u32[]{:S(2)}) copy-start(bf16[32,5120]{1,0:T(8,128)(2,1)} %refs_1_.7) | copy-start | bytes 983044
  0.7 10.0 %collective-permute-start = (bf16[32,2048]{1,0:T(8,128)(2,1)}, bf16[32,2048]{1,0:T(8,128)(2,1)S(1)}, u32[]{:S(2)}, u32[]{:S(2)}) collective-permute-start(bf16[32,2048]{1,0:T(8,128)(2,1)} %param.8), channel_id=1, source_target_pairs={{0,8},{4,12},{8,0},{12,4},{16,24},{20,28},{24,16},{28,20},{1,9},{5... | collective-permute-start | bytes 393224 | tf_op jit(solution)/shard_map/ppermute | solution.py:145
  2.9 8.1 %collective-permute-start.1 = (bf16[32,2048]{1,0:T(8,128)(2,1)}, bf16[32,2048]{1,0:T(8,128)(2,1)S(1)}, u32[]{:S(2)}, u32[]{:S(2)}) collective-permute-start(bf16[32,2048]{1,0:T(8,128)(2,1)} %param.8), channel_id=1, source_target_pairs={{0,24},{4,28},{8,16},{12,20},{16,8},{20,12},{24,0},{28,4},{1,25},{... | collective-permute-start | bytes 393224 | tf_op jit(solution)/shard_map/ppermute | solution.py:145
  5.0 5.9 %collective-permute-start.2 = (bf16[32,2048]{1,0:T(8,128)(2,1)}, bf16[32,2048]{1,0:T(8,128)(2,1)S(1)}, u32[]{:S(2)}, u32[]{:S(2)}) collective-permute-start(bf16[32,2048]{1,0:T(8,128)(2,1)} %param.8), channel_id=1, source_target_pairs={{0,4},{4,0},{8,12},{12,8},{16,20},{20,16},{24,28},{28,24},{1,5},{5... | collective-permute-start | bytes 393224 | tf_op jit(solution)/shard_map/ppermute | solution.py:145
  6.3 4.7 %collective-permute-start.3 = (bf16[32,2048]{1,0:T(8,128)(2,1)}, bf16[32,2048]{1,0:T(8,128)(2,1)S(1)}, u32[]{:S(2)}, u32[]{:S(2)}) collective-permute-start(bf16[32,2048]{1,0:T(8,128)(2,1)} %param.8), channel_id=1, source_target_pairs={{0,2},{1,3},{2,0},{3,1},{4,6},{5,7},{6,4},{7,5},{8,10},{9,11},{10,... | collective-permute-start | bytes 393224 | tf_op jit(solution)/shard_map/ppermute | solution.py:145
  7.5 5.7 %collective-permute-start.4 = (bf16[32,2048]{1,0:T(8,128)(2,1)}, bf16[32,2048]{1,0:T(8,128)(2,1)S(1)}, u32[]{:S(2)}, u32[]{:S(2)}) collective-permute-start(bf16[32,2048]{1,0:T(8,128)(2,1)} %param.8), channel_id=1, source_target_pairs={{0,6},{1,7},{2,4},{3,5},{4,2},{5,3},{6,0},{7,1},{8,14},{9,15},{10,... | collective-permute-start | bytes 393224 | tf_op jit(solution)/shard_map/ppermute | solution.py:163
  13.4 7.3 %collective-permute-start.5 = (bf16[64,2048]{1,0:T(8,128)(2,1)S(1)}, bf16[64,2048]{1,0:T(8,128)(2,1)S(1)}, u32[]{:S(2)}, u32[]{:S(2)}) collective-permute-start(bf16[64,2048]{1,0:T(8,128)(2,1)S(1)} %get-tuple-element.81), channel_id=1, source_target_pairs={{0,4},{4,0},{8,12},{12,8},{16,20},{20,16},{24,28},{28,24},{1,5},{5... | collective-permute-start | bytes 786440 | tf_op jit(solution)/shard_map/ppermute | solution.py:145
  14.1 6.6 %collective-permute-start.6 = (bf16[64,2048]{1,0:T(8,128)(2,1)S(1)}, bf16[64,2048]{1,0:T(8,128)(2,1)S(1)}, u32[]{:S(2)}, u32[]{:S(2)}) collective-permute-start(bf16[64,2048]{1,0:T(8,128)(2,1)S(1)} %get-tuple-element.81), channel_id=1, source_target_pairs={{0,2},{1,3},{2,0},{3,1},{4,6},{5,7},{6,4},{7,5},{8,10},{9,11},{10,... | collective-permute-start | bytes 786440 | tf_op jit(solution)/shard_map/ppermute | solution.py:145
  14.6 6.0 %collective-permute-start.7 = (bf16[32,2048]{1,0:T(8,128)(2,1)S(1)}, bf16[32,2048]{1,0:T(8,128)(2,1)S(1)}, u32[]{:S(2)}, u32[]{:S(2)}) collective-permute-start(bf16[32,2048]{1,0:T(8,128)(2,1)S(1)} %collective-permute-done.1), channel_id=1, source_target_pairs={{0,8},{4,12},{8,0},{12,4},{16,24},{20,28},{24,16},{28,20},{1,9},{5... | collective-permute-start | bytes 393224 | tf_op jit(solution)/shard_map/ppermute | solution.py:145
  14.7 5.9 %collective-permute-start.8 = (bf16[32,2048]{1,0:T(8,128)(2,1)S(1)}, bf16[32,2048]{1,0:T(8,128)(2,1)S(1)}, u32[]{:S(2)}, u32[]{:S(2)}) collective-permute-start(bf16[32,2048]{1,0:T(8,128)(2,1)S(1)} %collective-permute-done.4), channel_id=1, source_target_pairs={{0,24},{4,28},{8,16},{12,20},{16,8},{20,12},{24,0},{28,4},{1,25},{... | collective-permute-start | bytes 393224 | tf_op jit(solution)/shard_map/ppermute | solution.py:145
  17.6 5.9 %collective-permute-start.12 = (bf16[224,2048]{1,0:T(8,128)(2,1)S(1)}, bf16[224,2048]{1,0:T(8,128)(2,1)S(1)}, u32[]{:S(2)}, u32[]{:S(2)}) collective-permute-start(bf16[224,2048]{1,0:T(8,128)(2,1)S(1)} %constant_dynamic-update-slice_fusion.2.refs_3_), channel_id=1, source_target_pairs={{0,1},{1,0},{2,3},{3,2},{4,5},{5,4},{6,7},{7,6},{8,9},{9,8},{10,11... | collective-permute-start | bytes 2752520 | tf_op jit(solution)/shard_map/ppermute | solution.py:145
  20.7 10.1 %collective-permute-start.10 = (bf16[64,2048]{1,0:T(8,128)(2,1)S(1)}, bf16[64,2048]{1,0:T(8,128)(2,1)S(1)}, u32[]{:S(2)}, u32[]{:S(2)}) collective-permute-start(bf16[64,2048]{1,0:T(8,128)(2,1)S(1)} %get-tuple-element.78), channel_id=1, source_target_pairs={{0,2},{1,3},{2,0},{3,1},{4,6},{5,7},{6,4},{7,5},{8,10},{9,11},{10,... | collective-permute-start | bytes 786440 | tf_op jit(solution)/shard_map/ppermute | solution.py:145
  22.2 8.7 %collective-permute-start.9 = (bf16[64,2048]{1,0:T(8,128)(2,1)S(1)}, bf16[64,2048]{1,0:T(8,128)(2,1)S(1)}, u32[]{:S(2)}, u32[]{:S(2)}) collective-permute-start(bf16[64,2048]{1,0:T(8,128)(2,1)S(1)} %get-tuple-element.79), channel_id=1, source_target_pairs={{0,4},{4,0},{8,12},{12,8},{16,20},{20,16},{24,28},{28,24},{1,5},{5... | collective-permute-start | bytes 786440 | tf_op jit(solution)/shard_map/ppermute | solution.py:145
  23.0 7.8 %collective-permute-start.11 = (bf16[32,2048]{1,0:T(8,128)(2,1)S(1)}, bf16[32,2048]{1,0:T(8,128)(2,1)S(1)}, u32[]{:S(2)}, u32[]{:S(2)}) collective-permute-start(bf16[32,2048]{1,0:T(8,128)(2,1)S(1)} %collective-permute-done.8), channel_id=1, source_target_pairs={{0,8},{4,12},{8,0},{12,4},{16,24},{20,28},{24,16},{28,20},{1,9},{5... | collective-permute-start | bytes 393224 | tf_op jit(solution)/shard_map/ppermute | solution.py:145
  25.6 7.4 %collective-permute-start.14 = (bf16[192,2048]{1,0:T(8,128)(2,1)S(1)}, bf16[192,2048]{1,0:T(8,128)(2,1)S(1)}, u32[]{:S(2)}, u32[]{:S(2)}) collective-permute-start(bf16[192,2048]{1,0:T(8,128)(2,1)S(1)} %constant_dynamic-update-slice_fusion.9.refs_3_), channel_id=1, source_target_pairs={{0,1},{1,0},{2,3},{3,2},{4,5},{5,4},{6,7},{7,6},{8,9},{9,8},{10,11... | collective-permute-start | bytes 2359304 | tf_op jit(solution)/shard_map/ppermute | solution.py:145
  30.9 4.1 %collective-permute-start.13 = (bf16[160,2048]{1,0:T(8,128)(2,1)S(1)}, bf16[160,2048]{1,0:T(8,128)(2,1)S(1)}, u32[]{:S(2)}, u32[]{:S(2)}) collective-permute-start(bf16[160,2048]{1,0:T(8,128)(2,1)S(1)} %constant_dynamic-update-slice_fusion.13.refs_5_), channel_id=1, source_target_pairs={{0,1},{1,0},{2,3},{3,2},{4,5},{5,4},{6,7},{7,6},{8,9},{9,8},{10,11... | collective-permute-start | bytes 1966088 | tf_op jit(solution)/shard_map/ppermute | solution.py:145

commit v12 on v11

--- a/solution.py
+++ b/solution.py
@@ -31,6 +31,9 @@
     refs = list(refs)
     spans, tq, sq = refs[:3]
     del refs[:3]
+    if last_call:
+        stage, sems = refs[-2:]
+        del refs[-2:]
     k_aug_ref = refs.pop()
     outs, refs = (refs[-2:], refs[:-2]) if last_call else (refs[-3:], refs[:-3])
     if not first_call:
@@ -100,17 +103,27 @@
             inverse = pl.reciprocal(denominator, approx=True)
             inverse = inverse * (2.0 - denominator * inverse)
             result = (summed * inverse).astype(jnp.bfloat16)
-            for j in range(GROUP):
-                outs[0][:, columns(g * GROUP + j)] = result[j * rows:(j + 1) * rows]
-                outs[1][:, columns(g * GROUP + j)] = result[half + j * rows:half + (j + 1) * rows]
+            for side in range(2):
+                for j in range(GROUP):
+                    start = (side * GROUP + j) * rows
+                    stage[side, :, columns(g * GROUP + j)] = result[start:start + rows]
+                output_copy(side, g).start()
         else:
             for out, state in zip(outs, (top, denominator, summed)):
                 out[g] = state
+
+    def output_copy(side, g):
+        group = pl.ds(g * GROUP * HEAD_SIZE, GROUP * HEAD_SIZE)
+        return pltpu.make_async_copy(stage.at[side, :, group], outs[side].at[:, group], sems.at[side, g])
 
     ahead = scores_of(0)
     for g in range(KEY_VALUE_HEADS):
         now, ahead = ahead, scores_of(g + 1) if g + 1 < KEY_VALUE_HEADS else None
         absorb_head(g, now)
+    if last_call:
+        for g in range(KEY_VALUE_HEADS):
+            for side in range(2):
+                output_copy(side, g).wait()
 
 
 def attend(spans, tq, sq, pieces, slots, tp_size, carry, last_call):
@@ -122,9 +135,13 @@
         operands += list(carry)
     if last_call:
         out_shape = [jax.ShapeDtypeStruct(tq.shape, jnp.bfloat16)] * 2
+        out_specs = [pl.BlockSpec(memory_space=pl.ANY)] * 2
+        scratch = [pltpu.VMEM((2, *tq.shape), jnp.bfloat16), pltpu.SemaphoreType.DMA((2, KEY_VALUE_HEADS))]
     else:
         state = (KEY_VALUE_HEADS, 2 * GROUP * rows, HEAD_SIZE)
         out_shape = [jax.ShapeDtypeStruct(state, jnp.float32)] * 3
+        out_specs = [vmem] * 3
+        scratch = []
     ranges = tuple((first * rows, last * rows) for _, first, last in pieces)
     all_rows = pl.cdiv(sum(stop - start for start, stop in ranges), HEAD_SIZE) * HEAD_SIZE
     flops = 2 * 2 * QUERY_HEADS * rows * all_rows * PAIR * 2
@@ -132,8 +149,8 @@
         functools.partial(attend_kernel, slots, ranges, tp_size, first_call, last_call),
         out_shape=out_shape,
         in_specs=[vmem] * len(operands),
-        out_specs=[vmem] * len(out_shape),
-        scratch_shapes=[pltpu.VMEM((all_rows, HEAD_SIZE), jnp.bfloat16)],
+        out_specs=out_specs,
+        scratch_shapes=[pltpu.VMEM((all_rows, HEAD_SIZE), jnp.bfloat16), *scratch],
         compiler_params=pltpu.CompilerParams(vmem_limit_bytes=32 * 1024 * 1024),
         cost_estimate=pl.CostEstimate(
             flops=COST_FACTOR * flops, bytes_accessed=all_rows * 4096, transcendentals=2 * QUERY_HEADS * rows * all_rows
@@ -186,7 +203,7 @@
         next_z, third_z = along_z(trace_key_value, 1), along_z(trace_key_value, 3)
         own_x, own_y = across_x(trace_key_value), across_y(trace_key_value)
         own_d = across_both(trace_key_value)
-        next_z, third_z, own_x, own_y, own_d, spans = barrier((next_z, third_z, own_x, own_y, own_d, spans))
+        own_d, third_z, next_z, own_y, own_x, spans = barrier((own_d, third_z, next_z, own_y, own_x, spans))
 
         near = jnp.concatenate([next_z, third_z], axis=0)
         far, third_d = along_z(third_z, 1), along_z(own_d, 3)

time: 37.7 us -> 37.5 us (level)
  starting transfers between devices: 23 us -> 20.7 us
  waiting for transfers between devices: 2.55 us -> 4.72 us
    ppermute x14, starting transfers between devices: 22.8 us -> 17.6 us  [swap(): return lax.ppermute(array, axis, [(i, i ^ bit) for i in range(size)])]
    ppermute x14, waiting for transfers between devices: 0.33 us -> 4.72 us  [swap(): return lax.ppermute(array, axis, [(i, i ^ bit) for i in range(size)])]
    ppermute x1, starting transfers between devices: 0.2 us -> 3.06 us  [local(): lax.ppermute(a, ('ctx', 'tp'), [(i * tp_size + j, (i ^ 1) * tp_size + (j...]
    ppermute x1, waiting for transfers between devices: 2.22 us -> 0.01 us  [local(): lax.ppermute(a, ('ctx', 'tp'), [(i * tp_size + j, (i ^ 1) * tp_size + (j...]
where the time goes in v12:
time: 37.5 us; the launch traced here: 37.2 us
  starting transfers between devices  20.7 us (55%)
  Pallas kernels  7.7 us (21%)
  waiting for transfers between devices  4.72 us (13%)
  between operations  2.78 us (7%)
  local copies, waits for them, and re-layouts  1.23 us (3%)
    ppermute x14, starting transfers between devices, swap(): return lax.ppermute(array, axis, [(i, i ^ bit) for i in range(size)])  17.6 us
    pallas_call x4, Pallas kernels, attend(): pl.pallas_call(functools.partial(attend_kernel, slots, ranges, tp_size, f...  7.7 us
    ppermute x14, waiting for transfers between devices, swap(): return lax.ppermute(array, axis, [(i, i ^ bit) for i in range(size)])  4.72 us
    ppermute x1, starting transfers between devices, local(): lax.ppermute(a, ('ctx', 'tp'), [(i * tp_size + j, (i ^ 1) * tp_size + (j...  3.06 us
    unnamed x17, local copies, waits for them, and re-layouts  1.12 us
  transfers between devices with their start and end apart: 15, of which 2 were waited for; matrix products, arithmetic and copies ran while one was open for 3% of the time, Pallas kernels for 14%

profile of v12, /device:TPU:1, one launch (start us, length us, event | category | flops | bytes accessed | tf_op | source)
XLA Modules:
  0.0 37.2 jit_solution(11336951876123611392)
XLA Ops:
  0.7 3.1 %collective-permute-start = (bf16[32,2048]{1,0:T(8,128)(2,1)}, bf16[32,2048]{1,0:T(8,128)(2,1)S(1)}, u32[]{:S(2)}, u32[]{:S(2)}) collective-permute-start(bf16[32,2048]{1,0:T(8,128)(2,1)} %param.8), channel_id=1, source_target_pairs={{0,6},{1,7},{2,4},{3,5},{4,2},{5,3},{6,0},{7,1},{8,14},{9,15},{10,... | collective-permute-start | bytes 393224 | tf_op jit(solution)/shard_map/ppermute | solution.py:180
  3.7 3.3 %collective-permute-start.1 = (bf16[32,2048]{1,0:T(8,128)(2,1)}, bf16[32,2048]{1,0:T(8,128)(2,1)S(1)}, u32[]{:S(2)}, u32[]{:S(2)}) collective-permute-start(bf16[32,2048]{1,0:T(8,128)(2,1)} %param.8), channel_id=1, source_target_pairs={{0,24},{4,28},{8,16},{12,20},{16,8},{20,12},{24,0},{28,4},{1,25},{... | collective-permute-start | bytes 393224 | tf_op jit(solution)/shard_map/ppermute | solution.py:162
  7.0 0.0 collective-permute-start.2
  7.0 0.2 collective-permute-start.3
  7.3 0.3 collective-permute-start.4
  7.5 0.9 %constant_dynamic-update-slice_fusion.8 = bf16[224,2048]{1,0:T(8,128)(2,1)S(1)} fusion(bf16[32,2048]{1,0:T(8,128)(2,1)} %param.8), kind=kLoop, calls=%fused_computation.10 | loop fusion | bytes 262144
  10.4 0.1 add_bitcast_fusion
  10.5 0.0 collective-permute-done
  10.5 2.9 %collective-permute-done.2 = bf16[32,2048]{1,0:T(8,128)(2,1)S(1)} collective-permute-done((bf16[32,2048]{1,0:T(8,128)(2,1)}, bf16[32,2048]{1,0:T(8,128)(2,1)S(1)}, u32[]{:S(2)}, u32[]{:S(2)}) %collective-permute-start.2) | collective-permute-done | bytes 131104 | tf_op jit(solution)/shard_map/ppermute | solution.py:162
  13.5 0.1 broadcast_in_dim.11.refs_0_
  13.6 0.3 collective-permute-start.5
  14.0 0.3 collective-permute-start.6
  14.3 0.6 %collective-permute-start.7 = (bf16[32,2048]{1,0:T(8,128)(2,1)S(1)}, bf16[32,2048]{1,0:T(8,128)(2,1)S(1)}, u32[]{:S(2)}, u32[]{:S(2)}) collective-permute-start(bf16[32,2048]{1,0:T(8,128)(2,1)S(1)} %collective-permute-done.1), channel_id=1, source_target_pairs={{0,8},{4,12},{8,0},{12,4},{16,24},{20,28},{24,16},{28,20},{1,9},{5... | collective-permute-start | bytes 393224 | tf_op jit(solution)/shard_map/ppermute | solution.py:162
  14.9 2.0 %collective-permute-start.8 = (bf16[32,2048]{1,0:T(8,128)(2,1)S(1)}, bf16[32,2048]{1,0:T(8,128)(2,1)S(1)}, u32[]{:S(2)}, u32[]{:S(2)}) collective-permute-start(bf16[32,2048]{1,0:T(8,128)(2,1)S(1)} %collective-permute-done), channel_id=1, source_target_pairs={{0,24},{4,28},{8,16},{12,20},{16,8},{20,12},{24,0},{28,4},{1,25},{... | collective-permute-start | bytes 393224 | tf_op jit(solution)/shard_map/ppermute | solution.py:162
  16.9 1.1 %shard_map.86 = (f32[8,320,128]{2,1,0:T(8,128)S(1)}, f32[8,320,128]{2,1,0:T(8,128)S(1)}, f32[8,320,128]{2,1,0:T(8,128)S(1)}) custom-call(s32[3,128]{1,0:T(4,128)S(1)} %broadcast_in_dim.11.refs_0_, bf16[32,5120]{1,0:T(8,128)(2,1)S(1)} %copy-done, bf16[32,5120]{1,0:T(8,128)(2,1)S(1)} %bitcast.12, bf16[224,2048]{1,0:T(8,128)(2,1)S(1)} %constant_dynamic-update-slice_fusion.2.refs_3_), custom_call_target="tpu_custom_call" | custom-call | flops 6710886400 | bytes 1048576 | tf_op jit(solution)/shard_map/pallas_call | solution.py:148
  18.1 1.9 %collective-permute-start.12 = (bf16[224,2048]{1,0:T(8,128)(2,1)S(1)}, bf16[224,2048]{1,0:T(8,128)(2,1)S(1)}, u32[]{:S(2)}, u32[]{:S(2)}) collective-permute-start(bf16[224,2048]{1,0:T(8,128)(2,1)S(1)} %constant_dynamic-update-slice_fusion.2.refs_3_), channel_id=1, source_target_pairs={{0,1},{1,0},{2,3},{3,2},{4,5},{5,4},{6,7},{7,6},{8,9},{9,8},{10,11... | collective-permute-start | bytes 2752520 | tf_op jit(solution)/shard_map/ppermute | solution.py:162
  19.9 1.7 %collective-permute-done.8 = bf16[32,2048]{1,0:T(8,128)(2,1)S(1)} collective-permute-done((bf16[32,2048]{1,0:T(8,128)(2,1)S(1)}, bf16[32,2048]{1,0:T(8,128)(2,1)S(1)}, u32[]{:S(2)}, u32[]{:S(2)}) %collective-permute-start.8) | collective-permute-done | bytes 131104 | tf_op jit(solution)/shard_map/ppermute | solution.py:162
  21.8 1.4 %collective-permute-start.10 = (bf16[64,2048]{1,0:T(8,128)(2,1)S(1)}, bf16[64,2048]{1,0:T(8,128)(2,1)S(1)}, u32[]{:S(2)}, u32[]{:S(2)}) collective-permute-start(bf16[64,2048]{1,0:T(8,128)(2,1)S(1)} %get-tuple-element.78), channel_id=1, source_target_pairs={{0,2},{1,3},{2,0},{3,1},{4,6},{5,7},{6,4},{7,5},{8,10},{9,11},{10,... | collective-permute-start | bytes 786440 | tf_op jit(solution)/shard_map/ppermute | solution.py:162
  23.1 1.2 %collective-permute-start.9 = (bf16[64,2048]{1,0:T(8,128)(2,1)S(1)}, bf16[64,2048]{1,0:T(8,128)(2,1)S(1)}, u32[]{:S(2)}, u32[]{:S(2)}) collective-permute-start(bf16[64,2048]{1,0:T(8,128)(2,1)S(1)} %get-tuple-element.79), channel_id=1, source_target_pairs={{0,4},{4,0},{8,12},{12,8},{16,20},{20,16},{24,28},{28,24},{1,5},{5... | collective-permute-start | bytes 786440 | tf_op jit(solution)/shard_map/ppermute | solution.py:162
  24.4 2.1 %shard_map.87 = (f32[8,320,128]{2,1,0:T(8,128)S(1)}, f32[8,320,128]{2,1,0:T(8,128)S(1)}, f32[8,320,128]{2,1,0:T(8,128)S(1)}) custom-call(s32[3,128]{1,0:T(4,128)S(1)} %broadcast_in_dim.11.refs_0_, bf16[32,5120]{1,0:T(8,128)(2,1)S(1)} %copy-done, bf16[32,5120]{1,0:T(8,128)(2,1)S(1)} %bitcast.13, ...), custom_call_target="tpu_custom_call" | custom-call | flops 10066329600 | bytes 1572864 | tf_op jit(solution)/shard_map/pallas_call | solution.py:148
  26.5 4.0 %collective-permute-start.14 = (bf16[192,2048]{1,0:T(8,128)(2,1)S(1)}, bf16[192,2048]{1,0:T(8,128)(2,1)S(1)}, u32[]{:S(2)}, u32[]{:S(2)}) collective-permute-start(bf16[192,2048]{1,0:T(8,128)(2,1)S(1)} %constant_dynamic-update-slice_fusion.9.refs_3_), channel_id=1, source_target_pairs={{0,1},{1,0},{2,3},{3,2},{4,5},{5,4},{6,7},{7,6},{8,9},{9,8},{10,11... | collective-permute-start | bytes 2359304 | tf_op jit(solution)/shard_map/ppermute | solution.py:162
  30.7 2.1 %collective-permute-start.13 = (bf16[160,2048]{1,0:T(8,128)(2,1)S(1)}, bf16[160,2048]{1,0:T(8,128)(2,1)S(1)}, u32[]{:S(2)}, u32[]{:S(2)}) collective-permute-start(bf16[160,2048]{1,0:T(8,128)(2,1)S(1)} %constant_dynamic-update-slice_fusion.13.refs_5_), channel_id=1, source_target_pairs={{0,1},{1,0},{2,3},{3,2},{4,5},{5,4},{6,7},{7,6},{8,9},{9,8},{10,11... | collective-permute-start | bytes 1966088 | tf_op jit(solution)/shard_map/ppermute | solution.py:162
  32.7 2.1 %shard_map.88 = (f32[8,320,128]{2,1,0:T(8,128)S(1)}, f32[8,320,128]{2,1,0:T(8,128)S(1)}, f32[8,320,128]{2,1,0:T(8,128)S(1)}) custom-call(s32[3,128]{1,0:T(4,128)S(1)} %broadcast_in_dim.11.refs_0_, bf16[32,5120]{1,0:T(8,128)(2,1)S(1)} %copy-done, bf16[32,5120]{1,0:T(8,128)(2,1)S(1)} %bitcast.14, ...), custom_call_target="tpu_custom_call" | custom-call | flops 10066329600 | bytes 1572864 | tf_op jit(solution)/shard_map/pallas_call | solution.py:148
  34.9 2.4 %shard_map.89 = (bf16[32,5120]{1,0:T(8,128)(2,1)}, bf16[32,5120]{1,0:T(8,128)(2,1)}) custom-call(s32[3,128]{1,0:T(4,128)S(1)} %broadcast_in_dim.11.refs_0_, bf16[32,5120]{1,0:T(8,128)(2,1)S(1)} %copy-done, bf16[32,5120]{1,0:T(8,128)(2,1)S(1)} %bitcast.15, bf16[160,2048]{1,0:T(8,128)(2,1)S(1)} %collective-permute-done.13.refs_3_, ...), custom_call_target="tpu_custom_call" | custom-call | flops 6710886400 | bytes 1048576 | tf_op jit(solution)/shard_map/pallas_call | solution.py:148
  (34 shorter events, 0.3 us)
Async XLA Ops:
  0.6 16.3 %copy-start.2 = (bf16[1,32,2048]{2,1,0:T(8,128)(2,1)S(1)}, bf16[1,32,2048]{2,1,0:T(8,128)(2,1)}, u32[]{:S(2)}) copy-start(bf16[1,32,2048]{2,1,0:T(8,128)(2,1)} %param.10) | copy-start | bytes 393220
  0.6 16.3 %copy-start.1 = (bf16[1,32,5120]{2,1,0:T(8,128)(2,1)S(1)}, bf16[1,32,5120]{2,1,0:T(8,128)(2,1)}, u32[]{:S(2)}) copy-start(bf16[1,32,5120]{2,1,0:T(8,128)(2,1)} %param.9) | copy-start | bytes 983044
  0.7 16.3 %copy-start = (bf16[32,5120]{1,0:T(8,128)(2,1)S(1)}, bf16[32,5120]{1,0:T(8,128)(2,1)}, u32[]{:S(2)}) copy-start(bf16[32,5120]{1,0:T(8,128)(2,1)} %refs_1_.7) | copy-start | bytes 983044
  0.7 9.8 %collective-permute-start = (bf16[32,2048]{1,0:T(8,128)(2,1)}, bf16[32,2048]{1,0:T(8,128)(2,1)S(1)}, u32[]{:S(2)}, u32[]{:S(2)}) collective-permute-start(bf16[32,2048]{1,0:T(8,128)(2,1)} %param.8), channel_id=1, source_target_pairs={{0,6},{1,7},{2,4},{3,5},{4,2},{5,3},{6,0},{7,1},{8,14},{9,15},{10,... | collective-permute-start | bytes 393224 | tf_op jit(solution)/shard_map/ppermute | solution.py:180
  3.7 6.8 %collective-permute-start.1 = (bf16[32,2048]{1,0:T(8,128)(2,1)}, bf16[32,2048]{1,0:T(8,128)(2,1)S(1)}, u32[]{:S(2)}, u32[]{:S(2)}) collective-permute-start(bf16[32,2048]{1,0:T(8,128)(2,1)} %param.8), channel_id=1, source_target_pairs={{0,24},{4,28},{8,16},{12,20},{16,8},{20,12},{24,0},{28,4},{1,25},{... | collective-permute-start | bytes 393224 | tf_op jit(solution)/shard_map/ppermute | solution.py:162
  7.0 6.4 %collective-permute-start.2 = (bf16[32,2048]{1,0:T(8,128)(2,1)}, bf16[32,2048]{1,0:T(8,128)(2,1)S(1)}, u32[]{:S(2)}, u32[]{:S(2)}) collective-permute-start(bf16[32,2048]{1,0:T(8,128)(2,1)} %param.8), channel_id=1, source_target_pairs={{0,8},{4,12},{8,0},{12,4},{16,24},{20,28},{24,16},{28,20},{1,9},{5... | collective-permute-start | bytes 393224 | tf_op jit(solution)/shard_map/ppermute | solution.py:162
  7.0 6.4 %collective-permute-start.3 = (bf16[32,2048]{1,0:T(8,128)(2,1)}, bf16[32,2048]{1,0:T(8,128)(2,1)S(1)}, u32[]{:S(2)}, u32[]{:S(2)}) collective-permute-start(bf16[32,2048]{1,0:T(8,128)(2,1)} %param.8), channel_id=1, source_target_pairs={{0,2},{1,3},{2,0},{3,1},{4,6},{5,7},{6,4},{7,5},{8,10},{9,11},{10,... | collective-permute-start | bytes 393224 | tf_op jit(solution)/shard_map/ppermute | solution.py:162
  7.3 6.2 %collective-permute-start.4 = (bf16[32,2048]{1,0:T(8,128)(2,1)}, bf16[32,2048]{1,0:T(8,128)(2,1)S(1)}, u32[]{:S(2)}, u32[]{:S(2)}) collective-permute-start(bf16[32,2048]{1,0:T(8,128)(2,1)} %param.8), channel_id=1, source_target_pairs={{0,4},{4,0},{8,12},{12,8},{16,20},{20,16},{24,28},{28,24},{1,5},{5... | collective-permute-start | bytes 393224 | tf_op jit(solution)/shard_map/ppermute | solution.py:162
  13.6 8.1 %collective-permute-start.5 = (bf16[64,2048]{1,0:T(8,128)(2,1)S(1)}, bf16[64,2048]{1,0:T(8,128)(2,1)S(1)}, u32[]{:S(2)}, u32[]{:S(2)}) collective-permute-start(bf16[64,2048]{1,0:T(8,128)(2,1)S(1)} %get-tuple-element.81), channel_id=1, source_target_pairs={{0,4},{4,0},{8,12},{12,8},{16,20},{20,16},{24,28},{28,24},{1,5},{5... | collective-permute-start | bytes 786440 | tf_op jit(solution)/shard_map/ppermute | solution.py:162
  14.0 7.7 %collective-permute-start.6 = (bf16[64,2048]{1,0:T(8,128)(2,1)S(1)}, bf16[64,2048]{1,0:T(8,128)(2,1)S(1)}, u32[]{:S(2)}, u32[]{:S(2)}) collective-permute-start(bf16[64,2048]{1,0:T(8,128)(2,1)S(1)} %get-tuple-element.81), channel_id=1, source_target_pairs={{0,2},{1,3},{2,0},{3,1},{4,6},{5,7},{6,4},{7,5},{8,10},{9,11},{10,... | collective-permute-start | bytes 786440 | tf_op jit(solution)/shard_map/ppermute | solution.py:162
  14.3 5.7 %collective-permute-start.7 = (bf16[32,2048]{1,0:T(8,128)(2,1)S(1)}, bf16[32,2048]{1,0:T(8,128)(2,1)S(1)}, u32[]{:S(2)}, u32[]{:S(2)}) collective-permute-start(bf16[32,2048]{1,0:T(8,128)(2,1)S(1)} %collective-permute-done.1), channel_id=1, source_target_pairs={{0,8},{4,12},{8,0},{12,4},{16,24},{20,28},{24,16},{28,20},{1,9},{5... | collective-permute-start | bytes 393224 | tf_op jit(solution)/shard_map/ppermute | solution.py:162
  14.9 6.8 %collective-permute-start.8 = (bf16[32,2048]{1,0:T(8,128)(2,1)S(1)}, bf16[32,2048]{1,0:T(8,128)(2,1)S(1)}, u32[]{:S(2)}, u32[]{:S(2)}) collective-permute-start(bf16[32,2048]{1,0:T(8,128)(2,1)S(1)} %collective-permute-done), channel_id=1, source_target_pairs={{0,24},{4,28},{8,16},{12,20},{16,8},{20,12},{24,0},{28,4},{1,25},{... | collective-permute-start | bytes 393224 | tf_op jit(solution)/shard_map/ppermute | solution.py:162
  18.1 6.4 %collective-permute-start.12 = (bf16[224,2048]{1,0:T(8,128)(2,1)S(1)}, bf16[224,2048]{1,0:T(8,128)(2,1)S(1)}, u32[]{:S(2)}, u32[]{:S(2)}) collective-permute-start(bf16[224,2048]{1,0:T(8,128)(2,1)S(1)} %constant_dynamic-update-slice_fusion.2.refs_3_), channel_id=1, source_target_pairs={{0,1},{1,0},{2,3},{3,2},{4,5},{5,4},{6,7},{7,6},{8,9},{9,8},{10,11... | collective-permute-start | bytes 2752520 | tf_op jit(solution)/shard_map/ppermute | solution.py:162
  21.8 8.8 %collective-permute-start.10 = (bf16[64,2048]{1,0:T(8,128)(2,1)S(1)}, bf16[64,2048]{1,0:T(8,128)(2,1)S(1)}, u32[]{:S(2)}, u32[]{:S(2)}) collective-permute-start(bf16[64,2048]{1,0:T(8,128)(2,1)S(1)} %get-tuple-element.78), channel_id=1, source_target_pairs={{0,2},{1,3},{2,0},{3,1},{4,6},{5,7},{6,4},{7,5},{8,10},{9,11},{10,... | collective-permute-start | bytes 786440 | tf_op jit(solution)/shard_map/ppermute | solution.py:162
  23.1 7.4 %collective-permute-start.9 = (bf16[64,2048]{1,0:T(8,128)(2,1)S(1)}, bf16[64,2048]{1,0:T(8,128)(2,1)S(1)}, u32[]{:S(2)}, u32[]{:S(2)}) collective-permute-start(bf16[64,2048]{1,0:T(8,128)(2,1)S(1)} %get-tuple-element.79), channel_id=1, source_target_pairs={{0,4},{4,0},{8,12},{12,8},{16,20},{20,16},{24,28},{28,24},{1,5},{5... | collective-permute-start | bytes 786440 | tf_op jit(solution)/shard_map/ppermute | solution.py:162
  24.3 6.2 %collective-permute-start.11 = (bf16[32,2048]{1,0:T(8,128)(2,1)S(1)}, bf16[32,2048]{1,0:T(8,128)(2,1)S(1)}, u32[]{:S(2)}, u32[]{:S(2)}) collective-permute-start(bf16[32,2048]{1,0:T(8,128)(2,1)S(1)} %collective-permute-done.8), channel_id=1, source_target_pairs={{0,8},{4,12},{8,0},{12,4},{16,24},{20,28},{24,16},{28,20},{1,9},{5... | collective-permute-start | bytes 393224 | tf_op jit(solution)/shard_map/ppermute | solution.py:162
  26.5 6.2 %collective-permute-start.14 = (bf16[192,2048]{1,0:T(8,128)(2,1)S(1)}, bf16[192,2048]{1,0:T(8,128)(2,1)S(1)}, u32[]{:S(2)}, u32[]{:S(2)}) collective-permute-start(bf16[192,2048]{1,0:T(8,128)(2,1)S(1)} %constant_dynamic-update-slice_fusion.9.refs_3_), channel_id=1, source_target_pairs={{0,1},{1,0},{2,3},{3,2},{4,5},{5,4},{6,7},{7,6},{8,9},{9,8},{10,11... | collective-permute-start | bytes 2359304 | tf_op jit(solution)/shard_map/ppermute | solution.py:162
  30.7 4.2 %collective-permute-start.13 = (bf16[160,2048]{1,0:T(8,128)(2,1)S(1)}, bf16[160,2048]{1,0:T(8,128)(2,1)S(1)}, u32[]{:S(2)}, u32[]{:S(2)}) collective-permute-start(bf16[160,2048]{1,0:T(8,128)(2,1)S(1)} %constant_dynamic-update-slice_fusion.13.refs_5_), channel_id=1, source_target_pairs={{0,1},{1,0},{2,3},{3,2},{4,5},{5,4},{6,7},{7,6},{8,9},{9,8},{10,11... | collective-permute-start | bytes 1966088 | tf_op jit(solution)/shard_map/ppermute | solution.py:162

commit v13 on v12

--- a/solution.py
+++ b/solution.py
@@ -208,24 +208,23 @@
         near = jnp.concatenate([next_z, third_z], axis=0)
         far, third_d = along_z(third_z, 1), along_z(own_d, 3)
         near_x, near_y = across_x(near), across_y(near)
+        far_x, far_y = across_x(far), across_y(jnp.concatenate([far, suffix_own], axis=0))
         plane = jnp.concatenate([trace_key_value, own_x, own_y, own_d, near, suffix_own], axis=0)
         here = [(0, 0, 0), (0, 1, 0), (0, 0, 1), (0, 1, 1), (1, 0, 0), (3, 0, 0), 0]
+        plane, far = barrier((plane, far))
         state = absorb([(plane, 0, 7)], slots_of(here), None)
-        plane, state = barrier((plane, state))
+
+        near_x, plane, state = barrier((near_x, plane, state))
         plane_sibling = core(plane)
-
-        near_x, near_y, far, third_d, state = barrier((near_x, near_y, far, third_d, state))
-        far_y = across_y(jnp.concatenate([far, suffix_own], axis=0))
-        far_x = across_x(jnp.concatenate([far, near_y[:rows]], axis=0))
-        far_d = along_z(third_d, 1)
+        near_y, state = barrier((near_y, state))
+        next_d, far_d = across_x(near_y[:rows]), along_z(third_d, 1)
         sides = jnp.concatenate([near_x, near_y, far, third_d], axis=0)
         near_here = [(1, 1, 0), (3, 1, 0), (1, 0, 1), (3, 0, 1), (2, 0, 0), (3, 1, 1)]
         state = absorb([(sides, 0, 6), (plane_sibling, 0, 6)], slots_of(near_here) + slots_of(here[:6], 1), state)
-        sides, state = barrier((sides, state))
         sides_sibling = core(sides)
 
-        far_x, far_y, far_d, state = barrier((far_x, far_y, far_d, state))
-        rest = jnp.concatenate([far_x, far_y, far_d], axis=0)
+        far_x, next_d, far_y, far_d, state = barrier((far_x, next_d, far_y, far_d, state))
+        rest = jnp.concatenate([far_x, next_d, far_y, far_d], axis=0)
         rest_sibling = core(rest)
         rest_here = [(2, 1, 0), (1, 1, 1), (2, 0, 1), 2, (2, 1, 1)]
         state = absorb(

time: 37.5 us -> 37.5 us (level)
  waiting for transfers between devices: 4.72 us -> 7.5 us
  starting transfers between devices: 20.7 us -> 18 us
    ppermute x14 -> x15, waiting for transfers between devices: 4.72 us -> 7.5 us  [swap(): return lax.ppermute(array, axis, [(i, i ^ bit) for i in range(size)])]
    ppermute x14 -> x15, starting transfers between devices: 17.6 us -> 15 us  [swap(): return lax.ppermute(array, axis, [(i, i ^ bit) for i in range(size)])]
    unnamed x17 -> x18, local copies, waits for them, and re-layouts: 1.12 us -> 1.12 us
  transfers between devices with their start and end apart: 15 -> 16, of which waited for: 2 -> 4; matrix products, arithmetic and copies ran while one was open for 3% -> 3% of each run, Pallas kernels for 14% -> 14%
where the time goes in v13:
time: 37.5 us; the launch traced here: 37.3 us
  starting transfers between devices  18 us (48%)
  Pallas kernels  7.69 us (21%)
  waiting for transfers between devices  7.5 us (20%)
  between operations  2.77 us (7%)
  local copies, waits for them, and re-layouts  1.23 us (3%)
    ppermute x15, starting transfers between devices, swap(): return lax.ppermute(array, axis, [(i, i ^ bit) for i in range(size)])  15 us
    pallas_call x4, Pallas kernels, attend(): pl.pallas_call(functools.partial(attend_kernel, slots, ranges, tp_size, f...  7.69 us
    ppermute x15, waiting for transfers between devices, swap(): return lax.ppermute(array, axis, [(i, i ^ bit) for i in range(size)])  7.5 us
    ppermute x1, starting transfers between devices, local(): lax.ppermute(a, ('ctx', 'tp'), [(i * tp_size + j, (i ^ 1) * tp_size + (j...  3.06 us
    unnamed x18, local copies, waits for them, and re-layouts  1.12 us
  transfers between devices with their start and end apart: 16, of which 4 were waited for; matrix products, arithmetic and copies ran while one was open for 3% of the time, Pallas kernels for 14%

profile of v13, /device:TPU:1, one launch (start us, length us, event | category | flops | bytes accessed | tf_op | source)
XLA Modules:
  0.0 37.3 jit_solution(10494460035381046510)
XLA Ops:
  0.7 3.1 %collective-permute-start = (bf16[32,2048]{1,0:T(8,128)(2,1)}, bf16[32,2048]{1,0:T(8,128)(2,1)S(1)}, u32[]{:S(2)}, u32[]{:S(2)}) collective-permute-start(bf16[32,2048]{1,0:T(8,128)(2,1)} %param.8), channel_id=1, source_target_pairs={{0,6},{1,7},{2,4},{3,5},{4,2},{5,3},{6,0},{7,1},{8,14},{9,15},{10,... | collective-permute-start | bytes 393224 | tf_op jit(solution)/shard_map/ppermute | solution.py:180
  3.7 3.3 %collective-permute-start.1 = (bf16[32,2048]{1,0:T(8,128)(2,1)}, bf16[32,2048]{1,0:T(8,128)(2,1)S(1)}, u32[]{:S(2)}, u32[]{:S(2)}) collective-permute-start(bf16[32,2048]{1,0:T(8,128)(2,1)} %param.8), channel_id=1, source_target_pairs={{0,24},{4,28},{8,16},{12,20},{16,8},{20,12},{24,0},{28,4},{1,25},{... | collective-permute-start | bytes 393224 | tf_op jit(solution)/shard_map/ppermute | solution.py:162
  7.0 0.2 collective-permute-start.3
  7.3 0.3 collective-permute-start.4
  7.5 0.9 %constant_dynamic-update-slice_fusion.8 = bf16[224,2048]{1,0:T(8,128)(2,1)S(1)} fusion(bf16[32,2048]{1,0:T(8,128)(2,1)} %param.8), kind=kLoop, calls=%fused_computation.9 | loop fusion | bytes 262144
  10.5 2.9 %collective-permute-done.2 = bf16[32,2048]{1,0:T(8,128)(2,1)S(1)} collective-permute-done((bf16[32,2048]{1,0:T(8,128)(2,1)}, bf16[32,2048]{1,0:T(8,128)(2,1)S(1)}, u32[]{:S(2)}, u32[]{:S(2)}) %collective-permute-start.2) | collective-permute-done | bytes 131104 | tf_op jit(solution)/shard_map/ppermute | solution.py:162
  13.5 0.8 %collective-permute-start.5 = (bf16[32,2048]{1,0:T(8,128)(2,1)S(1)}, bf16[32,2048]{1,0:T(8,128)(2,1)S(1)}, u32[]{:S(2)}, u32[]{:S(2)}) collective-permute-start(bf16[32,2048]{1,0:T(8,128)(2,1)S(1)} %collective-permute-done.1), channel_id=1, source_target_pairs={{0,8},{4,12},{8,0},{12,4},{16,24},{20,28},{24,16},{28,20},{1,9},{5... | collective-permute-start | bytes 393224 | tf_op jit(solution)/shard_map/ppermute | solution.py:162
  14.4 0.3 collective-permute-start.8
  14.7 0.2 collective-permute-start.7
  14.9 2.0 %collective-permute-start.11 = (bf16[32,2048]{1,0:T(8,128)(2,1)S(1)}, bf16[32,2048]{1,0:T(8,128)(2,1)S(1)}, u32[]{:S(2)}, u32[]{:S(2)}) collective-permute-start(bf16[32,2048]{1,0:T(8,128)(2,1)S(1)} %collective-permute-done), channel_id=1, source_target_pairs={{0,24},{4,28},{8,16},{12,20},{16,8},{20,12},{24,0},{28,4},{1,25},{... | collective-permute-start | bytes 393224 | tf_op jit(solution)/shard_map/ppermute | solution.py:162
  16.9 0.4 %collective-permute-done.5 = bf16[32,2048]{1,0:T(8,128)(2,1)S(1)} collective-permute-done((bf16[32,2048]{1,0:T(8,128)(2,1)S(1)}, bf16[32,2048]{1,0:T(8,128)(2,1)S(1)}, u32[]{:S(2)}, u32[]{:S(2)}) %collective-permute-start.5) | collective-permute-done | bytes 131104 | tf_op jit(solution)/shard_map/ppermute | solution.py:162
  17.4 1.1 %shard_map.86 = (f32[8,320,128]{2,1,0:T(8,128)S(1)}, f32[8,320,128]{2,1,0:T(8,128)S(1)}, f32[8,320,128]{2,1,0:T(8,128)S(1)}) custom-call(s32[3,128]{1,0:T(4,128)S(1)} %broadcast_in_dim.11.refs_0_, bf16[32,5120]{1,0:T(8,128)(2,1)S(1)} %copy-done, bf16[32,5120]{1,0:T(8,128)(2,1)S(1)} %bitcast.12, bf16[224,2048]{1,0:T(8,128)(2,1)S(1)} %constant_dynamic-update-slice_fusion.2.refs_3_), custom_call_target="tpu_custom_call" | custom-call | flops 6710886400 | bytes 1048576 | tf_op jit(solution)/shard_map/pallas_call | solution.py:148
  18.5 1.7 %collective-permute-done.8 = bf16[64,2048]{1,0:T(8,128)(2,1)S(1)} collective-permute-done((bf16[64,2048]{1,0:T(8,128)(2,1)S(1)}, bf16[64,2048]{1,0:T(8,128)(2,1)S(1)}, u32[]{:S(2)}, u32[]{:S(2)}) %collective-permute-start.8) | collective-permute-done | bytes 262176 | tf_op jit(solution)/shard_map/ppermute | solution.py:162
  20.1 3.0 %collective-permute-start.13 = (bf16[224,2048]{1,0:T(8,128)(2,1)S(1)}, bf16[224,2048]{1,0:T(8,128)(2,1)S(1)}, u32[]{:S(2)}, u32[]{:S(2)}) collective-permute-start(bf16[224,2048]{1,0:T(8,128)(2,1)S(1)} %constant_dynamic-update-slice_fusion.2.refs_3_), channel_id=1, source_target_pairs={{0,1},{1,0},{2,3},{3,2},{4,5},{5,4},{6,7},{7,6},{8,9},{9,8},{10,11... | collective-permute-start | bytes 2752520 | tf_op jit(solution)/shard_map/ppermute | solution.py:162
  23.2 0.7 %collective-permute-start.10 = (bf16[64,2048]{1,0:T(8,128)(2,1)S(1)}, bf16[64,2048]{1,0:T(8,128)(2,1)S(1)}, u32[]{:S(2)}, u32[]{:S(2)}) collective-permute-start(bf16[64,2048]{1,0:T(8,128)(2,1)S(1)} %pad_maximum_fusion), channel_id=1, source_target_pairs={{0,2},{1,3},{2,0},{3,1},{4,6},{5,7},{6,4},{7,5},{8,10},{9,11},{10,... | collective-permute-start | bytes 786440 | tf_op jit(solution)/shard_map/ppermute | solution.py:162
  23.9 0.3 collective-permute-start.6
  24.2 0.6 %collective-permute-start.12 = (bf16[32,2048]{1,0:T(8,128)(2,1)S(1)}, bf16[32,2048]{1,0:T(8,128)(2,1)S(1)}, u32[]{:S(2)}, u32[]{:S(2)}) collective-permute-start(bf16[32,2048]{1,0:T(8,128)(2,1)S(1)} %collective-permute-done.11), channel_id=1, source_target_pairs={{0,8},{4,12},{8,0},{12,4},{16,24},{20,28},{24,16},{28,20},{1,9},{5... | collective-permute-start | bytes 393224 | tf_op jit(solution)/shard_map/ppermute | solution.py:162
  24.8 1.0 %collective-permute-start.9 = (bf16[32,2048]{1,0:T(8,128)(2,1)S(1)}, bf16[32,2048]{1,0:T(8,128)(2,1)S(1)}, u32[]{:S(2)}, u32[]{:S(2)}) collective-permute-start(bf16[32,2048]{1,0:T(8,128)(2,1)S(1)} %slice.3), channel_id=1, source_target_pairs={{0,4},{4,0},{8,12},{12,8},{16,20},{20,16},{24,28},{28,24},{1,5},{5... | collective-permute-start | bytes 393224 | tf_op jit(solution)/shard_map/ppermute | solution.py:162
  25.8 1.2 %collective-permute-start.15 = (bf16[192,2048]{1,0:T(8,128)(2,1)S(1)}, bf16[192,2048]{1,0:T(8,128)(2,1)S(1)}, u32[]{:S(2)}, u32[]{:S(2)}) collective-permute-start(bf16[192,2048]{1,0:T(8,128)(2,1)S(1)} %constant_dynamic-update-slice_fusion.9.refs_3_), channel_id=1, source_target_pairs={{0,1},{1,0},{2,3},{3,2},{4,5},{5,4},{6,7},{7,6},{8,9},{9,8},{10,11... | collective-permute-start | bytes 2359304 | tf_op jit(solution)/shard_map/ppermute | solution.py:162
  27.0 2.0 %shard_map.87 = (f32[8,320,128]{2,1,0:T(8,128)S(1)}, f32[8,320,128]{2,1,0:T(8,128)S(1)}, f32[8,320,128]{2,1,0:T(8,128)S(1)}) custom-call(s32[3,128]{1,0:T(4,128)S(1)} %broadcast_in_dim.11.refs_0_, bf16[32,5120]{1,0:T(8,128)(2,1)S(1)} %copy-done, bf16[32,5120]{1,0:T(8,128)(2,1)S(1)} %bitcast.13, ...), custom_call_target="tpu_custom_call" | custom-call | flops 10066329600 | bytes 1572864 | tf_op jit(solution)/shard_map/pallas_call | solution.py:148
  29.1 2.4 %collective-permute-done.9 = bf16[32,2048]{1,0:T(8,128)(2,1)S(1)} collective-permute-done((bf16[32,2048]{1,0:T(8,128)(2,1)S(1)}, bf16[32,2048]{1,0:T(8,128)(2,1)S(1)}, u32[]{:S(2)}, u32[]{:S(2)}) %collective-permute-start.9) | collective-permute-done | bytes 131104 | tf_op jit(solution)/shard_map/ppermute | solution.py:162
  31.6 1.2 %collective-permute-start.14 = (bf16[160,2048]{1,0:T(8,128)(2,1)S(1)}, bf16[160,2048]{1,0:T(8,128)(2,1)S(1)}, u32[]{:S(2)}, u32[]{:S(2)}) collective-permute-start(bf16[160,2048]{1,0:T(8,128)(2,1)S(1)} %constant_dynamic-update-slice_fusion.13.refs_5_), channel_id=1, source_target_pairs={{0,1},{1,0},{2,3},{3,2},{4,5},{5,4},{6,7},{7,6},{8,9},{9,8},{10,11... | collective-permute-start | bytes 1966088 | tf_op jit(solution)/shard_map/ppermute | solution.py:162
  32.8 2.1 %shard_map.88 = (f32[8,320,128]{2,1,0:T(8,128)S(1)}, f32[8,320,128]{2,1,0:T(8,128)S(1)}, f32[8,320,128]{2,1,0:T(8,128)S(1)}) custom-call(s32[3,128]{1,0:T(4,128)S(1)} %broadcast_in_dim.11.refs_0_, bf16[32,5120]{1,0:T(8,128)(2,1)S(1)} %copy-done, bf16[32,5120]{1,0:T(8,128)(2,1)S(1)} %bitcast.14, ...), custom_call_target="tpu_custom_call" | custom-call | flops 10066329600 | bytes 1572864 | tf_op jit(solution)/shard_map/pallas_call | solution.py:148
  35.0 2.4 %shard_map.89 = (bf16[32,5120]{1,0:T(8,128)(2,1)}, bf16[32,5120]{1,0:T(8,128)(2,1)}) custom-call(s32[3,128]{1,0:T(4,128)S(1)} %broadcast_in_dim.11.refs_0_, bf16[32,5120]{1,0:T(8,128)(2,1)S(1)} %copy-done, bf16[32,5120]{1,0:T(8,128)(2,1)S(1)} %bitcast.15, bf16[160,2048]{1,0:T(8,128)(2,1)S(1)} %collective-permute-done.14.refs_3_, ...), custom_call_target="tpu_custom_call" | custom-call | flops 6710886400 | bytes 1048576 | tf_op jit(solution)/shard_map/pallas_call | solution.py:148
  (37 shorter events, 0.4 us)
Async XLA Ops:
  0.6 16.3 %copy-start.2 = (bf16[1,32,2048]{2,1,0:T(8,128)(2,1)S(1)}, bf16[1,32,2048]{2,1,0:T(8,128)(2,1)}, u32[]{:S(2)}) copy-start(bf16[1,32,2048]{2,1,0:T(8,128)(2,1)} %param.10) | copy-start | bytes 393220
  0.6 16.7 %copy-start.1 = (bf16[1,32,5120]{2,1,0:T(8,128)(2,1)S(1)}, bf16[1,32,5120]{2,1,0:T(8,128)(2,1)}, u32[]{:S(2)}) copy-start(bf16[1,32,5120]{2,1,0:T(8,128)(2,1)} %param.9) | copy-start | bytes 983044
  0.7 16.7 %copy-start = (bf16[32,5120]{1,0:T(8,128)(2,1)S(1)}, bf16[32,5120]{1,0:T(8,128)(2,1)}, u32[]{:S(2)}) copy-start(bf16[32,5120]{1,0:T(8,128)(2,1)} %refs_1_.7) | copy-start | bytes 983044
  0.7 9.8 %collective-permute-start = (bf16[32,2048]{1,0:T(8,128)(2,1)}, bf16[32,2048]{1,0:T(8,128)(2,1)S(1)}, u32[]{:S(2)}, u32[]{:S(2)}) collective-permute-start(bf16[32,2048]{1,0:T(8,128)(2,1)} %param.8), channel_id=1, source_target_pairs={{0,6},{1,7},{2,4},{3,5},{4,2},{5,3},{6,0},{7,1},{8,14},{9,15},{10,... | collective-permute-start | bytes 393224 | tf_op jit(solution)/shard_map/ppermute | solution.py:180
  3.7 6.8 %collective-permute-start.1 = (bf16[32,2048]{1,0:T(8,128)(2,1)}, bf16[32,2048]{1,0:T(8,128)(2,1)S(1)}, u32[]{:S(2)}, u32[]{:S(2)}) collective-permute-start(bf16[32,2048]{1,0:T(8,128)(2,1)} %param.8), channel_id=1, source_target_pairs={{0,24},{4,28},{8,16},{12,20},{16,8},{20,12},{24,0},{28,4},{1,25},{... | collective-permute-start | bytes 393224 | tf_op jit(solution)/shard_map/ppermute | solution.py:162
  7.0 6.4 %collective-permute-start.2 = (bf16[32,2048]{1,0:T(8,128)(2,1)}, bf16[32,2048]{1,0:T(8,128)(2,1)S(1)}, u32[]{:S(2)}, u32[]{:S(2)}) collective-permute-start(bf16[32,2048]{1,0:T(8,128)(2,1)} %param.8), channel_id=1, source_target_pairs={{0,8},{4,12},{8,0},{12,4},{16,24},{20,28},{24,16},{28,20},{1,9},{5... | collective-permute-start | bytes 393224 | tf_op jit(solution)/shard_map/ppermute | solution.py:162
  7.0 6.4 %collective-permute-start.3 = (bf16[32,2048]{1,0:T(8,128)(2,1)}, bf16[32,2048]{1,0:T(8,128)(2,1)S(1)}, u32[]{:S(2)}, u32[]{:S(2)}) collective-permute-start(bf16[32,2048]{1,0:T(8,128)(2,1)} %param.8), channel_id=1, source_target_pairs={{0,2},{1,3},{2,0},{3,1},{4,6},{5,7},{6,4},{7,5},{8,10},{9,11},{10,... | collective-permute-start | bytes 393224 | tf_op jit(solution)/shard_map/ppermute | solution.py:162
  7.3 6.2 %collective-permute-start.4 = (bf16[32,2048]{1,0:T(8,128)(2,1)}, bf16[32,2048]{1,0:T(8,128)(2,1)S(1)}, u32[]{:S(2)}, u32[]{:S(2)}) collective-permute-start(bf16[32,2048]{1,0:T(8,128)(2,1)} %param.8), channel_id=1, source_target_pairs={{0,4},{4,0},{8,12},{12,8},{16,20},{20,16},{24,28},{28,24},{1,5},{5... | collective-permute-start | bytes 393224 | tf_op jit(solution)/shard_map/ppermute | solution.py:162
  13.5 3.8 %collective-permute-start.5 = (bf16[32,2048]{1,0:T(8,128)(2,1)S(1)}, bf16[32,2048]{1,0:T(8,128)(2,1)S(1)}, u32[]{:S(2)}, u32[]{:S(2)}) collective-permute-start(bf16[32,2048]{1,0:T(8,128)(2,1)S(1)} %collective-permute-done.1), channel_id=1, source_target_pairs={{0,8},{4,12},{8,0},{12,4},{16,24},{20,28},{24,16},{28,20},{1,9},{5... | collective-permute-start | bytes 393224 | tf_op jit(solution)/shard_map/ppermute | solution.py:162
  14.4 5.8 %collective-permute-start.8 = (bf16[64,2048]{1,0:T(8,128)(2,1)S(1)}, bf16[64,2048]{1,0:T(8,128)(2,1)S(1)}, u32[]{:S(2)}, u32[]{:S(2)}) collective-permute-start(bf16[64,2048]{1,0:T(8,128)(2,1)S(1)} %get-tuple-element.73), channel_id=1, source_target_pairs={{0,4},{4,0},{8,12},{12,8},{16,20},{20,16},{24,28},{28,24},{1,5},{5... | collective-permute-start | bytes 786440 | tf_op jit(solution)/shard_map/ppermute | solution.py:162
  14.7 10.0 %collective-permute-start.7 = (bf16[64,2048]{1,0:T(8,128)(2,1)S(1)}, bf16[64,2048]{1,0:T(8,128)(2,1)S(1)}, u32[]{:S(2)}, u32[]{:S(2)}) collective-permute-start(bf16[64,2048]{1,0:T(8,128)(2,1)S(1)} %get-tuple-element.73), channel_id=1, source_target_pairs={{0,2},{1,3},{2,0},{3,1},{4,6},{5,7},{6,4},{7,5},{8,10},{9,11},{10,... | collective-permute-start | bytes 786440 | tf_op jit(solution)/shard_map/ppermute | solution.py:162
  14.9 9.3 %collective-permute-start.11 = (bf16[32,2048]{1,0:T(8,128)(2,1)S(1)}, bf16[32,2048]{1,0:T(8,128)(2,1)S(1)}, u32[]{:S(2)}, u32[]{:S(2)}) collective-permute-start(bf16[32,2048]{1,0:T(8,128)(2,1)S(1)} %collective-permute-done), channel_id=1, source_target_pairs={{0,24},{4,28},{8,16},{12,20},{16,8},{20,12},{24,0},{28,4},{1,25},{... | collective-permute-start | bytes 393224 | tf_op jit(solution)/shard_map/ppermute | solution.py:162
  20.1 5.7 %collective-permute-start.13 = (bf16[224,2048]{1,0:T(8,128)(2,1)S(1)}, bf16[224,2048]{1,0:T(8,128)(2,1)S(1)}, u32[]{:S(2)}, u32[]{:S(2)}) collective-permute-start(bf16[224,2048]{1,0:T(8,128)(2,1)S(1)} %constant_dynamic-update-slice_fusion.2.refs_3_), channel_id=1, source_target_pairs={{0,1},{1,0},{2,3},{3,2},{4,5},{5,4},{6,7},{7,6},{8,9},{9,8},{10,11... | collective-permute-start | bytes 2752520 | tf_op jit(solution)/shard_map/ppermute | solution.py:162
  23.2 8.4 %collective-permute-start.10 = (bf16[64,2048]{1,0:T(8,128)(2,1)S(1)}, bf16[64,2048]{1,0:T(8,128)(2,1)S(1)}, u32[]{:S(2)}, u32[]{:S(2)}) collective-permute-start(bf16[64,2048]{1,0:T(8,128)(2,1)S(1)} %pad_maximum_fusion), channel_id=1, source_target_pairs={{0,2},{1,3},{2,0},{3,1},{4,6},{5,7},{6,4},{7,5},{8,10},{9,11},{10,... | collective-permute-start | bytes 786440 | tf_op jit(solution)/shard_map/ppermute | solution.py:162
  23.9 5.2 %collective-permute-start.6 = (bf16[32,2048]{1,0:T(8,128)(2,1)S(1)}, bf16[32,2048]{1,0:T(8,128)(2,1)S(1)}, u32[]{:S(2)}, u32[]{:S(2)}) collective-permute-start(bf16[32,2048]{1,0:T(8,128)(2,1)S(1)} %collective-permute-done.5), channel_id=1, source_target_pairs={{0,4},{4,0},{8,12},{12,8},{16,20},{20,16},{24,28},{28,24},{1,5},{5... | collective-permute-start | bytes 393224 | tf_op jit(solution)/shard_map/ppermute | solution.py:162
  24.2 4.9 %collective-permute-start.12 = (bf16[32,2048]{1,0:T(8,128)(2,1)S(1)}, bf16[32,2048]{1,0:T(8,128)(2,1)S(1)}, u32[]{:S(2)}, u32[]{:S(2)}) collective-permute-start(bf16[32,2048]{1,0:T(8,128)(2,1)S(1)} %collective-permute-done.11), channel_id=1, source_target_pairs={{0,8},{4,12},{8,0},{12,4},{16,24},{20,28},{24,16},{28,20},{1,9},{5... | collective-permute-start | bytes 393224 | tf_op jit(solution)/shard_map/ppermute | solution.py:162
  24.8 6.8 %collective-permute-start.9 = (bf16[32,2048]{1,0:T(8,128)(2,1)S(1)}, bf16[32,2048]{1,0:T(8,128)(2,1)S(1)}, u32[]{:S(2)}, u32[]{:S(2)}) collective-permute-start(bf16[32,2048]{1,0:T(8,128)(2,1)S(1)} %slice.3), channel_id=1, source_target_pairs={{0,4},{4,0},{8,12},{12,8},{16,20},{20,16},{24,28},{28,24},{1,5},{5... | collective-permute-start | bytes 393224 | tf_op jit(solution)/shard_map/ppermute | solution.py:162
  25.8 7.0 %collective-permute-start.15 = (bf16[192,2048]{1,0:T(8,128)(2,1)S(1)}, bf16[192,2048]{1,0:T(8,128)(2,1)S(1)}, u32[]{:S(2)}, u32[]{:S(2)}) collective-permute-start(bf16[192,2048]{1,0:T(8,128)(2,1)S(1)} %constant_dynamic-update-slice_fusion.9.refs_3_), channel_id=1, source_target_pairs={{0,1},{1,0},{2,3},{3,2},{4,5},{5,4},{6,7},{7,6},{8,9},{9,8},{10,11... | collective-permute-start | bytes 2359304 | tf_op jit(solution)/shard_map/ppermute | solution.py:162
  31.6 3.3 %collective-permute-start.14 = (bf16[160,2048]{1,0:T(8,128)(2,1)S(1)}, bf16[160,2048]{1,0:T(8,128)(2,1)S(1)}, u32[]{:S(2)}, u32[]{:S(2)}) collective-permute-start(bf16[160,2048]{1,0:T(8,128)(2,1)S(1)} %constant_dynamic-update-slice_fusion.13.refs_5_), channel_id=1, source_target_pairs={{0,1},{1,0},{2,3},{3,2},{4,5},{5,4},{6,7},{7,6},{8,9},{9,8},{10,11... | collective-permute-start | bytes 1966088 | tf_op jit(solution)/shard_map/ppermute | solution.py:162

commit v14 on v13

--- a/solution.py
+++ b/solution.py
@@ -214,9 +214,9 @@
         plane, far = barrier((plane, far))
         state = absorb([(plane, 0, 7)], slots_of(here), None)
 
-        near_x, plane, state = barrier((near_x, plane, state))
+        near_y, plane, state = barrier((near_y, plane, state))
         plane_sibling = core(plane)
-        near_y, state = barrier((near_y, state))
+        near_x, state = barrier((near_x, state))
         next_d, far_d = across_x(near_y[:rows]), along_z(third_d, 1)
         sides = jnp.concatenate([near_x, near_y, far, third_d], axis=0)
         near_here = [(1, 1, 0), (3, 1, 0), (1, 0, 1), (3, 0, 1), (2, 0, 0), (3, 1, 1)]

time: 37.5 us -> 37.5 us (level)
  no operation moved by 1% of the time
where the time goes in v14:
time: 37.5 us; the launch traced here: 37.3 us
  starting transfers between devices  18.1 us (48%)
  Pallas kernels  7.68 us (20%)
  waiting for transfers between devices  7.49 us (20%)
  between operations  2.77 us (7%)
  local copies, waits for them, and re-layouts  1.23 us (3%)
    ppermute x15, starting transfers between devices, swap(): return lax.ppermute(array, axis, [(i, i ^ bit) for i in range(size)])  15 us
    pallas_call x4, Pallas kernels, attend(): pl.pallas_call(functools.partial(attend_kernel, slots, ranges, tp_size, f...  7.68 us
    ppermute x15, waiting for transfers between devices, swap(): return lax.ppermute(array, axis, [(i, i ^ bit) for i in range(size)])  7.49 us
    ppermute x1, starting transfers between devices, local(): lax.ppermute(a, ('ctx', 'tp'), [(i * tp_size + j, (i ^ 1) * tp_size + (j...  3.06 us
    unnamed x18, local copies, waits for them, and re-layouts  1.12 us
  transfers between devices with their start and end apart: 16, of which 4 were waited for; matrix products, arithmetic and copies ran while one was open for 3% of the time, Pallas kernels for 14%

profile of v14, /device:TPU:1, one launch (start us, length us, event | category | flops | bytes accessed | tf_op | source)
XLA Modules:
  0.0 37.3 jit_solution(11520240457884266953)
XLA Ops:
  0.7 3.1 %collective-permute-start = (bf16[32,2048]{1,0:T(8,128)(2,1)}, bf16[32,2048]{1,0:T(8,128)(2,1)S(1)}, u32[]{:S(2)}, u32[]{:S(2)}) collective-permute-start(bf16[32,2048]{1,0:T(8,128)(2,1)} %param.8), channel_id=1, source_target_pairs={{0,6},{1,7},{2,4},{3,5},{4,2},{5,3},{6,0},{7,1},{8,14},{9,15},{10,... | collective-permute-start | bytes 393224 | tf_op jit(solution)/shard_map/ppermute | solution.py:180
  3.7 3.3 %collective-permute-start.1 = (bf16[32,2048]{1,0:T(8,128)(2,1)}, bf16[32,2048]{1,0:T(8,128)(2,1)S(1)}, u32[]{:S(2)}, u32[]{:S(2)}) collective-permute-start(bf16[32,2048]{1,0:T(8,128)(2,1)} %param.8), channel_id=1, source_target_pairs={{0,24},{4,28},{8,16},{12,20},{16,8},{20,12},{24,0},{28,4},{1,25},{... | collective-permute-start | bytes 393224 | tf_op jit(solution)/shard_map/ppermute | solution.py:162
  7.0 0.2 collective-permute-start.3
  7.3 0.3 collective-permute-start.4
  7.5 0.9 %constant_dynamic-update-slice_fusion.8 = bf16[224,2048]{1,0:T(8,128)(2,1)S(1)} fusion(bf16[32,2048]{1,0:T(8,128)(2,1)} %param.8), kind=kLoop, calls=%fused_computation.9 | loop fusion | bytes 262144
  10.5 2.9 %collective-permute-done.2 = bf16[32,2048]{1,0:T(8,128)(2,1)S(1)} collective-permute-done((bf16[32,2048]{1,0:T(8,128)(2,1)}, bf16[32,2048]{1,0:T(8,128)(2,1)S(1)}, u32[]{:S(2)}, u32[]{:S(2)}) %collective-permute-start.2) | collective-permute-done | bytes 131104 | tf_op jit(solution)/shard_map/ppermute | solution.py:162
  13.5 0.8 %collective-permute-start.5 = (bf16[32,2048]{1,0:T(8,128)(2,1)S(1)}, bf16[32,2048]{1,0:T(8,128)(2,1)S(1)}, u32[]{:S(2)}, u32[]{:S(2)}) collective-permute-start(bf16[32,2048]{1,0:T(8,128)(2,1)S(1)} %collective-permute-done.1), channel_id=1, source_target_pairs={{0,8},{4,12},{8,0},{12,4},{16,24},{20,28},{24,16},{28,20},{1,9},{5... | collective-permute-start | bytes 393224 | tf_op jit(solution)/shard_map/ppermute | solution.py:162
  14.4 0.3 collective-permute-start.7
  14.7 0.3 collective-permute-start.12
  14.9 2.0 %collective-permute-start.10 = (bf16[32,2048]{1,0:T(8,128)(2,1)S(1)}, bf16[32,2048]{1,0:T(8,128)(2,1)S(1)}, u32[]{:S(2)}, u32[]{:S(2)}) collective-permute-start(bf16[32,2048]{1,0:T(8,128)(2,1)S(1)} %collective-permute-done), channel_id=1, source_target_pairs={{0,24},{4,28},{8,16},{12,20},{16,8},{20,12},{24,0},{28,4},{1,25},{... | collective-permute-start | bytes 393224 | tf_op jit(solution)/shard_map/ppermute | solution.py:162
  16.9 0.4 %collective-permute-done.5 = bf16[32,2048]{1,0:T(8,128)(2,1)S(1)} collective-permute-done((bf16[32,2048]{1,0:T(8,128)(2,1)S(1)}, bf16[32,2048]{1,0:T(8,128)(2,1)S(1)}, u32[]{:S(2)}, u32[]{:S(2)}) %collective-permute-start.5) | collective-permute-done | bytes 131104 | tf_op jit(solution)/shard_map/ppermute | solution.py:162
  17.4 1.1 %shard_map.86 = (f32[8,320,128]{2,1,0:T(8,128)S(1)}, f32[8,320,128]{2,1,0:T(8,128)S(1)}, f32[8,320,128]{2,1,0:T(8,128)S(1)}) custom-call(s32[3,128]{1,0:T(4,128)S(1)} %broadcast_in_dim.11.refs_0_, bf16[32,5120]{1,0:T(8,128)(2,1)S(1)} %copy-done, bf16[32,5120]{1,0:T(8,128)(2,1)S(1)} %bitcast.12, bf16[224,2048]{1,0:T(8,128)(2,1)S(1)} %constant_dynamic-update-slice_fusion.2.refs_3_), custom_call_target="tpu_custom_call" | custom-call | flops 6710886400 | bytes 1048576 | tf_op jit(solution)/shard_map/pallas_call | solution.py:148
  18.5 1.7 %collective-permute-done.7 = bf16[64,2048]{1,0:T(8,128)(2,1)S(1)} collective-permute-done((bf16[64,2048]{1,0:T(8,128)(2,1)S(1)}, bf16[64,2048]{1,0:T(8,128)(2,1)S(1)}, u32[]{:S(2)}, u32[]{:S(2)}) %collective-permute-start.7) | collective-permute-done | bytes 262176 | tf_op jit(solution)/shard_map/ppermute | solution.py:162
  20.1 3.0 %collective-permute-start.13 = (bf16[224,2048]{1,0:T(8,128)(2,1)S(1)}, bf16[224,2048]{1,0:T(8,128)(2,1)S(1)}, u32[]{:S(2)}, u32[]{:S(2)}) collective-permute-start(bf16[224,2048]{1,0:T(8,128)(2,1)S(1)} %constant_dynamic-update-slice_fusion.2.refs_3_), channel_id=1, source_target_pairs={{0,1},{1,0},{2,3},{3,2},{4,5},{5,4},{6,7},{7,6},{8,9},{9,8},{10,11... | collective-permute-start | bytes 2752520 | tf_op jit(solution)/shard_map/ppermute | solution.py:162
  23.2 0.7 %collective-permute-start.9 = (bf16[64,2048]{1,0:T(8,128)(2,1)S(1)}, bf16[64,2048]{1,0:T(8,128)(2,1)S(1)}, u32[]{:S(2)}, u32[]{:S(2)}) collective-permute-start(bf16[64,2048]{1,0:T(8,128)(2,1)S(1)} %pad_maximum_fusion), channel_id=1, source_target_pairs={{0,2},{1,3},{2,0},{3,1},{4,6},{5,7},{6,4},{7,5},{8,10},{9,11},{10,... | collective-permute-start | bytes 786440 | tf_op jit(solution)/shard_map/ppermute | solution.py:162
  23.9 0.3 collective-permute-start.6
  24.2 0.6 %collective-permute-start.11 = (bf16[32,2048]{1,0:T(8,128)(2,1)S(1)}, bf16[32,2048]{1,0:T(8,128)(2,1)S(1)}, u32[]{:S(2)}, u32[]{:S(2)}) collective-permute-start(bf16[32,2048]{1,0:T(8,128)(2,1)S(1)} %collective-permute-done.10), channel_id=1, source_target_pairs={{0,8},{4,12},{8,0},{12,4},{16,24},{20,28},{24,16},{28,20},{1,9},{5... | collective-permute-start | bytes 393224 | tf_op jit(solution)/shard_map/ppermute | solution.py:162
  24.8 1.0 %collective-permute-start.8 = (bf16[32,2048]{1,0:T(8,128)(2,1)S(1)}, bf16[32,2048]{1,0:T(8,128)(2,1)S(1)}, u32[]{:S(2)}, u32[]{:S(2)}) collective-permute-start(bf16[32,2048]{1,0:T(8,128)(2,1)S(1)} %slice.3), channel_id=1, source_target_pairs={{0,4},{4,0},{8,12},{12,8},{16,20},{20,16},{24,28},{28,24},{1,5},{5... | collective-permute-start | bytes 393224 | tf_op jit(solution)/shard_map/ppermute | solution.py:162
  25.8 1.2 %collective-permute-start.15 = (bf16[192,2048]{1,0:T(8,128)(2,1)S(1)}, bf16[192,2048]{1,0:T(8,128)(2,1)S(1)}, u32[]{:S(2)}, u32[]{:S(2)}) collective-permute-start(bf16[192,2048]{1,0:T(8,128)(2,1)S(1)} %constant_dynamic-update-slice_fusion.9.refs_3_), channel_id=1, source_target_pairs={{0,1},{1,0},{2,3},{3,2},{4,5},{5,4},{6,7},{7,6},{8,9},{9,8},{10,11... | collective-permute-start | bytes 2359304 | tf_op jit(solution)/shard_map/ppermute | solution.py:162
  27.1 2.0 %shard_map.87 = (f32[8,320,128]{2,1,0:T(8,128)S(1)}, f32[8,320,128]{2,1,0:T(8,128)S(1)}, f32[8,320,128]{2,1,0:T(8,128)S(1)}) custom-call(s32[3,128]{1,0:T(4,128)S(1)} %broadcast_in_dim.11.refs_0_, bf16[32,5120]{1,0:T(8,128)(2,1)S(1)} %copy-done, bf16[32,5120]{1,0:T(8,128)(2,1)S(1)} %bitcast.13, ...), custom_call_target="tpu_custom_call" | custom-call | flops 10066329600 | bytes 1572864 | tf_op jit(solution)/shard_map/pallas_call | solution.py:148
  29.1 2.4 %collective-permute-done.8 = bf16[32,2048]{1,0:T(8,128)(2,1)S(1)} collective-permute-done((bf16[32,2048]{1,0:T(8,128)(2,1)S(1)}, bf16[32,2048]{1,0:T(8,128)(2,1)S(1)}, u32[]{:S(2)}, u32[]{:S(2)}) %collective-permute-start.8) | collective-permute-done | bytes 131104 | tf_op jit(solution)/shard_map/ppermute | solution.py:162
  31.6 1.2 %collective-permute-start.14 = (bf16[160,2048]{1,0:T(8,128)(2,1)S(1)}, bf16[160,2048]{1,0:T(8,128)(2,1)S(1)}, u32[]{:S(2)}, u32[]{:S(2)}) collective-permute-start(bf16[160,2048]{1,0:T(8,128)(2,1)S(1)} %constant_dynamic-update-slice_fusion.13.refs_5_), channel_id=1, source_target_pairs={{0,1},{1,0},{2,3},{3,2},{4,5},{5,4},{6,7},{7,6},{8,9},{9,8},{10,11... | collective-permute-start | bytes 1966088 | tf_op jit(solution)/shard_map/ppermute | solution.py:162
  32.8 2.1 %shard_map.88 = (f32[8,320,128]{2,1,0:T(8,128)S(1)}, f32[8,320,128]{2,1,0:T(8,128)S(1)}, f32[8,320,128]{2,1,0:T(8,128)S(1)}) custom-call(s32[3,128]{1,0:T(4,128)S(1)} %broadcast_in_dim.11.refs_0_, bf16[32,5120]{1,0:T(8,128)(2,1)S(1)} %copy-done, bf16[32,5120]{1,0:T(8,128)(2,1)S(1)} %bitcast.14, ...), custom_call_target="tpu_custom_call" | custom-call | flops 10066329600 | bytes 1572864 | tf_op jit(solution)/shard_map/pallas_call | solution.py:148
  35.0 2.4 %shard_map.89 = (bf16[32,5120]{1,0:T(8,128)(2,1)}, bf16[32,5120]{1,0:T(8,128)(2,1)}) custom-call(s32[3,128]{1,0:T(4,128)S(1)} %broadcast_in_dim.11.refs_0_, bf16[32,5120]{1,0:T(8,128)(2,1)S(1)} %copy-done, bf16[32,5120]{1,0:T(8,128)(2,1)S(1)} %bitcast.15, bf16[160,2048]{1,0:T(8,128)(2,1)S(1)} %collective-permute-done.14.refs_3_, ...), custom_call_target="tpu_custom_call" | custom-call | flops 6710886400 | bytes 1048576 | tf_op jit(solution)/shard_map/pallas_call | solution.py:148
  (37 shorter events, 0.4 us)
Async XLA Ops:
  0.6 16.3 %copy-start.2 = (bf16[1,32,2048]{2,1,0:T(8,128)(2,1)S(1)}, bf16[1,32,2048]{2,1,0:T(8,128)(2,1)}, u32[]{:S(2)}) copy-start(bf16[1,32,2048]{2,1,0:T(8,128)(2,1)} %param.10) | copy-start | bytes 393220
  0.6 16.7 %copy-start.1 = (bf16[1,32,5120]{2,1,0:T(8,128)(2,1)S(1)}, bf16[1,32,5120]{2,1,0:T(8,128)(2,1)}, u32[]{:S(2)}) copy-start(bf16[1,32,5120]{2,1,0:T(8,128)(2,1)} %param.9) | copy-start | bytes 983044
  0.7 16.7 %copy-start = (bf16[32,5120]{1,0:T(8,128)(2,1)S(1)}, bf16[32,5120]{1,0:T(8,128)(2,1)}, u32[]{:S(2)}) copy-start(bf16[32,5120]{1,0:T(8,128)(2,1)} %refs_1_.7) | copy-start | bytes 983044
  0.7 9.8 %collective-permute-start = (bf16[32,2048]{1,0:T(8,128)(2,1)}, bf16[32,2048]{1,0:T(8,128)(2,1)S(1)}, u32[]{:S(2)}, u32[]{:S(2)}) collective-permute-start(bf16[32,2048]{1,0:T(8,128)(2,1)} %param.8), channel_id=1, source_target_pairs={{0,6},{1,7},{2,4},{3,5},{4,2},{5,3},{6,0},{7,1},{8,14},{9,15},{10,... | collective-permute-start | bytes 393224 | tf_op jit(solution)/shard_map/ppermute | solution.py:180
  3.7 6.8 %collective-permute-start.1 = (bf16[32,2048]{1,0:T(8,128)(2,1)}, bf16[32,2048]{1,0:T(8,128)(2,1)S(1)}, u32[]{:S(2)}, u32[]{:S(2)}) collective-permute-start(bf16[32,2048]{1,0:T(8,128)(2,1)} %param.8), channel_id=1, source_target_pairs={{0,24},{4,28},{8,16},{12,20},{16,8},{20,12},{24,0},{28,4},{1,25},{... | collective-permute-start | bytes 393224 | tf_op jit(solution)/shard_map/ppermute | solution.py:162
  7.0 6.4 %collective-permute-start.2 = (bf16[32,2048]{1,0:T(8,128)(2,1)}, bf16[32,2048]{1,0:T(8,128)(2,1)S(1)}, u32[]{:S(2)}, u32[]{:S(2)}) collective-permute-start(bf16[32,2048]{1,0:T(8,128)(2,1)} %param.8), channel_id=1, source_target_pairs={{0,8},{4,12},{8,0},{12,4},{16,24},{20,28},{24,16},{28,20},{1,9},{5... | collective-permute-start | bytes 393224 | tf_op jit(solution)/shard_map/ppermute | solution.py:162
  7.0 6.4 %collective-permute-start.3 = (bf16[32,2048]{1,0:T(8,128)(2,1)}, bf16[32,2048]{1,0:T(8,128)(2,1)S(1)}, u32[]{:S(2)}, u32[]{:S(2)}) collective-permute-start(bf16[32,2048]{1,0:T(8,128)(2,1)} %param.8), channel_id=1, source_target_pairs={{0,2},{1,3},{2,0},{3,1},{4,6},{5,7},{6,4},{7,5},{8,10},{9,11},{10,... | collective-permute-start | bytes 393224 | tf_op jit(solution)/shard_map/ppermute | solution.py:162
  7.3 6.2 %collective-permute-start.4 = (bf16[32,2048]{1,0:T(8,128)(2,1)}, bf16[32,2048]{1,0:T(8,128)(2,1)S(1)}, u32[]{:S(2)}, u32[]{:S(2)}) collective-permute-start(bf16[32,2048]{1,0:T(8,128)(2,1)} %param.8), channel_id=1, source_target_pairs={{0,4},{4,0},{8,12},{12,8},{16,20},{20,16},{24,28},{28,24},{1,5},{5... | collective-permute-start | bytes 393224 | tf_op jit(solution)/shard_map/ppermute | solution.py:162
  13.5 3.8 %collective-permute-start.5 = (bf16[32,2048]{1,0:T(8,128)(2,1)S(1)}, bf16[32,2048]{1,0:T(8,128)(2,1)S(1)}, u32[]{:S(2)}, u32[]{:S(2)}) collective-permute-start(bf16[32,2048]{1,0:T(8,128)(2,1)S(1)} %collective-permute-done.1), channel_id=1, source_target_pairs={{0,8},{4,12},{8,0},{12,4},{16,24},{20,28},{24,16},{28,20},{1,9},{5... | collective-permute-start | bytes 393224 | tf_op jit(solution)/shard_map/ppermute | solution.py:162
  14.4 5.8 %collective-permute-start.7 = (bf16[64,2048]{1,0:T(8,128)(2,1)S(1)}, bf16[64,2048]{1,0:T(8,128)(2,1)S(1)}, u32[]{:S(2)}, u32[]{:S(2)}) collective-permute-start(bf16[64,2048]{1,0:T(8,128)(2,1)S(1)} %get-tuple-element.73), channel_id=1, source_target_pairs={{0,2},{1,3},{2,0},{3,1},{4,6},{5,7},{6,4},{7,5},{8,10},{9,11},{10,... | collective-permute-start | bytes 786440 | tf_op jit(solution)/shard_map/ppermute | solution.py:162
  14.7 10.1 %collective-permute-start.12 = (bf16[64,2048]{1,0:T(8,128)(2,1)S(1)}, bf16[64,2048]{1,0:T(8,128)(2,1)S(1)}, u32[]{:S(2)}, u32[]{:S(2)}) collective-permute-start(bf16[64,2048]{1,0:T(8,128)(2,1)S(1)} %get-tuple-element.73), channel_id=1, source_target_pairs={{0,4},{4,0},{8,12},{12,8},{16,20},{20,16},{24,28},{28,24},{1,5},{5... | collective-permute-start | bytes 786440 | tf_op jit(solution)/shard_map/ppermute | solution.py:162
  14.9 9.3 %collective-permute-start.10 = (bf16[32,2048]{1,0:T(8,128)(2,1)S(1)}, bf16[32,2048]{1,0:T(8,128)(2,1)S(1)}, u32[]{:S(2)}, u32[]{:S(2)}) collective-permute-start(bf16[32,2048]{1,0:T(8,128)(2,1)S(1)} %collective-permute-done), channel_id=1, source_target_pairs={{0,24},{4,28},{8,16},{12,20},{16,8},{20,12},{24,0},{28,4},{1,25},{... | collective-permute-start | bytes 393224 | tf_op jit(solution)/shard_map/ppermute | solution.py:162
  20.1 5.7 %collective-permute-start.13 = (bf16[224,2048]{1,0:T(8,128)(2,1)S(1)}, bf16[224,2048]{1,0:T(8,128)(2,1)S(1)}, u32[]{:S(2)}, u32[]{:S(2)}) collective-permute-start(bf16[224,2048]{1,0:T(8,128)(2,1)S(1)} %constant_dynamic-update-slice_fusion.2.refs_3_), channel_id=1, source_target_pairs={{0,1},{1,0},{2,3},{3,2},{4,5},{5,4},{6,7},{7,6},{8,9},{9,8},{10,11... | collective-permute-start | bytes 2752520 | tf_op jit(solution)/shard_map/ppermute | solution.py:162
  23.2 8.4 %collective-permute-start.9 = (bf16[64,2048]{1,0:T(8,128)(2,1)S(1)}, bf16[64,2048]{1,0:T(8,128)(2,1)S(1)}, u32[]{:S(2)}, u32[]{:S(2)}) collective-permute-start(bf16[64,2048]{1,0:T(8,128)(2,1)S(1)} %pad_maximum_fusion), channel_id=1, source_target_pairs={{0,2},{1,3},{2,0},{3,1},{4,6},{5,7},{6,4},{7,5},{8,10},{9,11},{10,... | collective-permute-start | bytes 786440 | tf_op jit(solution)/shard_map/ppermute | solution.py:162
  23.9 5.2 %collective-permute-start.6 = (bf16[32,2048]{1,0:T(8,128)(2,1)S(1)}, bf16[32,2048]{1,0:T(8,128)(2,1)S(1)}, u32[]{:S(2)}, u32[]{:S(2)}) collective-permute-start(bf16[32,2048]{1,0:T(8,128)(2,1)S(1)} %collective-permute-done.5), channel_id=1, source_target_pairs={{0,4},{4,0},{8,12},{12,8},{16,20},{20,16},{24,28},{28,24},{1,5},{5... | collective-permute-start | bytes 393224 | tf_op jit(solution)/shard_map/ppermute | solution.py:162
  24.2 4.9 %collective-permute-start.11 = (bf16[32,2048]{1,0:T(8,128)(2,1)S(1)}, bf16[32,2048]{1,0:T(8,128)(2,1)S(1)}, u32[]{:S(2)}, u32[]{:S(2)}) collective-permute-start(bf16[32,2048]{1,0:T(8,128)(2,1)S(1)} %collective-permute-done.10), channel_id=1, source_target_pairs={{0,8},{4,12},{8,0},{12,4},{16,24},{20,28},{24,16},{28,20},{1,9},{5... | collective-permute-start | bytes 393224 | tf_op jit(solution)/shard_map/ppermute | solution.py:162
  24.8 6.8 %collective-permute-start.8 = (bf16[32,2048]{1,0:T(8,128)(2,1)S(1)}, bf16[32,2048]{1,0:T(8,128)(2,1)S(1)}, u32[]{:S(2)}, u32[]{:S(2)}) collective-permute-start(bf16[32,2048]{1,0:T(8,128)(2,1)S(1)} %slice.3), channel_id=1, source_target_pairs={{0,4},{4,0},{8,12},{12,8},{16,20},{20,16},{24,28},{28,24},{1,5},{5... | collective-permute-start | bytes 393224 | tf_op jit(solution)/shard_map/ppermute | solution.py:162
  25.8 7.0 %collective-permute-start.15 = (bf16[192,2048]{1,0:T(8,128)(2,1)S(1)}, bf16[192,2048]{1,0:T(8,128)(2,1)S(1)}, u32[]{:S(2)}, u32[]{:S(2)}) collective-permute-start(bf16[192,2048]{1,0:T(8,128)(2,1)S(1)} %constant_dynamic-update-slice_fusion.9.refs_3_), channel_id=1, source_target_pairs={{0,1},{1,0},{2,3},{3,2},{4,5},{5,4},{6,7},{7,6},{8,9},{9,8},{10,11... | collective-permute-start | bytes 2359304 | tf_op jit(solution)/shard_map/ppermute | solution.py:162
  31.6 3.3 %collective-permute-start.14 = (bf16[160,2048]{1,0:T(8,128)(2,1)S(1)}, bf16[160,2048]{1,0:T(8,128)(2,1)S(1)}, u32[]{:S(2)}, u32[]{:S(2)}) collective-permute-start(bf16[160,2048]{1,0:T(8,128)(2,1)S(1)} %constant_dynamic-update-slice_fusion.13.refs_5_), channel_id=1, source_target_pairs={{0,1},{1,0},{2,3},{3,2},{4,5},{5,4},{6,7},{7,6},{8,9},{9,8},{10,11... | collective-permute-start | bytes 1966088 | tf_op jit(solution)/shard_map/ppermute | solution.py:162

commit v15 on v14

--- a/solution.py
+++ b/solution.py
@@ -223,16 +223,23 @@
         state = absorb([(sides, 0, 6), (plane_sibling, 0, 6)], slots_of(near_here) + slots_of(here[:6], 1), state)
         sides_sibling = core(sides)
 
-        far_x, next_d, far_y, far_d, state = barrier((far_x, next_d, far_y, far_d, state))
-        rest = jnp.concatenate([far_x, next_d, far_y, far_d], axis=0)
+        far_x, far_y, far_d, state = barrier((far_x, far_y, far_d, state))
+        rest = jnp.concatenate([far_x, far_y, far_d], axis=0)
         rest_sibling = core(rest)
-        rest_here = [(2, 1, 0), (1, 1, 1), (2, 0, 1), 2, (2, 1, 1)]
+        rest_here = [(2, 1, 0), (2, 0, 1), 2, (2, 1, 1)]
         state = absorb(
-            [(plane_sibling, 6, 7), (sides_sibling, 0, 6), (rest, 0, 5)],
+            [(plane_sibling, 6, 7), (sides_sibling, 0, 6), (rest, 0, 4)],
             slots_of(here[6:] + near_here, 1) + slots_of(rest_here),
             state,
         )
-        trace_out, suffix_out = absorb([(rest_sibling, 0, 5)], slots_of(rest_here, 1), state, True)
+        next_d, state = barrier((next_d, state))
+        last = [(1, 1, 1)]
+        trace_out, suffix_out = absorb(
+            [(next_d, 0, 1), (rest_sibling, 0, 4), (core(next_d), 0, 1)],
+            slots_of(last) + slots_of(rest_here + last, 1),
+            state,
+            True,
+        )
     else:
         gathered = lax.all_gather(trace_key_value, ("ctx", "tp"), axis=0, tiled=True)
         suffix_all = lax.all_gather(suffix_own, "tp", axis=0, tiled=True)

time: 37.5 us -> 38.2 us (1.019)
  waiting for transfers between devices: 7.49 us -> 8.79 us
  starting transfers between devices: 18.1 us -> 17.5 us
    ppermute x15 -> x16, waiting for transfers between devices: 7.49 us -> 8.79 us  [swap(): return lax.ppermute(array, axis, [(i, i ^ bit) for i in range(size)])]
    ppermute x15 -> x16, starting transfers between devices: 15 us -> 14.4 us  [swap(): return lax.ppermute(array, axis, [(i, i ^ bit) for i in range(size)])]
    unnamed x18 -> x17, local copies, waits for them, and re-layouts: 1.12 us -> 1.11 us
  transfers between devices with their start and end apart: 16 -> 17, of which waited for: 4 -> 5; matrix products, arithmetic and copies ran while one was open for 3% -> 3% of each run, Pallas kernels for 14% -> 14%
where the time goes in v15:
time: 38.2 us; the launch traced here: 38 us
  starting transfers between devices  17.5 us (46%)
  waiting for transfers between devices  8.79 us (23%)
  Pallas kernels  7.61 us (20%)
  between operations  2.76 us (7%)
  local copies, waits for them, and re-layouts  1.22 us (3%)
    ppermute x16, starting transfers between devices, swap(): return lax.ppermute(array, axis, [(i, i ^ bit) for i in range(size)])  14.4 us
    ppermute x16, waiting for transfers between devices, swap(): return lax.ppermute(array, axis, [(i, i ^ bit) for i in range(size)])  8.79 us
    pallas_call x4, Pallas kernels, attend(): pl.pallas_call(functools.partial(attend_kernel, slots, ranges, tp_size, f...  7.61 us
    ppermute x1, starting transfers between devices, local(): lax.ppermute(a, ('ctx', 'tp'), [(i * tp_size + j, (i ^ 1) * tp_size + (j...  3.06 us
    unnamed x17, local copies, waits for them, and re-layouts  1.11 us
  transfers between devices with their start and end apart: 17, of which 5 were waited for; matrix products, arithmetic and copies ran while one was open for 3% of the time, Pallas kernels for 14%

profile of v15, /device:TPU:1, one launch (start us, length us, event | category | flops | bytes accessed | tf_op | source)
XLA Modules:
  0.0 38.0 jit_solution(14345765655562424263)
XLA Ops:
  0.7 3.1 %collective-permute-start = (bf16[32,2048]{1,0:T(8,128)(2,1)}, bf16[32,2048]{1,0:T(8,128)(2,1)S(1)}, u32[]{:S(2)}, u32[]{:S(2)}) collective-permute-start(bf16[32,2048]{1,0:T(8,128)(2,1)} %param.8), channel_id=1, source_target_pairs={{0,6},{1,7},{2,4},{3,5},{4,2},{5,3},{6,0},{7,1},{8,14},{9,15},{10,... | collective-permute-start | bytes 393224 | tf_op jit(solution)/shard_map/ppermute | solution.py:180
  3.7 3.3 %collective-permute-start.1 = (bf16[32,2048]{1,0:T(8,128)(2,1)}, bf16[32,2048]{1,0:T(8,128)(2,1)S(1)}, u32[]{:S(2)}, u32[]{:S(2)}) collective-permute-start(bf16[32,2048]{1,0:T(8,128)(2,1)} %param.8), channel_id=1, source_target_pairs={{0,24},{4,28},{8,16},{12,20},{16,8},{20,12},{24,0},{28,4},{1,25},{... | collective-permute-start | bytes 393224 | tf_op jit(solution)/shard_map/ppermute | solution.py:162
  7.3 0.3 collective-permute-start.4
  7.5 0.9 %constant_dynamic-update-slice_fusion.8 = bf16[224,2048]{1,0:T(8,128)(2,1)S(1)} fusion(bf16[32,2048]{1,0:T(8,128)(2,1)} %param.8), kind=kLoop, calls=%fused_computation.9 | loop fusion | bytes 262144
  10.5 2.9 %collective-permute-done.2 = bf16[32,2048]{1,0:T(8,128)(2,1)S(1)} collective-permute-done((bf16[32,2048]{1,0:T(8,128)(2,1)}, bf16[32,2048]{1,0:T(8,128)(2,1)S(1)}, u32[]{:S(2)}, u32[]{:S(2)}) %collective-permute-start.2) | collective-permute-done | bytes 131104 | tf_op jit(solution)/shard_map/ppermute | solution.py:162
  13.5 0.8 %collective-permute-start.6 = (bf16[32,2048]{1,0:T(8,128)(2,1)S(1)}, bf16[32,2048]{1,0:T(8,128)(2,1)S(1)}, u32[]{:S(2)}, u32[]{:S(2)}) collective-permute-start(bf16[32,2048]{1,0:T(8,128)(2,1)S(1)} %collective-permute-done.1), channel_id=1, source_target_pairs={{0,8},{4,12},{8,0},{12,4},{16,24},{20,28},{24,16},{28,20},{1,9},{5... | collective-permute-start | bytes 393224 | tf_op jit(solution)/shard_map/ppermute | solution.py:162
  14.4 0.3 collective-permute-start.5
  14.7 0.3 collective-permute-start.9
  14.9 2.0 %collective-permute-start.10 = (bf16[32,2048]{1,0:T(8,128)(2,1)S(1)}, bf16[32,2048]{1,0:T(8,128)(2,1)S(1)}, u32[]{:S(2)}, u32[]{:S(2)}) collective-permute-start(bf16[32,2048]{1,0:T(8,128)(2,1)S(1)} %collective-permute-done), channel_id=1, source_target_pairs={{0,24},{4,28},{8,16},{12,20},{16,8},{20,12},{24,0},{28,4},{1,25},{... | collective-permute-start | bytes 393224 | tf_op jit(solution)/shard_map/ppermute | solution.py:162
  16.9 0.4 %collective-permute-done.6 = bf16[32,2048]{1,0:T(8,128)(2,1)S(1)} collective-permute-done((bf16[32,2048]{1,0:T(8,128)(2,1)S(1)}, bf16[32,2048]{1,0:T(8,128)(2,1)S(1)}, u32[]{:S(2)}, u32[]{:S(2)}) %collective-permute-start.6) | collective-permute-done | bytes 131104 | tf_op jit(solution)/shard_map/ppermute | solution.py:162
  17.4 1.1 %shard_map.86 = (f32[8,320,128]{2,1,0:T(8,128)S(1)}, f32[8,320,128]{2,1,0:T(8,128)S(1)}, f32[8,320,128]{2,1,0:T(8,128)S(1)}) custom-call(s32[3,128]{1,0:T(4,128)S(1)} %broadcast_in_dim.11.refs_0_, bf16[32,5120]{1,0:T(8,128)(2,1)S(1)} %copy-done, bf16[32,5120]{1,0:T(8,128)(2,1)S(1)} %bitcast.12, bf16[224,2048]{1,0:T(8,128)(2,1)S(1)} %constant_dynamic-update-slice_fusion.2.refs_3_), custom_call_target="tpu_custom_call" | custom-call | flops 6710886400 | bytes 1048576 | tf_op jit(solution)/shard_map/pallas_call | solution.py:148
  18.5 1.7 %collective-permute-done.5 = bf16[64,2048]{1,0:T(8,128)(2,1)S(1)} collective-permute-done((bf16[64,2048]{1,0:T(8,128)(2,1)S(1)}, bf16[64,2048]{1,0:T(8,128)(2,1)S(1)}, u32[]{:S(2)}, u32[]{:S(2)}) %collective-permute-start.5) | collective-permute-done | bytes 262176 | tf_op jit(solution)/shard_map/ppermute | solution.py:162
  20.1 3.0 %collective-permute-start.8 = (bf16[224,2048]{1,0:T(8,128)(2,1)S(1)}, bf16[224,2048]{1,0:T(8,128)(2,1)S(1)}, u32[]{:S(2)}, u32[]{:S(2)}) collective-permute-start(bf16[224,2048]{1,0:T(8,128)(2,1)S(1)} %constant_dynamic-update-slice_fusion.2.refs_3_), channel_id=1, source_target_pairs={{0,1},{1,0},{2,3},{3,2},{4,5},{5,4},{6,7},{7,6},{8,9},{9,8},{10,11... | collective-permute-start | bytes 2752520 | tf_op jit(solution)/shard_map/ppermute | solution.py:162
  23.2 0.7 %collective-permute-start.13 = (bf16[64,2048]{1,0:T(8,128)(2,1)S(1)}, bf16[64,2048]{1,0:T(8,128)(2,1)S(1)}, u32[]{:S(2)}, u32[]{:S(2)}) collective-permute-start(bf16[64,2048]{1,0:T(8,128)(2,1)S(1)} %pad_maximum_fusion), channel_id=1, source_target_pairs={{0,2},{1,3},{2,0},{3,1},{4,6},{5,7},{6,4},{7,5},{8,10},{9,11},{10,... | collective-permute-start | bytes 786440 | tf_op jit(solution)/shard_map/ppermute | solution.py:162
  23.9 0.3 collective-permute-start.12
  24.2 0.6 %collective-permute-start.14 = (bf16[32,2048]{1,0:T(8,128)(2,1)S(1)}, bf16[32,2048]{1,0:T(8,128)(2,1)S(1)}, u32[]{:S(2)}, u32[]{:S(2)}) collective-permute-start(bf16[32,2048]{1,0:T(8,128)(2,1)S(1)} %collective-permute-done.10), channel_id=1, source_target_pairs={{0,8},{4,12},{8,0},{12,4},{16,24},{20,28},{24,16},{28,20},{1,9},{5... | collective-permute-start | bytes 393224 | tf_op jit(solution)/shard_map/ppermute | solution.py:162
  24.9 0.9 %collective-permute-start.11 = (bf16[192,2048]{1,0:T(8,128)(2,1)S(1)}, bf16[192,2048]{1,0:T(8,128)(2,1)S(1)}, u32[]{:S(2)}, u32[]{:S(2)}) collective-permute-start(bf16[192,2048]{1,0:T(8,128)(2,1)S(1)} %constant_dynamic-update-slice_fusion.9.refs_3_), channel_id=1, source_target_pairs={{0,1},{1,0},{2,3},{3,2},{4,5},{5,4},{6,7},{7,6},{8,9},{9,8},{10,11... | collective-permute-start | bytes 2359304 | tf_op jit(solution)/shard_map/ppermute | solution.py:162
  25.8 0.9 %collective-permute-start.7 = (bf16[32,2048]{1,0:T(8,128)(2,1)S(1)}, bf16[32,2048]{1,0:T(8,128)(2,1)S(1)}, u32[]{:S(2)}, u32[]{:S(2)}) collective-permute-start(bf16[32,2048]{1,0:T(8,128)(2,1)S(1)} %slice.3), channel_id=1, source_target_pairs={{0,4},{4,0},{8,12},{12,8},{16,20},{20,16},{24,28},{28,24},{1,5},{5... | collective-permute-start | bytes 393224 | tf_op jit(solution)/shard_map/ppermute | solution.py:162
  26.7 2.0 %shard_map.87 = (f32[8,320,128]{2,1,0:T(8,128)S(1)}, f32[8,320,128]{2,1,0:T(8,128)S(1)}, f32[8,320,128]{2,1,0:T(8,128)S(1)}) custom-call(s32[3,128]{1,0:T(4,128)S(1)} %broadcast_in_dim.11.refs_0_, bf16[32,5120]{1,0:T(8,128)(2,1)S(1)} %copy-done, bf16[32,5120]{1,0:T(8,128)(2,1)S(1)} %bitcast.13, ...), custom_call_target="tpu_custom_call" | custom-call | flops 10066329600 | bytes 1572864 | tf_op jit(solution)/shard_map/pallas_call | solution.py:148
  28.8 2.4 %collective-permute-done.13 = bf16[64,2048]{1,0:T(8,128)(2,1)S(1)} collective-permute-done((bf16[64,2048]{1,0:T(8,128)(2,1)S(1)}, bf16[64,2048]{1,0:T(8,128)(2,1)S(1)}, u32[]{:S(2)}, u32[]{:S(2)}) %collective-permute-start.13) | collective-permute-done | bytes 262176 | tf_op jit(solution)/shard_map/ppermute | solution.py:162
  31.3 0.8 %collective-permute-start.15 = (bf16[128,2048]{1,0:T(8,128)(2,1)S(1)}, bf16[128,2048]{1,0:T(8,128)(2,1)S(1)}, u32[]{:S(2)}, u32[]{:S(2)}) collective-permute-start(bf16[128,2048]{1,0:T(8,128)(2,1)S(1)} %constant_dynamic-update-slice_fusion.13.refs_5_), channel_id=1, source_target_pairs={{0,1},{1,0},{2,3},{3,2},{4,5},{5,4},{6,7},{7,6},{8,9},{9,8},{10,11... | collective-permute-start | bytes 1572872 | tf_op jit(solution)/shard_map/ppermute | solution.py:162
  32.1 2.1 %shard_map.88 = (f32[8,320,128]{2,1,0:T(8,128)S(1)}, f32[8,320,128]{2,1,0:T(8,128)S(1)}, f32[8,320,128]{2,1,0:T(8,128)S(1)}) custom-call(s32[3,128]{1,0:T(4,128)S(1)} %broadcast_in_dim.11.refs_0_, bf16[32,5120]{1,0:T(8,128)(2,1)S(1)} %copy-done, bf16[32,5120]{1,0:T(8,128)(2,1)S(1)} %bitcast.14, bf16[224,2048]{1,0:T(8,128)(2,1)S(1)} %collective-permute-done.8.refs_4_.refs_3_, ...), custom_call_target="tpu_custom_call" | custom-call | flops 10066329600 | bytes 1572864 | tf_op jit(solution)/shard_map/pallas_call | solution.py:148
  34.3 1.3 %collective-permute-done.16.refs_5_ = bf16[32,2048]{1,0:T(8,128)(2,1)S(1)} collective-permute-done((bf16[32,2048]{1,0:T(8,128)(2,1)S(1)}, bf16[32,2048]{1,0:T(8,128)(2,1)S(1)}, u32[]{:S(2)}, u32[]{:S(2)}) %collective-permute-start.16) | collective-permute-done | bytes 131104 | tf_op jit(solution)/shard_map/ppermute | solution.py:162
  35.6 2.4 %shard_map.89 = (bf16[32,5120]{1,0:T(8,128)(2,1)}, bf16[32,5120]{1,0:T(8,128)(2,1)}) custom-call(s32[3,128]{1,0:T(4,128)S(1)} %broadcast_in_dim.11.refs_0_, bf16[32,5120]{1,0:T(8,128)(2,1)S(1)} %copy-done, bf16[32,5120]{1,0:T(8,128)(2,1)S(1)} %bitcast.15, bf16[32,2048]{1,0:T(8,128)(2,1)S(1)} %collective-permute-done.7.refs_3_, ...), custom_call_target="tpu_custom_call" | custom-call | flops 6710886400 | bytes 1048576 | tf_op jit(solution)/shard_map/pallas_call | solution.py:148
  (38 shorter events, 0.7 us)
Async XLA Ops:
  0.6 16.3 %copy-start.2 = (bf16[1,32,2048]{2,1,0:T(8,128)(2,1)S(1)}, bf16[1,32,2048]{2,1,0:T(8,128)(2,1)}, u32[]{:S(2)}) copy-start(bf16[1,32,2048]{2,1,0:T(8,128)(2,1)} %param.10) | copy-start | bytes 393220
  0.6 16.7 %copy-start.1 = (bf16[1,32,5120]{2,1,0:T(8,128)(2,1)S(1)}, bf16[1,32,5120]{2,1,0:T(8,128)(2,1)}, u32[]{:S(2)}) copy-start(bf16[1,32,5120]{2,1,0:T(8,128)(2,1)} %param.9) | copy-start | bytes 983044
  0.7 16.7 %copy-start = (bf16[32,5120]{1,0:T(8,128)(2,1)S(1)}, bf16[32,5120]{1,0:T(8,128)(2,1)}, u32[]{:S(2)}) copy-start(bf16[32,5120]{1,0:T(8,128)(2,1)} %refs_1_.7) | copy-start | bytes 983044
  0.7 9.8 %collective-permute-start = (bf16[32,2048]{1,0:T(8,128)(2,1)}, bf16[32,2048]{1,0:T(8,128)(2,1)S(1)}, u32[]{:S(2)}, u32[]{:S(2)}) collective-permute-start(bf16[32,2048]{1,0:T(8,128)(2,1)} %param.8), channel_id=1, source_target_pairs={{0,6},{1,7},{2,4},{3,5},{4,2},{5,3},{6,0},{7,1},{8,14},{9,15},{10,... | collective-permute-start | bytes 393224 | tf_op jit(solution)/shard_map/ppermute | solution.py:180
  3.7 6.8 %collective-permute-start.1 = (bf16[32,2048]{1,0:T(8,128)(2,1)}, bf16[32,2048]{1,0:T(8,128)(2,1)S(1)}, u32[]{:S(2)}, u32[]{:S(2)}) collective-permute-start(bf16[32,2048]{1,0:T(8,128)(2,1)} %param.8), channel_id=1, source_target_pairs={{0,24},{4,28},{8,16},{12,20},{16,8},{20,12},{24,0},{28,4},{1,25},{... | collective-permute-start | bytes 393224 | tf_op jit(solution)/shard_map/ppermute | solution.py:162
  7.0 6.4 %collective-permute-start.2 = (bf16[32,2048]{1,0:T(8,128)(2,1)}, bf16[32,2048]{1,0:T(8,128)(2,1)S(1)}, u32[]{:S(2)}, u32[]{:S(2)}) collective-permute-start(bf16[32,2048]{1,0:T(8,128)(2,1)} %param.8), channel_id=1, source_target_pairs={{0,8},{4,12},{8,0},{12,4},{16,24},{20,28},{24,16},{28,20},{1,9},{5... | collective-permute-start | bytes 393224 | tf_op jit(solution)/shard_map/ppermute | solution.py:162
  7.0 6.4 %collective-permute-start.3 = (bf16[32,2048]{1,0:T(8,128)(2,1)}, bf16[32,2048]{1,0:T(8,128)(2,1)S(1)}, u32[]{:S(2)}, u32[]{:S(2)}) collective-permute-start(bf16[32,2048]{1,0:T(8,128)(2,1)} %param.8), channel_id=1, source_target_pairs={{0,2},{1,3},{2,0},{3,1},{4,6},{5,7},{6,4},{7,5},{8,10},{9,11},{10,... | collective-permute-start | bytes 393224 | tf_op jit(solution)/shard_map/ppermute | solution.py:162
  7.3 6.2 %collective-permute-start.4 = (bf16[32,2048]{1,0:T(8,128)(2,1)}, bf16[32,2048]{1,0:T(8,128)(2,1)S(1)}, u32[]{:S(2)}, u32[]{:S(2)}) collective-permute-start(bf16[32,2048]{1,0:T(8,128)(2,1)} %param.8), channel_id=1, source_target_pairs={{0,4},{4,0},{8,12},{12,8},{16,20},{20,16},{24,28},{28,24},{1,5},{5... | collective-permute-start | bytes 393224 | tf_op jit(solution)/shard_map/ppermute | solution.py:162
  13.5 3.8 %collective-permute-start.6 = (bf16[32,2048]{1,0:T(8,128)(2,1)S(1)}, bf16[32,2048]{1,0:T(8,128)(2,1)S(1)}, u32[]{:S(2)}, u32[]{:S(2)}) collective-permute-start(bf16[32,2048]{1,0:T(8,128)(2,1)S(1)} %collective-permute-done.1), channel_id=1, source_target_pairs={{0,8},{4,12},{8,0},{12,4},{16,24},{20,28},{24,16},{28,20},{1,9},{5... | collective-permute-start | bytes 393224 | tf_op jit(solution)/shard_map/ppermute | solution.py:162
  14.4 5.8 %collective-permute-start.5 = (bf16[64,2048]{1,0:T(8,128)(2,1)S(1)}, bf16[64,2048]{1,0:T(8,128)(2,1)S(1)}, u32[]{:S(2)}, u32[]{:S(2)}) collective-permute-start(bf16[64,2048]{1,0:T(8,128)(2,1)S(1)} %get-tuple-element.79), channel_id=1, source_target_pairs={{0,2},{1,3},{2,0},{3,1},{4,6},{5,7},{6,4},{7,5},{8,10},{9,11},{10,... | collective-permute-start | bytes 786440 | tf_op jit(solution)/shard_map/ppermute | solution.py:162
  14.7 10.1 %collective-permute-start.9 = (bf16[64,2048]{1,0:T(8,128)(2,1)S(1)}, bf16[64,2048]{1,0:T(8,128)(2,1)S(1)}, u32[]{:S(2)}, u32[]{:S(2)}) collective-permute-start(bf16[64,2048]{1,0:T(8,128)(2,1)S(1)} %get-tuple-element.79), channel_id=1, source_target_pairs={{0,4},{4,0},{8,12},{12,8},{16,20},{20,16},{24,28},{28,24},{1,5},{5... | collective-permute-start | bytes 786440 | tf_op jit(solution)/shard_map/ppermute | solution.py:162
  14.9 9.3 %collective-permute-start.10 = (bf16[32,2048]{1,0:T(8,128)(2,1)S(1)}, bf16[32,2048]{1,0:T(8,128)(2,1)S(1)}, u32[]{:S(2)}, u32[]{:S(2)}) collective-permute-start(bf16[32,2048]{1,0:T(8,128)(2,1)S(1)} %collective-permute-done), channel_id=1, source_target_pairs={{0,24},{4,28},{8,16},{12,20},{16,8},{20,12},{24,0},{28,4},{1,25},{... | collective-permute-start | bytes 393224 | tf_op jit(solution)/shard_map/ppermute | solution.py:162
  20.1 5.6 %collective-permute-start.8 = (bf16[224,2048]{1,0:T(8,128)(2,1)S(1)}, bf16[224,2048]{1,0:T(8,128)(2,1)S(1)}, u32[]{:S(2)}, u32[]{:S(2)}) collective-permute-start(bf16[224,2048]{1,0:T(8,128)(2,1)S(1)} %constant_dynamic-update-slice_fusion.2.refs_3_), channel_id=1, source_target_pairs={{0,1},{1,0},{2,3},{3,2},{4,5},{5,4},{6,7},{7,6},{8,9},{9,8},{10,11... | collective-permute-start | bytes 2752520 | tf_op jit(solution)/shard_map/ppermute | solution.py:162
  23.2 8.0 %collective-permute-start.13 = (bf16[64,2048]{1,0:T(8,128)(2,1)S(1)}, bf16[64,2048]{1,0:T(8,128)(2,1)S(1)}, u32[]{:S(2)}, u32[]{:S(2)}) collective-permute-start(bf16[64,2048]{1,0:T(8,128)(2,1)S(1)} %pad_maximum_fusion), channel_id=1, source_target_pairs={{0,2},{1,3},{2,0},{3,1},{4,6},{5,7},{6,4},{7,5},{8,10},{9,11},{10,... | collective-permute-start | bytes 786440 | tf_op jit(solution)/shard_map/ppermute | solution.py:162
  23.9 4.8 %collective-permute-start.12 = (bf16[32,2048]{1,0:T(8,128)(2,1)S(1)}, bf16[32,2048]{1,0:T(8,128)(2,1)S(1)}, u32[]{:S(2)}, u32[]{:S(2)}) collective-permute-start(bf16[32,2048]{1,0:T(8,128)(2,1)S(1)} %collective-permute-done.6), channel_id=1, source_target_pairs={{0,4},{4,0},{8,12},{12,8},{16,20},{20,16},{24,28},{28,24},{1,5},{5... | collective-permute-start | bytes 393224 | tf_op jit(solution)/shard_map/ppermute | solution.py:162
  24.2 4.6 %collective-permute-start.14 = (bf16[32,2048]{1,0:T(8,128)(2,1)S(1)}, bf16[32,2048]{1,0:T(8,128)(2,1)S(1)}, u32[]{:S(2)}, u32[]{:S(2)}) collective-permute-start(bf16[32,2048]{1,0:T(8,128)(2,1)S(1)} %collective-permute-done.10), channel_id=1, source_target_pairs={{0,8},{4,12},{8,0},{12,4},{16,24},{20,28},{24,16},{28,20},{1,9},{5... | collective-permute-start | bytes 393224 | tf_op jit(solution)/shard_map/ppermute | solution.py:162
  24.9 7.2 %collective-permute-start.11 = (bf16[192,2048]{1,0:T(8,128)(2,1)S(1)}, bf16[192,2048]{1,0:T(8,128)(2,1)S(1)}, u32[]{:S(2)}, u32[]{:S(2)}) collective-permute-start(bf16[192,2048]{1,0:T(8,128)(2,1)S(1)} %constant_dynamic-update-slice_fusion.9.refs_3_), channel_id=1, source_target_pairs={{0,1},{1,0},{2,3},{3,2},{4,5},{5,4},{6,7},{7,6},{8,9},{9,8},{10,11... | collective-permute-start | bytes 2359304 | tf_op jit(solution)/shard_map/ppermute | solution.py:162
  25.8 8.4 %collective-permute-start.7 = (bf16[32,2048]{1,0:T(8,128)(2,1)S(1)}, bf16[32,2048]{1,0:T(8,128)(2,1)S(1)}, u32[]{:S(2)}, u32[]{:S(2)}) collective-permute-start(bf16[32,2048]{1,0:T(8,128)(2,1)S(1)} %slice.3), channel_id=1, source_target_pairs={{0,4},{4,0},{8,12},{12,8},{16,20},{20,16},{24,28},{28,24},{1,5},{5... | collective-permute-start | bytes 393224 | tf_op jit(solution)/shard_map/ppermute | solution.py:162
  31.3 4.4 %collective-permute-start.15 = (bf16[128,2048]{1,0:T(8,128)(2,1)S(1)}, bf16[128,2048]{1,0:T(8,128)(2,1)S(1)}, u32[]{:S(2)}, u32[]{:S(2)}) collective-permute-start(bf16[128,2048]{1,0:T(8,128)(2,1)S(1)} %constant_dynamic-update-slice_fusion.13.refs_5_), channel_id=1, source_target_pairs={{0,1},{1,0},{2,3},{3,2},{4,5},{5,4},{6,7},{7,6},{8,9},{9,8},{10,11... | collective-permute-start | bytes 1572872 | tf_op jit(solution)/shard_map/ppermute | solution.py:162
  34.2 1.4 %collective-permute-start.16 = (bf16[32,2048]{1,0:T(8,128)(2,1)S(1)}, bf16[32,2048]{1,0:T(8,128)(2,1)S(1)}, u32[]{:S(2)}, u32[]{:S(2)}) collective-permute-start(bf16[32,2048]{1,0:T(8,128)(2,1)S(1)} %collective-permute-done.7.refs_3_), channel_id=1, source_target_pairs={{0,1},{1,0},{2,3},{3,2},{4,5},{5,4},{6,7},{7,6},{8,9},{9,8},{10,11... | collective-permute-start | bytes 393224 | tf_op jit(solution)/shard_map/ppermute | solution.py:162

commit v16 on v12

--- a/solution.py
+++ b/solution.py
@@ -210,12 +210,13 @@
         near_x, near_y = across_x(near), across_y(near)
         plane = jnp.concatenate([trace_key_value, own_x, own_y, own_d, near, suffix_own], axis=0)
         here = [(0, 0, 0), (0, 1, 0), (0, 0, 1), (0, 1, 1), (1, 0, 0), (3, 0, 0), 0]
+        far_y = across_y(jnp.concatenate([far, suffix_own], axis=0))
+        plane, far = barrier((plane, far))
         state = absorb([(plane, 0, 7)], slots_of(here), None)
         plane, state = barrier((plane, state))
         plane_sibling = core(plane)
 
-        near_x, near_y, far, third_d, state = barrier((near_x, near_y, far, third_d, state))
-        far_y = across_y(jnp.concatenate([far, suffix_own], axis=0))
+        near_x, near_y, third_d, state = barrier((near_x, near_y, third_d, state))
         far_x = across_x(jnp.concatenate([far, near_y[:rows]], axis=0))
         far_d = along_z(third_d, 1)
         sides = jnp.concatenate([near_x, near_y, far, third_d], axis=0)

time: 37.5 us -> 36.4 us (0.971)
  waiting for transfers between devices: 4.72 us -> 3.66 us
    ppermute x14, waiting for transfers between devices: 4.72 us -> 3.66 us  [swap(): return lax.ppermute(array, axis, [(i, i ^ bit) for i in range(size)])]
  transfers between devices with their start and end apart: 15 -> 15, of which waited for: 2 -> 3; matrix products, arithmetic and copies ran while one was open for 3% -> 3% of each run, Pallas kernels for 14% -> 15%
where the time goes in v16:
time: 36.4 us; the launch traced here: 36.3 us
  starting transfers between devices  20.8 us (57%)
  Pallas kernels  7.69 us (21%)
  waiting for transfers between devices  3.66 us (10%)
  between operations  2.76 us (8%)
  local copies, waits for them, and re-layouts  1.23 us (3%)
    ppermute x14, starting transfers between devices, swap(): return lax.ppermute(array, axis, [(i, i ^ bit) for i in range(size)])  17.8 us
    pallas_call x4, Pallas kernels, attend(): pl.pallas_call(functools.partial(attend_kernel, slots, ranges, tp_size, f...  7.69 us
    ppermute x14, waiting for transfers between devices, swap(): return lax.ppermute(array, axis, [(i, i ^ bit) for i in range(size)])  3.66 us
    ppermute x1, starting transfers between devices, local(): lax.ppermute(a, ('ctx', 'tp'), [(i * tp_size + j, (i ^ 1) * tp_size + (j...  3.06 us
    unnamed x17, local copies, waits for them, and re-layouts  1.12 us
  transfers between devices with their start and end apart: 15, of which 3 were waited for; matrix products, arithmetic and copies ran while one was open for 3% of the time, Pallas kernels for 15%

profile of v16, /device:TPU:1, one launch (start us, length us, event | category | flops | bytes accessed | tf_op | source)
XLA Modules:
  0.0 36.3 jit_solution(17028884246828661753)
XLA Ops:
  0.7 3.1 %collective-permute-start = (bf16[32,2048]{1,0:T(8,128)(2,1)}, bf16[32,2048]{1,0:T(8,128)(2,1)S(1)}, u32[]{:S(2)}, u32[]{:S(2)}) collective-permute-start(bf16[32,2048]{1,0:T(8,128)(2,1)} %param.8), channel_id=1, source_target_pairs={{0,6},{1,7},{2,4},{3,5},{4,2},{5,3},{6,0},{7,1},{8,14},{9,15},{10,... | collective-permute-start | bytes 393224 | tf_op jit(solution)/shard_map/ppermute | solution.py:180
  3.7 3.3 %collective-permute-start.1 = (bf16[32,2048]{1,0:T(8,128)(2,1)}, bf16[32,2048]{1,0:T(8,128)(2,1)S(1)}, u32[]{:S(2)}, u32[]{:S(2)}) collective-permute-start(bf16[32,2048]{1,0:T(8,128)(2,1)} %param.8), channel_id=1, source_target_pairs={{0,24},{4,28},{8,16},{12,20},{16,8},{20,12},{24,0},{28,4},{1,25},{... | collective-permute-start | bytes 393224 | tf_op jit(solution)/shard_map/ppermute | solution.py:162
  7.0 0.2 collective-permute-start.3
  7.3 0.3 collective-permute-start.4
  7.5 0.9 %constant_dynamic-update-slice_fusion.6 = bf16[224,2048]{1,0:T(8,128)(2,1)S(1)} fusion(bf16[32,2048]{1,0:T(8,128)(2,1)} %param.8), kind=kLoop, calls=%fused_computation.8 | loop fusion | bytes 262144
  10.4 0.1 add_bitcast_fusion
  10.5 2.9 %collective-permute-done.2 = bf16[32,2048]{1,0:T(8,128)(2,1)S(1)} collective-permute-done((bf16[32,2048]{1,0:T(8,128)(2,1)}, bf16[32,2048]{1,0:T(8,128)(2,1)S(1)}, u32[]{:S(2)}, u32[]{:S(2)}) %collective-permute-start.2) | collective-permute-done | bytes 131104 | tf_op jit(solution)/shard_map/ppermute | solution.py:162
  13.5 0.1 broadcast_in_dim.11.refs_0_
  13.5 0.8 %collective-permute-start.5 = (bf16[32,2048]{1,0:T(8,128)(2,1)S(1)}, bf16[32,2048]{1,0:T(8,128)(2,1)S(1)}, u32[]{:S(2)}, u32[]{:S(2)}) collective-permute-start(bf16[32,2048]{1,0:T(8,128)(2,1)S(1)} %collective-permute-done.1), channel_id=1, source_target_pairs={{0,8},{4,12},{8,0},{12,4},{16,24},{20,28},{24,16},{28,20},{1,9},{5... | collective-permute-start | bytes 393224 | tf_op jit(solution)/shard_map/ppermute | solution.py:162
  14.4 0.3 collective-permute-start.6
  14.7 0.2 collective-permute-start.7
  14.9 2.0 %collective-permute-start.8 = (bf16[32,2048]{1,0:T(8,128)(2,1)S(1)}, bf16[32,2048]{1,0:T(8,128)(2,1)S(1)}, u32[]{:S(2)}, u32[]{:S(2)}) collective-permute-start(bf16[32,2048]{1,0:T(8,128)(2,1)S(1)} %collective-permute-done), channel_id=1, source_target_pairs={{0,24},{4,28},{8,16},{12,20},{16,8},{20,12},{24,0},{28,4},{1,25},{... | collective-permute-start | bytes 393224 | tf_op jit(solution)/shard_map/ppermute | solution.py:162
  16.9 0.4 %collective-permute-done.5 = bf16[32,2048]{1,0:T(8,128)(2,1)S(1)} collective-permute-done((bf16[32,2048]{1,0:T(8,128)(2,1)S(1)}, bf16[32,2048]{1,0:T(8,128)(2,1)S(1)}, u32[]{:S(2)}, u32[]{:S(2)}) %collective-permute-start.5) | collective-permute-done | bytes 131104 | tf_op jit(solution)/shard_map/ppermute | solution.py:162
  17.4 1.1 %shard_map.86 = (f32[8,320,128]{2,1,0:T(8,128)S(1)}, f32[8,320,128]{2,1,0:T(8,128)S(1)}, f32[8,320,128]{2,1,0:T(8,128)S(1)}) custom-call(s32[3,128]{1,0:T(4,128)S(1)} %broadcast_in_dim.11.refs_0_, bf16[32,5120]{1,0:T(8,128)(2,1)S(1)} %copy-done, bf16[32,5120]{1,0:T(8,128)(2,1)S(1)} %bitcast.12, bf16[224,2048]{1,0:T(8,128)(2,1)S(1)} %constant_dynamic-update-slice_fusion.refs_3_), custom_call_target="tpu_custom_call" | custom-call | flops 6710886400 | bytes 1048576 | tf_op jit(solution)/shard_map/pallas_call | solution.py:148
  18.5 2.7 %collective-permute-start.12 = (bf16[224,2048]{1,0:T(8,128)(2,1)S(1)}, bf16[224,2048]{1,0:T(8,128)(2,1)S(1)}, u32[]{:S(2)}, u32[]{:S(2)}) collective-permute-start(bf16[224,2048]{1,0:T(8,128)(2,1)S(1)} %constant_dynamic-update-slice_fusion.refs_3_), channel_id=1, source_target_pairs={{0,1},{1,0},{2,3},{3,2},{4,5},{5,4},{6,7},{7,6},{8,9},{9,8},{10,11... | collective-permute-start | bytes 2752520 | tf_op jit(solution)/shard_map/ppermute | solution.py:162
  21.2 0.7 %collective-permute-start.10 = (bf16[64,2048]{1,0:T(8,128)(2,1)S(1)}, bf16[64,2048]{1,0:T(8,128)(2,1)S(1)}, u32[]{:S(2)}, u32[]{:S(2)}) collective-permute-start(bf16[64,2048]{1,0:T(8,128)(2,1)S(1)} %pad_maximum_fusion.1), channel_id=1, source_target_pairs={{0,2},{1,3},{2,0},{3,1},{4,6},{5,7},{6,4},{7,5},{8,10},{9,11},{10,... | collective-permute-start | bytes 786440 | tf_op jit(solution)/shard_map/ppermute | solution.py:162
  22.0 0.7 %collective-permute-start.9 = (bf16[64,2048]{1,0:T(8,128)(2,1)S(1)}, bf16[64,2048]{1,0:T(8,128)(2,1)S(1)}, u32[]{:S(2)}, u32[]{:S(2)}) collective-permute-start(bf16[64,2048]{1,0:T(8,128)(2,1)S(1)} %pad_maximum_fusion), channel_id=1, source_target_pairs={{0,4},{4,0},{8,12},{12,8},{16,20},{20,16},{24,28},{28,24},{1,5},{5... | collective-permute-start | bytes 786440 | tf_op jit(solution)/shard_map/ppermute | solution.py:162
  22.7 2.2 %collective-permute-start.11 = (bf16[32,2048]{1,0:T(8,128)(2,1)S(1)}, bf16[32,2048]{1,0:T(8,128)(2,1)S(1)}, u32[]{:S(2)}, u32[]{:S(2)}) collective-permute-start(bf16[32,2048]{1,0:T(8,128)(2,1)S(1)} %collective-permute-done.8), channel_id=1, source_target_pairs={{0,8},{4,12},{8,0},{12,4},{16,24},{20,28},{24,16},{28,20},{1,9},{5... | collective-permute-start | bytes 393224 | tf_op jit(solution)/shard_map/ppermute | solution.py:162
  25.0 2.1 %shard_map.87 = (f32[8,320,128]{2,1,0:T(8,128)S(1)}, f32[8,320,128]{2,1,0:T(8,128)S(1)}, f32[8,320,128]{2,1,0:T(8,128)S(1)}) custom-call(s32[3,128]{1,0:T(4,128)S(1)} %broadcast_in_dim.11.refs_0_, bf16[32,5120]{1,0:T(8,128)(2,1)S(1)} %copy-done, bf16[32,5120]{1,0:T(8,128)(2,1)S(1)} %bitcast.13, ...), custom_call_target="tpu_custom_call" | custom-call | flops 10066329600 | bytes 1572864 | tf_op jit(solution)/shard_map/pallas_call | solution.py:148
  27.0 1.9 %collective-permute-start.14 = (bf16[192,2048]{1,0:T(8,128)(2,1)S(1)}, bf16[192,2048]{1,0:T(8,128)(2,1)S(1)}, u32[]{:S(2)}, u32[]{:S(2)}) collective-permute-start(bf16[192,2048]{1,0:T(8,128)(2,1)S(1)} %constant_dynamic-update-slice_fusion.9.refs_3_), channel_id=1, source_target_pairs={{0,1},{1,0},{2,3},{3,2},{4,5},{5,4},{6,7},{7,6},{8,9},{9,8},{10,11... | collective-permute-start | bytes 2359304 | tf_op jit(solution)/shard_map/ppermute | solution.py:162
  28.9 0.2 collective-permute-done.10
  29.2 2.5 %collective-permute-start.13 = (bf16[160,2048]{1,0:T(8,128)(2,1)S(1)}, bf16[160,2048]{1,0:T(8,128)(2,1)S(1)}, u32[]{:S(2)}, u32[]{:S(2)}) collective-permute-start(bf16[160,2048]{1,0:T(8,128)(2,1)S(1)} %constant_dynamic-update-slice_fusion.13.refs_5_), channel_id=1, source_target_pairs={{0,1},{1,0},{2,3},{3,2},{4,5},{5,4},{6,7},{7,6},{8,9},{9,8},{10,11... | collective-permute-start | bytes 1966088 | tf_op jit(solution)/shard_map/ppermute | solution.py:162
  31.8 2.1 %shard_map.88 = (f32[8,320,128]{2,1,0:T(8,128)S(1)}, f32[8,320,128]{2,1,0:T(8,128)S(1)}, f32[8,320,128]{2,1,0:T(8,128)S(1)}) custom-call(s32[3,128]{1,0:T(4,128)S(1)} %broadcast_in_dim.11.refs_0_, bf16[32,5120]{1,0:T(8,128)(2,1)S(1)} %copy-done, bf16[32,5120]{1,0:T(8,128)(2,1)S(1)} %bitcast.14, ...), custom_call_target="tpu_custom_call" | custom-call | flops 10066329600 | bytes 1572864 | tf_op jit(solution)/shard_map/pallas_call | solution.py:148
  33.9 2.4 %shard_map.89 = (bf16[32,5120]{1,0:T(8,128)(2,1)}, bf16[32,5120]{1,0:T(8,128)(2,1)}) custom-call(s32[3,128]{1,0:T(4,128)S(1)} %broadcast_in_dim.11.refs_0_, bf16[32,5120]{1,0:T(8,128)(2,1)S(1)} %copy-done, bf16[32,5120]{1,0:T(8,128)(2,1)S(1)} %bitcast.15, bf16[160,2048]{1,0:T(8,128)(2,1)S(1)} %collective-permute-done.13.refs_3_, ...), custom_call_target="tpu_custom_call" | custom-call | flops 6710886400 | bytes 1048576 | tf_op jit(solution)/shard_map/pallas_call | solution.py:148
  (35 shorter events, 0.3 us)
Async XLA Ops:
  0.6 16.3 %copy-start.2 = (bf16[1,32,2048]{2,1,0:T(8,128)(2,1)S(1)}, bf16[1,32,2048]{2,1,0:T(8,128)(2,1)}, u32[]{:S(2)}) copy-start(bf16[1,32,2048]{2,1,0:T(8,128)(2,1)} %param.10) | copy-start | bytes 393220
  0.6 16.7 %copy-start.1 = (bf16[1,32,5120]{2,1,0:T(8,128)(2,1)S(1)}, bf16[1,32,5120]{2,1,0:T(8,128)(2,1)}, u32[]{:S(2)}) copy-start(bf16[1,32,5120]{2,1,0:T(8,128)(2,1)} %param.9) | copy-start | bytes 983044
  0.7 16.7 %copy-start = (bf16[32,5120]{1,0:T(8,128)(2,1)S(1)}, bf16[32,5120]{1,0:T(8,128)(2,1)}, u32[]{:S(2)}) copy-start(bf16[32,5120]{1,0:T(8,128)(2,1)} %refs_1_.7) | copy-start | bytes 983044
  0.7 9.8 %collective-permute-start = (bf16[32,2048]{1,0:T(8,128)(2,1)}, bf16[32,2048]{1,0:T(8,128)(2,1)S(1)}, u32[]{:S(2)}, u32[]{:S(2)}) collective-permute-start(bf16[32,2048]{1,0:T(8,128)(2,1)} %param.8), channel_id=1, source_target_pairs={{0,6},{1,7},{2,4},{3,5},{4,2},{5,3},{6,0},{7,1},{8,14},{9,15},{10,... | collective-permute-start | bytes 393224 | tf_op jit(solution)/shard_map/ppermute | solution.py:180
  3.7 6.8 %collective-permute-start.1 = (bf16[32,2048]{1,0:T(8,128)(2,1)}, bf16[32,2048]{1,0:T(8,128)(2,1)S(1)}, u32[]{:S(2)}, u32[]{:S(2)}) collective-permute-start(bf16[32,2048]{1,0:T(8,128)(2,1)} %param.8), channel_id=1, source_target_pairs={{0,24},{4,28},{8,16},{12,20},{16,8},{20,12},{24,0},{28,4},{1,25},{... | collective-permute-start | bytes 393224 | tf_op jit(solution)/shard_map/ppermute | solution.py:162
  7.0 6.4 %collective-permute-start.2 = (bf16[32,2048]{1,0:T(8,128)(2,1)}, bf16[32,2048]{1,0:T(8,128)(2,1)S(1)}, u32[]{:S(2)}, u32[]{:S(2)}) collective-permute-start(bf16[32,2048]{1,0:T(8,128)(2,1)} %param.8), channel_id=1, source_target_pairs={{0,8},{4,12},{8,0},{12,4},{16,24},{20,28},{24,16},{28,20},{1,9},{5... | collective-permute-start | bytes 393224 | tf_op jit(solution)/shard_map/ppermute | solution.py:162
  7.0 6.4 %collective-permute-start.3 = (bf16[32,2048]{1,0:T(8,128)(2,1)}, bf16[32,2048]{1,0:T(8,128)(2,1)S(1)}, u32[]{:S(2)}, u32[]{:S(2)}) collective-permute-start(bf16[32,2048]{1,0:T(8,128)(2,1)} %param.8), channel_id=1, source_target_pairs={{0,2},{1,3},{2,0},{3,1},{4,6},{5,7},{6,4},{7,5},{8,10},{9,11},{10,... | collective-permute-start | bytes 393224 | tf_op jit(solution)/shard_map/ppermute | solution.py:162
  7.3 6.2 %collective-permute-start.4 = (bf16[32,2048]{1,0:T(8,128)(2,1)}, bf16[32,2048]{1,0:T(8,128)(2,1)S(1)}, u32[]{:S(2)}, u32[]{:S(2)}) collective-permute-start(bf16[32,2048]{1,0:T(8,128)(2,1)} %param.8), channel_id=1, source_target_pairs={{0,4},{4,0},{8,12},{12,8},{16,20},{20,16},{24,28},{28,24},{1,5},{5... | collective-permute-start | bytes 393224 | tf_op jit(solution)/shard_map/ppermute | solution.py:162
  13.5 3.8 %collective-permute-start.5 = (bf16[32,2048]{1,0:T(8,128)(2,1)S(1)}, bf16[32,2048]{1,0:T(8,128)(2,1)S(1)}, u32[]{:S(2)}, u32[]{:S(2)}) collective-permute-start(bf16[32,2048]{1,0:T(8,128)(2,1)S(1)} %collective-permute-done.1), channel_id=1, source_target_pairs={{0,8},{4,12},{8,0},{12,4},{16,24},{20,28},{24,16},{28,20},{1,9},{5... | collective-permute-start | bytes 393224 | tf_op jit(solution)/shard_map/ppermute | solution.py:162
  14.4 7.5 %collective-permute-start.6 = (bf16[64,2048]{1,0:T(8,128)(2,1)S(1)}, bf16[64,2048]{1,0:T(8,128)(2,1)S(1)}, u32[]{:S(2)}, u32[]{:S(2)}) collective-permute-start(bf16[64,2048]{1,0:T(8,128)(2,1)S(1)} %get-tuple-element.81), channel_id=1, source_target_pairs={{0,4},{4,0},{8,12},{12,8},{16,20},{20,16},{24,28},{28,24},{1,5},{5... | collective-permute-start | bytes 786440 | tf_op jit(solution)/shard_map/ppermute | solution.py:162
  14.7 7.2 %collective-permute-start.7 = (bf16[64,2048]{1,0:T(8,128)(2,1)S(1)}, bf16[64,2048]{1,0:T(8,128)(2,1)S(1)}, u32[]{:S(2)}, u32[]{:S(2)}) collective-permute-start(bf16[64,2048]{1,0:T(8,128)(2,1)S(1)} %get-tuple-element.81), channel_id=1, source_target_pairs={{0,2},{1,3},{2,0},{3,1},{4,6},{5,7},{6,4},{7,5},{8,10},{9,11},{10,... | collective-permute-start | bytes 786440 | tf_op jit(solution)/shard_map/ppermute | solution.py:162
  14.9 7.0 %collective-permute-start.8 = (bf16[32,2048]{1,0:T(8,128)(2,1)S(1)}, bf16[32,2048]{1,0:T(8,128)(2,1)S(1)}, u32[]{:S(2)}, u32[]{:S(2)}) collective-permute-start(bf16[32,2048]{1,0:T(8,128)(2,1)S(1)} %collective-permute-done), channel_id=1, source_target_pairs={{0,24},{4,28},{8,16},{12,20},{16,8},{20,12},{24,0},{28,4},{1,25},{... | collective-permute-start | bytes 393224 | tf_op jit(solution)/shard_map/ppermute | solution.py:162
  18.5 6.5 %collective-permute-start.12 = (bf16[224,2048]{1,0:T(8,128)(2,1)S(1)}, bf16[224,2048]{1,0:T(8,128)(2,1)S(1)}, u32[]{:S(2)}, u32[]{:S(2)}) collective-permute-start(bf16[224,2048]{1,0:T(8,128)(2,1)S(1)} %constant_dynamic-update-slice_fusion.refs_3_), channel_id=1, source_target_pairs={{0,1},{1,0},{2,3},{3,2},{4,5},{5,4},{6,7},{7,6},{8,9},{9,8},{10,11... | collective-permute-start | bytes 2752520 | tf_op jit(solution)/shard_map/ppermute | solution.py:162
  21.2 8.0 %collective-permute-start.10 = (bf16[64,2048]{1,0:T(8,128)(2,1)S(1)}, bf16[64,2048]{1,0:T(8,128)(2,1)S(1)}, u32[]{:S(2)}, u32[]{:S(2)}) collective-permute-start(bf16[64,2048]{1,0:T(8,128)(2,1)S(1)} %pad_maximum_fusion.1), channel_id=1, source_target_pairs={{0,2},{1,3},{2,0},{3,1},{4,6},{5,7},{6,4},{7,5},{8,10},{9,11},{10,... | collective-permute-start | bytes 786440 | tf_op jit(solution)/shard_map/ppermute | solution.py:162
  22.0 7.2 %collective-permute-start.9 = (bf16[64,2048]{1,0:T(8,128)(2,1)S(1)}, bf16[64,2048]{1,0:T(8,128)(2,1)S(1)}, u32[]{:S(2)}, u32[]{:S(2)}) collective-permute-start(bf16[64,2048]{1,0:T(8,128)(2,1)S(1)} %pad_maximum_fusion), channel_id=1, source_target_pairs={{0,4},{4,0},{8,12},{12,8},{16,20},{20,16},{24,28},{28,24},{1,5},{5... | collective-permute-start | bytes 786440 | tf_op jit(solution)/shard_map/ppermute | solution.py:162
  22.7 6.2 %collective-permute-start.11 = (bf16[32,2048]{1,0:T(8,128)(2,1)S(1)}, bf16[32,2048]{1,0:T(8,128)(2,1)S(1)}, u32[]{:S(2)}, u32[]{:S(2)}) collective-permute-start(bf16[32,2048]{1,0:T(8,128)(2,1)S(1)} %collective-permute-done.8), channel_id=1, source_target_pairs={{0,8},{4,12},{8,0},{12,4},{16,24},{20,28},{24,16},{28,20},{1,9},{5... | collective-permute-start | bytes 393224 | tf_op jit(solution)/shard_map/ppermute | solution.py:162
  27.0 4.7 %collective-permute-start.14 = (bf16[192,2048]{1,0:T(8,128)(2,1)S(1)}, bf16[192,2048]{1,0:T(8,128)(2,1)S(1)}, u32[]{:S(2)}, u32[]{:S(2)}) collective-permute-start(bf16[192,2048]{1,0:T(8,128)(2,1)S(1)} %constant_dynamic-update-slice_fusion.9.refs_3_), channel_id=1, source_target_pairs={{0,1},{1,0},{2,3},{3,2},{4,5},{5,4},{6,7},{7,6},{8,9},{9,8},{10,11... | collective-permute-start | bytes 2359304 | tf_op jit(solution)/shard_map/ppermute | solution.py:162
  29.2 4.7 %collective-permute-start.13 = (bf16[160,2048]{1,0:T(8,128)(2,1)S(1)}, bf16[160,2048]{1,0:T(8,128)(2,1)S(1)}, u32[]{:S(2)}, u32[]{:S(2)}) collective-permute-start(bf16[160,2048]{1,0:T(8,128)(2,1)S(1)} %constant_dynamic-update-slice_fusion.13.refs_5_), channel_id=1, source_target_pairs={{0,1},{1,0},{2,3},{3,2},{4,5},{5,4},{6,7},{7,6},{8,9},{9,8},{10,11... | collective-permute-start | bytes 1966088 | tf_op jit(solution)/shard_map/ppermute | solution.py:162

commit v17 on v16

--- a/solution.py
+++ b/solution.py
@@ -213,11 +213,10 @@
         far_y = across_y(jnp.concatenate([far, suffix_own], axis=0))
         plane, far = barrier((plane, far))
         state = absorb([(plane, 0, 7)], slots_of(here), None)
-        plane, state = barrier((plane, state))
+        near_x, near_y, plane, state = barrier((near_x, near_y, plane, state))
         plane_sibling = core(plane)
-
-        near_x, near_y, third_d, state = barrier((near_x, near_y, third_d, state))
         far_x = across_x(jnp.concatenate([far, near_y[:rows]], axis=0))
+        third_d, plane_sibling = barrier((third_d, plane_sibling))
         far_d = along_z(third_d, 1)
         sides = jnp.concatenate([near_x, near_y, far, third_d], axis=0)
         near_here = [(1, 1, 0), (3, 1, 0), (1, 0, 1), (3, 0, 1), (2, 0, 0), (3, 1, 1)]

time: 36.4 us -> 39.9 us (1.096)
  waiting for transfers between devices: 3.66 us -> 8.46 us
  starting transfers between devices: 20.8 us -> 19.5 us
    ppermute x14, waiting for transfers between devices: 3.66 us -> 8.46 us  [swap(): return lax.ppermute(array, axis, [(i, i ^ bit) for i in range(size)])]
    ppermute x14, starting transfers between devices: 17.8 us -> 16.4 us  [swap(): return lax.ppermute(array, axis, [(i, i ^ bit) for i in range(size)])]
  transfers between devices with their start and end apart: 15 -> 15, of which waited for: 3 -> 6; matrix products, arithmetic and copies ran while one was open for 3% -> 3% of each run, Pallas kernels for 15% -> 13%
where the time goes in v17:
time: 39.9 us; the launch traced here: 39.7 us
  starting transfers between devices  19.5 us (49%)
  waiting for transfers between devices  8.46 us (21%)
  Pallas kernels  7.7 us (19%)
  between operations  2.75 us (7%)
  local copies, waits for them, and re-layouts  1.22 us (3%)
    ppermute x14, starting transfers between devices, swap(): return lax.ppermute(array, axis, [(i, i ^ bit) for i in range(size)])  16.4 us
    ppermute x14, waiting for transfers between devices, swap(): return lax.ppermute(array, axis, [(i, i ^ bit) for i in range(size)])  8.46 us
    pallas_call x4, Pallas kernels, attend(): pl.pallas_call(functools.partial(attend_kernel, slots, ranges, tp_size, f...  7.7 us
    ppermute x1, starting transfers between devices, local(): lax.ppermute(a, ('ctx', 'tp'), [(i * tp_size + j, (i ^ 1) * tp_size + (j...  3.06 us
    unnamed x17, local copies, waits for them, and re-layouts  1.12 us
  transfers between devices with their start and end apart: 15, of which 6 were waited for; matrix products, arithmetic and copies ran while one was open for 3% of the time, Pallas kernels for 13%

profile of v17, /device:TPU:1, one launch (start us, length us, event | category | flops | bytes accessed | tf_op | source)
XLA Modules:
  0.0 39.7 jit_solution(11792299851543236269)
XLA Ops:
  0.7 3.1 %collective-permute-start = (bf16[32,2048]{1,0:T(8,128)(2,1)}, bf16[32,2048]{1,0:T(8,128)(2,1)S(1)}, u32[]{:S(2)}, u32[]{:S(2)}) collective-permute-start(bf16[32,2048]{1,0:T(8,128)(2,1)} %param.8), channel_id=1, source_target_pairs={{0,6},{1,7},{2,4},{3,5},{4,2},{5,3},{6,0},{7,1},{8,14},{9,15},{10,... | collective-permute-start | bytes 393224 | tf_op jit(solution)/shard_map/ppermute | solution.py:180
  3.7 3.3 %collective-permute-start.1 = (bf16[32,2048]{1,0:T(8,128)(2,1)}, bf16[32,2048]{1,0:T(8,128)(2,1)S(1)}, u32[]{:S(2)}, u32[]{:S(2)}) collective-permute-start(bf16[32,2048]{1,0:T(8,128)(2,1)} %param.8), channel_id=1, source_target_pairs={{0,24},{4,28},{8,16},{12,20},{16,8},{20,12},{24,0},{28,4},{1,25},{... | collective-permute-start | bytes 393224 | tf_op jit(solution)/shard_map/ppermute | solution.py:162
  7.0 0.2 collective-permute-start.3
  7.3 0.3 collective-permute-start.4
  7.5 0.9 %constant_dynamic-update-slice_fusion.6 = bf16[224,2048]{1,0:T(8,128)(2,1)S(1)} fusion(bf16[32,2048]{1,0:T(8,128)(2,1)} %param.8), kind=kLoop, calls=%fused_computation.8 | loop fusion | bytes 262144
  10.5 2.9 %collective-permute-done.2 = bf16[32,2048]{1,0:T(8,128)(2,1)S(1)} collective-permute-done((bf16[32,2048]{1,0:T(8,128)(2,1)}, bf16[32,2048]{1,0:T(8,128)(2,1)S(1)}, u32[]{:S(2)}, u32[]{:S(2)}) %collective-permute-start.2) | collective-permute-done | bytes 131104 | tf_op jit(solution)/shard_map/ppermute | solution.py:162
  13.5 0.8 %collective-permute-start.5 = (bf16[32,2048]{1,0:T(8,128)(2,1)S(1)}, bf16[32,2048]{1,0:T(8,128)(2,1)S(1)}, u32[]{:S(2)}, u32[]{:S(2)}) collective-permute-start(bf16[32,2048]{1,0:T(8,128)(2,1)S(1)} %collective-permute-done.1), channel_id=1, source_target_pairs={{0,8},{4,12},{8,0},{12,4},{16,24},{20,28},{24,16},{28,20},{1,9},{5... | collective-permute-start | bytes 393224 | tf_op jit(solution)/shard_map/ppermute | solution.py:162
  14.4 0.3 collective-permute-start.6
  14.7 0.2 collective-permute-start.7
  14.9 2.0 %collective-permute-start.10 = (bf16[32,2048]{1,0:T(8,128)(2,1)S(1)}, bf16[32,2048]{1,0:T(8,128)(2,1)S(1)}, u32[]{:S(2)}, u32[]{:S(2)}) collective-permute-start(bf16[32,2048]{1,0:T(8,128)(2,1)S(1)} %collective-permute-done), channel_id=1, source_target_pairs={{0,24},{4,28},{8,16},{12,20},{16,8},{20,12},{24,0},{28,4},{1,25},{... | collective-permute-start | bytes 393224 | tf_op jit(solution)/shard_map/ppermute | solution.py:162
  16.9 0.4 %collective-permute-done.5 = bf16[32,2048]{1,0:T(8,128)(2,1)S(1)} collective-permute-done((bf16[32,2048]{1,0:T(8,128)(2,1)S(1)}, bf16[32,2048]{1,0:T(8,128)(2,1)S(1)}, u32[]{:S(2)}, u32[]{:S(2)}) %collective-permute-start.5) | collective-permute-done | bytes 131104 | tf_op jit(solution)/shard_map/ppermute | solution.py:162
  17.4 0.3 collective-permute-start.9
  17.7 1.1 %shard_map.86 = (f32[8,320,128]{2,1,0:T(8,128)S(1)}, f32[8,320,128]{2,1,0:T(8,128)S(1)}, f32[8,320,128]{2,1,0:T(8,128)S(1)}) custom-call(s32[3,128]{1,0:T(4,128)S(1)} %broadcast_in_dim.11.refs_0_, bf16[32,5120]{1,0:T(8,128)(2,1)S(1)} %copy-done, bf16[32,5120]{1,0:T(8,128)(2,1)S(1)} %bitcast.12, bf16[224,2048]{1,0:T(8,128)(2,1)S(1)} %constant_dynamic-update-slice_fusion.refs_3_), custom_call_target="tpu_custom_call" | custom-call | flops 6710886400 | bytes 1048576 | tf_op jit(solution)/shard_map/pallas_call | solution.py:148
  18.8 1.3 %collective-permute-done.6 = bf16[64,2048]{1,0:T(8,128)(2,1)S(1)} collective-permute-done((bf16[64,2048]{1,0:T(8,128)(2,1)S(1)}, bf16[64,2048]{1,0:T(8,128)(2,1)S(1)}, u32[]{:S(2)}, u32[]{:S(2)}) %collective-permute-start.6) | collective-permute-done | bytes 262176 | tf_op jit(solution)/shard_map/ppermute | solution.py:162
  20.2 6.0 %collective-permute-start.11 = (bf16[224,2048]{1,0:T(8,128)(2,1)S(1)}, bf16[224,2048]{1,0:T(8,128)(2,1)S(1)}, u32[]{:S(2)}, u32[]{:S(2)}) collective-permute-start(bf16[224,2048]{1,0:T(8,128)(2,1)S(1)} %constant_dynamic-update-slice_fusion.refs_3_), channel_id=1, source_target_pairs={{0,1},{1,0},{2,3},{3,2},{4,5},{5,4},{6,7},{7,6},{8,9},{9,8},{10,11... | collective-permute-start | bytes 2752520 | tf_op jit(solution)/shard_map/ppermute | solution.py:162
  26.3 1.3 %collective-permute-start.8 = (bf16[64,2048]{1,0:T(8,128)(2,1)S(1)}, bf16[64,2048]{1,0:T(8,128)(2,1)S(1)}, u32[]{:S(2)}, u32[]{:S(2)}) collective-permute-start(bf16[64,2048]{1,0:T(8,128)(2,1)S(1)} %pad_maximum_fusion), channel_id=1, source_target_pairs={{0,4},{4,0},{8,12},{12,8},{16,20},{20,16},{24,28},{28,24},{1,5},{5... | collective-permute-start | bytes 786440 | tf_op jit(solution)/shard_map/ppermute | solution.py:162
  27.6 0.7 %collective-permute-done.11.refs_4_.refs_3_ = bf16[224,2048]{1,0:T(8,128)(2,1)S(1)} collective-permute-done((bf16[224,2048]{1,0:T(8,128)(2,1)S(1)}, bf16[224,2048]{1,0:T(8,128)(2,1)S(1)}, u32[]{:S(2)}, u32[]{:S(2)}) %collective-permute-start.11) | collective-permute-done | bytes 917536 | tf_op jit(solution)/shard_map/ppermute | solution.py:162
  28.3 0.2 collective-permute-start.12
  28.5 2.1 %shard_map.87 = (f32[8,320,128]{2,1,0:T(8,128)S(1)}, f32[8,320,128]{2,1,0:T(8,128)S(1)}, f32[8,320,128]{2,1,0:T(8,128)S(1)}) custom-call(s32[3,128]{1,0:T(4,128)S(1)} %broadcast_in_dim.11.refs_0_, bf16[32,5120]{1,0:T(8,128)(2,1)S(1)} %copy-done, bf16[32,5120]{1,0:T(8,128)(2,1)S(1)} %bitcast.13, ...), custom_call_target="tpu_custom_call" | custom-call | flops 10066329600 | bytes 1572864 | tf_op jit(solution)/shard_map/pallas_call | solution.py:148
  30.6 0.7 %collective-permute-start.14 = (bf16[192,2048]{1,0:T(8,128)(2,1)S(1)}, bf16[192,2048]{1,0:T(8,128)(2,1)S(1)}, u32[]{:S(2)}, u32[]{:S(2)}) collective-permute-start(bf16[192,2048]{1,0:T(8,128)(2,1)S(1)} %constant_dynamic-update-slice_fusion.9.refs_3_), channel_id=1, source_target_pairs={{0,1},{1,0},{2,3},{3,2},{4,5},{5,4},{6,7},{7,6},{8,9},{9,8},{10,11... | collective-permute-start | bytes 2359304 | tf_op jit(solution)/shard_map/ppermute | solution.py:162
  31.3 2.9 %collective-permute-done.8 = bf16[64,2048]{1,0:T(8,128)(2,1)S(1)} collective-permute-done((bf16[64,2048]{1,0:T(8,128)(2,1)S(1)}, bf16[64,2048]{1,0:T(8,128)(2,1)S(1)}, u32[]{:S(2)}, u32[]{:S(2)}) %collective-permute-start.8) | collective-permute-done | bytes 262176 | tf_op jit(solution)/shard_map/ppermute | solution.py:162
  34.4 0.8 %collective-permute-start.13 = (bf16[160,2048]{1,0:T(8,128)(2,1)S(1)}, bf16[160,2048]{1,0:T(8,128)(2,1)S(1)}, u32[]{:S(2)}, u32[]{:S(2)}) collective-permute-start(bf16[160,2048]{1,0:T(8,128)(2,1)S(1)} %constant_dynamic-update-slice_fusion.13.refs_5_), channel_id=1, source_target_pairs={{0,1},{1,0},{2,3},{3,2},{4,5},{5,4},{6,7},{7,6},{8,9},{9,8},{10,11... | collective-permute-start | bytes 1966088 | tf_op jit(solution)/shard_map/ppermute | solution.py:162
  35.2 2.1 %shard_map.88 = (f32[8,320,128]{2,1,0:T(8,128)S(1)}, f32[8,320,128]{2,1,0:T(8,128)S(1)}, f32[8,320,128]{2,1,0:T(8,128)S(1)}) custom-call(s32[3,128]{1,0:T(4,128)S(1)} %broadcast_in_dim.11.refs_0_, bf16[32,5120]{1,0:T(8,128)(2,1)S(1)} %copy-done, bf16[32,5120]{1,0:T(8,128)(2,1)S(1)} %bitcast.14, ...), custom_call_target="tpu_custom_call" | custom-call | flops 10066329600 | bytes 1572864 | tf_op jit(solution)/shard_map/pallas_call | solution.py:148
  37.4 2.4 %shard_map.89 = (bf16[32,5120]{1,0:T(8,128)(2,1)}, bf16[32,5120]{1,0:T(8,128)(2,1)}) custom-call(s32[3,128]{1,0:T(4,128)S(1)} %broadcast_in_dim.11.refs_0_, bf16[32,5120]{1,0:T(8,128)(2,1)S(1)} %copy-done, bf16[32,5120]{1,0:T(8,128)(2,1)S(1)} %bitcast.15, bf16[160,2048]{1,0:T(8,128)(2,1)S(1)} %collective-permute-done.13.refs_3_, ...), custom_call_target="tpu_custom_call" | custom-call | flops 6710886400 | bytes 1048576 | tf_op jit(solution)/shard_map/pallas_call | solution.py:148
  (35 shorter events, 0.5 us)
Async XLA Ops:
  0.6 16.3 %copy-start.2 = (bf16[1,32,2048]{2,1,0:T(8,128)(2,1)S(1)}, bf16[1,32,2048]{2,1,0:T(8,128)(2,1)}, u32[]{:S(2)}) copy-start(bf16[1,32,2048]{2,1,0:T(8,128)(2,1)} %param.10) | copy-start | bytes 393220
  0.6 17.0 %copy-start.1 = (bf16[1,32,5120]{2,1,0:T(8,128)(2,1)S(1)}, bf16[1,32,5120]{2,1,0:T(8,128)(2,1)}, u32[]{:S(2)}) copy-start(bf16[1,32,5120]{2,1,0:T(8,128)(2,1)} %param.9) | copy-start | bytes 983044
  0.7 17.0 %copy-start = (bf16[32,5120]{1,0:T(8,128)(2,1)S(1)}, bf16[32,5120]{1,0:T(8,128)(2,1)}, u32[]{:S(2)}) copy-start(bf16[32,5120]{1,0:T(8,128)(2,1)} %refs_1_.7) | copy-start | bytes 983044
  0.7 9.8 %collective-permute-start = (bf16[32,2048]{1,0:T(8,128)(2,1)}, bf16[32,2048]{1,0:T(8,128)(2,1)S(1)}, u32[]{:S(2)}, u32[]{:S(2)}) collective-permute-start(bf16[32,2048]{1,0:T(8,128)(2,1)} %param.8), channel_id=1, source_target_pairs={{0,6},{1,7},{2,4},{3,5},{4,2},{5,3},{6,0},{7,1},{8,14},{9,15},{10,... | collective-permute-start | bytes 393224 | tf_op jit(solution)/shard_map/ppermute | solution.py:180
  3.7 6.8 %collective-permute-start.1 = (bf16[32,2048]{1,0:T(8,128)(2,1)}, bf16[32,2048]{1,0:T(8,128)(2,1)S(1)}, u32[]{:S(2)}, u32[]{:S(2)}) collective-permute-start(bf16[32,2048]{1,0:T(8,128)(2,1)} %param.8), channel_id=1, source_target_pairs={{0,24},{4,28},{8,16},{12,20},{16,8},{20,12},{24,0},{28,4},{1,25},{... | collective-permute-start | bytes 393224 | tf_op jit(solution)/shard_map/ppermute | solution.py:162
  7.0 6.4 %collective-permute-start.2 = (bf16[32,2048]{1,0:T(8,128)(2,1)}, bf16[32,2048]{1,0:T(8,128)(2,1)S(1)}, u32[]{:S(2)}, u32[]{:S(2)}) collective-permute-start(bf16[32,2048]{1,0:T(8,128)(2,1)} %param.8), channel_id=1, source_target_pairs={{0,8},{4,12},{8,0},{12,4},{16,24},{20,28},{24,16},{28,20},{1,9},{5... | collective-permute-start | bytes 393224 | tf_op jit(solution)/shard_map/ppermute | solution.py:162
  7.0 6.4 %collective-permute-start.3 = (bf16[32,2048]{1,0:T(8,128)(2,1)}, bf16[32,2048]{1,0:T(8,128)(2,1)S(1)}, u32[]{:S(2)}, u32[]{:S(2)}) collective-permute-start(bf16[32,2048]{1,0:T(8,128)(2,1)} %param.8), channel_id=1, source_target_pairs={{0,2},{1,3},{2,0},{3,1},{4,6},{5,7},{6,4},{7,5},{8,10},{9,11},{10,... | collective-permute-start | bytes 393224 | tf_op jit(solution)/shard_map/ppermute | solution.py:162
  7.3 6.2 %collective-permute-start.4 = (bf16[32,2048]{1,0:T(8,128)(2,1)}, bf16[32,2048]{1,0:T(8,128)(2,1)S(1)}, u32[]{:S(2)}, u32[]{:S(2)}) collective-permute-start(bf16[32,2048]{1,0:T(8,128)(2,1)} %param.8), channel_id=1, source_target_pairs={{0,4},{4,0},{8,12},{12,8},{16,20},{20,16},{24,28},{28,24},{1,5},{5... | collective-permute-start | bytes 393224 | tf_op jit(solution)/shard_map/ppermute | solution.py:162
  13.5 3.8 %collective-permute-start.5 = (bf16[32,2048]{1,0:T(8,128)(2,1)S(1)}, bf16[32,2048]{1,0:T(8,128)(2,1)S(1)}, u32[]{:S(2)}, u32[]{:S(2)}) collective-permute-start(bf16[32,2048]{1,0:T(8,128)(2,1)S(1)} %collective-permute-done.1), channel_id=1, source_target_pairs={{0,8},{4,12},{8,0},{12,4},{16,24},{20,28},{24,16},{28,20},{1,9},{5... | collective-permute-start | bytes 393224 | tf_op jit(solution)/shard_map/ppermute | solution.py:162
  14.4 5.8 %collective-permute-start.6 = (bf16[64,2048]{1,0:T(8,128)(2,1)S(1)}, bf16[64,2048]{1,0:T(8,128)(2,1)S(1)}, u32[]{:S(2)}, u32[]{:S(2)}) collective-permute-start(bf16[64,2048]{1,0:T(8,128)(2,1)S(1)} %get-tuple-element.77), channel_id=1, source_target_pairs={{0,4},{4,0},{8,12},{12,8},{16,20},{20,16},{24,28},{28,24},{1,5},{5... | collective-permute-start | bytes 786440 | tf_op jit(solution)/shard_map/ppermute | solution.py:162
  14.7 5.5 %collective-permute-start.7 = (bf16[64,2048]{1,0:T(8,128)(2,1)S(1)}, bf16[64,2048]{1,0:T(8,128)(2,1)S(1)}, u32[]{:S(2)}, u32[]{:S(2)}) collective-permute-start(bf16[64,2048]{1,0:T(8,128)(2,1)S(1)} %get-tuple-element.77), channel_id=1, source_target_pairs={{0,2},{1,3},{2,0},{3,1},{4,6},{5,7},{6,4},{7,5},{8,10},{9,11},{10,... | collective-permute-start | bytes 786440 | tf_op jit(solution)/shard_map/ppermute | solution.py:162
  14.9 12.7 %collective-permute-start.10 = (bf16[32,2048]{1,0:T(8,128)(2,1)S(1)}, bf16[32,2048]{1,0:T(8,128)(2,1)S(1)}, u32[]{:S(2)}, u32[]{:S(2)}) collective-permute-start(bf16[32,2048]{1,0:T(8,128)(2,1)S(1)} %collective-permute-done), channel_id=1, source_target_pairs={{0,24},{4,28},{8,16},{12,20},{16,8},{20,12},{24,0},{28,4},{1,25},{... | collective-permute-start | bytes 393224 | tf_op jit(solution)/shard_map/ppermute | solution.py:162
  17.4 14.0 %collective-permute-start.9 = (bf16[64,2048]{1,0:T(8,128)(2,1)S(1)}, bf16[64,2048]{1,0:T(8,128)(2,1)S(1)}, u32[]{:S(2)}, u32[]{:S(2)}) collective-permute-start(bf16[64,2048]{1,0:T(8,128)(2,1)S(1)} %pad_maximum_fusion.1), channel_id=1, source_target_pairs={{0,2},{1,3},{2,0},{3,1},{4,6},{5,7},{6,4},{7,5},{8,10},{9,11},{10,... | collective-permute-start | bytes 786440 | tf_op jit(solution)/shard_map/ppermute | solution.py:162
  20.2 8.1 %collective-permute-start.11 = (bf16[224,2048]{1,0:T(8,128)(2,1)S(1)}, bf16[224,2048]{1,0:T(8,128)(2,1)S(1)}, u32[]{:S(2)}, u32[]{:S(2)}) collective-permute-start(bf16[224,2048]{1,0:T(8,128)(2,1)S(1)} %constant_dynamic-update-slice_fusion.refs_3_), channel_id=1, source_target_pairs={{0,1},{1,0},{2,3},{3,2},{4,5},{5,4},{6,7},{7,6},{8,9},{9,8},{10,11... | collective-permute-start | bytes 2752520 | tf_op jit(solution)/shard_map/ppermute | solution.py:162
  26.3 8.0 %collective-permute-start.8 = (bf16[64,2048]{1,0:T(8,128)(2,1)S(1)}, bf16[64,2048]{1,0:T(8,128)(2,1)S(1)}, u32[]{:S(2)}, u32[]{:S(2)}) collective-permute-start(bf16[64,2048]{1,0:T(8,128)(2,1)S(1)} %pad_maximum_fusion), channel_id=1, source_target_pairs={{0,4},{4,0},{8,12},{12,8},{16,20},{20,16},{24,28},{28,24},{1,5},{5... | collective-permute-start | bytes 786440 | tf_op jit(solution)/shard_map/ppermute | solution.py:162
  28.3 5.9 %collective-permute-start.12 = (bf16[32,2048]{1,0:T(8,128)(2,1)S(1)}, bf16[32,2048]{1,0:T(8,128)(2,1)S(1)}, u32[]{:S(2)}, u32[]{:S(2)}) collective-permute-start(bf16[32,2048]{1,0:T(8,128)(2,1)S(1)} %collective-permute-done.10), channel_id=1, source_target_pairs={{0,8},{4,12},{8,0},{12,4},{16,24},{20,28},{24,16},{28,20},{1,9},{5... | collective-permute-start | bytes 393224 | tf_op jit(solution)/shard_map/ppermute | solution.py:162
  30.6 4.6 %collective-permute-start.14 = (bf16[192,2048]{1,0:T(8,128)(2,1)S(1)}, bf16[192,2048]{1,0:T(8,128)(2,1)S(1)}, u32[]{:S(2)}, u32[]{:S(2)}) collective-permute-start(bf16[192,2048]{1,0:T(8,128)(2,1)S(1)} %constant_dynamic-update-slice_fusion.9.refs_3_), channel_id=1, source_target_pairs={{0,1},{1,0},{2,3},{3,2},{4,5},{5,4},{6,7},{7,6},{8,9},{9,8},{10,11... | collective-permute-start | bytes 2359304 | tf_op jit(solution)/shard_map/ppermute | solution.py:162
  34.4 3.0 %collective-permute-start.13 = (bf16[160,2048]{1,0:T(8,128)(2,1)S(1)}, bf16[160,2048]{1,0:T(8,128)(2,1)S(1)}, u32[]{:S(2)}, u32[]{:S(2)}) collective-permute-start(bf16[160,2048]{1,0:T(8,128)(2,1)S(1)} %constant_dynamic-update-slice_fusion.13.refs_5_), channel_id=1, source_target_pairs={{0,1},{1,0},{2,3},{3,2},{4,5},{5,4},{6,7},{7,6},{8,9},{9,8},{10,11... | collective-permute-start | bytes 1966088 | tf_op jit(solution)/shard_map/ppermute | solution.py:162
